TPU v7x, 512 devices: a whole 4x8x8 slice. The times are simulated.
512 devices in a mesh: dp: 32 (over z, x_hi, core), sub: 16 (over x_lo, y).
Axes of the slice: x: 4 (x_hi: 2, x_lo: 2; x = x_hi * 2 + x_lo), y: 8, z: 8, core: 2. Of those that a mesh axis runs over, the one named last changes fastest.
Arguments:
- samples: bfloat16 [65536, 1024], P(('dp', 'sub')), may hold values from -12 to 12
- rotation: bfloat16 [1024, 1024], P(None, 'sub'), may hold values from -0.1875 to 0.1875
- codebook: float32 [16, 256, 64], P('sub'), may hold values from -4 to 4
Outputs:
- recon: bfloat16 [65536, 1024], P(('dp', 'sub'))
- new_codebook: float32 [16, 256, 64], P('sub')
- cross: float32 [1024, 1024], P(('dp', 'sub'))
All inputs are finite; a program needn't handle non-finite values.
Results may differ from a plain program's by a relative error of at most 0.02.
Values may be sent and summed in bfloat16 or wider, within the bound.
No kernel may reach another device: no remote copies, remote signals or barrier semaphores. Data moves between devices by JAX's collectives and lax.ppermute only.
A program may use at most 64 MiB of HBM per device.

v0:
```python
import jax
import jax.numpy as jnp
from jax import lax
from jax.sharding import PartitionSpec as P


def per_device(samples, rotation, codebook):
    full_rotation = lax.all_gather(rotation, "sub", axis=1, tiled=True)
    rotated = jnp.dot(samples, full_rotation, preferred_element_type=jnp.float32).astype(
        jnp.bfloat16
    )
    grouped = lax.all_to_all(rotated, "sub", split_axis=1, concat_axis=0, tiled=True)
    group_rows = grouped.shape[0]
    sub_width = grouped.shape[1]
    code_count = codebook.shape[1]
    block_rows = min(2048, group_rows)
    count_blocks = group_rows // block_rows
    codes_low = codebook[0].astype(jnp.bfloat16)
    code_square = jnp.sum(codebook[0] * codebook[0], axis=-1)

    def assign(carry, block):
        sums, counts = carry
        inner = lax.dot_general(
            block, codes_low, (((1,), (1,)), ((), ())), preferred_element_type=jnp.float32
        )
        block_wide = block.astype(jnp.float32)
        row_square = jnp.sum(block_wide * block_wide, axis=-1, keepdims=True)
        logits = -0.125 * (row_square - 2.0 * inner + code_square[None])
        weights = jax.nn.softmax(logits, axis=-1).astype(jnp.bfloat16)
        rebuilt = jnp.dot(weights, codes_low, preferred_element_type=jnp.float32).astype(
            jnp.bfloat16
        )
        sums = sums + lax.dot_general(
            weights, block, (((0,), (0,)), ((), ())), preferred_element_type=jnp.float32
        )
        counts = counts + jnp.sum(weights.astype(jnp.float32), axis=0)
        return ((sums, counts), rebuilt)

    start = (jnp.zeros((code_count, sub_width), jnp.float32), jnp.zeros((code_count,), jnp.float32))
    (sums, counts), rebuilt = lax.scan(
        assign, start, grouped.reshape(count_blocks, block_rows, sub_width)
    )
    rebuilt = rebuilt.reshape(group_rows, sub_width)
    recon = lax.all_to_all(rebuilt, "sub", split_axis=0, concat_axis=1, tiled=True)
    cross = lax.psum_scatter(
        lax.dot_general(
            samples, recon, (((0,), (0,)), ((), ())), preferred_element_type=jnp.float32
        ),
        ("dp", "sub"),
        scatter_dimension=0,
        tiled=True,
    )
    sums, counts = (
        lax.psum(sums.astype(jnp.bfloat16), "dp").astype(jnp.float32),
        lax.psum(counts.astype(jnp.bfloat16), "dp").astype(jnp.float32),
    )
    new_codes = (sums + codebook[0]) / (counts[:, None] + 1.0)
    return (recon, new_codes[None], cross)


def solution(mesh):
    in_specs = (P(("dp", "sub"), None), P(None, "sub"), P("sub", None, None))
    out_specs = (P(("dp", "sub"), None), P("sub", None, None), P(("dp", "sub"), None))
    return jax.shard_map(
        per_device, mesh=mesh, in_specs=in_specs, out_specs=out_specs, check_vma=False
    )
```

profile of v0, /device:TPU:1, one launch (start us, length us, event | category | flops | bytes accessed | tf_op | source)
XLA Modules:
  0.0 422.8 jit_solution(10128244937608133555)
XLA Ops:
  7.2 0.0 copy-start
  7.2 0.0 copy-start.4
  7.2 0.0 all-gather.2.cloned.1.call-start
  7.2 0.7 all-gather.2.cloned.1.call-update
  7.9 72.2 %all-gather.2.cloned.1.call-done = bf16[1024,1024]{0,1:T(8,128)(2,1)} async-done(((bf16[1024,64]{0,1:T(8,128)(2,1)}), bf16[1024,1024]{0,1:T(8,128)(2,1)}) %all-gather.2.cloned.1.call-update) | async-done | bytes 2097168 | tf_op jit(solution)/shard_map/all_gather | solution.py:8
  80.1 0.0 copy-done
  80.1 2.4 convolution_convert_fusion
  82.5 0.8 copy.30
  83.4 4.7 %all-to-all-start = ((bf16[128,16,64]{0,2,1:T(8,128)(2,1)}), bf16[128,16,64]{0,2,1:T(8,128)(2,1)S(1)}, u32[]{:S(2)}, u32[]{:S(2)}) async-start(bf16[128,16,64]{0,2,1:T(8,128)(2,1)} %bitcast), calls=%async_computation | async-start | bytes 524288 | tf_op jit(solution)/shard_map/all_to_all | solution.py:12
  88.1 0.0 all-reduce.4.cloned.1.call-start
  88.2 0.0 copy-done.4
  88.2 0.1 copy.33
  88.3 0.0 copy-start.2
  88.3 0.1 multiply_reduce_fusion.1
  88.4 7.5 %all-to-all-done = bf16[128,16,64]{0,2,1:T(8,128)(2,1)S(1)} async-done(((bf16[128,16,64]{0,2,1:T(8,128)(2,1)}), bf16[128,16,64]{0,2,1:T(8,128)(2,1)S(1)}, u32[]{:S(2)}, u32[]{:S(2)}) %all-to-all-start) | async-done | bytes 262176 | tf_op jit(solution)/shard_map/all_to_all | solution.py:12
  95.9 0.1 multiply_reduce_fusion
  96.0 2.1 fusion.11
  98.1 0.0 copy-done.2
  98.1 3.9 online-softmax
  102.0 1.3 convert_element_type.42
  103.3 0.2 copy.34
  103.5 11.6 %all_to_all.35 = bf16[16,128,64]{1,2,0:T(8,128)(2,1)S(1)} all-to-all(bf16[16,128,64]{1,2,0:T(8,128)(2,1)S(1)} %copy.34), channel_id=1, replica_groups=mesh['dp'=32,'sub'=16] {'sub'}, dimensions={0} | all-to-all | bytes 524288 | tf_op jit(solution)/shard_map/all_to_all | solution.py:44
  115.1 2.7 convolution_bitcast_fusion
  117.8 0.0 copy-start.1
  117.8 0.0 all-reduce.4.cloned.1.call-update
  117.8 1.6 copy-done.1
  119.4 0.6 fusion.3
  120.0 0.0 copy-start.3
  120.0 0.7 fusion.10
  120.8 0.3 convolution_convert_fusion.1
  121.1 0.1 copy.35
  121.2 135.8 %all-reduce.1 = (bf16[256,64]{1,0:T(8,128)(2,1)S(1)}, bf16[256]{0:T(256)(128)(2,1)S(1)}) all-reduce(bf16[256,64]{1,0:T(8,128)(2,1)S(1)} %copy.35, bf16[256]{0:T(256)(128)(2,1)S(1)} %get-tuple-element.38), channel_id=1, replica_groups=mesh['dp'=32,'sub'=16] {'dp'}, use_global_device_ids=true, to_apply=%region_4.0 | all-reduce | flops 16640 | bytes 66560 | tf_op jit(solution)/shard_map/psum | solution.py:54
  257.0 0.0 copy-done.3
  257.0 0.1 divide_bitcast_fusion
  257.1 0.7 copy.37
  257.8 0.8 copy.36
  258.7 155.3 %all-reduce.4.cloned.1.call-done = f32[1024,1024]{0,1:T(8,128)} async-done(((f32[1024,1024]{0,1:T(8,128)}), f32[1024,1024]{0,1:T(8,128)}) %all-reduce.4.cloned.1.call-update) | async-done | bytes 4194320
  413.9 1.2 constant_dynamic-slice_fusion
  415.2 0.8 copy.38
  (1 shorter events, 0.0 us)
Async XLA Ops:
  7.2 73.0 %copy-start = (bf16[128,1024]{1,0:T(8,128)(2,1)S(1)}, bf16[128,1024]{1,0:T(8,128)(2,1)}, u32[]{:S(2)}) copy-start(bf16[128,1024]{1,0:T(8,128)(2,1)} %param.3) | copy-start | bytes 786436
  7.2 81.0 %copy-start.4 = (f32[1,256,64]{1,2,0:T(8,128)S(1)}, f32[1,256,64]{1,2,0:T(8,128)}, u32[]{:S(2)}) copy-start(f32[1,256,64]{1,2,0:T(8,128)} %param.5) | copy-start | bytes 196612
  7.2 72.9 %all-gather.2.cloned.1.call-start = ((), (), s32[]{:S(2)}) async-start(), calls=%async_computation.2 | async-start | bytes 2228224 | tf_op jit(solution)/shard_map/all_gather | solution.py:8
  83.4 12.5 %all-to-all-start = ((bf16[128,16,64]{0,2,1:T(8,128)(2,1)}), bf16[128,16,64]{0,2,1:T(8,128)(2,1)S(1)}, u32[]{:S(2)}, u32[]{:S(2)}) async-start(bf16[128,16,64]{0,2,1:T(8,128)(2,1)} %bitcast), calls=%async_computation | async-start | bytes 524288 | tf_op jit(solution)/shard_map/all_to_all | solution.py:12
  88.1 325.8 %all-reduce.4.cloned.1.call-start = ((), (), s32[]{:S(2)}) async-start(), calls=%async_computation.3 | async-start | bytes 8388608
  88.3 9.8 %copy-start.2 = (f32[1,256,64]{2,1,0:T(8,128)}, f32[1,256,64]{2,1,0:T(8,128)S(1)}, u32[]{:S(2)}) copy-start(f32[1,256,64]{2,1,0:T(8,128)S(1)} %copy.33) | copy-start | bytes 196612
  117.8 1.6 copy-start.1
  120.0 137.0 %copy-start.3 = (f32[1,256,64]{2,1,0:T(8,128)S(1)}, f32[1,256,64]{2,1,0:T(8,128)}, u32[]{:S(2)}) copy-start(f32[1,256,64]{2,1,0:T(8,128)} %copy-done.2) | copy-start | bytes 196612
Sparse Core Ops, SparseCore 0:
  10.1 69.9 all-gather.1
  117.9 295.9 all-reduce.3
where the time goes:
time: 424 us; the launch traced here: 423 us
  waiting for transfers between devices  236 us (56%)
  blocking collectives  147 us (35%)
  between operations  14.2 us (3%)
  matrix products  7.51 us (2%)
  local copies, waits for them, and re-layouts  6.44 us (2%)
  starting transfers between devices  4.81 us (1%)
    unnamed x3, waiting for transfers between devices  156 us
    psum x1, blocking collectives, per_device(): lax.psum(sums.astype(jnp.bfloat16), 'dp').astype(jnp.float32)  136 us
    all_gather x1, waiting for transfers between devices, per_device(): full_rotation = lax.all_gather(rotation, 'sub', axis=1, tiled=True)  72.2 us
    all_to_all x1, blocking collectives, per_device(): lax.all_to_all(rebuilt, 'sub', split_axis=0, concat_axis=1, tiled=True)  11.6 us
  transfers between devices with their start and end apart: 3, of which 3 were waited for; matrix products, arithmetic and copies ran while one was open for 1% of the time, Pallas kernels for 0%

commit v1 on v0

v1 whole, which is shorter than its diff:
```python
import functools

import jax
import jax.numpy as jnp
from jax import lax
from jax.experimental import pallas as pl
from jax.experimental.pallas import tpu as pltpu
from jax.sharding import Mesh
from jax.sharding import PartitionSpec as P

SIZES = (8, 2, 2, 2, 4, 2)
NAMES = ("z", "xh", "core", "xl", "yh", "yl")
DP = ("z", "xh", "core")
SUB = ("xl", "yh", "yl")
TEAM = ("core", "xl", "yl")
TEAMS = ("z", "xh", "yh")
BF = jnp.bfloat16
F32 = jnp.float32
NT = (((1,), (1,)), ((), ()))
VMEM = pl.BlockSpec(memory_space=pltpu.VMEM)
SMEM = pl.BlockSpec(memory_space=pltpu.SMEM)


def half_mask(shape):
    return lax.broadcasted_iota(jnp.int32, shape, len(shape) - 1) < 64


def swap_halves(x):
    return pltpu.roll(x, 64, 1)


def pack_kernel(turn_t, codes_t, pack):
    codes = codes_t[...]
    square = jnp.sum(codes * codes, axis=0, keepdims=True)
    high = square.astype(BF).astype(F32)
    mid = (square - high).astype(BF).astype(F32)
    low = square - high - mid
    pack[0:64, 0:1024] = turn_t[...]
    pack[0:64, 1024:] = codes.astype(BF)
    pack[64:80, 0:1024] = jnp.zeros((16, 1024), BF)
    pack[64:80, 1024:] = jnp.concatenate([high, mid, low, jnp.zeros((13, 256), F32)], axis=0).astype(BF)


def assign_kernel(place, mine, other, first, second, send, recon, cross, sums):
    rows, chunk = 512, 256
    core, odd = place[0], place[1]
    w0, w1 = first[...], second[...]
    wa = jnp.where(odd == 0, w0, w1)
    wb = jnp.where(odd == 0, w1, w0)
    turn = jnp.concatenate([wa[:64, :1024], wb[:64, :1024]], axis=0)
    zero = jnp.zeros((64, 256), BF)
    codes_t = jnp.concatenate(
        [
            jnp.concatenate([wa[:64, 1024:], zero], axis=1),
            jnp.concatenate([zero, wb[:64, 1024:]], axis=1),
        ],
        axis=0,
    )
    squares = jnp.concatenate([wa[64:80, 1024:], wb[64:80, 1024:]], axis=1)
    left = jnp.concatenate(
        [codes_t * BF(-2.0), squares, jnp.zeros((112, 512), BF)], axis=0
    ).T
    lane = lax.broadcasted_iota(jnp.int32, (chunk, 128), 1)
    three = jnp.where(lane < 3, 1.0, 0.0).astype(BF)
    ones = jnp.ones((chunk, 128), BF)
    row8 = lax.broadcasted_iota(jnp.int32, (8, 128), 0)
    low = half_mask((8, 128))
    pick = jnp.where(low == (row8 == 0), 1.0, 0.0).astype(F32)
    for part, ref in enumerate((mine, other)):
        for c in range(rows // chunk):
            x = ref[c * chunk : (c + 1) * chunk, :]
            rot = lax.dot_general(x, turn, NT, preferred_element_type=F32).astype(BF)
            wide = rot.astype(F32)
            row_square = lax.dot_general(
                pick, wide * wide, NT, precision=lax.Precision.HIGHEST, preferred_element_type=F32
            )
            near = lax.dot_general(
                left, jnp.concatenate([rot, three], axis=1), NT, preferred_element_type=F32
            )
            parts = []
            for i in range(2):
                logits = -0.125 * (row_square[i : i + 1] + near[i * 256 : (i + 1) * 256])
                e = jnp.exp(logits - jnp.max(logits, axis=0, keepdims=True))
                parts.append((e * (1.0 / jnp.sum(e, axis=0, keepdims=True))).astype(BF))
            weights = jnp.concatenate(parts, axis=0)
            rebuilt = jnp.dot(codes_t, weights, preferred_element_type=F32).astype(BF)
            s = jnp.dot(weights, jnp.concatenate([rot, ones], axis=1), preferred_element_type=F32)
            k = jnp.dot(rebuilt, x, preferred_element_type=F32)
            if part == 0 and c == 0:
                sums[...] = s
                cross[...] = k
            else:
                sums[...] += s
                cross[...] += k
            block = (core if part == 0 else 1 - core) * 4 + c * 2
            back = rebuilt.T
            recon[block, 0:128, :] = back[:128]
            recon[block + 1, 0:128, :] = back[128:]
    recon[:, 128:144, :] = jnp.zeros((8, 16, 128), BF)
    r = lax.broadcasted_iota(jnp.int32, (128, 128), 0)
    wanted = (
        (r & 64) | ((r & 8) << 2) | ((r & 4) << 2) | ((r & 48) >> 2) | (r & 3)
    )
    order = jnp.where(lax.broadcasted_iota(jnp.int32, (128, 128), 1) == wanted, 1.0, 0.0).astype(BF)
    for z in range(8):
        piece = lax.dot_general(
            order, cross[:, z * 128 : (z + 1) * 128].astype(BF), NT, preferred_element_type=F32
        ).astype(BF)
        for t in range(8):
            send[z * 8 + t, 0:16, :] = piece[t * 16 : (t + 1) * 16]
    for i in range(2):
        for q in range(16):
            at = i * 256 + q * 16
            a, b = sums[at : at + 8, :128], sums[at + 8 : at + 16, :128]
            if i == 0:
                total = jnp.where(low, a, swap_halves(b))
            else:
                total = jnp.where(low, swap_halves(a), b)
            count = jnp.where(low, sums[at : at + 8, 128:], sums[at + 8 : at + 16, 128:])
            tile = jnp.concatenate([total, count], axis=0).astype(BF)
            send[q * 4 + i, 16:32, :] = tile
            send[q * 4 + i + 2, 16:32, :] = tile


def reduce_kernel(place, got, codes, recon_in, recon, new_codes):
    recon[:, 0:128, :] = recon_in[:, 0:128, :]
    total = jnp.sum(got[...].astype(F32), axis=0)
    cross = total[:16]
    high = cross.astype(BF)
    rest = (cross - high.astype(F32)).astype(BF)
    both = jnp.concatenate([high, rest], axis=0).astype(F32)
    for c in range(8):
        tile = jnp.concatenate(
            [both[2 * c : 2 * c + 2], both[16 + 2 * c : 18 + 2 * c], jnp.zeros((12, 128), F32)], axis=0
        )
        recon[c, 128:144, :] = tile.astype(BF)
    at = pl.multiple_of(place[0] * 16, 16)
    own = codes[pl.ds(at, 16), :]
    own = jnp.concatenate([own[:8], own[8:]], axis=1)
    fresh = (total[16:24] + own) / (total[24:32] + 1.0)
    for c in range(32):
        new_codes[c] = fresh


def finish_kernel(got, recon, cross):
    low = half_mask((144, 128))
    for xl in range(2):
        for core in range(2):
            a = got[core * 4 + xl * 2].astype(F32)
            b = got[core * 4 + xl * 2 + 1].astype(F32)
            at = (xl * 2 + core) * 256
            for i in range(2):
                if i == 0:
                    t = jnp.where(low, a, swap_halves(b))
                else:
                    t = jnp.where(low, swap_halves(a), b)
                recon[:, at + i * 128 : at + (i + 1) * 128] = t[:128].astype(BF)
                cross[:, at + i * 128 : at + (i + 1) * 128] = t[128:130] + t[130:132]


def per_device(samples, rotation, codebook):
    core, yh = lax.axis_index("core"), lax.axis_index("yh")
    codes_t = codebook[0].T
    pack = pl.pallas_call(
        pack_kernel,
        out_shape=jax.ShapeDtypeStruct((80, 1280), BF),
        in_specs=[VMEM] * 2,
        out_specs=VMEM,
        name="pack",
    )(rotation.T, codes_t)
    packs = []
    for p in range(2):
        pairs = [
            (c * 4 + y, (y >> 1) * 4 + 2 * c + ((y & 1) ^ p)) for c in range(2) for y in range(4)
        ]
        packs.append(lax.ppermute(pack, ("core", "yh"), pairs))
    mine = lax.all_to_all(
        jnp.broadcast_to(samples[None], (4, 128, 1024)), ("xl", "yl"), 0, 0, tiled=True
    ).reshape(512, 1024)
    mine, *packs = lax.optimization_barrier((mine, *packs))
    other = lax.ppermute(mine, "core", [(0, 1), (1, 0)])
    place = jnp.stack([core, yh & 1]).astype(jnp.int32)
    send, recon = pl.pallas_call(
        assign_kernel,
        out_shape=(
            jax.ShapeDtypeStruct((64, 32, 128), BF),
            jax.ShapeDtypeStruct((8, 144, 128), BF),
        ),
        in_specs=[SMEM] + [VMEM] * 4,
        out_specs=(VMEM, VMEM),
        scratch_shapes=[pltpu.VMEM((128, 1024), F32), pltpu.VMEM((512, 256), F32)],
        compiler_params=pltpu.CompilerParams(vmem_limit_bytes=40 * 1024 * 1024),
        name="assign",
    )(place, mine, other, packs[0], packs[1])
    got = lax.all_to_all(send, TEAMS, 0, 0, tiled=True)
    chunk = (lax.axis_index("z") * 2 + lax.axis_index("xh")).astype(jnp.int32).reshape(1)
    recon, fresh = pl.pallas_call(
        reduce_kernel,
        out_shape=(
            jax.ShapeDtypeStruct((8, 144, 128), BF),
            jax.ShapeDtypeStruct((32, 8, 128), F32),
        ),
        in_specs=[SMEM] + [VMEM] * 3,
        out_specs=(VMEM, VMEM),
        compiler_params=pltpu.CompilerParams(vmem_limit_bytes=40 * 1024 * 1024),
        name="reduce",
    )(chunk, got, codebook[0], recon)
    back = lax.all_to_all(recon, TEAM, 0, 0, tiled=True)
    spread = lax.all_to_all(fresh, DP, 0, 0, tiled=True)
    recon, cross = pl.pallas_call(
        finish_kernel,
        out_shape=(
            jax.ShapeDtypeStruct((128, 1024), BF),
            jax.ShapeDtypeStruct((2, 1024), F32),
        ),
        in_specs=[VMEM],
        out_specs=(VMEM, VMEM),
        compiler_params=pltpu.CompilerParams(vmem_limit_bytes=40 * 1024 * 1024),
        name="finish",
    )(back)
    spread = lax.dynamic_index_in_dim(spread.reshape(16, 2, 8, 128), yh >> 1, 1, keepdims=False)
    new_codes = spread.reshape(16, 8, 2, 64).transpose(0, 2, 1, 3).reshape(1, 256, 64)
    return recon, new_codes, cross


def solution(mesh):
    fine = Mesh(mesh.devices.reshape(SIZES), NAMES)
    rows = P(DP + SUB, None)
    return jax.shard_map(
        per_device,
        mesh=fine,
        in_specs=(rows, P(None, SUB), P(SUB, None, None)),
        out_specs=(rows, P(SUB, None, None), rows),
        check_vma=False,
    )
```

time: 424 us -> 109 us (0.26)
  waiting for transfers between devices: 236 us -> 42.3 us
  blocking collectives: 147 us -> 17.9 us
  starting transfers between devices: 4.81 us -> 34.2 us
  between operations: 14.2 us -> 0.71 us
  matrix products: 7.51 us -> 0 us
  Pallas kernels: 3.92 us -> 9.76 us
    unnamed x3 -> x0, waiting for transfers between devices: 156 us -> none
    psum x1 -> x0, blocking collectives: 136 us -> none  [per_device(): lax.psum(sums.astype(jnp.bfloat16), 'dp').astype(jnp.float32)]
    all_gather x1 -> x0, waiting for transfers between devices: 72.2 us -> none  [per_device(): full_rotation = lax.all_gather(rotation, 'sub', axis=1, tiled=True)]
    ppermute x0 -> x3, waiting for transfers between devices: none -> 17.7 us  [the longest x2 15.2 us: per_device(): packs.append(lax.ppermute(pack, ('core', 'yh'), pairs))]
    all_to_all x1 -> x3, starting transfers between devices: 4.73 us -> 22.3 us  [the longest x1 13.7 us: per_device(): got = lax.all_to_all(send, TEAMS, 0, 0, tiled=True)]
    all_to_all x1 -> x3, waiting for transfers between devices: 7.49 us -> 24.6 us  [the longest x1 18.9 us: per_device(): got = lax.all_to_all(send, TEAMS, 0, 0, tiled=True)]
    ppermute x0 -> x3, starting transfers between devices: none -> 11.9 us  [the longest x2 9.95 us: per_device(): packs.append(lax.ppermute(pack, ('core', 'yh'), pairs))]
    pallas_call x0 -> x4, Pallas kernels: none -> 9.76 us  [the longest x1 6.47 us: per_device(): pl.pallas_call(assign_kernel, out_shape=(jax.ShapeDtypeStruct((64, 32, 12...]
  transfers between devices with their start and end apart: 3 -> 6, of which waited for: 3 -> 4; matrix products, arithmetic and copies ran while one was open for 1% -> 1% of each run, Pallas kernels for 0% -> 1%
where the time goes in v1:
time: 109 us; the launch traced here: 108 us
  waiting for transfers between devices  42.3 us (39%)
  starting transfers between devices  34.2 us (31%)
  blocking collectives  17.9 us (16%)
  Pallas kernels  9.76 us (9%)
  local copies, waits for them, and re-layouts  3.01 us (3%)
    all_to_all x1, waiting for transfers between devices, per_device(): got = lax.all_to_all(send, TEAMS, 0, 0, tiled=True)  18.9 us
    all_to_all x1, blocking collectives, per_device(): spread = lax.all_to_all(fresh, DP, 0, 0, tiled=True)  17.9 us
    ppermute x2, waiting for transfers between devices, per_device(): packs.append(lax.ppermute(pack, ('core', 'yh'), pairs))  15.2 us
    all_to_all x1, starting transfers between devices, per_device(): got = lax.all_to_all(send, TEAMS, 0, 0, tiled=True)  13.7 us
    ppermute x2, starting transfers between devices, per_device(): packs.append(lax.ppermute(pack, ('core', 'yh'), pairs))  9.95 us
    pallas_call x1, Pallas kernels, per_device(): pl.pallas_call(assign_kernel, out_shape=(jax.ShapeDtypeStruct((64, 32, 12...  6.47 us
    all_to_all x1, waiting for transfers between devices, per_device(): back = lax.all_to_all(recon, TEAM, 0, 0, tiled=True)  5.72 us
    all_to_all x1, starting transfers between devices, per_device(): lax.all_to_all(jnp.broadcast_to(samples[None], (4, 128, 1024)), ('xl', 'y...  4.32 us
  transfers between devices with their start and end apart: 6, of which 4 were waited for; matrix products, arithmetic and copies ran while one was open for 1% of the time, Pallas kernels for 1%

profile of v1, /device:TPU:1, one launch (start us, length us, event | category | flops | bytes accessed | tf_op | source)
XLA Modules:
  0.0 108.0 jit_solution(2544174478174843771)
XLA Ops:
  0.6 2.1 %broadcast_in_dim.2 = bf16[4,128,1024]{2,1,0:T(8,128)(2,1)} broadcast(bf16[128,1024]{1,0:T(8,128)(2,1)} %param.3), dimensions={1,2} | broadcast | bytes 1310720 | tf_op jit(solution)/shard_map/broadcast_in_dim | solution.py:178
  2.7 4.3 %all-to-all-start = ((bf16[4,128,1024]{2,1,0:T(8,128)(2,1)}), bf16[4,128,1024]{2,1,0:T(8,128)(2,1)S(1)}, u32[]{:S(2)}, u32[]{:S(2)}) async-start(bf16[4,128,1024]{2,1,0:T(8,128)(2,1)} %broadcast_in_dim.2), calls=%async_computation | async-start | bytes 2097152 | tf_op jit(solution)/shard_map/all_to_all | solution.py:177
  7.0 1.6 %pack.1 = bf16[80,1280]{1,0:T(8,128)(2,1)} custom-call(bf16[64,1024]{1,0:T(8,128)(2,1)} %bitcast.24, f32[64,256]{1,0:T(8,128)} %bitcast.23), custom_call_target="tpu_custom_call" | custom-call | tf_op jit(solution)/shard_map/pack/pallas_call | solution.py:164
  8.6 8.0 %collective-permute-start = (bf16[80,1280]{1,0:T(8,128)(2,1)}, bf16[80,1280]{1,0:T(8,128)(2,1)S(1)}, u32[]{:S(2)}, u32[]{:S(2)}) collective-permute-start(bf16[80,1280]{1,0:T(8,128)(2,1)} %pack.1), channel_id=1, source_target_pairs={{0,0},{2,2},{4,16},{6,18},{16,4},{18,6},{20,20},{22,22},{1,1},{3,3... | collective-permute-start | bytes 614408 | tf_op jit(solution)/shard_map/ppermute | solution.py:176
  16.7 1.9 %collective-permute-start.1 = (bf16[80,1280]{1,0:T(8,128)(2,1)}, bf16[80,1280]{1,0:T(8,128)(2,1)S(1)}, u32[]{:S(2)}, u32[]{:S(2)}) collective-permute-start(bf16[80,1280]{1,0:T(8,128)(2,1)} %pack.1), channel_id=1, source_target_pairs={{0,2},{2,0},{4,18},{6,16},{16,6},{18,4},{20,22},{22,20},{1,3},{3,1... | collective-permute-start | bytes 614408 | tf_op jit(solution)/shard_map/ppermute | solution.py:176
  18.6 15.2 %collective-permute-done.first = bf16[80,1280]{1,0:T(8,128)(2,1)S(1)} collective-permute-done((bf16[80,1280]{1,0:T(8,128)(2,1)}, bf16[80,1280]{1,0:T(8,128)(2,1)S(1)}, u32[]{:S(2)}, u32[]{:S(2)}) %collective-permute-start) | collective-permute-done | bytes 204832 | tf_op jit(solution)/shard_map/ppermute | solution.py:176
  33.8 0.0 collective-permute-done.1.second
  33.8 0.0 all-to-all-done
  33.8 1.9 %collective-permute-start.2 = (bf16[512,1024]{1,0:T(8,128)(2,1)S(1)}, bf16[512,1024]{1,0:T(8,128)(2,1)S(1)}, u32[]{:S(2)}, u32[]{:S(2)}) collective-permute-start(bf16[512,1024]{1,0:T(8,128)(2,1)S(1)} %bitcast.17), channel_id=1, source_target_pairs={{0,16},{16,0},{1,17},{17,1},{2,18},{18,2},{3,19},{19,3},{4,20},{20... | collective-permute-start | bytes 3145736 | tf_op jit(solution)/shard_map/ppermute | solution.py:181
  35.7 0.1 pad_add_fusion.place
  35.8 2.5 %collective-permute-done.2.other = bf16[512,1024]{1,0:T(8,128)(2,1)S(1)} collective-permute-done((bf16[512,1024]{1,0:T(8,128)(2,1)S(1)}, bf16[512,1024]{1,0:T(8,128)(2,1)S(1)}, u32[]{:S(2)}, u32[]{:S(2)}) %collective-permute-start.2) | collective-permute-done | bytes 1048608 | tf_op jit(solution)/shard_map/ppermute | solution.py:181
  38.3 6.5 %assign.1 = (bf16[64,32,128]{2,1,0:T(8,128)(2,1)}, bf16[8,144,128]{2,1,0:T(8,128)(2,1)S(1)}) custom-call(s32[2]{0:T(128)S(1)} %pad_add_fusion.place, bf16[512,1024]{1,0:T(8,128)(2,1)S(1)} %bitcast.18, bf16[512,1024]{1,0:T(8,128)(2,1)S(1)} %collective-permute-done.2.other, bf16[80,1280]{1,0:T(8,128)(2,1)S(1)} %collective-permute-done.first, ...), custom_call_target="tpu_custom_call" | custom-call | tf_op jit(solution)/shard_map/assign/pallas_call | solution.py:183
  44.8 0.0 copy-start
  44.8 13.7 %all-to-all-start.1 = ((bf16[64,32,128]{2,1,0:T(8,128)(2,1)}), bf16[64,32,128]{2,1,0:T(8,128)(2,1)S(1)}, u32[]{:S(2)}, u32[]{:S(2)}) async-start(bf16[64,32,128]{2,1,0:T(8,128)(2,1)} %get-tuple-element.15), calls=%async_computation.1 | async-start | bytes 1048576 | tf_op jit(solution)/shard_map/all_to_all | solution.py:195
  58.5 0.0 copy-done
  58.5 0.1 copy.8
  58.6 18.9 %all-to-all-done.1.got = bf16[64,32,128]{2,1,0:T(8,128)(2,1)S(1)} async-done(((bf16[64,32,128]{2,1,0:T(8,128)(2,1)}), bf16[64,32,128]{2,1,0:T(8,128)(2,1)S(1)}, u32[]{:S(2)}, u32[]{:S(2)}) %all-to-all-start.1) | async-done | bytes 524320 | tf_op jit(solution)/shard_map/all_to_all | solution.py:195
  77.5 0.8 reduce.1
  78.4 17.9 %all_to_all.20 = f32[32,8,128]{2,1,0:T(8,128)S(1)} all-to-all(f32[32,8,128]{2,1,0:T(8,128)S(1)} %get-tuple-element.19), channel_id=1, replica_groups=mesh['z'=8,'xh'=2,'core'=2,'xl'=2,'yh'=4,'yl'=2] {'z','xh','core'}, dimensions={0} | all-to-all | bytes 262144 | tf_op jit(solution)/shard_map/all_to_all | solution.py:209
  96.2 4.3 %all-to-all-start.2 = ((bf16[8,144,128]{2,1,0:T(8,128)(2,1)}), bf16[8,144,128]{2,1,0:T(8,128)(2,1)S(1)}, u32[]{:S(2)}, u32[]{:S(2)}) async-start(bf16[8,144,128]{2,1,0:T(8,128)(2,1)} %get-tuple-element.17), calls=%async_computation.2 | async-start | bytes 589824 | tf_op jit(solution)/shard_map/all_to_all | solution.py:208
  100.5 0.1 reshape.26
  100.7 0.7 copy.12
  101.4 5.7 %all-to-all-done.2.got = bf16[8,144,128]{2,1,0:T(8,128)(2,1)S(1)} async-done(((bf16[8,144,128]{2,1,0:T(8,128)(2,1)}), bf16[8,144,128]{2,1,0:T(8,128)(2,1)S(1)}, u32[]{:S(2)}, u32[]{:S(2)}) %all-to-all-start.2) | async-done | bytes 294944 | tf_op jit(solution)/shard_map/all_to_all | solution.py:208
  107.1 0.9 finish.1
  (2 shorter events, 0.0 us)
Async XLA Ops:
  2.7 31.1 %all-to-all-start = ((bf16[4,128,1024]{2,1,0:T(8,128)(2,1)}), bf16[4,128,1024]{2,1,0:T(8,128)(2,1)S(1)}, u32[]{:S(2)}, u32[]{:S(2)}) async-start(bf16[4,128,1024]{2,1,0:T(8,128)(2,1)} %broadcast_in_dim.2), calls=%async_computation | async-start | bytes 2097152 | tf_op jit(solution)/shard_map/all_to_all | solution.py:177
  8.6 25.1 %collective-permute-start = (bf16[80,1280]{1,0:T(8,128)(2,1)}, bf16[80,1280]{1,0:T(8,128)(2,1)S(1)}, u32[]{:S(2)}, u32[]{:S(2)}) collective-permute-start(bf16[80,1280]{1,0:T(8,128)(2,1)} %pack.1), channel_id=1, source_target_pairs={{0,0},{2,2},{4,16},{6,18},{16,4},{18,6},{20,20},{22,22},{1,1},{3,3... | collective-permute-start | bytes 614408 | tf_op jit(solution)/shard_map/ppermute | solution.py:176
  16.7 17.1 %collective-permute-start.1 = (bf16[80,1280]{1,0:T(8,128)(2,1)}, bf16[80,1280]{1,0:T(8,128)(2,1)S(1)}, u32[]{:S(2)}, u32[]{:S(2)}) collective-permute-start(bf16[80,1280]{1,0:T(8,128)(2,1)} %pack.1), channel_id=1, source_target_pairs={{0,2},{2,0},{4,18},{6,16},{16,6},{18,4},{20,22},{22,20},{1,3},{3,1... | collective-permute-start | bytes 614408 | tf_op jit(solution)/shard_map/ppermute | solution.py:176
  33.8 4.5 %collective-permute-start.2 = (bf16[512,1024]{1,0:T(8,128)(2,1)S(1)}, bf16[512,1024]{1,0:T(8,128)(2,1)S(1)}, u32[]{:S(2)}, u32[]{:S(2)}) collective-permute-start(bf16[512,1024]{1,0:T(8,128)(2,1)S(1)} %bitcast.17), channel_id=1, source_target_pairs={{0,16},{16,0},{1,17},{17,1},{2,18},{18,2},{3,19},{19,3},{4,20},{20... | collective-permute-start | bytes 3145736 | tf_op jit(solution)/shard_map/ppermute | solution.py:181
  44.8 13.7 %copy-start = (f32[1,256,64]{1,2,0:T(8,128)S(1)}, f32[1,256,64]{1,2,0:T(8,128)}, u32[]{:S(2)}) copy-start(f32[1,256,64]{1,2,0:T(8,128)} %param.5) | copy-start | bytes 196612
  44.8 32.7 %all-to-all-start.1 = ((bf16[64,32,128]{2,1,0:T(8,128)(2,1)}), bf16[64,32,128]{2,1,0:T(8,128)(2,1)S(1)}, u32[]{:S(2)}, u32[]{:S(2)}) async-start(bf16[64,32,128]{2,1,0:T(8,128)(2,1)} %get-tuple-element.15), calls=%async_computation.1 | async-start | bytes 1048576 | tf_op jit(solution)/shard_map/all_to_all | solution.py:195
  96.2 10.9 %all-to-all-start.2 = ((bf16[8,144,128]{2,1,0:T(8,128)(2,1)}), bf16[8,144,128]{2,1,0:T(8,128)(2,1)S(1)}, u32[]{:S(2)}, u32[]{:S(2)}) async-start(bf16[8,144,128]{2,1,0:T(8,128)(2,1)} %get-tuple-element.17), calls=%async_computation.2 | async-start | bytes 589824 | tf_op jit(solution)/shard_map/all_to_all | solution.py:208

commit v2 on v1

v2 whole, which is shorter than its diff:
```python
import functools

import jax
import jax.numpy as jnp
from jax import lax
from jax.experimental import pallas as pl
from jax.experimental.pallas import tpu as pltpu
from jax.sharding import Mesh
from jax.sharding import PartitionSpec as P

SIZES = (8, 2, 2, 2, 4, 2)
NAMES = ("z", "xh", "core", "xl", "yh", "yl")
DP = ("z", "xh", "core")
SUB = ("xl", "yh", "yl")
TEAM = ("core", "xl", "yl")
TEAMS = ("z", "xh", "yh")
BF = jnp.bfloat16
F32 = jnp.float32
NT = (((1,), (1,)), ((), ()))
VMEM = pl.BlockSpec(memory_space=pltpu.VMEM)
SMEM = pl.BlockSpec(memory_space=pltpu.SMEM)


def half_mask(shape):
    return lax.broadcasted_iota(jnp.int32, shape, len(shape) - 1) < 64


def swap_halves(x):
    return pltpu.roll(x, 64, 1)


def pack_kernel(turn_t, codes_t, pack):
    codes = codes_t[...]
    square = jnp.sum(codes * codes, axis=0, keepdims=True)
    high = square.astype(BF).astype(F32)
    mid = (square - high).astype(BF).astype(F32)
    low = square - high - mid
    pack[0:64, 0:1024] = turn_t[...]
    pack[0:64, 1024:] = codes.astype(BF)
    pack[64:80, 0:1024] = jnp.zeros((16, 1024), BF)
    pack[64:80, 1024:] = jnp.concatenate([high, mid, low, jnp.zeros((13, 256), F32)], axis=0).astype(BF)


def prepare_kernel(place, first, second, turn, codes_t, left):
    odd = place[1]
    w0, w1 = first[...], second[...]
    wa = jnp.where(odd == 0, w0, w1)
    wb = jnp.where(odd == 0, w1, w0)
    turn[0:64, :] = wa[:64, :1024]
    turn[64:128, :] = wb[:64, :1024]
    zero = jnp.zeros((64, 256), BF)
    both = jnp.concatenate(
        [
            jnp.concatenate([wa[:64, 1024:], zero], axis=1),
            jnp.concatenate([zero, wb[:64, 1024:]], axis=1),
        ],
        axis=0,
    )
    codes_t[...] = both
    squares = jnp.concatenate([wa[64:80, 1024:], wb[64:80, 1024:]], axis=1)
    left[...] = jnp.concatenate([both * BF(-2.0), squares, jnp.zeros((112, 512), BF)], axis=0).T


def assign_rows(samples, turn, codes_t, left, sums, cross, first, put):
    rows, chunk = 512, 256
    lane = lax.broadcasted_iota(jnp.int32, (chunk, 128), 1)
    three = jnp.where(lane < 3, 1.0, 0.0).astype(BF)
    ones = jnp.ones((chunk, 128), BF)
    row8 = lax.broadcasted_iota(jnp.int32, (8, 128), 0)
    pick = jnp.where(half_mask((8, 128)) == (row8 == 0), 1.0, 0.0).astype(F32)
    for c in range(rows // chunk):
        x = samples[c * chunk : (c + 1) * chunk, :]
        rot = lax.dot_general(x, turn[...], NT, preferred_element_type=F32).astype(BF)
        wide = rot.astype(F32)
        row_square = lax.dot_general(
            pick, wide * wide, NT, precision=lax.Precision.HIGHEST, preferred_element_type=F32
        )
        near = lax.dot_general(
            left[...], jnp.concatenate([rot, three], axis=1), NT, preferred_element_type=F32
        )
        parts = []
        for i in range(2):
            logits = -0.125 * (row_square[i : i + 1] + near[i * 256 : (i + 1) * 256])
            e = jnp.exp(logits - jnp.max(logits, axis=0, keepdims=True))
            parts.append((e * (1.0 / jnp.sum(e, axis=0, keepdims=True))).astype(BF))
        weights = jnp.concatenate(parts, axis=0)
        rebuilt = jnp.dot(codes_t[...], weights, preferred_element_type=F32).astype(BF)
        s = jnp.dot(weights, jnp.concatenate([rot, ones], axis=1), preferred_element_type=F32)
        k = jnp.dot(rebuilt, x, preferred_element_type=F32)
        if first and c == 0:
            sums[...] = s
            cross[...] = k
        else:
            sums[...] += s
            cross[...] += k
        back = rebuilt.T
        put(2 * c, back[:128])
        put(2 * c + 1, back[128:])


def early_kernel(samples, turn, codes_t, left, sums, cross, recon):
    def put(block, tile):
        recon[block] = tile

    assign_rows(samples, turn, codes_t, left, sums, cross, True, put)


def late_kernel(
    place, samples, turn, codes_t, left, sums_in, cross_in, recon_in, send, recon, sums, cross
):
    core = place[0]
    sums[...] = sums_in[...]
    cross[...] = cross_in[...]

    def put(block, tile):
        recon[(1 - core) * 4 + block, 0:128, :] = tile

    assign_rows(samples, turn, codes_t, left, sums, cross, False, put)
    for block in range(4):
        recon[core * 4 + block, 0:128, :] = recon_in[block]
    recon[:, 128:144, :] = jnp.zeros((8, 16, 128), BF)
    r = lax.broadcasted_iota(jnp.int32, (128, 128), 0)
    wanted = (r & 64) | ((r & 8) << 2) | ((r & 4) << 2) | ((r & 48) >> 2) | (r & 3)
    order = jnp.where(lax.broadcasted_iota(jnp.int32, (128, 128), 1) == wanted, 1.0, 0.0).astype(BF)
    for z in range(8):
        piece = lax.dot_general(
            order, cross[:, z * 128 : (z + 1) * 128].astype(BF), NT, preferred_element_type=F32
        ).astype(BF)
        for t in range(8):
            send[z * 8 + t, 0:16, :] = piece[t * 16 : (t + 1) * 16]
    low = half_mask((8, 128))
    for i in range(2):
        for q in range(16):
            at = i * 256 + q * 16
            a, b = sums[at : at + 8, :128], sums[at + 8 : at + 16, :128]
            if i == 0:
                total = jnp.where(low, a, swap_halves(b))
            else:
                total = jnp.where(low, swap_halves(a), b)
            count = jnp.where(low, sums[at : at + 8, 128:], sums[at + 8 : at + 16, 128:])
            tile = jnp.concatenate([total, count], axis=0).astype(BF)
            send[q * 4 + i, 16:32, :] = tile
            send[q * 4 + i + 2, 16:32, :] = tile


def reduce_kernel(place, got, codes, recon_in, recon):
    total = jnp.sum(got[...].astype(F32), axis=0)
    cross = total[:16]
    high = cross.astype(BF)
    rest = (cross - high.astype(F32)).astype(BF)
    both = jnp.concatenate([high, rest], axis=0).astype(F32)
    at = pl.multiple_of(place[0] * 16, 16)
    own = codes[pl.ds(at, 16), :]
    own = jnp.concatenate([own[:8], own[8:]], axis=1)
    fresh = (total[16:24] + own) / (total[24:32] + 1.0)
    for c in range(8):
        recon[c, 0:128, :] = recon_in[c, 0:128, :]
        tile = jnp.concatenate(
            [both[2 * c : 2 * c + 2], both[16 + 2 * c : 18 + 2 * c], jnp.zeros((4, 128), F32), fresh],
            axis=0,
        )
        recon[c, 128:144, :] = tile.astype(BF)


def pick_kernel(place, got, spread):
    tile = got[place[0], 128:144, :]
    for q in range(16):
        spread[q] = tile


def finish_kernel(got, recon, cross):
    low = half_mask((144, 128))
    for xl in range(2):
        for core in range(2):
            a = got[core * 4 + xl * 2].astype(F32)
            b = got[core * 4 + xl * 2 + 1].astype(F32)
            at = (xl * 2 + core) * 256
            for i in range(2):
                if i == 0:
                    t = jnp.where(low, a, swap_halves(b))
                else:
                    t = jnp.where(low, swap_halves(a), b)
                recon[:, at + i * 128 : at + (i + 1) * 128] = t[:128].astype(BF)
                cross[:, at + i * 128 : at + (i + 1) * 128] = t[128:130] + t[130:132]


def codes_kernel(got, codes_t):
    tiles = []
    for q in range(16):
        t = got[q].astype(F32)[8:]
        tiles += [t, swap_halves(t)]
    codes_t[...] = jnp.concatenate(tiles, axis=0).T[:64]


def call(kernel, name, outs, args, flops=0, moved=0, scratch=()):
    return pl.pallas_call(
        kernel,
        out_shape=tuple(jax.ShapeDtypeStruct(*o) for o in outs),
        in_specs=[SMEM if a.ndim == 1 else VMEM for a in args],
        out_specs=(VMEM,) * len(outs),
        scratch_shapes=list(scratch),
        compiler_params=pltpu.CompilerParams(vmem_limit_bytes=40 * 1024 * 1024),
        cost_estimate=pl.CostEstimate(flops=flops, bytes_accessed=moved, transcendentals=0),
        name=name,
    )(*args)


def per_device(samples, rotation, codebook):
    core, yh = lax.axis_index("core"), lax.axis_index("yh")
    codes_t = codebook[0].T
    pack = pl.pallas_call(
        pack_kernel,
        out_shape=jax.ShapeDtypeStruct((80, 1280), BF),
        in_specs=[VMEM] * 2,
        out_specs=VMEM,
        name="pack",
    )(rotation.T, codes_t)
    packs = []
    for p in range(2):
        pairs = [
            (c * 4 + y, (y >> 1) * 4 + 2 * c + ((y & 1) ^ p)) for c in range(2) for y in range(4)
        ]
        packs.append(lax.ppermute(pack, ("core", "yh"), pairs))
    mine = lax.all_to_all(
        jnp.broadcast_to(samples[None], (4, 128, 1024)), ("xl", "yl"), 0, 0, tiled=True
    ).reshape(512, 1024)
    place = jnp.stack([core, yh & 1]).astype(jnp.int32)
    tools = call(
        prepare_kernel,
        "prepare",
        [((128, 1024), BF), ((128, 512), BF), ((512, 256), BF)],
        (place, *packs),
        moved=300_000_000,
    )
    mine, *tools = lax.optimization_barrier((mine, *tools))
    other = lax.ppermute(mine, "core", [(0, 1), (1, 0)])
    sums, cross, early = call(
        early_kernel,
        "early",
        [((512, 256), F32), ((128, 1024), F32), ((4, 128, 128), BF)],
        (mine, *tools),
        moved=8_000_000,
    )
    send, recon = call(
        late_kernel,
        "late",
        [((64, 32, 128), BF), ((8, 144, 128), BF)],
        (place, other, *tools, sums, cross, early),
        moved=8_000_000,
        scratch=[pltpu.VMEM((512, 256), F32), pltpu.VMEM((128, 1024), F32)],
    )
    got = lax.all_to_all(send, TEAMS, 0, 0, tiled=True)
    chunk = (lax.axis_index("z") * 2 + lax.axis_index("xh")).astype(jnp.int32).reshape(1)
    (recon,) = call(
        reduce_kernel, "reduce", [((8, 144, 128), BF)], (chunk, got, codebook[0], recon)
    )
    back = lax.all_to_all(recon, TEAM, 0, 0, tiled=True)
    source = (yh >> 1) * 4 + lax.axis_index("xl") * 2 + lax.axis_index("yl")
    (spread,) = call(
        pick_kernel, "pick", [((16, 16, 128), BF)], (source.astype(jnp.int32).reshape(1), back)
    )
    spread = lax.all_to_all(spread, ("z", "xh"), 0, 0, tiled=True)
    recon, cross = call(finish_kernel, "finish", [((128, 1024), BF), ((2, 1024), F32)], (back,))
    (new_codes,) = call(codes_kernel, "codes", [((64, 256), F32)], (spread,))
    return recon, new_codes.T[None], cross


def solution(mesh):
    fine = Mesh(mesh.devices.reshape(SIZES), NAMES)
    rows = P(DP + SUB, None)
    return jax.shard_map(
        per_device,
        mesh=fine,
        in_specs=(rows, P(None, SUB), P(SUB, None, None)),
        out_specs=(rows, P(SUB, None, None), rows),
        check_vma=False,
    )
```

time: 109 us -> 106 us (0.972)
  blocking collectives: 17.9 us -> 0 us
  waiting for transfers between devices: 42.3 us -> 49.4 us
  starting transfers between devices: 34.2 us -> 41.1 us
  Pallas kernels: 9.76 us -> 12.2 us
    all_to_all x1 -> x0, blocking collectives: 17.9 us -> none  [per_device(): spread = lax.all_to_all(fresh, DP, 0, 0, tiled=True)]
    all_to_all x0 -> x1, waiting for transfers between devices: none -> 8.56 us  [per_device(): spread = lax.all_to_all(spread, ('z', 'xh'), 0, 0, tiled=True)]
    all_to_all x0 -> x1, starting transfers between devices: none -> 3.5 us  [per_device(): spread = lax.all_to_all(spread, ('z', 'xh'), 0, 0, tiled=True)]
    all_to_all x1, starting transfers between devices: 4.27 us -> 7.35 us  [per_device(): back = lax.all_to_all(recon, TEAM, 0, 0, tiled=True)]
    ppermute x1, waiting for transfers between devices: 2.54 us -> 0.03 us  [per_device(): other = lax.ppermute(mine, 'core', [(0, 1), (1, 0)])]
    pallas_call x3 -> x7, Pallas kernels: 8.15 us -> 10.6 us  [call(): pl.pallas_call(kernel, out_shape=tuple((jax.ShapeDtypeStruct(*o) for o in...]
  transfers between devices with their start and end apart: 6 -> 7, of which waited for: 4 -> 4; matrix products, arithmetic and copies ran while one was open for 1% -> 0% of each run, Pallas kernels for 1% -> 5%
where the time goes in v2:
time: 106 us
  waiting for transfers between devices  49.4 us (47%)
  starting transfers between devices  41.1 us (39%)
  Pallas kernels  12.2 us (12%)
  local copies, waits for them, and re-layouts  2.16 us (2%)
    all_to_all x1, waiting for transfers between devices, per_device(): got = lax.all_to_all(send, TEAMS, 0, 0, tiled=True)  19.2 us
    ppermute x2, waiting for transfers between devices, per_device(): packs.append(lax.ppermute(pack, ('core', 'yh'), pairs))  15.1 us
    all_to_all x1, starting transfers between devices, per_device(): got = lax.all_to_all(send, TEAMS, 0, 0, tiled=True)  14.1 us
    pallas_call x7, Pallas kernels, call(): pl.pallas_call(kernel, out_shape=tuple((jax.ShapeDtypeStruct(*o) for o in...  10.6 us
    ppermute x2, starting transfers between devices, per_device(): packs.append(lax.ppermute(pack, ('core', 'yh'), pairs))  9.95 us
    all_to_all x1, waiting for transfers between devices, per_device(): spread = lax.all_to_all(spread, ('z', 'xh'), 0, 0, tiled=True)  8.56 us
    all_to_all x1, starting transfers between devices, per_device(): back = lax.all_to_all(recon, TEAM, 0, 0, tiled=True)  7.35 us
    all_to_all x1, waiting for transfers between devices, per_device(): back = lax.all_to_all(recon, TEAM, 0, 0, tiled=True)  6.6 us
  transfers between devices with their start and end apart: 7, of which 4 were waited for; matrix products, arithmetic and copies ran while one was open for 0% of the time, Pallas kernels for 5%

profile of v2, /device:TPU:1, one launch (start us, length us, event | category | flops | bytes accessed | tf_op | source)
XLA Modules:
  0.0 105.7 jit_solution(4229129108209485899)
XLA Ops:
  0.6 2.1 %broadcast_in_dim.4 = bf16[4,128,1024]{2,1,0:T(8,128)(2,1)} broadcast(bf16[128,1024]{1,0:T(8,128)(2,1)} %param.3), dimensions={1,2} | broadcast | bytes 1310720 | tf_op jit(solution)/shard_map/broadcast_in_dim | solution.py:225
  2.7 4.3 %all-to-all-start = ((bf16[4,128,1024]{2,1,0:T(8,128)(2,1)}), bf16[4,128,1024]{2,1,0:T(8,128)(2,1)S(1)}, u32[]{:S(2)}, u32[]{:S(2)}) async-start(bf16[4,128,1024]{2,1,0:T(8,128)(2,1)} %broadcast_in_dim.4), calls=%async_computation | async-start | bytes 2097152 | tf_op jit(solution)/shard_map/all_to_all | solution.py:224
  7.0 1.6 %pack.1 = bf16[80,1280]{1,0:T(8,128)(2,1)} custom-call(bf16[64,1024]{1,0:T(8,128)(2,1)} %bitcast.16, f32[64,256]{1,0:T(8,128)} %bitcast.15), custom_call_target="tpu_custom_call" | custom-call | tf_op jit(solution)/shard_map/pack/pallas_call | solution.py:211
  8.6 8.0 %collective-permute-start = (bf16[80,1280]{1,0:T(8,128)(2,1)}, bf16[80,1280]{1,0:T(8,128)(2,1)S(1)}, u32[]{:S(2)}, u32[]{:S(2)}) collective-permute-start(bf16[80,1280]{1,0:T(8,128)(2,1)} %pack.1), channel_id=1, source_target_pairs={{0,0},{2,2},{4,16},{6,18},{16,4},{18,6},{20,20},{22,22},{1,1},{3,3... | collective-permute-start | bytes 614408 | tf_op jit(solution)/shard_map/ppermute | solution.py:223
  16.7 1.9 %collective-permute-start.1 = (bf16[80,1280]{1,0:T(8,128)(2,1)}, bf16[80,1280]{1,0:T(8,128)(2,1)S(1)}, u32[]{:S(2)}, u32[]{:S(2)}) collective-permute-start(bf16[80,1280]{1,0:T(8,128)(2,1)} %pack.1), channel_id=1, source_target_pairs={{0,2},{2,0},{4,18},{6,16},{16,6},{18,4},{20,22},{22,20},{1,3},{3,1... | collective-permute-start | bytes 614408 | tf_op jit(solution)/shard_map/ppermute | solution.py:223
  18.6 0.1 pad_add_fusion.place
  18.7 15.1 %collective-permute-done.first = bf16[80,1280]{1,0:T(8,128)(2,1)S(1)} collective-permute-done((bf16[80,1280]{1,0:T(8,128)(2,1)}, bf16[80,1280]{1,0:T(8,128)(2,1)S(1)}, u32[]{:S(2)}, u32[]{:S(2)}) %collective-permute-start) | collective-permute-done | bytes 204832 | tf_op jit(solution)/shard_map/ppermute | solution.py:223
  33.8 0.0 collective-permute-done.1.second
  33.8 0.7 prepare.1
  34.5 0.0 all-to-all-done
  34.5 1.9 %collective-permute-start.2 = (bf16[512,1024]{1,0:T(8,128)(2,1)S(1)}, bf16[512,1024]{1,0:T(8,128)(2,1)S(1)}, u32[]{:S(2)}, u32[]{:S(2)}) collective-permute-start(bf16[512,1024]{1,0:T(8,128)(2,1)S(1)} %bitcast.12), channel_id=1, source_target_pairs={{0,16},{16,0},{1,17},{17,1},{2,18},{18,2},{3,19},{19,3},{4,20},{20... | collective-permute-start | bytes 3145736 | tf_op jit(solution)/shard_map/ppermute | solution.py:236
  36.4 2.6 %early.1 = (f32[512,256]{1,0:T(8,128)S(1)}, f32[128,1024]{1,0:T(8,128)S(1)}, bf16[4,128,128]{2,1,0:T(8,128)(2,1)S(1)}) custom-call(bf16[512,1024]{1,0:T(8,128)(2,1)S(1)} %bitcast.13, bf16[128,1024]{1,0:T(8,128)(2,1)S(1)} %get-tuple-element.21.turn, bf16[128,512]{1,0:T(8,128)(2,1)S(1)} %get-tuple-element.22.codes_t, bf16[512,256]{1,0:T(8,128)(2,1)S(1)} %get-tuple-element.23.left), custom_call_target="tpu_custom_call" | custom-call | bytes 8000000 | tf_op jit(solution)/shard_map/early/pallas_call | solution.py:196
  39.0 0.0 collective-permute-done.2.samples
  39.0 4.3 %late.1 = (bf16[64,32,128]{2,1,0:T(8,128)(2,1)}, bf16[8,144,128]{2,1,0:T(8,128)(2,1)S(1)}) custom-call(s32[2]{0:T(128)S(1)} %pad_add_fusion.place, bf16[512,1024]{1,0:T(8,128)(2,1)S(1)} %collective-permute-done.2.samples, bf16[128,1024]{1,0:T(8,128)(2,1)S(1)} %get-tuple-element.21.turn, bf16[128,512]{1,0:T(8,128)(2,1)S(1)} %get-tuple-element.22.codes_t, ...), custom_call_target="tpu_custom_call" | custom-call | bytes 8000000 | tf_op jit(solution)/shard_map/late/pallas_call | solution.py:196
  43.3 0.0 copy-start
  43.3 14.1 %all-to-all-start.1 = ((bf16[64,32,128]{2,1,0:T(8,128)(2,1)}), bf16[64,32,128]{2,1,0:T(8,128)(2,1)S(1)}, u32[]{:S(2)}, u32[]{:S(2)}) async-start(bf16[64,32,128]{2,1,0:T(8,128)(2,1)} %get-tuple-element.27), calls=%async_computation.1 | async-start | bytes 1048576 | tf_op jit(solution)/shard_map/all_to_all | solution.py:252
  57.4 0.0 copy-done
  57.4 0.1 copy.6
  57.5 19.2 %all-to-all-done.1.got = bf16[64,32,128]{2,1,0:T(8,128)(2,1)S(1)} async-done(((bf16[64,32,128]{2,1,0:T(8,128)(2,1)}), bf16[64,32,128]{2,1,0:T(8,128)(2,1)S(1)}, u32[]{:S(2)}, u32[]{:S(2)}) %all-to-all-start.1) | async-done | bytes 524320 | tf_op jit(solution)/shard_map/all_to_all | solution.py:252
  76.6 0.8 reduce.1
  77.4 7.4 %all-to-all-start.2 = ((bf16[8,144,128]{2,1,0:T(8,128)(2,1)}), bf16[8,144,128]{2,1,0:T(8,128)(2,1)S(1)}, u32[]{:S(2)}, u32[]{:S(2)}) async-start(bf16[8,144,128]{2,1,0:T(8,128)(2,1)} %reduce.1), calls=%async_computation.2 | async-start | bytes 589824 | tf_op jit(solution)/shard_map/all_to_all | solution.py:257
  84.8 6.6 %all-to-all-done.2.got = bf16[8,144,128]{2,1,0:T(8,128)(2,1)S(1)} async-done(((bf16[8,144,128]{2,1,0:T(8,128)(2,1)}), bf16[8,144,128]{2,1,0:T(8,128)(2,1)S(1)}, u32[]{:S(2)}, u32[]{:S(2)}) %all-to-all-start.2) | async-done | bytes 294944 | tf_op jit(solution)/shard_map/all_to_all | solution.py:257
  91.4 0.6 pick.1
  92.0 3.5 %all-to-all-start.3 = ((bf16[16,16,128]{2,1,0:T(8,128)(2,1)}), bf16[16,16,128]{2,1,0:T(8,128)(2,1)S(1)}, u32[]{:S(2)}, u32[]{:S(2)}) async-start(bf16[16,16,128]{2,1,0:T(8,128)(2,1)} %pick.1), calls=%async_computation.3 | async-start | bytes 131072 | tf_op jit(solution)/shard_map/all_to_all | solution.py:262
  95.5 0.9 finish.1
  96.4 8.6 %all-to-all-done.3.got = bf16[16,16,128]{2,1,0:T(8,128)(2,1)S(1)} async-done(((bf16[16,16,128]{2,1,0:T(8,128)(2,1)}), bf16[16,16,128]{2,1,0:T(8,128)(2,1)S(1)}, u32[]{:S(2)}, u32[]{:S(2)}) %all-to-all-start.3) | async-done | bytes 65568 | tf_op jit(solution)/shard_map/all_to_all | solution.py:262
  104.9 0.8 codes.1
Async XLA Ops:
  2.7 31.8 %all-to-all-start = ((bf16[4,128,1024]{2,1,0:T(8,128)(2,1)}), bf16[4,128,1024]{2,1,0:T(8,128)(2,1)S(1)}, u32[]{:S(2)}, u32[]{:S(2)}) async-start(bf16[4,128,1024]{2,1,0:T(8,128)(2,1)} %broadcast_in_dim.4), calls=%async_computation | async-start | bytes 2097152 | tf_op jit(solution)/shard_map/all_to_all | solution.py:224
  8.6 25.1 %collective-permute-start = (bf16[80,1280]{1,0:T(8,128)(2,1)}, bf16[80,1280]{1,0:T(8,128)(2,1)S(1)}, u32[]{:S(2)}, u32[]{:S(2)}) collective-permute-start(bf16[80,1280]{1,0:T(8,128)(2,1)} %pack.1), channel_id=1, source_target_pairs={{0,0},{2,2},{4,16},{6,18},{16,4},{18,6},{20,20},{22,22},{1,1},{3,3... | collective-permute-start | bytes 614408 | tf_op jit(solution)/shard_map/ppermute | solution.py:223
  16.7 17.1 %collective-permute-start.1 = (bf16[80,1280]{1,0:T(8,128)(2,1)}, bf16[80,1280]{1,0:T(8,128)(2,1)S(1)}, u32[]{:S(2)}, u32[]{:S(2)}) collective-permute-start(bf16[80,1280]{1,0:T(8,128)(2,1)} %pack.1), channel_id=1, source_target_pairs={{0,2},{2,0},{4,18},{6,16},{16,6},{18,4},{20,22},{22,20},{1,3},{3,1... | collective-permute-start | bytes 614408 | tf_op jit(solution)/shard_map/ppermute | solution.py:223
  34.5 4.6 %collective-permute-start.2 = (bf16[512,1024]{1,0:T(8,128)(2,1)S(1)}, bf16[512,1024]{1,0:T(8,128)(2,1)S(1)}, u32[]{:S(2)}, u32[]{:S(2)}) collective-permute-start(bf16[512,1024]{1,0:T(8,128)(2,1)S(1)} %bitcast.12), channel_id=1, source_target_pairs={{0,16},{16,0},{1,17},{17,1},{2,18},{18,2},{3,19},{19,3},{4,20},{20... | collective-permute-start | bytes 3145736 | tf_op jit(solution)/shard_map/ppermute | solution.py:236
  43.3 14.1 %copy-start = (f32[1,256,64]{1,2,0:T(8,128)S(1)}, f32[1,256,64]{1,2,0:T(8,128)}, u32[]{:S(2)}) copy-start(f32[1,256,64]{1,2,0:T(8,128)} %param.5) | copy-start | bytes 196612
  43.3 33.3 %all-to-all-start.1 = ((bf16[64,32,128]{2,1,0:T(8,128)(2,1)}), bf16[64,32,128]{2,1,0:T(8,128)(2,1)S(1)}, u32[]{:S(2)}, u32[]{:S(2)}) async-start(bf16[64,32,128]{2,1,0:T(8,128)(2,1)} %get-tuple-element.27), calls=%async_computation.1 | async-start | bytes 1048576 | tf_op jit(solution)/shard_map/all_to_all | solution.py:252
  77.4 14.0 %all-to-all-start.2 = ((bf16[8,144,128]{2,1,0:T(8,128)(2,1)}), bf16[8,144,128]{2,1,0:T(8,128)(2,1)S(1)}, u32[]{:S(2)}, u32[]{:S(2)}) async-start(bf16[8,144,128]{2,1,0:T(8,128)(2,1)} %reduce.1), calls=%async_computation.2 | async-start | bytes 589824 | tf_op jit(solution)/shard_map/all_to_all | solution.py:257
  92.0 12.9 %all-to-all-start.3 = ((bf16[16,16,128]{2,1,0:T(8,128)(2,1)}), bf16[16,16,128]{2,1,0:T(8,128)(2,1)S(1)}, u32[]{:S(2)}, u32[]{:S(2)}) async-start(bf16[16,16,128]{2,1,0:T(8,128)(2,1)} %pick.1), calls=%async_computation.3 | async-start | bytes 131072 | tf_op jit(solution)/shard_map/all_to_all | solution.py:262

commit v3 on v2

v3 whole, which is shorter than its diff:
```python
import functools

import jax
import jax.numpy as jnp
from jax import lax
from jax.experimental import pallas as pl
from jax.experimental.pallas import tpu as pltpu
from jax.sharding import Mesh
from jax.sharding import PartitionSpec as P

SIZES = (4, 2, 2, 2, 2, 8)
NAMES = ("zh", "zl", "xh", "core", "xl", "y")
DP = ("zh", "zl", "xh", "core")
SUB = ("xl", "y")
TEAM = ("zl", "core", "xl")
FAR = ("zh", "xh")
BF = jnp.bfloat16
F32 = jnp.float32
NT = (((1,), (1,)), ((), ()))
VMEM = pl.BlockSpec(memory_space=pltpu.VMEM)
SMEM = pl.BlockSpec(memory_space=pltpu.SMEM)


def half_mask(shape):
    return lax.broadcasted_iota(jnp.int32, shape, len(shape) - 1) < 64


def swap_halves(x):
    return pltpu.roll(x, 64, 1)


def pack_kernel(turn_t, codes_t, pack):
    codes = codes_t[...]
    square = jnp.sum(codes * codes, axis=0, keepdims=True)
    high = square.astype(BF).astype(F32)
    mid = (square - high).astype(BF).astype(F32)
    low = square - high - mid
    squares = jnp.concatenate([high, mid, low, jnp.zeros((13, 256), F32)], axis=0).astype(BF)
    pack[:, 0:1024] = turn_t[...]
    pack[:, 1024:1280] = codes.astype(BF)
    pack[0:16, 1280:] = squares[:, :128]
    pack[16:32, 1280:] = squares[:, 128:]
    pack[32:64, 1280:] = jnp.zeros((32, 128), BF)


def prepare_kernel(place, first, second, turn, codes_t, left):
    odd = place[1]
    w0, w1 = first[...], second[...]
    wa = jnp.where(odd == 0, w0, w1)
    wb = jnp.where(odd == 0, w1, w0)
    turn[0:64, :] = wa[:, :1024]
    turn[64:128, :] = wb[:, :1024]
    zero = jnp.zeros((64, 256), BF)
    both = jnp.concatenate(
        [
            jnp.concatenate([wa[:, 1024:1280], zero], axis=1),
            jnp.concatenate([zero, wb[:, 1024:1280]], axis=1),
        ],
        axis=0,
    )
    codes_t[...] = both
    squares = jnp.concatenate(
        [wa[0:16, 1280:], wa[16:32, 1280:], wb[0:16, 1280:], wb[16:32, 1280:]], axis=1
    )
    left[...] = jnp.concatenate([both * BF(-2.0), squares, jnp.zeros((112, 512), BF)], axis=0).T


def assign_rows(samples, turn, codes_t, left, sums, cross, first, put):
    rows, chunk = 512, 256
    lane = lax.broadcasted_iota(jnp.int32, (chunk, 128), 1)
    three = jnp.where(lane < 3, 1.0, 0.0).astype(BF)
    ones = jnp.ones((chunk, 128), BF)
    row8 = lax.broadcasted_iota(jnp.int32, (8, 128), 0)
    pick = jnp.where(half_mask((8, 128)) == (row8 == 0), 1.0, 0.0).astype(F32)
    for c in range(rows // chunk):
        x = samples[c * chunk : (c + 1) * chunk, :]
        rot = lax.dot_general(x, turn[...], NT, preferred_element_type=F32).astype(BF)
        wide = rot.astype(F32)
        row_square = lax.dot_general(
            pick, wide * wide, NT, precision=lax.Precision.HIGHEST, preferred_element_type=F32
        )
        near = lax.dot_general(
            left[...], jnp.concatenate([rot, three], axis=1), NT, preferred_element_type=F32
        )
        parts = []
        for i in range(2):
            logits = -0.125 * (row_square[i : i + 1] + near[i * 256 : (i + 1) * 256])
            e = jnp.exp(logits - jnp.max(logits, axis=0, keepdims=True))
            parts.append((e * (1.0 / jnp.sum(e, axis=0, keepdims=True))).astype(BF))
        weights = jnp.concatenate(parts, axis=0)
        rebuilt = jnp.dot(codes_t[...], weights, preferred_element_type=F32).astype(BF)
        s = jnp.dot(weights, jnp.concatenate([rot, ones], axis=1), preferred_element_type=F32)
        k = jnp.dot(rebuilt, x, preferred_element_type=F32)
        if first and c == 0:
            sums[...] = s
            cross[...] = k
        else:
            sums[...] += s
            cross[...] += k
        back = rebuilt.T
        put(2 * c, back[:128])
        put(2 * c + 1, back[128:])


def early_kernel(samples, turn, codes_t, left, sums, cross, recon):
    def put(block, tile):
        recon[block] = tile

    assign_rows(samples, turn, codes_t, left, sums, cross, True, put)


def late_kernel(
    place, samples, turn, codes_t, left, sums_in, cross_in, recon_in, send, recon, sums, cross
):
    core = place[0]
    sums[...] = sums_in[...]
    cross[...] = cross_in[...]

    def put(block, tile):
        recon[(block >> 1) * 4 + (1 - core) * 2 + (block & 1), 0:128, :] = tile

    assign_rows(samples, turn, codes_t, left, sums, cross, False, put)
    for block in range(4):
        recon[(block >> 1) * 4 + core * 2 + (block & 1), 0:128, :] = recon_in[block]
    recon[:, 128:160, :] = jnp.zeros((8, 32, 128), BF)
    r = lax.broadcasted_iota(jnp.int32, (256, 256), 0)
    wanted = (
        ((r & 8) << 4) | ((r & 128) >> 1) | ((r & 4) << 3) | ((r & 2) << 3) | ((r & 112) >> 3) | (r & 1)
    )
    order = jnp.where(lax.broadcasted_iota(jnp.int32, (256, 256), 1) == wanted, 1.0, 0.0).astype(BF)
    for zh in range(4):
        piece = lax.dot_general(
            order, cross[:, zh * 256 : (zh + 1) * 256].astype(BF), NT, preferred_element_type=F32
        ).astype(BF)
        send[zh * 2, 0:128, :] = piece[:128]
        send[zh * 2 + 1, 0:128, :] = piece[128:]
    low = half_mask((32, 128))
    even = (lax.broadcasted_iota(jnp.int32, (16, 128), 1) & 32) == 0
    for q in range(8):
        at = q * 32
        a, b = sums[at : at + 32, :], sums[256 + at : 288 + at, :]
        send[q, 128:160, :] = jnp.where(low, a[:, :128], b[:, :128]).astype(BF)
        count = jnp.where(low, a[:, 128:], b[:, 128:])
        send[q, 160:176, :] = jnp.where(even, count[:16], count[16:]).astype(BF)


def middle_kernel(got, send):
    total = jnp.sum(got[...].astype(F32), axis=0)
    sums, count = total[128:160], total[160:176]
    lane = lax.broadcasted_iota(jnp.int32, (16, 128), 1)
    low = half_mask((16, 128))
    halves = []
    for i in range(2):
        if i == 0:
            base = count
            tile = jnp.where(low, sums[:16], swap_halves(sums[16:]))
        else:
            base = swap_halves(count)
            tile = jnp.where(low, swap_halves(sums[:16]), sums[16:])
        wide = jnp.where(
            lane < 32, base, jnp.where(lane < 96, pltpu.roll(base, 32, 1), swap_halves(base))
        )
        halves.append(jnp.concatenate([tile, wide], axis=0).astype(BF))
    for y in range(8):
        send[y, 0:16, :] = total[y * 16 : y * 16 + 16].astype(BF)
        send[y, 16:48, :] = halves[y & 1]


def reduce_kernel(place, got, codes, recon_in, recon):
    total = jnp.sum(got[...].astype(F32), axis=0)
    cross = total[:16]
    high = cross.astype(BF)
    rest = (cross - high.astype(F32)).astype(BF)
    both = jnp.concatenate([high, rest], axis=0).astype(F32)
    at = pl.multiple_of(place[0] * 32, 32)
    own = codes[pl.ds(at, 32), :]
    own = jnp.concatenate([own[:16], own[16:]], axis=1)
    fresh = ((total[16:32] + own) / (total[32:48] + 1.0)).astype(BF)
    for c in range(8):
        recon[c, 0:128, :] = recon_in[c, 0:128, :]
        tile = jnp.concatenate(
            [both[2 * c : 2 * c + 2], both[16 + 2 * c : 18 + 2 * c], jnp.zeros((12, 128), F32)], axis=0
        )
        recon[c, 128:144, :] = tile.astype(BF)
        recon[c, 144:160, :] = fresh


def pick_kernel(place, got, spread):
    tile = got[place[0], 144:160, :]
    for q in range(8):
        spread[q] = tile


def finish_kernel(got, recon, cross):
    for c in range(8):
        zl, core, xl = c >> 2, (c >> 1) & 1, c & 1
        at = (xl * 4 + zl * 2 + core) * 128
        recon[:, at : at + 128] = got[c, 0:128, :]
        t = got[c, 128:144, :].astype(F32)
        cross[:, at : at + 128] = t[0:2] + t[2:4]


def codes_kernel(got, codes_t):
    tiles = []
    for q in range(8):
        t = got[q].astype(F32)
        tiles += [t, swap_halves(t)]
    codes_t[...] = jnp.concatenate(tiles, axis=0).T[:64]


def call(kernel, name, outs, args, flops=0, moved=0, scratch=()):
    return pl.pallas_call(
        kernel,
        out_shape=tuple(jax.ShapeDtypeStruct(*o) for o in outs),
        in_specs=[SMEM if a.ndim == 1 else VMEM for a in args],
        out_specs=(VMEM,) * len(outs),
        scratch_shapes=list(scratch),
        compiler_params=pltpu.CompilerParams(vmem_limit_bytes=40 * 1024 * 1024),
        cost_estimate=pl.CostEstimate(flops=flops, bytes_accessed=moved, transcendentals=0),
        name=name,
    )(*args)


def per_device(samples, rotation, codebook):
    core, xl, y = lax.axis_index("core"), lax.axis_index("xl"), lax.axis_index("y")
    (pack,) = call(pack_kernel, "pack", [((64, 1408), BF)], (rotation.T, codebook[0].T))
    packs = []
    for p in range(2):
        pairs = [(k * 8 + n, (n >> 1) * 8 + 2 * k + ((n & 1) ^ p)) for k in range(4) for n in range(8)]
        packs.append(lax.ppermute(pack, ("zl", "core", "y"), pairs))
    mine = lax.all_to_all(
        jnp.broadcast_to(samples[None], (4, 128, 1024)), ("zl", "xl"), 0, 0, tiled=True
    ).reshape(512, 1024)
    place = jnp.stack([core, y & 1]).astype(jnp.int32)
    tools = call(
        prepare_kernel,
        "prepare",
        [((128, 1024), BF), ((128, 512), BF), ((512, 256), BF)],
        (place, *packs),
    )
    mine, *tools = lax.optimization_barrier((mine, *tools))
    other = lax.ppermute(mine, "core", [(0, 1), (1, 0)])
    sums, cross, early = call(
        early_kernel,
        "early",
        [((512, 256), F32), ((128, 1024), F32), ((4, 128, 128), BF)],
        (mine, *tools),
        moved=8_000_000,
    )
    send, recon = call(
        late_kernel,
        "late",
        [((8, 176, 128), BF), ((8, 160, 128), BF)],
        (place, other, *tools, sums, cross, early),
        moved=8_000_000,
        scratch=[pltpu.VMEM((512, 256), F32), pltpu.VMEM((128, 1024), F32)],
    )
    got = lax.all_to_all(send, FAR, 0, 0, tiled=True)
    (send,) = call(middle_kernel, "middle", [((8, 48, 128), BF)], (got,))
    got = lax.all_to_all(send, "y", 0, 0, tiled=True)
    chunk = (lax.axis_index("zh") * 2 + lax.axis_index("xh")).astype(jnp.int32).reshape(1)
    (recon,) = call(
        reduce_kernel, "reduce", [((8, 160, 128), BF)], (chunk, got, codebook[0], recon)
    )
    back = lax.all_to_all(recon, TEAM, 0, 0, tiled=True)
    source = (y >> 1) * 2 + xl
    (spread,) = call(
        pick_kernel, "pick", [((8, 16, 128), BF)], (source.astype(jnp.int32).reshape(1), back)
    )
    spread = lax.all_to_all(spread, FAR, 0, 0, tiled=True)
    recon, cross = call(finish_kernel, "finish", [((128, 1024), BF), ((2, 1024), F32)], (back,))
    (new_codes,) = call(codes_kernel, "codes", [((64, 256), F32)], (spread,))
    return recon, new_codes.T[None], cross


def solution(mesh):
    fine = Mesh(mesh.devices.reshape(SIZES), NAMES)
    rows = P(DP + SUB, None)
    return jax.shard_map(
        per_device,
        mesh=fine,
        in_specs=(rows, P(None, SUB), P(SUB, None, None)),
        out_specs=(rows, P(SUB, None, None), rows),
        check_vma=False,
    )
```

time: 106 us -> 107 us (level)
  blocking collectives: 0 us -> 21.9 us
  waiting for transfers between devices: 49.4 us -> 31.2 us
  Pallas kernels: 12.2 us -> 10.5 us
  starting transfers between devices: 41.1 us -> 39.8 us
    all_to_all x0 -> x1, blocking collectives: none -> 21.9 us  [per_device(): got = lax.all_to_all(send, FAR, 0, 0, tiled=True)]
    all_to_all x3, waiting for transfers between devices: 27.7 us -> 15.6 us  [the longest x1 8.13 us: per_device(): spread = lax.all_to_all(spread, FAR, 0, 0, tiled=True)]
    ppermute x2, waiting for transfers between devices: 15.1 us -> 9.04 us  [per_device(): packs.append(lax.ppermute(pack, ('zl', 'core', 'y'), pairs))]
    ppermute x2, starting transfers between devices: 9.95 us -> 7.99 us  [per_device(): packs.append(lax.ppermute(pack, ('zl', 'core', 'y'), pairs))]
    pallas_call x1 -> x0, Pallas kernels: 1.62 us -> none  [per_device(): pl.pallas_call(pack_kernel, out_shape=jax.ShapeDtypeStruct((80, 1280), BF...]
    pallas_call x7 -> x9, Pallas kernels: 10.6 us -> 10.5 us  [call(): pl.pallas_call(kernel, out_shape=tuple((jax.ShapeDtypeStruct(*o) for o in...]
  transfers between devices with their start and end apart: 7 -> 7, of which waited for: 4 -> 5; matrix products, arithmetic and copies ran while one was open for 0% -> 0% of each run, Pallas kernels for 5% -> 4%
where the time goes in v3:
time: 107 us; the launch traced here: 106 us
  starting transfers between devices  39.8 us (37%)
  waiting for transfers between devices  31.2 us (29%)
  blocking collectives  21.9 us (20%)
  Pallas kernels  10.5 us (10%)
  local copies, waits for them, and re-layouts  2.15 us (2%)
    all_to_all x1, blocking collectives, per_device(): got = lax.all_to_all(send, FAR, 0, 0, tiled=True)  21.9 us
    all_to_all x1, starting transfers between devices, per_device(): got = lax.all_to_all(send, 'y', 0, 0, tiled=True)  13.8 us
    pallas_call x9, Pallas kernels, call(): pl.pallas_call(kernel, out_shape=tuple((jax.ShapeDtypeStruct(*o) for o in...  10.5 us
    ppermute x2, waiting for transfers between devices, per_device(): packs.append(lax.ppermute(pack, ('zl', 'core', 'y'), pairs))  9.04 us
    all_to_all x1, waiting for transfers between devices, per_device(): spread = lax.all_to_all(spread, FAR, 0, 0, tiled=True)  8.13 us
    ppermute x2, starting transfers between devices, per_device(): packs.append(lax.ppermute(pack, ('zl', 'core', 'y'), pairs))  7.99 us
    all_to_all x1, waiting for transfers between devices, per_device(): got = lax.all_to_all(send, 'y', 0, 0, tiled=True)  7.48 us
    all_to_all x1, starting transfers between devices, per_device(): back = lax.all_to_all(recon, TEAM, 0, 0, tiled=True)  7.02 us
  transfers between devices with their start and end apart: 7, of which 5 were waited for; matrix products, arithmetic and copies ran while one was open for 0% of the time, Pallas kernels for 4%

profile of v3, /device:TPU:1, one launch (start us, length us, event | category | flops | bytes accessed | tf_op | source)
XLA Modules:
  0.0 106.4 jit_solution(6533443632155055590)
XLA Ops:
  0.6 2.1 %broadcast_in_dim.4 = bf16[4,128,1024]{2,1,0:T(8,128)(2,1)} broadcast(bf16[128,1024]{1,0:T(8,128)(2,1)} %param.3), dimensions={1,2} | broadcast | bytes 1310720 | tf_op jit(solution)/shard_map/broadcast_in_dim | solution.py:232
  2.7 0.0 copy-start
  2.7 0.0 copy-start.1
  2.7 5.2 %all-to-all-start = ((bf16[4,128,1024]{2,1,0:T(8,128)(2,1)}), bf16[4,128,1024]{2,1,0:T(8,128)(2,1)S(1)}, u32[]{:S(2)}, u32[]{:S(2)}) async-start(bf16[4,128,1024]{2,1,0:T(8,128)(2,1)} %broadcast_in_dim.4), calls=%async_computation | async-start | bytes 2097152 | tf_op jit(solution)/shard_map/all_to_all | solution.py:231
  7.9 0.0 copy-done
  7.9 0.0 copy-done.1
  8.0 5.1 %collective-permute-start = (bf16[64,1408]{1,0:T(8,128)(2,1)S(1)}, bf16[64,1408]{1,0:T(8,128)(2,1)S(1)}, u32[]{:S(2)}, u32[]{:S(2)}) collective-permute-start(bf16[64,1408]{1,0:T(8,128)(2,1)S(1)} %pack.1), channel_id=1, source_target_pairs={{0,0},{1,1},{2,16},{3,17},{4,64},{5,65},{6,80},{7,81},{16,2},{17,3... | collective-permute-start | bytes 540680 | tf_op jit(solution)/shard_map/ppermute | solution.py:230
  13.0 2.9 %collective-permute-start.1 = (bf16[64,1408]{1,0:T(8,128)(2,1)S(1)}, bf16[64,1408]{1,0:T(8,128)(2,1)S(1)}, u32[]{:S(2)}, u32[]{:S(2)}) collective-permute-start(bf16[64,1408]{1,0:T(8,128)(2,1)S(1)} %pack.1), channel_id=1, source_target_pairs={{0,1},{1,0},{2,17},{3,16},{4,65},{5,64},{6,81},{7,80},{16,3},{17,2... | collective-permute-start | bytes 540680 | tf_op jit(solution)/shard_map/ppermute | solution.py:230
  16.0 0.1 pad_add_fusion.place
  16.1 1.1 collective-permute-done.first
  17.1 8.0 %collective-permute-done.1.second = bf16[64,1408]{1,0:T(8,128)(2,1)S(1)} collective-permute-done((bf16[64,1408]{1,0:T(8,128)(2,1)S(1)}, bf16[64,1408]{1,0:T(8,128)(2,1)S(1)}, u32[]{:S(2)}, u32[]{:S(2)}) %collective-permute-start.1) | collective-permute-done | bytes 180256 | tf_op jit(solution)/shard_map/ppermute | solution.py:230
  25.1 0.7 prepare.1
  25.8 0.0 all-to-all-done
  25.8 2.4 %collective-permute-start.2 = (bf16[512,1024]{1,0:T(8,128)(2,1)S(1)}, bf16[512,1024]{1,0:T(8,128)(2,1)S(1)}, u32[]{:S(2)}, u32[]{:S(2)}) collective-permute-start(bf16[512,1024]{1,0:T(8,128)(2,1)S(1)} %bitcast.12), channel_id=1, source_target_pairs={{0,16},{16,0},{1,17},{17,1},{2,18},{18,2},{3,19},{19,3},{4,20},{20... | collective-permute-start | bytes 3145736 | tf_op jit(solution)/shard_map/ppermute | solution.py:242
  28.2 2.6 %early.1 = (f32[512,256]{1,0:T(8,128)S(1)}, f32[128,1024]{1,0:T(8,128)S(1)}, bf16[4,128,128]{2,1,0:T(8,128)(2,1)S(1)}) custom-call(bf16[512,1024]{1,0:T(8,128)(2,1)S(1)} %bitcast.13, bf16[128,1024]{1,0:T(8,128)(2,1)S(1)} %get-tuple-element.21.turn, bf16[128,512]{1,0:T(8,128)(2,1)S(1)} %get-tuple-element.22.codes_t, bf16[512,256]{1,0:T(8,128)(2,1)S(1)} %get-tuple-element.23.left), custom_call_target="tpu_custom_call" | custom-call | bytes 8000000 | tf_op jit(solution)/shard_map/early/pallas_call | solution.py:212
  30.8 0.0 collective-permute-done.2.samples
  30.8 3.5 %late.1 = (bf16[8,176,128]{2,1,0:T(8,128)(2,1)S(1)}, bf16[8,160,128]{2,1,0:T(8,128)(2,1)S(1)}) custom-call(s32[2]{0:T(128)S(1)} %pad_add_fusion.place, bf16[512,1024]{1,0:T(8,128)(2,1)S(1)} %collective-permute-done.2.samples, bf16[128,1024]{1,0:T(8,128)(2,1)S(1)} %get-tuple-element.21.turn, bf16[128,512]{1,0:T(8,128)(2,1)S(1)} %get-tuple-element.22.codes_t, ...), custom_call_target="tpu_custom_call" | custom-call | bytes 8000000 | tf_op jit(solution)/shard_map/late/pallas_call | solution.py:212
  34.3 21.9 %all_to_all.25.got = bf16[8,176,128]{2,1,0:T(8,128)(2,1)S(1)} all-to-all(bf16[8,176,128]{2,1,0:T(8,128)(2,1)S(1)} %get-tuple-element.27), channel_id=1, replica_groups=mesh['zh'=4,'zl'=2,'xh'=2,'core'=2,'xl'=2,'y'=8] {'zh','xh'}, dimensions={0} | all-to-all | bytes 720896 | tf_op jit(solution)/shard_map/all_to_all | solution.py:258
  56.2 0.8 middle.1
  57.0 13.8 %all-to-all-start.2 = ((bf16[8,48,128]{2,1,0:T(8,128)(2,1)}), bf16[8,48,128]{2,1,0:T(8,128)(2,1)S(1)}, u32[]{:S(2)}, u32[]{:S(2)}) async-start(bf16[8,48,128]{2,1,0:T(8,128)(2,1)} %middle.1), calls=%async_computation.2 | async-start | bytes 196608 | tf_op jit(solution)/shard_map/all_to_all | solution.py:260
  70.8 0.1 copy.6
  70.9 7.5 %all-to-all-done.2.got = bf16[8,48,128]{2,1,0:T(8,128)(2,1)S(1)} async-done(((bf16[8,48,128]{2,1,0:T(8,128)(2,1)}), bf16[8,48,128]{2,1,0:T(8,128)(2,1)S(1)}, u32[]{:S(2)}, u32[]{:S(2)}) %all-to-all-start.2) | async-done | bytes 98336 | tf_op jit(solution)/shard_map/all_to_all | solution.py:260
  78.4 0.8 reduce.1
  79.2 7.0 %all-to-all-start.3 = ((bf16[8,160,128]{2,1,0:T(8,128)(2,1)}), bf16[8,160,128]{2,1,0:T(8,128)(2,1)S(1)}, u32[]{:S(2)}, u32[]{:S(2)}) async-start(bf16[8,160,128]{2,1,0:T(8,128)(2,1)} %reduce.1), calls=%async_computation.3 | async-start | bytes 655360 | tf_op jit(solution)/shard_map/all_to_all | solution.py:265
  86.2 6.5 %all-to-all-done.3.got = bf16[8,160,128]{2,1,0:T(8,128)(2,1)S(1)} async-done(((bf16[8,160,128]{2,1,0:T(8,128)(2,1)}), bf16[8,160,128]{2,1,0:T(8,128)(2,1)S(1)}, u32[]{:S(2)}, u32[]{:S(2)}) %all-to-all-start.3) | async-done | bytes 327712 | tf_op jit(solution)/shard_map/all_to_all | solution.py:265
  92.8 0.6 pick.1
  93.4 3.3 %all-to-all-start.4 = ((bf16[8,16,128]{2,1,0:T(8,128)(2,1)}), bf16[8,16,128]{2,1,0:T(8,128)(2,1)S(1)}, u32[]{:S(2)}, u32[]{:S(2)}) async-start(bf16[8,16,128]{2,1,0:T(8,128)(2,1)} %pick.1), calls=%async_computation.4 | async-start | bytes 65536 | tf_op jit(solution)/shard_map/all_to_all | solution.py:270
  96.7 0.8 finish.1
  97.5 8.1 %all-to-all-done.4.got = bf16[8,16,128]{2,1,0:T(8,128)(2,1)S(1)} async-done(((bf16[8,16,128]{2,1,0:T(8,128)(2,1)}), bf16[8,16,128]{2,1,0:T(8,128)(2,1)S(1)}, u32[]{:S(2)}, u32[]{:S(2)}) %all-to-all-start.4) | async-done | bytes 32800 | tf_op jit(solution)/shard_map/all_to_all | solution.py:270
  105.6 0.8 codes.1
  (1 shorter events, 0.0 us)
Async XLA Ops:
  2.7 5.3 %copy-start = (f32[1,256,64]{1,2,0:T(8,128)S(1)}, f32[1,256,64]{1,2,0:T(8,128)}, u32[]{:S(2)}) copy-start(f32[1,256,64]{1,2,0:T(8,128)} %param.5) | copy-start | bytes 196612
  2.7 5.3 %copy-start.1 = (bf16[1024,64]{0,1:T(8,128)(2,1)S(1)}, bf16[1024,64]{0,1:T(8,128)(2,1)}, u32[]{:S(2)}) copy-start(bf16[1024,64]{0,1:T(8,128)(2,1)} %param.4) | copy-start | bytes 393220
  2.7 23.1 %all-to-all-start = ((bf16[4,128,1024]{2,1,0:T(8,128)(2,1)}), bf16[4,128,1024]{2,1,0:T(8,128)(2,1)S(1)}, u32[]{:S(2)}, u32[]{:S(2)}) async-start(bf16[4,128,1024]{2,1,0:T(8,128)(2,1)} %broadcast_in_dim.4), calls=%async_computation | async-start | bytes 2097152 | tf_op jit(solution)/shard_map/all_to_all | solution.py:231
  8.0 9.1 %collective-permute-start = (bf16[64,1408]{1,0:T(8,128)(2,1)S(1)}, bf16[64,1408]{1,0:T(8,128)(2,1)S(1)}, u32[]{:S(2)}, u32[]{:S(2)}) collective-permute-start(bf16[64,1408]{1,0:T(8,128)(2,1)S(1)} %pack.1), channel_id=1, source_target_pairs={{0,0},{1,1},{2,16},{3,17},{4,64},{5,65},{6,80},{7,81},{16,2},{17,3... | collective-permute-start | bytes 540680 | tf_op jit(solution)/shard_map/ppermute | solution.py:230
  13.0 12.1 %collective-permute-start.1 = (bf16[64,1408]{1,0:T(8,128)(2,1)S(1)}, bf16[64,1408]{1,0:T(8,128)(2,1)S(1)}, u32[]{:S(2)}, u32[]{:S(2)}) collective-permute-start(bf16[64,1408]{1,0:T(8,128)(2,1)S(1)} %pack.1), channel_id=1, source_target_pairs={{0,1},{1,0},{2,17},{3,16},{4,65},{5,64},{6,81},{7,80},{16,3},{17,2... | collective-permute-start | bytes 540680 | tf_op jit(solution)/shard_map/ppermute | solution.py:230
  25.8 5.0 %collective-permute-start.2 = (bf16[512,1024]{1,0:T(8,128)(2,1)S(1)}, bf16[512,1024]{1,0:T(8,128)(2,1)S(1)}, u32[]{:S(2)}, u32[]{:S(2)}) collective-permute-start(bf16[512,1024]{1,0:T(8,128)(2,1)S(1)} %bitcast.12), channel_id=1, source_target_pairs={{0,16},{16,0},{1,17},{17,1},{2,18},{18,2},{3,19},{19,3},{4,20},{20... | collective-permute-start | bytes 3145736 | tf_op jit(solution)/shard_map/ppermute | solution.py:242
  57.0 21.4 %all-to-all-start.2 = ((bf16[8,48,128]{2,1,0:T(8,128)(2,1)}), bf16[8,48,128]{2,1,0:T(8,128)(2,1)S(1)}, u32[]{:S(2)}, u32[]{:S(2)}) async-start(bf16[8,48,128]{2,1,0:T(8,128)(2,1)} %middle.1), calls=%async_computation.2 | async-start | bytes 196608 | tf_op jit(solution)/shard_map/all_to_all | solution.py:260
  79.2 13.6 %all-to-all-start.3 = ((bf16[8,160,128]{2,1,0:T(8,128)(2,1)}), bf16[8,160,128]{2,1,0:T(8,128)(2,1)S(1)}, u32[]{:S(2)}, u32[]{:S(2)}) async-start(bf16[8,160,128]{2,1,0:T(8,128)(2,1)} %reduce.1), calls=%async_computation.3 | async-start | bytes 655360 | tf_op jit(solution)/shard_map/all_to_all | solution.py:265
  93.4 12.3 %all-to-all-start.4 = ((bf16[8,16,128]{2,1,0:T(8,128)(2,1)}), bf16[8,16,128]{2,1,0:T(8,128)(2,1)S(1)}, u32[]{:S(2)}, u32[]{:S(2)}) async-start(bf16[8,16,128]{2,1,0:T(8,128)(2,1)} %pick.1), calls=%async_computation.4 | async-start | bytes 65536 | tf_op jit(solution)/shard_map/all_to_all | solution.py:270

commit v4 on v3

v4 whole, which is shorter than its diff:
```python
import functools

import jax
import jax.numpy as jnp
from jax import lax
from jax.experimental import pallas as pl
from jax.experimental.pallas import tpu as pltpu
from jax.sharding import Mesh
from jax.sharding import PartitionSpec as P

SIZES = (8, 2, 2, 2, 4, 2)
NAMES = ("z", "xh", "core", "xl", "yh", "yl")
DP = ("z", "xh", "core")
SUB = ("xl", "yh", "yl")
FAR = ("z", "xh")
NEAR = ("core", "xl", "yh", "yl")
BF = jnp.bfloat16
F32 = jnp.float32
NT = (((1,), (1,)), ((), ()))
VMEM = pl.BlockSpec(memory_space=pltpu.VMEM)
SMEM = pl.BlockSpec(memory_space=pltpu.SMEM)


def half_mask(shape):
    return lax.broadcasted_iota(jnp.int32, shape, len(shape) - 1) < 64


def swap_halves(x):
    return pltpu.roll(x, 64, 1)


def pack_kernel(turn_t, codes_t, pack):
    codes = codes_t[...]
    square = jnp.sum(codes * codes, axis=0, keepdims=True)
    high = square.astype(BF).astype(F32)
    mid = (square - high).astype(BF).astype(F32)
    low = square - high - mid
    squares = jnp.concatenate([high, mid, low, jnp.zeros((13, 256), F32)], axis=0).astype(BF)
    pack[:, 0:1024] = turn_t[...]
    pack[:, 1024:1280] = codes.astype(BF)
    pack[0:16, 1280:] = squares[:, :128]
    pack[16:32, 1280:] = squares[:, 128:]
    pack[32:64, 1280:] = jnp.zeros((32, 128), BF)


def prepare_kernel(place, first, second, turn, codes_t, left):
    odd = place[1]
    w0, w1 = first[...], second[...]
    wa = jnp.where(odd == 0, w0, w1)
    wb = jnp.where(odd == 0, w1, w0)
    turn[0:64, :] = wa[:, :1024]
    turn[64:128, :] = wb[:, :1024]
    zero = jnp.zeros((64, 256), BF)
    both = jnp.concatenate(
        [
            jnp.concatenate([wa[:, 1024:1280], zero], axis=1),
            jnp.concatenate([zero, wb[:, 1024:1280]], axis=1),
        ],
        axis=0,
    )
    codes_t[...] = both
    squares = jnp.concatenate(
        [wa[0:16, 1280:], wa[16:32, 1280:], wb[0:16, 1280:], wb[16:32, 1280:]], axis=1
    )
    left[...] = jnp.concatenate([both * BF(-2.0), squares, jnp.zeros((112, 512), BF)], axis=0).T


def assign_rows(samples, turn, codes_t, left, sums, cross, first, put):
    rows, chunk = 512, 256
    lane = lax.broadcasted_iota(jnp.int32, (chunk, 128), 1)
    three = jnp.where(lane < 3, 1.0, 0.0).astype(BF)
    ones = jnp.ones((chunk, 128), BF)
    row8 = lax.broadcasted_iota(jnp.int32, (8, 128), 0)
    pick = jnp.where(half_mask((8, 128)) == (row8 == 0), 1.0, 0.0).astype(F32)
    for c in range(rows // chunk):
        x = samples[c * chunk : (c + 1) * chunk, :]
        rot = lax.dot_general(x, turn[...], NT, preferred_element_type=F32).astype(BF)
        wide = rot.astype(F32)
        row_square = lax.dot_general(
            pick, wide * wide, NT, precision=lax.Precision.HIGHEST, preferred_element_type=F32
        )
        near = lax.dot_general(
            left[...], jnp.concatenate([rot, three], axis=1), NT, preferred_element_type=F32
        )
        parts = []
        for i in range(2):
            logits = -0.125 * (row_square[i : i + 1] + near[i * 256 : (i + 1) * 256])
            e = jnp.exp(logits - jnp.max(logits, axis=0, keepdims=True))
            parts.append((e * (1.0 / jnp.sum(e, axis=0, keepdims=True))).astype(BF))
        weights = jnp.concatenate(parts, axis=0)
        rebuilt = jnp.dot(codes_t[...], weights, preferred_element_type=F32).astype(BF)
        s = jnp.dot(weights, jnp.concatenate([rot, ones], axis=1), preferred_element_type=F32)
        k = jnp.dot(rebuilt, x, preferred_element_type=F32)
        if first and c == 0:
            sums[...] = s
            cross[...] = k
        else:
            sums[...] += s
            cross[...] += k
        back = rebuilt.T
        put(2 * c, back[:128])
        put(2 * c + 1, back[128:])


def early_kernel(samples, turn, codes_t, left, sums, cross, recon):
    def put(block, tile):
        recon[block] = tile

    assign_rows(samples, turn, codes_t, left, sums, cross, True, put)


def late_kernel(samples, turn, codes_t, left, sums_in, cross_in, send, recon, sums, cross):
    sums[...] = sums_in[...]
    cross[...] = cross_in[...]

    def put(block, tile):
        recon[block] = tile

    assign_rows(samples, turn, codes_t, left, sums, cross, False, put)
    eye = (
        lax.broadcasted_iota(jnp.int32, (128, 128), 0)
        == lax.broadcasted_iota(jnp.int32, (128, 128), 1)
    )
    eye = jnp.where(eye, 1.0, 0.0).astype(BF)
    for z in range(8):
        piece = lax.dot_general(
            eye, cross[:, z * 128 : (z + 1) * 128].astype(BF), NT, preferred_element_type=F32
        ).astype(BF)
        send[z * 2, 0:64, :] = piece[:64]
        send[z * 2 + 1, 0:64, :] = piece[64:]
    low = half_mask((16, 128))
    for q in range(16):
        at = q * 16
        a, b = sums[at : at + 16, :], sums[256 + at : 272 + at, :]
        send[q, 64:80, :] = jnp.where(low, a[:, :128], b[:, :128]).astype(BF)
        send[q, 80:96, :] = jnp.where(low, a[:, 128:], b[:, 128:]).astype(BF)


def split(x):
    high = x.astype(BF).astype(F32)
    return high, x - high


def middle_kernel(got, send):
    total = jnp.sum(got[...].astype(F32), axis=0)
    cross_high, cross_low = split(total[:64])
    sums, count = total[64:80], total[80:96]
    low = half_mask((8, 128))
    wide_low = half_mask((16, 128))
    lane = lax.broadcasted_iota(jnp.int32, (16, 128), 1)
    own = (lane >> 3) == lax.broadcasted_iota(jnp.int32, (16, 128), 0)
    turned = swap_halves(count)
    heads, tails = [], []
    for i in range(2):
        if i == 0:
            tail = jnp.where(low, sums[:8], swap_halves(sums[8:]))
            each = jnp.where(wide_low, count, turned)
        else:
            tail = jnp.where(low, swap_halves(sums[:8]), sums[8:])
            each = jnp.where(wide_low, turned, count)
        line_high, line_low = split(jnp.sum(jnp.where(own, each, 0.0), axis=0, keepdims=True))
        heads.append(jnp.concatenate([line_high, line_low, jnp.zeros((2, 128), F32)], axis=0))
        tails.append(tail)
    for d in range(32):
        i = (d >> 1) & 1
        send[d] = jnp.concatenate(
            [cross_high[2 * d : 2 * d + 2], cross_low[2 * d : 2 * d + 2], heads[i], tails[i]], axis=0
        ).astype(BF)


def reduce_kernel(place, got, codes, cross, spread):
    low = half_mask((2, 128))
    for xl in range(2):
        for core in range(2):
            ab = []
            for yl in range(2):
                t = jnp.zeros((16, 128), F32)
                for yh in range(4):
                    t += got[core * 16 + xl * 8 + yh * 2 + yl].astype(F32)
                ab.append(t[0:2] + t[2:4])
            a, b = ab
            at = (xl * 2 + core) * 256
            cross[:, at : at + 128] = jnp.where(low, a, swap_halves(b))
            cross[:, at + 128 : at + 256] = jnp.where(low, swap_halves(a), b)
    t = jnp.zeros((16, 128), F32)
    for yh in range(4):
        t += got[place[1] + yh * 2].astype(F32)
    lane = lax.broadcasted_iota(jnp.int32, (16, 128), 1)
    mine = (lane >> 3) == lax.broadcasted_iota(jnp.int32, (16, 128), 0)
    line = jnp.broadcast_to(t[4:5] + t[5:6], (16, 128))
    count = 0.125 * jnp.sum(jnp.where(mine, line, 0.0), axis=1, keepdims=True)
    count = jnp.where(half_mask((8, 128)), count[:8], count[8:])
    at = pl.multiple_of(place[0] * 16, 16)
    own = codes[pl.ds(at, 16), :]
    own = jnp.concatenate([own[:8], own[8:]], axis=1)
    fresh = (t[8:16] + own) / (count + 1.0)
    for q in range(16):
        spread[q] = fresh


def codes_kernel(got, codes_t):
    tiles = []
    for q in range(16):
        t = got[q]
        tiles += [t, swap_halves(t)]
    codes_t[...] = jnp.concatenate(tiles, axis=0).T[:64]


def second_kernel(place, early, got, send):
    xl = place[1]
    for yl in range(2):
        send[yl] = early[(1 - xl) * 2 + yl]
        send[2 + yl] = got[(1 - xl) * 2 + yl]


def third_kernel(place, early, got, got2, send):
    xl, yl = place[1], place[2]
    send[0] = early[xl * 2 + 1 - yl]
    send[1] = got[xl * 2 + 1 - yl]
    send[2] = got2[1 - yl]
    send[3] = got2[2 + 1 - yl]


def home_kernel(place, early, got, got2, got3, recon):
    core, xl, yl = place[0], place[1], place[2]
    low = half_mask((128, 128))
    here = [[early[xl * 2 + yl], got[xl * 2 + yl]], [got2[yl], got2[2 + yl]]]
    for across in range(2):
        for other in range(2):
            near = here[across][other].astype(F32)
            far = got3[across * 2 + other].astype(F32)
            a = jnp.where(yl == 0, near, far)
            b = jnp.where(yl == 0, far, near)
            side = (1 - xl) if across else xl
            half = (1 - core) if other else core
            at = pl.multiple_of((side * 2 + half) * 256, 256)
            recon[:, pl.ds(at, 128)] = jnp.where(low, a, swap_halves(b)).astype(BF)
            recon[:, pl.ds(at + 128, 128)] = jnp.where(low, swap_halves(a), b).astype(BF)


def call(kernel, name, outs, args, flops=0, moved=0, scratch=()):
    return pl.pallas_call(
        kernel,
        out_shape=tuple(jax.ShapeDtypeStruct(*o) for o in outs),
        in_specs=[SMEM if a.ndim == 1 else VMEM for a in args],
        out_specs=(VMEM,) * len(outs),
        scratch_shapes=list(scratch),
        compiler_params=pltpu.CompilerParams(vmem_limit_bytes=40 * 1024 * 1024),
        cost_estimate=pl.CostEstimate(flops=flops, bytes_accessed=moved, transcendentals=0),
        name=name,
    )(*args)


def per_device(samples, rotation, codebook):
    core, xl = lax.axis_index("core"), lax.axis_index("xl")
    yh, yl = lax.axis_index("yh"), lax.axis_index("yl")
    (pack,) = call(pack_kernel, "pack", [((64, 1408), BF)], (rotation.T, codebook[0].T))
    packs = []
    for p in range(2):
        pairs = [
            (c * 4 + y, (y >> 1) * 4 + 2 * c + ((y & 1) ^ p)) for c in range(2) for y in range(4)
        ]
        packs.append(lax.ppermute(pack, ("core", "yh"), pairs))
    mine = lax.all_to_all(
        jnp.broadcast_to(samples[None], (4, 128, 1024)), ("xl", "yl"), 0, 0, tiled=True
    ).reshape(512, 1024)
    tools = call(
        prepare_kernel,
        "prepare",
        [((128, 1024), BF), ((128, 512), BF), ((512, 256), BF)],
        (jnp.stack([core, yh & 1]).astype(jnp.int32), *packs),
    )
    mine, *tools = lax.optimization_barrier((mine, *tools))
    swap = [(0, 1), (1, 0)]
    other = lax.ppermute(mine, "core", swap)
    sums, cross, early = call(
        early_kernel,
        "early",
        [((512, 256), F32), ((128, 1024), F32), ((4, 128, 128), BF)],
        (mine, *tools),
        moved=8_000_000,
    )
    send, late = call(
        late_kernel,
        "late",
        [((16, 96, 128), BF), ((4, 128, 128), BF)],
        (other, *tools, sums, cross),
        moved=8_000_000,
        scratch=[pltpu.VMEM((512, 256), F32), pltpu.VMEM((128, 1024), F32)],
    )
    place = jnp.stack([core, xl, yl]).astype(jnp.int32)
    block = [((4, 128, 128), BF)]
    home = lax.ppermute(late, "core", swap)
    (second,) = call(second_kernel, "second", block, (place, early, home))
    home2 = lax.ppermute(second, "xl", swap)
    got = lax.all_to_all(send, FAR, 0, 0, tiled=True)
    got, home2 = lax.optimization_barrier((got, home2))
    (send,) = call(middle_kernel, "middle", [((32, 16, 128), BF)], (got,))
    (third,) = call(third_kernel, "third", block, (place, early, home, home2))
    home3 = lax.ppermute(third, "yl", swap)
    got = lax.all_to_all(send, NEAR, 0, 0, tiled=True)
    got, home3 = lax.optimization_barrier((got, home3))
    chunk = lax.axis_index("z") * 2 + lax.axis_index("xh")
    source = (yh >> 1) * 16 + xl * 8 + yl
    cross, spread = call(
        reduce_kernel,
        "reduce",
        [((2, 1024), F32), ((16, 8, 128), F32)],
        (jnp.stack([chunk, source]).astype(jnp.int32), got, codebook[0]),
    )
    spread = lax.all_to_all(spread, FAR, 0, 0, tiled=True)
    (recon,) = call(home_kernel, "home", [((128, 1024), BF)], (place, early, home, home2, home3))
    (new_codes,) = call(codes_kernel, "codes", [((64, 256), F32)], (spread,))
    return recon, new_codes.T[None], cross


def solution(mesh):
    fine = Mesh(mesh.devices.reshape(SIZES), NAMES)
    rows = P(DP + SUB, None)
    return jax.shard_map(
        per_device,
        mesh=fine,
        in_specs=(rows, P(None, SUB), P(SUB, None, None)),
        out_specs=(rows, P(SUB, None, None), rows),
        check_vma=False,
    )
```

time: 107 us -> 104 us (0.972); the launches traced: 106 us -> 102 us
  blocking collectives: 21.9 us -> 0 us
  starting transfers between devices: 39.8 us -> 49.5 us
  waiting for transfers between devices: 31.2 us -> 37.3 us
  Pallas kernels: 10.5 us -> 12.3 us
    all_to_all x1 -> x0, blocking collectives: 21.9 us -> none  [per_device(): got = lax.all_to_all(send, FAR, 0, 0, tiled=True)]
    ppermute x3 -> x6, waiting for transfers between devices: 9.05 us -> 26.9 us  [the longest x2 15.6 us: per_device(): packs.append(lax.ppermute(pack, ('core', 'yh'), pairs))]
    all_to_all x3, waiting for transfers between devices: 14 us -> 2.39 us  [the longest x1 1.72 us: per_device(): got = lax.all_to_all(send, FAR, 0, 0, tiled=True)]
    ppermute x3 -> x6, starting transfers between devices: 10.4 us -> 20.6 us  [the longest x2 9.98 us: per_device(): packs.append(lax.ppermute(pack, ('core', 'yh'), pairs))]
    all_to_all x3, starting transfers between devices: 26.1 us -> 22.6 us  [the longest x1 12.6 us: per_device(): got = lax.all_to_all(send, FAR, 0, 0, tiled=True)]
    all_to_all x1, starting transfers between devices: 3.34 us -> 6.35 us  [per_device(): spread = lax.all_to_all(spread, FAR, 0, 0, tiled=True)]
    pallas_call x9 -> x10, Pallas kernels: 10.5 us -> 12.3 us  [call(): pl.pallas_call(kernel, out_shape=tuple((jax.ShapeDtypeStruct(*o) for o in...]
  transfers between devices with their start and end apart: 7 -> 10, of which waited for: 5 -> 7; matrix products, arithmetic and copies ran while one was open for 0% -> 0% of each run, Pallas kernels for 4% -> 6%
where the time goes in v4:
time: 104 us; the launch traced here: 102 us
  starting transfers between devices  49.5 us (48%)
  waiting for transfers between devices  37.3 us (36%)
  Pallas kernels  12.3 us (12%)
  local copies, waits for them, and re-layouts  2.16 us (2%)
    ppermute x2, waiting for transfers between devices, per_device(): packs.append(lax.ppermute(pack, ('core', 'yh'), pairs))  15.6 us
    all_to_all x1, starting transfers between devices, per_device(): got = lax.all_to_all(send, FAR, 0, 0, tiled=True)  12.6 us
    pallas_call x10, Pallas kernels, call(): pl.pallas_call(kernel, out_shape=tuple((jax.ShapeDtypeStruct(*o) for o in...  12.3 us
    ppermute x2, starting transfers between devices, per_device(): packs.append(lax.ppermute(pack, ('core', 'yh'), pairs))  9.98 us
    all_to_all x1, waiting for transfers between devices, per_device(): spread = lax.all_to_all(spread, FAR, 0, 0, tiled=True)  8 us
    ppermute x1, waiting for transfers between devices, per_device(): home2 = lax.ppermute(second, 'xl', swap)  6.37 us
    all_to_all x1, starting transfers between devices, per_device(): spread = lax.all_to_all(spread, FAR, 0, 0, tiled=True)  6.35 us
    all_to_all x1, starting transfers between devices, per_device(): got = lax.all_to_all(send, NEAR, 0, 0, tiled=True)  5.51 us
  transfers between devices with their start and end apart: 10, of which 7 were waited for; matrix products, arithmetic and copies ran while one was open for 0% of the time, Pallas kernels for 6%

profile of v4, /device:TPU:1, one launch (start us, length us, event | category | flops | bytes accessed | tf_op | source)
XLA Modules:
  0.0 102.2 jit_solution(12132871197841136255)
XLA Ops:
  0.6 2.1 %broadcast_in_dim.4 = bf16[4,128,1024]{2,1,0:T(8,128)(2,1)} broadcast(bf16[128,1024]{1,0:T(8,128)(2,1)} %param.3), dimensions={1,2} | broadcast | bytes 1310720 | tf_op jit(solution)/shard_map/broadcast_in_dim | solution.py:265
  2.7 0.0 copy-start
  2.7 0.0 copy-start.1
  2.7 4.5 %all-to-all-start = ((bf16[4,128,1024]{2,1,0:T(8,128)(2,1)}), bf16[4,128,1024]{2,1,0:T(8,128)(2,1)S(1)}, u32[]{:S(2)}, u32[]{:S(2)}) async-start(bf16[4,128,1024]{2,1,0:T(8,128)(2,1)} %broadcast_in_dim.4), calls=%async_computation | async-start | bytes 2097152 | tf_op jit(solution)/shard_map/all_to_all | solution.py:264
  7.1 0.0 copy-done
  7.1 0.0 copy-done.1
  7.2 8.1 %collective-permute-start = (bf16[64,1408]{1,0:T(8,128)(2,1)S(1)}, bf16[64,1408]{1,0:T(8,128)(2,1)S(1)}, u32[]{:S(2)}, u32[]{:S(2)}) collective-permute-start(bf16[64,1408]{1,0:T(8,128)(2,1)S(1)} %pack.1), channel_id=1, source_target_pairs={{0,0},{2,2},{4,16},{6,18},{16,4},{18,6},{20,20},{22,22},{1,1},{3,3... | collective-permute-start | bytes 540680 | tf_op jit(solution)/shard_map/ppermute | solution.py:263
  15.3 1.9 %collective-permute-start.1 = (bf16[64,1408]{1,0:T(8,128)(2,1)S(1)}, bf16[64,1408]{1,0:T(8,128)(2,1)S(1)}, u32[]{:S(2)}, u32[]{:S(2)}) collective-permute-start(bf16[64,1408]{1,0:T(8,128)(2,1)S(1)} %pack.1), channel_id=1, source_target_pairs={{0,2},{2,0},{4,18},{6,16},{16,6},{18,4},{20,22},{22,20},{1,3},{3,1... | collective-permute-start | bytes 540680 | tf_op jit(solution)/shard_map/ppermute | solution.py:263
  17.2 0.1 pad_add_fusion.1.place
  17.3 15.6 %collective-permute-done.first = bf16[64,1408]{1,0:T(8,128)(2,1)S(1)} collective-permute-done((bf16[64,1408]{1,0:T(8,128)(2,1)S(1)}, bf16[64,1408]{1,0:T(8,128)(2,1)S(1)}, u32[]{:S(2)}, u32[]{:S(2)}) %collective-permute-start) | collective-permute-done | bytes 180256 | tf_op jit(solution)/shard_map/ppermute | solution.py:263
  32.9 0.0 collective-permute-done.1.second
  32.9 0.7 prepare.1
  33.5 0.0 all-to-all-done
  33.6 1.9 %collective-permute-start.2 = (bf16[512,1024]{1,0:T(8,128)(2,1)S(1)}, bf16[512,1024]{1,0:T(8,128)(2,1)S(1)}, u32[]{:S(2)}, u32[]{:S(2)}) collective-permute-start(bf16[512,1024]{1,0:T(8,128)(2,1)S(1)} %bitcast.14), channel_id=1, source_target_pairs={{0,16},{16,0},{1,17},{17,1},{2,18},{18,2},{3,19},{19,3},{4,20},{20... | collective-permute-start | bytes 3145736 | tf_op jit(solution)/shard_map/ppermute | solution.py:275
  35.5 2.6 %early.1 = (f32[512,256]{1,0:T(8,128)S(1)}, f32[128,1024]{1,0:T(8,128)S(1)}, bf16[4,128,128]{2,1,0:T(8,128)(2,1)S(1)}) custom-call(bf16[512,1024]{1,0:T(8,128)(2,1)S(1)} %bitcast.15, bf16[128,1024]{1,0:T(8,128)(2,1)S(1)} %get-tuple-element.25.turn, bf16[128,512]{1,0:T(8,128)(2,1)S(1)} %get-tuple-element.26.codes_t, bf16[512,256]{1,0:T(8,128)(2,1)S(1)} %get-tuple-element.27.left), custom_call_target="tpu_custom_call" | custom-call | bytes 8000000 | tf_op jit(solution)/shard_map/early/pallas_call | solution.py:242
  38.1 0.0 collective-permute-done.2.samples
  38.1 3.7 %late.1 = (bf16[16,96,128]{2,1,0:T(8,128)(2,1)}, bf16[4,128,128]{2,1,0:T(8,128)(2,1)S(1)}) custom-call(bf16[512,1024]{1,0:T(8,128)(2,1)S(1)} %collective-permute-done.2.samples, bf16[128,1024]{1,0:T(8,128)(2,1)S(1)} %get-tuple-element.25.turn, bf16[128,512]{1,0:T(8,128)(2,1)S(1)} %get-tuple-element.26.codes_t, bf16[512,256]{1,0:T(8,128)(2,1)S(1)} %get-tuple-element.27.left, ...), custom_call_target="tpu_custom_call" | custom-call | bytes 8000000 | tf_op jit(solution)/shard_map/late/pallas_call | solution.py:242
  41.8 12.6 %all-to-all-start.1 = ((bf16[16,96,128]{2,1,0:T(8,128)(2,1)}), bf16[16,96,128]{2,1,0:T(8,128)(2,1)S(1)}, u32[]{:S(2)}, u32[]{:S(2)}) async-start(bf16[16,96,128]{2,1,0:T(8,128)(2,1)} %get-tuple-element.32), calls=%async_computation.1 | async-start | bytes 786432 | tf_op jit(solution)/shard_map/all_to_all | solution.py:296
  54.4 2.7 %collective-permute-start.3 = (bf16[4,128,128]{2,1,0:T(8,128)(2,1)S(1)}, bf16[4,128,128]{2,1,0:T(8,128)(2,1)S(1)}, u32[]{:S(2)}, u32[]{:S(2)}) collective-permute-start(bf16[4,128,128]{2,1,0:T(8,128)(2,1)S(1)} %get-tuple-element.31), channel_id=1, source_target_pairs={{0,16},{16,0},{1,17},{17,1},{2,18},{18,2},{3,19},{19,3},{4,20},{20... | collective-permute-start | bytes 393224 | tf_op jit(solution)/shard_map/ppermute | solution.py:293
  57.0 0.1 pad_add_fusion.place
  57.1 0.9 collective-permute-done.3.got
  58.0 0.6 second.1
  58.6 2.7 %collective-permute-start.4 = (bf16[4,128,128]{2,1,0:T(8,128)(2,1)S(1)}, bf16[4,128,128]{2,1,0:T(8,128)(2,1)S(1)}, u32[]{:S(2)}, u32[]{:S(2)}) collective-permute-start(bf16[4,128,128]{2,1,0:T(8,128)(2,1)S(1)} %second.1), channel_id=1, source_target_pairs={{0,8},{8,0},{1,9},{9,1},{2,10},{10,2},{3,11},{11,3},{4,12},{12,4},... | collective-permute-start | bytes 393224 | tf_op jit(solution)/shard_map/ppermute | solution.py:295
  61.3 6.4 %collective-permute-done.4.got2 = bf16[4,128,128]{2,1,0:T(8,128)(2,1)S(1)} collective-permute-done((bf16[4,128,128]{2,1,0:T(8,128)(2,1)S(1)}, bf16[4,128,128]{2,1,0:T(8,128)(2,1)S(1)}, u32[]{:S(2)}, u32[]{:S(2)}) %collective-permute-start.4) | collective-permute-done | bytes 131104 | tf_op jit(solution)/shard_map/ppermute | solution.py:295
  67.7 1.7 %all-to-all-done.1.got = bf16[16,96,128]{2,1,0:T(8,128)(2,1)S(1)} async-done(((bf16[16,96,128]{2,1,0:T(8,128)(2,1)}), bf16[16,96,128]{2,1,0:T(8,128)(2,1)S(1)}, u32[]{:S(2)}, u32[]{:S(2)}) %all-to-all-start.1) | async-done | bytes 393248 | tf_op jit(solution)/shard_map/all_to_all | solution.py:296
  69.4 0.8 middle.1
  70.1 5.5 %all-to-all-start.2 = ((bf16[32,16,128]{2,1,0:T(8,128)(2,1)}), bf16[32,16,128]{2,1,0:T(8,128)(2,1)S(1)}, u32[]{:S(2)}, u32[]{:S(2)}) async-start(bf16[32,16,128]{2,1,0:T(8,128)(2,1)} %middle.1), calls=%async_computation.2 | async-start | bytes 262144 | tf_op jit(solution)/shard_map/all_to_all | solution.py:301
  75.7 0.6 third.1
  76.2 3.3 %collective-permute-start.5 = (bf16[4,128,128]{2,1,0:T(8,128)(2,1)S(1)}, bf16[4,128,128]{2,1,0:T(8,128)(2,1)S(1)}, u32[]{:S(2)}, u32[]{:S(2)}) collective-permute-start(bf16[4,128,128]{2,1,0:T(8,128)(2,1)S(1)} %third.1), channel_id=1, source_target_pairs={{0,1},{1,0},{2,3},{3,2},{4,5},{5,4},{6,7},{7,6},{8,9},{9,8},{10,11... | collective-permute-start | bytes 393224 | tf_op jit(solution)/shard_map/ppermute | solution.py:300
  79.5 0.1 copy.6
  79.6 0.1 pad_add_fusion.2.place
  79.7 4.1 %collective-permute-done.5.got3 = bf16[4,128,128]{2,1,0:T(8,128)(2,1)S(1)} collective-permute-done((bf16[4,128,128]{2,1,0:T(8,128)(2,1)S(1)}, bf16[4,128,128]{2,1,0:T(8,128)(2,1)S(1)}, u32[]{:S(2)}, u32[]{:S(2)}) %collective-permute-start.5) | collective-permute-done | bytes 131104 | tf_op jit(solution)/shard_map/ppermute | solution.py:300
  83.8 0.7 all-to-all-done.2.got
  84.4 1.3 %reduce.1 = (f32[2,1024]{1,0:T(2,128)}, f32[16,8,128]{2,1,0:T(8,128)}) custom-call(s32[2]{0:T(128)S(1)} %pad_add_fusion.2.place, bf16[32,16,128]{2,1,0:T(8,128)(2,1)S(1)} %all-to-all-done.2.got, f32[256,64]{1,0:T(8,128)S(1)} %bitcast.16), custom_call_target="tpu_custom_call" | custom-call | tf_op jit(solution)/shard_map/reduce/pallas_call | solution.py:242
  85.7 6.3 %all-to-all-start.3 = ((f32[16,8,128]{2,1,0:T(8,128)}), f32[16,8,128]{2,1,0:T(8,128)S(1)}, u32[]{:S(2)}, u32[]{:S(2)}) async-start(f32[16,8,128]{2,1,0:T(8,128)} %get-tuple-element.37), calls=%async_computation.3 | async-start | bytes 131072 | tf_op jit(solution)/shard_map/all_to_all | solution.py:311
  92.1 1.4 %home.1 = bf16[128,1024]{1,0:T(8,128)(2,1)} custom-call(s32[3]{0:T(128)S(1)} %pad_add_fusion.place, bf16[4,128,128]{2,1,0:T(8,128)(2,1)S(1)} %get-tuple-element.28.early, bf16[4,128,128]{2,1,0:T(8,128)(2,1)S(1)} %collective-permute-done.3.got, bf16[4,128,128]{2,1,0:T(8,128)(2,1)S(1)} %collective-permute-done.4.got2, ...), custom_call_target="tpu_custom_call" | custom-call | tf_op jit(solution)/shard_map/home/pallas_call | solution.py:242
  93.5 8.0 %all-to-all-done.3.got = f32[16,8,128]{2,1,0:T(8,128)S(1)} async-done(((f32[16,8,128]{2,1,0:T(8,128)}), f32[16,8,128]{2,1,0:T(8,128)S(1)}, u32[]{:S(2)}, u32[]{:S(2)}) %all-to-all-start.3) | async-done | bytes 65568 | tf_op jit(solution)/shard_map/all_to_all | solution.py:311
  101.5 0.8 codes.1
  (1 shorter events, 0.0 us)
Async XLA Ops:
  2.7 4.5 %copy-start = (f32[1,256,64]{1,2,0:T(8,128)S(1)}, f32[1,256,64]{1,2,0:T(8,128)}, u32[]{:S(2)}) copy-start(f32[1,256,64]{1,2,0:T(8,128)} %param.5) | copy-start | bytes 196612
  2.7 4.5 %copy-start.1 = (bf16[1024,64]{0,1:T(8,128)(2,1)S(1)}, bf16[1024,64]{0,1:T(8,128)(2,1)}, u32[]{:S(2)}) copy-start(bf16[1024,64]{0,1:T(8,128)(2,1)} %param.4) | copy-start | bytes 393220
  2.7 30.9 %all-to-all-start = ((bf16[4,128,1024]{2,1,0:T(8,128)(2,1)}), bf16[4,128,1024]{2,1,0:T(8,128)(2,1)S(1)}, u32[]{:S(2)}, u32[]{:S(2)}) async-start(bf16[4,128,1024]{2,1,0:T(8,128)(2,1)} %broadcast_in_dim.4), calls=%async_computation | async-start | bytes 2097152 | tf_op jit(solution)/shard_map/all_to_all | solution.py:264
  7.2 25.7 %collective-permute-start = (bf16[64,1408]{1,0:T(8,128)(2,1)S(1)}, bf16[64,1408]{1,0:T(8,128)(2,1)S(1)}, u32[]{:S(2)}, u32[]{:S(2)}) collective-permute-start(bf16[64,1408]{1,0:T(8,128)(2,1)S(1)} %pack.1), channel_id=1, source_target_pairs={{0,0},{2,2},{4,16},{6,18},{16,4},{18,6},{20,20},{22,22},{1,1},{3,3... | collective-permute-start | bytes 540680 | tf_op jit(solution)/shard_map/ppermute | solution.py:263
  15.3 17.6 %collective-permute-start.1 = (bf16[64,1408]{1,0:T(8,128)(2,1)S(1)}, bf16[64,1408]{1,0:T(8,128)(2,1)S(1)}, u32[]{:S(2)}, u32[]{:S(2)}) collective-permute-start(bf16[64,1408]{1,0:T(8,128)(2,1)S(1)} %pack.1), channel_id=1, source_target_pairs={{0,2},{2,0},{4,18},{6,16},{16,6},{18,4},{20,22},{22,20},{1,3},{3,1... | collective-permute-start | bytes 540680 | tf_op jit(solution)/shard_map/ppermute | solution.py:263
  33.6 4.6 %collective-permute-start.2 = (bf16[512,1024]{1,0:T(8,128)(2,1)S(1)}, bf16[512,1024]{1,0:T(8,128)(2,1)S(1)}, u32[]{:S(2)}, u32[]{:S(2)}) collective-permute-start(bf16[512,1024]{1,0:T(8,128)(2,1)S(1)} %bitcast.14), channel_id=1, source_target_pairs={{0,16},{16,0},{1,17},{17,1},{2,18},{18,2},{3,19},{19,3},{4,20},{20... | collective-permute-start | bytes 3145736 | tf_op jit(solution)/shard_map/ppermute | solution.py:275
  41.8 27.6 %all-to-all-start.1 = ((bf16[16,96,128]{2,1,0:T(8,128)(2,1)}), bf16[16,96,128]{2,1,0:T(8,128)(2,1)S(1)}, u32[]{:S(2)}, u32[]{:S(2)}) async-start(bf16[16,96,128]{2,1,0:T(8,128)(2,1)} %get-tuple-element.32), calls=%async_computation.1 | async-start | bytes 786432 | tf_op jit(solution)/shard_map/all_to_all | solution.py:296
  54.4 3.6 %collective-permute-start.3 = (bf16[4,128,128]{2,1,0:T(8,128)(2,1)S(1)}, bf16[4,128,128]{2,1,0:T(8,128)(2,1)S(1)}, u32[]{:S(2)}, u32[]{:S(2)}) collective-permute-start(bf16[4,128,128]{2,1,0:T(8,128)(2,1)S(1)} %get-tuple-element.31), channel_id=1, source_target_pairs={{0,16},{16,0},{1,17},{17,1},{2,18},{18,2},{3,19},{19,3},{4,20},{20... | collective-permute-start | bytes 393224 | tf_op jit(solution)/shard_map/ppermute | solution.py:293
  58.6 9.1 %collective-permute-start.4 = (bf16[4,128,128]{2,1,0:T(8,128)(2,1)S(1)}, bf16[4,128,128]{2,1,0:T(8,128)(2,1)S(1)}, u32[]{:S(2)}, u32[]{:S(2)}) collective-permute-start(bf16[4,128,128]{2,1,0:T(8,128)(2,1)S(1)} %second.1), channel_id=1, source_target_pairs={{0,8},{8,0},{1,9},{9,1},{2,10},{10,2},{3,11},{11,3},{4,12},{12,4},... | collective-permute-start | bytes 393224 | tf_op jit(solution)/shard_map/ppermute | solution.py:295
  70.1 14.3 %all-to-all-start.2 = ((bf16[32,16,128]{2,1,0:T(8,128)(2,1)}), bf16[32,16,128]{2,1,0:T(8,128)(2,1)S(1)}, u32[]{:S(2)}, u32[]{:S(2)}) async-start(bf16[32,16,128]{2,1,0:T(8,128)(2,1)} %middle.1), calls=%async_computation.2 | async-start | bytes 262144 | tf_op jit(solution)/shard_map/all_to_all | solution.py:301
  76.2 7.5 %collective-permute-start.5 = (bf16[4,128,128]{2,1,0:T(8,128)(2,1)S(1)}, bf16[4,128,128]{2,1,0:T(8,128)(2,1)S(1)}, u32[]{:S(2)}, u32[]{:S(2)}) collective-permute-start(bf16[4,128,128]{2,1,0:T(8,128)(2,1)S(1)} %third.1), channel_id=1, source_target_pairs={{0,1},{1,0},{2,3},{3,2},{4,5},{5,4},{6,7},{7,6},{8,9},{9,8},{10,11... | collective-permute-start | bytes 393224 | tf_op jit(solution)/shard_map/ppermute | solution.py:300
  85.7 15.8 %all-to-all-start.3 = ((f32[16,8,128]{2,1,0:T(8,128)}), f32[16,8,128]{2,1,0:T(8,128)S(1)}, u32[]{:S(2)}, u32[]{:S(2)}) async-start(f32[16,8,128]{2,1,0:T(8,128)} %get-tuple-element.37), calls=%async_computation.3 | async-start | bytes 131072 | tf_op jit(solution)/shard_map/all_to_all | solution.py:311

commit v5 on v4

--- a/solution.py
+++ b/solution.py
@@ -43,11 +43,11 @@
     pack[32:64, 1280:] = jnp.zeros((32, 128), BF)
 
 
-def prepare_kernel(place, first, second, turn, codes_t, left):
-    odd = place[1]
-    w0, w1 = first[...], second[...]
-    wa = jnp.where(odd == 0, w0, w1)
-    wb = jnp.where(odd == 0, w1, w0)
+def prepare_kernel(place, pack, first, second, turn, codes_t, left):
+    core, yl = place[0], place[3]
+    w0, w1, w2 = pack[...], first[...], second[...]
+    wa = jnp.where(core == 0, w0, jnp.where(yl == 0, w2, w1))
+    wb = jnp.where(core == 0, w1, jnp.where(yl == 0, w1, w2))
     turn[0:64, :] = wa[:, :1024]
     turn[64:128, :] = wb[:, :1024]
     zero = jnp.zeros((64, 256), BF)
@@ -109,7 +109,9 @@
     assign_rows(samples, turn, codes_t, left, sums, cross, True, put)
 
 
-def late_kernel(samples, turn, codes_t, left, sums_in, cross_in, send, recon, sums, cross):
+def late_kernel(
+    place, samples, turn, codes_t, left, sums_in, cross_in, early, send, recon, give, sums, cross
+):
     sums[...] = sums_in[...]
     cross[...] = cross_in[...]
 
@@ -117,6 +119,10 @@
         recon[block] = tile
 
     assign_rows(samples, turn, codes_t, left, sums, cross, False, put)
+    xl = place[1]
+    for yl in range(2):
+        give[yl] = early[(1 - xl) * 2 + yl]
+        give[2 + yl] = recon[(1 - xl) * 2 + yl]
     eye = (
         lax.broadcasted_iota(jnp.int32, (128, 128), 0)
         == lax.broadcasted_iota(jnp.int32, (128, 128), 1)
@@ -141,7 +147,7 @@
     return high, x - high
 
 
-def middle_kernel(got, send):
+def middle_kernel(place, got, send):
     total = jnp.sum(got[...].astype(F32), axis=0)
     cross_high, cross_low = split(total[:64])
     sums, count = total[64:80], total[80:96]
@@ -161,36 +167,51 @@
         line_high, line_low = split(jnp.sum(jnp.where(own, each, 0.0), axis=0, keepdims=True))
         heads.append(jnp.concatenate([line_high, line_low, jnp.zeros((2, 128), F32)], axis=0))
         tails.append(tail)
-    for d in range(32):
-        i = (d >> 1) & 1
-        send[d] = jnp.concatenate(
-            [cross_high[2 * d : 2 * d + 2], cross_low[2 * d : 2 * d + 2], heads[i], tails[i]], axis=0
-        ).astype(BF)
+    core, yh, yl = place[0], place[2], place[3]
+    last = jnp.where(core == 0, 5 - yl, 7 - 4 * yl)
+    for y in range(8):
+        is_last = ((y + 8 - 2 * yh) & 7) == last
+        head = jnp.where(is_last, heads[1], heads[0])
+        tail = jnp.where(is_last, tails[1], tails[0])
+        for c in range(4):
+            d = c * 8 + y
+            send[d] = jnp.concatenate(
+                [cross_high[2 * d : 2 * d + 2], cross_low[2 * d : 2 * d + 2], head, tail], axis=0
+            ).astype(BF)
+
+
+def arrange(low, a, b, c, d):
+    turned = swap_halves(b)
+    return [jnp.where(low, a, turned), d, jnp.where(low, turned, a), c]
 
 
 def reduce_kernel(place, got, codes, cross, spread):
     low = half_mask((2, 128))
     for xl in range(2):
-        for core in range(2):
-            ab = []
-            for yl in range(2):
-                t = jnp.zeros((16, 128), F32)
-                for yh in range(4):
-                    t += got[core * 16 + xl * 8 + yh * 2 + yl].astype(F32)
-                ab.append(t[0:2] + t[2:4])
-            a, b = ab
-            at = (xl * 2 + core) * 256
-            cross[:, at : at + 128] = jnp.where(low, a, swap_halves(b))
-            cross[:, at + 128 : at + 256] = jnp.where(low, swap_halves(a), b)
+        total = [jnp.zeros((2, 128), F32)] * 4
+        for yh in range(4):
+            blocks = []
+            for core in range(2):
+                for yl in range(2):
+                    t = got[core * 16 + xl * 8 + yh * 2 + yl].astype(F32)
+                    blocks.append(t[0:2] + t[2:4])
+            for p, tile in enumerate(arrange(low, *blocks)):
+                total[(yh + p) & 3] += tile
+        for p in range(4):
+            at = (xl * 4 + p) * 128
+            cross[:, at : at + 128] = total[p]
+    my_xl, my_yh, my_yl = place[1], place[2], place[3]
     t = jnp.zeros((16, 128), F32)
     for yh in range(4):
-        t += got[place[1] + yh * 2].astype(F32)
+        r = (2 * my_yh + my_yl + 8 - 2 * yh) & 7
+        yl = jnp.where((r >= 1) & (r <= 4), 1, 0)
+        t += got[((r >> 1) & 1) * 16 + my_xl * 8 + yh * 2 + yl].astype(F32)
     lane = lax.broadcasted_iota(jnp.int32, (16, 128), 1)
     mine = (lane >> 3) == lax.broadcasted_iota(jnp.int32, (16, 128), 0)
     line = jnp.broadcast_to(t[4:5] + t[5:6], (16, 128))
     count = 0.125 * jnp.sum(jnp.where(mine, line, 0.0), axis=1, keepdims=True)
     count = jnp.where(half_mask((8, 128)), count[:8], count[8:])
-    at = pl.multiple_of(place[0] * 16, 16)
+    at = pl.multiple_of(place[4] * 16, 16)
     own = codes[pl.ds(at, 16), :]
     own = jnp.concatenate([own[:8], own[8:]], axis=1)
     fresh = (t[8:16] + own) / (count + 1.0)
@@ -206,36 +227,39 @@
     codes_t[...] = jnp.concatenate(tiles, axis=0).T[:64]
 
 
-def second_kernel(place, early, got, send):
-    xl = place[1]
-    for yl in range(2):
-        send[yl] = early[(1 - xl) * 2 + yl]
-        send[2 + yl] = got[(1 - xl) * 2 + yl]
-
-
-def third_kernel(place, early, got, got2, send):
-    xl, yl = place[1], place[2]
+def second_kernel(place, early, late, got, send):
+    xl, yl = place[1], place[3]
     send[0] = early[xl * 2 + 1 - yl]
-    send[1] = got[xl * 2 + 1 - yl]
-    send[2] = got2[1 - yl]
-    send[3] = got2[2 + 1 - yl]
+    send[1] = late[xl * 2 + 1 - yl]
+    send[2] = got[1 - yl]
+    send[3] = got[2 + 1 - yl]
+
+
+def third_kernel(place, late, got, got2, send):
+    xl, yl = place[1], place[3]
+    send[0] = late[xl * 2 + yl]
+    send[1] = got2[1]
+    send[2] = got[2 + yl]
+    send[3] = got2[3]
 
 
 def home_kernel(place, early, got, got2, got3, recon):
-    core, xl, yl = place[0], place[1], place[2]
+    core, xl, yh, yl = place[0], place[1], place[2], place[3]
     low = half_mask((128, 128))
-    here = [[early[xl * 2 + yl], got[xl * 2 + yl]], [got2[yl], got2[2 + yl]]]
+    same = [[early[xl * 2 + yl], got2[0]], [got[yl], got2[2]]]
     for across in range(2):
-        for other in range(2):
-            near = here[across][other].astype(F32)
-            far = got3[across * 2 + other].astype(F32)
-            a = jnp.where(yl == 0, near, far)
-            b = jnp.where(yl == 0, far, near)
-            side = (1 - xl) if across else xl
-            half = (1 - core) if other else core
-            at = pl.multiple_of((side * 2 + half) * 256, 256)
-            recon[:, pl.ds(at, 128)] = jnp.where(low, a, swap_halves(b)).astype(BF)
-            recon[:, pl.ds(at + 128, 128)] = jnp.where(low, swap_halves(a), b).astype(BF)
+        mine = same[across]
+        theirs = [got3[across * 2], got3[across * 2 + 1]]
+        blocks = []
+        for c in range(2):
+            near = jnp.where(core == c, mine[0], theirs[0])
+            far = jnp.where(core == c, mine[1], theirs[1])
+            for y in range(2):
+                blocks.append(jnp.where(yl == y, near, far).astype(F32))
+        side = (1 - xl) if across else xl
+        for p, tile in enumerate(arrange(low, *blocks)):
+            at = pl.multiple_of((side * 4 + ((yh + p) & 3)) * 128, 128)
+            recon[:, pl.ds(at, 128)] = tile.astype(BF)
 
 
 def call(kernel, name, outs, args, flops=0, moved=0, scratch=()):
@@ -254,13 +278,18 @@
 def per_device(samples, rotation, codebook):
     core, xl = lax.axis_index("core"), lax.axis_index("xl")
     yh, yl = lax.axis_index("yh"), lax.axis_index("yl")
+    chunk = lax.axis_index("z") * 2 + lax.axis_index("xh")
+    place = jnp.stack([core, xl, yh, yl, chunk]).astype(jnp.int32)
     (pack,) = call(pack_kernel, "pack", [((64, 1408), BF)], (rotation.T, codebook[0].T))
     packs = []
-    for p in range(2):
+    for steps in ((3, 1), (None, 2)):
         pairs = [
-            (c * 4 + y, (y >> 1) * 4 + 2 * c + ((y & 1) ^ p)) for c in range(2) for y in range(4)
+            (c * 8 + ((y + step if y & 1 else y - step) & 7), c * 8 + y)
+            for c, step in enumerate(steps)
+            for y in range(8)
+            if step is not None
         ]
-        packs.append(lax.ppermute(pack, ("core", "yh"), pairs))
+        packs.append(lax.ppermute(pack, ("core", "yh", "yl"), pairs))
     mine = lax.all_to_all(
         jnp.broadcast_to(samples[None], (4, 128, 1024)), ("xl", "yl"), 0, 0, tiled=True
     ).reshape(512, 1024)
@@ -268,48 +297,46 @@
         prepare_kernel,
         "prepare",
         [((128, 1024), BF), ((128, 512), BF), ((512, 256), BF)],
-        (jnp.stack([core, yh & 1]).astype(jnp.int32), *packs),
+        (place, pack, *packs),
     )
     mine, *tools = lax.optimization_barrier((mine, *tools))
     swap = [(0, 1), (1, 0)]
     other = lax.ppermute(mine, "core", swap)
+    block = ((4, 128, 128), BF)
     sums, cross, early = call(
         early_kernel,
         "early",
-        [((512, 256), F32), ((128, 1024), F32), ((4, 128, 128), BF)],
+        [((512, 256), F32), ((128, 1024), F32), block],
         (mine, *tools),
         moved=8_000_000,
     )
-    send, late = call(
+    send, late, give = call(
         late_kernel,
         "late",
-        [((16, 96, 128), BF), ((4, 128, 128), BF)],
-        (other, *tools, sums, cross),
+        [((16, 96, 128), BF), block, block],
+        (place, other, *tools, sums, cross, early),
         moved=8_000_000,
         scratch=[pltpu.VMEM((512, 256), F32), pltpu.VMEM((128, 1024), F32)],
     )
-    place = jnp.stack([core, xl, yl]).astype(jnp.int32)
-    block = [((4, 128, 128), BF)]
-    home = lax.ppermute(late, "core", swap)
-    (second,) = call(second_kernel, "second", block, (place, early, home))
-    home2 = lax.ppermute(second, "xl", swap)
+    home = lax.ppermute(give, "xl", swap)
     got = lax.all_to_all(send, FAR, 0, 0, tiled=True)
+    got, home = lax.optimization_barrier((got, home))
+    (send,) = call(middle_kernel, "middle", [((32, 16, 128), BF)], (place, got))
+    (second,) = call(second_kernel, "second", [block], (place, early, late, home))
+    home2 = lax.ppermute(second, "yl", swap)
+    got = lax.all_to_all(send, NEAR, 0, 0, tiled=True)
     got, home2 = lax.optimization_barrier((got, home2))
-    (send,) = call(middle_kernel, "middle", [((32, 16, 128), BF)], (got,))
-    (third,) = call(third_kernel, "third", block, (place, early, home, home2))
-    home3 = lax.ppermute(third, "yl", swap)
-    got = lax.all_to_all(send, NEAR, 0, 0, tiled=True)
-    got, home3 = lax.optimization_barrier((got, home3))
-    chunk = lax.axis_index("z") * 2 + lax.axis_index("xh")
-    source = (yh >> 1) * 16 + xl * 8 + yl
     cross, spread = call(
         reduce_kernel,
         "reduce",
         [((2, 1024), F32), ((16, 8, 128), F32)],
-        (jnp.stack([chunk, source]).astype(jnp.int32), got, codebook[0]),
+        (place, got, codebook[0]),
     )
     spread = lax.all_to_all(spread, FAR, 0, 0, tiled=True)
+    (third,) = call(third_kernel, "third", [block], (place, late, home, home2))
+    home3 = lax.ppermute(third, "core", swap)
     (recon,) = call(home_kernel, "home", [((128, 1024), BF)], (place, early, home, home2, home3))
+    spread, recon = lax.optimization_barrier((spread, recon))
     (new_codes,) = call(codes_kernel, "codes", [((64, 256), F32)], (spread,))
     return recon, new_codes.T[None], cross
 

time: 104 us -> 102 us (0.981)
  starting transfers between devices: 49.5 us -> 47.3 us
  Pallas kernels: 12.3 us -> 13.4 us
    ppermute x5, waiting for transfers between devices: 26.9 us -> 20.4 us  [the longest x2 12.1 us: per_device(): packs.append(lax.ppermute(pack, ('core', 'yh', 'yl'), pairs))]
    all_to_all x1, waiting for transfers between devices: 1.72 us -> 8.1 us  [per_device(): got = lax.all_to_all(send, FAR, 0, 0, tiled=True)]
    all_to_all x1, starting transfers between devices: 6.35 us -> 3.87 us  [per_device(): spread = lax.all_to_all(spread, FAR, 0, 0, tiled=True)]
    all_to_all x1, starting transfers between devices: 5.51 us -> 6.9 us  [per_device(): got = lax.all_to_all(send, NEAR, 0, 0, tiled=True)]
    pallas_call x10, Pallas kernels: 12.3 us -> 13.4 us  [call(): pl.pallas_call(kernel, out_shape=tuple((jax.ShapeDtypeStruct(*o) for o in...]
where the time goes in v5:
time: 102 us; the launch traced here: 101 us
  starting transfers between devices  47.3 us (46%)
  waiting for transfers between devices  37.2 us (36%)
  Pallas kernels  13.4 us (13%)
  local copies, waits for them, and re-layouts  2.24 us (2%)
    pallas_call x10, Pallas kernels, call(): pl.pallas_call(kernel, out_shape=tuple((jax.ShapeDtypeStruct(*o) for o in...  13.4 us
    all_to_all x1, starting transfers between devices, per_device(): got = lax.all_to_all(send, FAR, 0, 0, tiled=True)  12.6 us
    ppermute x2, waiting for transfers between devices, per_device(): packs.append(lax.ppermute(pack, ('core', 'yh', 'yl'), pairs))  12.1 us
    all_to_all x1, waiting for transfers between devices, per_device(): got = lax.all_to_all(send, FAR, 0, 0, tiled=True)  8.1 us
    ppermute x2, starting transfers between devices, per_device(): packs.append(lax.ppermute(pack, ('core', 'yh', 'yl'), pairs))  8.08 us
    all_to_all x1, waiting for transfers between devices, per_device(): spread = lax.all_to_all(spread, FAR, 0, 0, tiled=True)  7.99 us
    all_to_all x1, starting transfers between devices, per_device(): got = lax.all_to_all(send, NEAR, 0, 0, tiled=True)  6.9 us
    all_to_all x1, starting transfers between devices, per_device(): lax.all_to_all(jnp.broadcast_to(samples[None], (4, 128, 1024)), ('xl', 'y...  4.45 us
  transfers between devices with their start and end apart: 10, of which 7 were waited for; matrix products, arithmetic and copies ran while one was open for 0% of the time, Pallas kernels for 6%

profile of v5, /device:TPU:1, one launch (start us, length us, event | category | flops | bytes accessed | tf_op | source)
XLA Modules:
  0.0 100.9 jit_solution(1362678188375670004)
XLA Ops:
  0.6 2.1 %broadcast_in_dim.4 = bf16[4,128,1024]{2,1,0:T(8,128)(2,1)} broadcast(bf16[128,1024]{1,0:T(8,128)(2,1)} %param.3), dimensions={1,2} | broadcast | bytes 1310720 | tf_op jit(solution)/shard_map/broadcast_in_dim | solution.py:294
  2.7 0.0 copy-start
  2.7 0.0 copy-start.1
  2.7 4.5 %all-to-all-start = ((bf16[4,128,1024]{2,1,0:T(8,128)(2,1)}), bf16[4,128,1024]{2,1,0:T(8,128)(2,1)S(1)}, u32[]{:S(2)}, u32[]{:S(2)}) async-start(bf16[4,128,1024]{2,1,0:T(8,128)(2,1)} %broadcast_in_dim.4), calls=%async_computation | async-start | bytes 2097152 | tf_op jit(solution)/shard_map/all_to_all | solution.py:293
  7.1 0.0 copy-done
  7.1 0.0 copy-done.1
  7.2 6.2 %collective-permute-start = (bf16[64,1408]{1,0:T(8,128)(2,1)S(1)}, bf16[64,1408]{1,0:T(8,128)(2,1)S(1)}, u32[]{:S(2)}, u32[]{:S(2)}) collective-permute-start(bf16[64,1408]{1,0:T(8,128)(2,1)S(1)} %pack.1), channel_id=1, source_target_pairs={{5,0},{4,1},{7,2},{6,3},{1,4},{0,5},{3,6},{2,7},{23,16},{18,17},{1... | collective-permute-start | bytes 540680 | tf_op jit(solution)/shard_map/ppermute | solution.py:292
  13.4 1.9 %collective-permute-start.1 = (bf16[64,1408]{1,0:T(8,128)(2,1)S(1)}, bf16[64,1408]{1,0:T(8,128)(2,1)S(1)}, u32[]{:S(2)}, u32[]{:S(2)}) collective-permute-start(bf16[64,1408]{1,0:T(8,128)(2,1)S(1)} %pack.1), channel_id=1, source_target_pairs={{22,16},{19,17},{16,18},{21,19},{18,20},{23,21},{20,22},{17,23},{3... | collective-permute-start | bytes 540680 | tf_op jit(solution)/shard_map/ppermute | solution.py:292
  15.3 0.1 stack.23.place
  15.4 0.9 collective-permute-done.first
  16.2 11.2 %collective-permute-done.1.second = bf16[64,1408]{1,0:T(8,128)(2,1)S(1)} collective-permute-done((bf16[64,1408]{1,0:T(8,128)(2,1)S(1)}, bf16[64,1408]{1,0:T(8,128)(2,1)S(1)}, u32[]{:S(2)}, u32[]{:S(2)}) %collective-permute-start.1) | collective-permute-done | bytes 180256 | tf_op jit(solution)/shard_map/ppermute | solution.py:292
  27.4 0.7 prepare.1
  28.1 0.0 all-to-all-done
  28.1 1.9 %collective-permute-start.2 = (bf16[512,1024]{1,0:T(8,128)(2,1)S(1)}, bf16[512,1024]{1,0:T(8,128)(2,1)S(1)}, u32[]{:S(2)}, u32[]{:S(2)}) collective-permute-start(bf16[512,1024]{1,0:T(8,128)(2,1)S(1)} %bitcast.13), channel_id=1, source_target_pairs={{0,16},{16,0},{1,17},{17,1},{2,18},{18,2},{3,19},{19,3},{4,20},{20... | collective-permute-start | bytes 3145736 | tf_op jit(solution)/shard_map/ppermute | solution.py:304
  30.1 2.6 %early.1 = (f32[512,256]{1,0:T(8,128)S(1)}, f32[128,1024]{1,0:T(8,128)S(1)}, bf16[4,128,128]{2,1,0:T(8,128)(2,1)S(1)}) custom-call(bf16[512,1024]{1,0:T(8,128)(2,1)S(1)} %bitcast.14, bf16[128,1024]{1,0:T(8,128)(2,1)S(1)} %get-tuple-element.28.turn, bf16[128,512]{1,0:T(8,128)(2,1)S(1)} %get-tuple-element.29.codes_t, bf16[512,256]{1,0:T(8,128)(2,1)S(1)} %get-tuple-element.30.left), custom_call_target="tpu_custom_call" | custom-call | bytes 8000000 | tf_op jit(solution)/shard_map/early/pallas_call | solution.py:266
  32.7 0.0 collective-permute-done.2.samples
  32.7 4.2 %late.1 = (bf16[16,96,128]{2,1,0:T(8,128)(2,1)}, bf16[4,128,128]{2,1,0:T(8,128)(2,1)S(1)}, bf16[4,128,128]{2,1,0:T(8,128)(2,1)S(1)}) custom-call(s32[5]{0:T(128)S(1)} %stack.23.place, bf16[512,1024]{1,0:T(8,128)(2,1)S(1)} %collective-permute-done.2.samples, bf16[128,1024]{1,0:T(8,128)(2,1)S(1)} %get-tuple-element.28.turn, ...), custom_call_target="tpu_custom_call" | custom-call | bytes 8000000 | tf_op jit(solution)/shard_map/late/pallas_call | solution.py:266
  36.9 12.6 %all-to-all-start.1 = ((bf16[16,96,128]{2,1,0:T(8,128)(2,1)}), bf16[16,96,128]{2,1,0:T(8,128)(2,1)S(1)}, u32[]{:S(2)}, u32[]{:S(2)}) async-start(bf16[16,96,128]{2,1,0:T(8,128)(2,1)} %get-tuple-element.34), calls=%async_computation.1 | async-start | bytes 786432 | tf_op jit(solution)/shard_map/all_to_all | solution.py:322
  49.5 2.8 %collective-permute-start.3 = (bf16[4,128,128]{2,1,0:T(8,128)(2,1)S(1)}, bf16[4,128,128]{2,1,0:T(8,128)(2,1)S(1)}, u32[]{:S(2)}, u32[]{:S(2)}) collective-permute-start(bf16[4,128,128]{2,1,0:T(8,128)(2,1)S(1)} %get-tuple-element.35), channel_id=1, source_target_pairs={{0,8},{8,0},{1,9},{9,1},{2,10},{10,2},{3,11},{11,3},{4,12},{12,4},... | collective-permute-start | bytes 393224 | tf_op jit(solution)/shard_map/ppermute | solution.py:321
  52.2 4.1 %collective-permute-done.3.got = bf16[4,128,128]{2,1,0:T(8,128)(2,1)S(1)} collective-permute-done((bf16[4,128,128]{2,1,0:T(8,128)(2,1)S(1)}, bf16[4,128,128]{2,1,0:T(8,128)(2,1)S(1)}, u32[]{:S(2)}, u32[]{:S(2)}) %collective-permute-start.3) | collective-permute-done | bytes 131104 | tf_op jit(solution)/shard_map/ppermute | solution.py:321
  56.3 8.1 %all-to-all-done.1.got = bf16[16,96,128]{2,1,0:T(8,128)(2,1)S(1)} async-done(((bf16[16,96,128]{2,1,0:T(8,128)(2,1)}), bf16[16,96,128]{2,1,0:T(8,128)(2,1)S(1)}, u32[]{:S(2)}, u32[]{:S(2)}) %all-to-all-start.1) | async-done | bytes 393248 | tf_op jit(solution)/shard_map/all_to_all | solution.py:322
  64.5 1.3 %middle.1 = bf16[32,16,128]{2,1,0:T(8,128)(2,1)} custom-call(s32[5]{0:T(128)S(1)} %stack.23.place, bf16[16,96,128]{2,1,0:T(8,128)(2,1)S(1)} %all-to-all-done.1.got), custom_call_target="tpu_custom_call" | custom-call | tf_op jit(solution)/shard_map/middle/pallas_call | solution.py:266
  65.8 6.9 %all-to-all-start.2 = ((bf16[32,16,128]{2,1,0:T(8,128)(2,1)}), bf16[32,16,128]{2,1,0:T(8,128)(2,1)S(1)}, u32[]{:S(2)}, u32[]{:S(2)}) async-start(bf16[32,16,128]{2,1,0:T(8,128)(2,1)} %middle.1), calls=%async_computation.2 | async-start | bytes 262144 | tf_op jit(solution)/shard_map/all_to_all | solution.py:327
  72.7 0.6 second.1
  73.2 3.3 %collective-permute-start.4 = (bf16[4,128,128]{2,1,0:T(8,128)(2,1)S(1)}, bf16[4,128,128]{2,1,0:T(8,128)(2,1)S(1)}, u32[]{:S(2)}, u32[]{:S(2)}) collective-permute-start(bf16[4,128,128]{2,1,0:T(8,128)(2,1)S(1)} %second.1), channel_id=1, source_target_pairs={{0,1},{1,0},{2,3},{3,2},{4,5},{5,4},{6,7},{7,6},{8,9},{9,8},{10,11... | collective-permute-start | bytes 393224 | tf_op jit(solution)/shard_map/ppermute | solution.py:326
  76.5 4.2 %collective-permute-done.4.got2 = bf16[4,128,128]{2,1,0:T(8,128)(2,1)S(1)} collective-permute-done((bf16[4,128,128]{2,1,0:T(8,128)(2,1)S(1)}, bf16[4,128,128]{2,1,0:T(8,128)(2,1)S(1)}, u32[]{:S(2)}, u32[]{:S(2)}) %collective-permute-start.4) | collective-permute-done | bytes 131104 | tf_op jit(solution)/shard_map/ppermute | solution.py:326
  80.8 0.7 all-to-all-done.2.got
  81.4 0.5 third.1
  82.0 3.5 %collective-permute-start.5 = (bf16[4,128,128]{2,1,0:T(8,128)(2,1)S(1)}, bf16[4,128,128]{2,1,0:T(8,128)(2,1)S(1)}, u32[]{:S(2)}, u32[]{:S(2)}) collective-permute-start(bf16[4,128,128]{2,1,0:T(8,128)(2,1)S(1)} %third.1), channel_id=1, source_target_pairs={{0,16},{16,0},{1,17},{17,1},{2,18},{18,2},{3,19},{19,3},{4,20},{20... | collective-permute-start | bytes 393224 | tf_op jit(solution)/shard_map/ppermute | solution.py:337
  85.5 0.1 copy.6
  85.6 1.3 %reduce.1 = (f32[2,1024]{1,0:T(2,128)}, f32[16,8,128]{2,1,0:T(8,128)}) custom-call(s32[5]{0:T(128)S(1)} %stack.23.place, bf16[32,16,128]{2,1,0:T(8,128)(2,1)S(1)} %all-to-all-done.2.got, f32[256,64]{1,0:T(8,128)S(1)} %bitcast.15), custom_call_target="tpu_custom_call" | custom-call | tf_op jit(solution)/shard_map/reduce/pallas_call | solution.py:266
  86.9 3.9 %all-to-all-start.3 = ((f32[16,8,128]{2,1,0:T(8,128)}), f32[16,8,128]{2,1,0:T(8,128)S(1)}, u32[]{:S(2)}, u32[]{:S(2)}) async-start(f32[16,8,128]{2,1,0:T(8,128)} %get-tuple-element.40), calls=%async_computation.3 | async-start | bytes 131072 | tf_op jit(solution)/shard_map/all_to_all | solution.py:335
  90.8 0.0 collective-permute-done.5.got3
  90.8 1.4 %home.1 = bf16[128,1024]{1,0:T(8,128)(2,1)} custom-call(s32[5]{0:T(128)S(1)} %stack.23.place, bf16[4,128,128]{2,1,0:T(8,128)(2,1)S(1)} %get-tuple-element.33.early, bf16[4,128,128]{2,1,0:T(8,128)(2,1)S(1)} %collective-permute-done.3.got, bf16[4,128,128]{2,1,0:T(8,128)(2,1)S(1)} %collective-permute-done.4.got2, ...), custom_call_target="tpu_custom_call" | custom-call | tf_op jit(solution)/shard_map/home/pallas_call | solution.py:266
  92.2 8.0 %all-to-all-done.3.got = f32[16,8,128]{2,1,0:T(8,128)S(1)} async-done(((f32[16,8,128]{2,1,0:T(8,128)}), f32[16,8,128]{2,1,0:T(8,128)S(1)}, u32[]{:S(2)}, u32[]{:S(2)}) %all-to-all-start.3) | async-done | bytes 65568 | tf_op jit(solution)/shard_map/all_to_all | solution.py:335
  100.2 0.8 codes.1
  (1 shorter events, 0.0 us)
Async XLA Ops:
  2.7 4.5 %copy-start = (f32[1,256,64]{1,2,0:T(8,128)S(1)}, f32[1,256,64]{1,2,0:T(8,128)}, u32[]{:S(2)}) copy-start(f32[1,256,64]{1,2,0:T(8,128)} %param.5) | copy-start | bytes 196612
  2.7 4.5 %copy-start.1 = (bf16[1024,64]{0,1:T(8,128)(2,1)S(1)}, bf16[1024,64]{0,1:T(8,128)(2,1)}, u32[]{:S(2)}) copy-start(bf16[1024,64]{0,1:T(8,128)(2,1)} %param.4) | copy-start | bytes 393220
  2.7 25.4 %all-to-all-start = ((bf16[4,128,1024]{2,1,0:T(8,128)(2,1)}), bf16[4,128,1024]{2,1,0:T(8,128)(2,1)S(1)}, u32[]{:S(2)}, u32[]{:S(2)}) async-start(bf16[4,128,1024]{2,1,0:T(8,128)(2,1)} %broadcast_in_dim.4), calls=%async_computation | async-start | bytes 2097152 | tf_op jit(solution)/shard_map/all_to_all | solution.py:293
  7.2 9.0 %collective-permute-start = (bf16[64,1408]{1,0:T(8,128)(2,1)S(1)}, bf16[64,1408]{1,0:T(8,128)(2,1)S(1)}, u32[]{:S(2)}, u32[]{:S(2)}) collective-permute-start(bf16[64,1408]{1,0:T(8,128)(2,1)S(1)} %pack.1), channel_id=1, source_target_pairs={{5,0},{4,1},{7,2},{6,3},{1,4},{0,5},{3,6},{2,7},{23,16},{18,17},{1... | collective-permute-start | bytes 540680 | tf_op jit(solution)/shard_map/ppermute | solution.py:292
  13.4 14.1 %collective-permute-start.1 = (bf16[64,1408]{1,0:T(8,128)(2,1)S(1)}, bf16[64,1408]{1,0:T(8,128)(2,1)S(1)}, u32[]{:S(2)}, u32[]{:S(2)}) collective-permute-start(bf16[64,1408]{1,0:T(8,128)(2,1)S(1)} %pack.1), channel_id=1, source_target_pairs={{22,16},{19,17},{16,18},{21,19},{18,20},{23,21},{20,22},{17,23},{3... | collective-permute-start | bytes 540680 | tf_op jit(solution)/shard_map/ppermute | solution.py:292
  28.1 4.6 %collective-permute-start.2 = (bf16[512,1024]{1,0:T(8,128)(2,1)S(1)}, bf16[512,1024]{1,0:T(8,128)(2,1)S(1)}, u32[]{:S(2)}, u32[]{:S(2)}) collective-permute-start(bf16[512,1024]{1,0:T(8,128)(2,1)S(1)} %bitcast.13), channel_id=1, source_target_pairs={{0,16},{16,0},{1,17},{17,1},{2,18},{18,2},{3,19},{19,3},{4,20},{20... | collective-permute-start | bytes 3145736 | tf_op jit(solution)/shard_map/ppermute | solution.py:304
  36.9 27.5 %all-to-all-start.1 = ((bf16[16,96,128]{2,1,0:T(8,128)(2,1)}), bf16[16,96,128]{2,1,0:T(8,128)(2,1)S(1)}, u32[]{:S(2)}, u32[]{:S(2)}) async-start(bf16[16,96,128]{2,1,0:T(8,128)(2,1)} %get-tuple-element.34), calls=%async_computation.1 | async-start | bytes 786432 | tf_op jit(solution)/shard_map/all_to_all | solution.py:322
  49.5 6.9 %collective-permute-start.3 = (bf16[4,128,128]{2,1,0:T(8,128)(2,1)S(1)}, bf16[4,128,128]{2,1,0:T(8,128)(2,1)S(1)}, u32[]{:S(2)}, u32[]{:S(2)}) collective-permute-start(bf16[4,128,128]{2,1,0:T(8,128)(2,1)S(1)} %get-tuple-element.35), channel_id=1, source_target_pairs={{0,8},{8,0},{1,9},{9,1},{2,10},{10,2},{3,11},{11,3},{4,12},{12,4},... | collective-permute-start | bytes 393224 | tf_op jit(solution)/shard_map/ppermute | solution.py:321
  65.8 15.7 %all-to-all-start.2 = ((bf16[32,16,128]{2,1,0:T(8,128)(2,1)}), bf16[32,16,128]{2,1,0:T(8,128)(2,1)S(1)}, u32[]{:S(2)}, u32[]{:S(2)}) async-start(bf16[32,16,128]{2,1,0:T(8,128)(2,1)} %middle.1), calls=%async_computation.2 | async-start | bytes 262144 | tf_op jit(solution)/shard_map/all_to_all | solution.py:327
  73.2 7.5 %collective-permute-start.4 = (bf16[4,128,128]{2,1,0:T(8,128)(2,1)S(1)}, bf16[4,128,128]{2,1,0:T(8,128)(2,1)S(1)}, u32[]{:S(2)}, u32[]{:S(2)}) collective-permute-start(bf16[4,128,128]{2,1,0:T(8,128)(2,1)S(1)} %second.1), channel_id=1, source_target_pairs={{0,1},{1,0},{2,3},{3,2},{4,5},{5,4},{6,7},{7,6},{8,9},{9,8},{10,11... | collective-permute-start | bytes 393224 | tf_op jit(solution)/shard_map/ppermute | solution.py:326
  82.0 8.8 %collective-permute-start.5 = (bf16[4,128,128]{2,1,0:T(8,128)(2,1)S(1)}, bf16[4,128,128]{2,1,0:T(8,128)(2,1)S(1)}, u32[]{:S(2)}, u32[]{:S(2)}) collective-permute-start(bf16[4,128,128]{2,1,0:T(8,128)(2,1)S(1)} %third.1), channel_id=1, source_target_pairs={{0,16},{16,0},{1,17},{17,1},{2,18},{18,2},{3,19},{19,3},{4,20},{20... | collective-permute-start | bytes 393224 | tf_op jit(solution)/shard_map/ppermute | solution.py:337
  86.9 13.3 %all-to-all-start.3 = ((f32[16,8,128]{2,1,0:T(8,128)}), f32[16,8,128]{2,1,0:T(8,128)S(1)}, u32[]{:S(2)}, u32[]{:S(2)}) async-start(f32[16,8,128]{2,1,0:T(8,128)} %get-tuple-element.40), calls=%async_computation.3 | async-start | bytes 131072 | tf_op jit(solution)/shard_map/all_to_all | solution.py:335

commit v6 on v5

--- a/solution.py
+++ b/solution.py
@@ -29,7 +29,14 @@
     return pltpu.roll(x, 64, 1)
 
 
-def pack_kernel(turn_t, codes_t, pack):
+def split(x):
+    high = x.astype(BF).astype(F32)
+    return high, x - high
+
+
+def open_kernel(samples, turn_t, codes_t, pack, copies):
+    for n in range(4):
+        copies[n] = samples[...]
     codes = codes_t[...]
     square = jnp.sum(codes * codes, axis=0, keepdims=True)
     high = square.astype(BF).astype(F32)
@@ -65,20 +72,20 @@
     left[...] = jnp.concatenate([both * BF(-2.0), squares, jnp.zeros((112, 512), BF)], axis=0).T
 
 
-def assign_rows(samples, turn, codes_t, left, sums, cross, first, put):
+def assign_rows(samples, turn, codes_t, left, sums, cross, put):
     rows, chunk = 512, 256
     lane = lax.broadcasted_iota(jnp.int32, (chunk, 128), 1)
     three = jnp.where(lane < 3, 1.0, 0.0).astype(BF)
     ones = jnp.ones((chunk, 128), BF)
-    row8 = lax.broadcasted_iota(jnp.int32, (8, 128), 0)
-    pick = jnp.where(half_mask((8, 128)) == (row8 == 0), 1.0, 0.0).astype(F32)
+    row16 = lax.broadcasted_iota(jnp.int32, (16, 256), 0)
+    pick = (lax.broadcasted_iota(jnp.int32, (16, 256), 1) & 64) == 0
+    pick = jnp.where(pick == (row16 == 0), 1.0, 0.0).astype(BF)
     for c in range(rows // chunk):
         x = samples[c * chunk : (c + 1) * chunk, :]
         rot = lax.dot_general(x, turn[...], NT, preferred_element_type=F32).astype(BF)
-        wide = rot.astype(F32)
-        row_square = lax.dot_general(
-            pick, wide * wide, NT, precision=lax.Precision.HIGHEST, preferred_element_type=F32
-        )
+        square_high, square_low = split(jnp.square(rot.astype(F32)))
+        square = jnp.concatenate([square_high, square_low], axis=1).astype(BF)
+        row_square = lax.dot_general(pick, square, NT, preferred_element_type=F32)
         near = lax.dot_general(
             left[...], jnp.concatenate([rot, three], axis=1), NT, preferred_element_type=F32
         )
@@ -91,34 +98,29 @@
         rebuilt = jnp.dot(codes_t[...], weights, preferred_element_type=F32).astype(BF)
         s = jnp.dot(weights, jnp.concatenate([rot, ones], axis=1), preferred_element_type=F32)
         k = jnp.dot(rebuilt, x, preferred_element_type=F32)
-        if first and c == 0:
-            sums[...] = s
-            cross[...] = k
-        else:
-            sums[...] += s
-            cross[...] += k
+        sums = s if sums is None else sums + s
+        cross = k if cross is None else cross + k
         back = rebuilt.T
         put(2 * c, back[:128])
         put(2 * c + 1, back[128:])
+    return sums, cross
 
 
 def early_kernel(samples, turn, codes_t, left, sums, cross, recon):
     def put(block, tile):
         recon[block] = tile
 
-    assign_rows(samples, turn, codes_t, left, sums, cross, True, put)
+    sums[...], cross[...] = assign_rows(samples, turn, codes_t, left, None, None, put)
 
 
 def late_kernel(
-    place, samples, turn, codes_t, left, sums_in, cross_in, early, send, recon, give, sums, cross
+    place, samples, turn, codes_t, left, sums, cross, early, send, recon, give
 ):
-    sums[...] = sums_in[...]
-    cross[...] = cross_in[...]
-
     def put(block, tile):
         recon[block] = tile
 
-    assign_rows(samples, turn, codes_t, left, sums, cross, False, put)
+    sums, cross = assign_rows(samples, turn, codes_t, left, sums[...], cross[...], put)
+    cross = cross.astype(BF)
     xl = place[1]
     for yl in range(2):
         give[yl] = early[(1 - xl) * 2 + yl]
@@ -130,41 +132,41 @@
     eye = jnp.where(eye, 1.0, 0.0).astype(BF)
     for z in range(8):
         piece = lax.dot_general(
-            eye, cross[:, z * 128 : (z + 1) * 128].astype(BF), NT, preferred_element_type=F32
+            eye, cross[:, z * 128 : (z + 1) * 128], NT, preferred_element_type=F32
         ).astype(BF)
         send[z * 2, 0:64, :] = piece[:64]
         send[z * 2 + 1, 0:64, :] = piece[64:]
     low = half_mask((16, 128))
+    even = (lax.broadcasted_iota(jnp.int32, (8, 128), 1) & 32) == 0
     for q in range(16):
         at = q * 16
         a, b = sums[at : at + 16, :], sums[256 + at : 272 + at, :]
-        send[q, 64:80, :] = jnp.where(low, a[:, :128], b[:, :128]).astype(BF)
-        send[q, 80:96, :] = jnp.where(low, a[:, 128:], b[:, 128:]).astype(BF)
-
-
-def split(x):
-    high = x.astype(BF).astype(F32)
-    return high, x - high
+        total = jnp.where(low, a[:, :128], b[:, :128])
+        count = jnp.where(low, a[:, 128:], b[:, 128:])
+        count = jnp.where(even, count[:8], count[8:])
+        send[q, 64:88, :] = jnp.concatenate([total, count], axis=0).astype(BF)
 
 
 def middle_kernel(place, got, send):
     total = jnp.sum(got[...].astype(F32), axis=0)
     cross_high, cross_low = split(total[:64])
-    sums, count = total[64:80], total[80:96]
+    sums, count = total[64:80], total[80:88]
     low = half_mask((8, 128))
-    wide_low = half_mask((16, 128))
-    lane = lax.broadcasted_iota(jnp.int32, (16, 128), 1)
-    own = (lane >> 3) == lax.broadcasted_iota(jnp.int32, (16, 128), 0)
+    row, lane = (lax.broadcasted_iota(jnp.int32, (8, 128), n) for n in range(2))
     turned = swap_halves(count)
     heads, tails = [], []
     for i in range(2):
         if i == 0:
             tail = jnp.where(low, sums[:8], swap_halves(sums[8:]))
-            each = jnp.where(wide_low, count, turned)
+            base = count
         else:
             tail = jnp.where(low, swap_halves(sums[:8]), sums[8:])
-            each = jnp.where(wide_low, turned, count)
-        line_high, line_low = split(jnp.sum(jnp.where(own, each, 0.0), axis=0, keepdims=True))
+            base = turned
+        each = jnp.where(
+            lane < 32, base, jnp.where(lane < 96, pltpu.roll(base, 32, 1), swap_halves(base))
+        )
+        line = jnp.sum(jnp.where(((lane >> 3) & 7) == row, each, 0.0), axis=0, keepdims=True)
+        line_high, line_low = split(line)
         heads.append(jnp.concatenate([line_high, line_low, jnp.zeros((2, 128), F32)], axis=0))
         tails.append(tail)
     core, yh, yl = place[0], place[2], place[3]
@@ -227,33 +229,30 @@
     codes_t[...] = jnp.concatenate(tiles, axis=0).T[:64]
 
 
-def second_kernel(place, early, late, got, send):
+def second_kernel(place, late, got, send):
+    xl = place[1]
+    for yl in range(2):
+        send[yl] = late[xl * 2 + yl]
+        send[2 + yl] = got[2 + yl]
+
+
+def third_kernel(place, early, got, got2, send):
     xl, yl = place[1], place[3]
     send[0] = early[xl * 2 + 1 - yl]
-    send[1] = late[xl * 2 + 1 - yl]
-    send[2] = got[1 - yl]
-    send[3] = got[2 + 1 - yl]
-
-
-def third_kernel(place, late, got, got2, send):
-    xl, yl = place[1], place[3]
-    send[0] = late[xl * 2 + yl]
-    send[1] = got2[1]
-    send[2] = got[2 + yl]
-    send[3] = got2[3]
+    send[1] = got[1 - yl]
+    send[2] = got2[1 - yl]
+    send[3] = got2[2 + 1 - yl]
 
 
 def home_kernel(place, early, got, got2, got3, recon):
     core, xl, yh, yl = place[0], place[1], place[2], place[3]
     low = half_mask((128, 128))
-    same = [[early[xl * 2 + yl], got2[0]], [got[yl], got2[2]]]
+    same = [[early[xl * 2 + yl], got[yl]], [got2[yl], got2[2 + yl]]]
     for across in range(2):
-        mine = same[across]
-        theirs = [got3[across * 2], got3[across * 2 + 1]]
         blocks = []
         for c in range(2):
-            near = jnp.where(core == c, mine[0], theirs[0])
-            far = jnp.where(core == c, mine[1], theirs[1])
+            near = jnp.where(core == c, same[0][across], same[1][across])
+            far = jnp.where(core == c, got3[across], got3[2 + across])
             for y in range(2):
                 blocks.append(jnp.where(yl == y, near, far).astype(F32))
         side = (1 - xl) if across else xl
@@ -262,14 +261,14 @@
             recon[:, pl.ds(at, 128)] = tile.astype(BF)
 
 
-def call(kernel, name, outs, args, flops=0, moved=0, scratch=()):
+def call(kernel, name, outs, args, flops=0, moved=0, scratch=(), vmem=40):
     return pl.pallas_call(
         kernel,
         out_shape=tuple(jax.ShapeDtypeStruct(*o) for o in outs),
         in_specs=[SMEM if a.ndim == 1 else VMEM for a in args],
         out_specs=(VMEM,) * len(outs),
         scratch_shapes=list(scratch),
-        compiler_params=pltpu.CompilerParams(vmem_limit_bytes=40 * 1024 * 1024),
+        compiler_params=pltpu.CompilerParams(vmem_limit_bytes=vmem * 1024 * 1024),
         cost_estimate=pl.CostEstimate(flops=flops, bytes_accessed=moved, transcendentals=0),
         name=name,
     )(*args)
@@ -280,7 +279,13 @@
     yh, yl = lax.axis_index("yh"), lax.axis_index("yl")
     chunk = lax.axis_index("z") * 2 + lax.axis_index("xh")
     place = jnp.stack([core, xl, yh, yl, chunk]).astype(jnp.int32)
-    (pack,) = call(pack_kernel, "pack", [((64, 1408), BF)], (rotation.T, codebook[0].T))
+    pack, copies = call(
+        open_kernel,
+        "open",
+        [((64, 1408), BF), ((4, 128, 1024), BF)],
+        (samples, rotation.T, codebook[0].T),
+        vmem=60,
+    )
     packs = []
     for steps in ((3, 1), (None, 2)):
         pairs = [
@@ -290,9 +295,7 @@
             if step is not None
         ]
         packs.append(lax.ppermute(pack, ("core", "yh", "yl"), pairs))
-    mine = lax.all_to_all(
-        jnp.broadcast_to(samples[None], (4, 128, 1024)), ("xl", "yl"), 0, 0, tiled=True
-    ).reshape(512, 1024)
+    mine = lax.all_to_all(copies, ("xl", "yl"), 0, 0, tiled=True).reshape(512, 1024)
     tools = call(
         prepare_kernel,
         "prepare",
@@ -313,19 +316,20 @@
     send, late, give = call(
         late_kernel,
         "late",
-        [((16, 96, 128), BF), block, block],
+        [((16, 88, 128), BF), block, block],
         (place, other, *tools, sums, cross, early),
         moved=8_000_000,
-        scratch=[pltpu.VMEM((512, 256), F32), pltpu.VMEM((128, 1024), F32)],
     )
     home = lax.ppermute(give, "xl", swap)
+    (second,) = call(second_kernel, "second", [block], (place, late, home))
+    home2 = lax.ppermute(second, "core", swap)
     got = lax.all_to_all(send, FAR, 0, 0, tiled=True)
-    got, home = lax.optimization_barrier((got, home))
+    got, home2 = lax.optimization_barrier((got, home2))
     (send,) = call(middle_kernel, "middle", [((32, 16, 128), BF)], (place, got))
-    (second,) = call(second_kernel, "second", [block], (place, early, late, home))
-    home2 = lax.ppermute(second, "yl", swap)
+    (third,) = call(third_kernel, "third", [block], (place, early, home, home2))
+    home3 = lax.ppermute(third, "yl", swap)
     got = lax.all_to_all(send, NEAR, 0, 0, tiled=True)
-    got, home2 = lax.optimization_barrier((got, home2))
+    got, home3 = lax.optimization_barrier((got, home3))
     cross, spread = call(
         reduce_kernel,
         "reduce",
@@ -333,8 +337,6 @@
         (place, got, codebook[0]),
     )
     spread = lax.all_to_all(spread, FAR, 0, 0, tiled=True)
-    (third,) = call(third_kernel, "third", [block], (place, late, home, home2))
-    home3 = lax.ppermute(third, "core", swap)
     (recon,) = call(home_kernel, "home", [((128, 1024), BF)], (place, early, home, home2, home3))
     spread, recon = lax.optimization_barrier((spread, recon))
     (new_codes,) = call(codes_kernel, "codes", [((64, 256), F32)], (spread,))

time: 102 us -> 101 us (level)
  starting transfers between devices: 47.3 us -> 51.4 us
  waiting for transfers between devices: 37.2 us -> 33.4 us
  local copies, waits for them, and re-layouts: 2.24 us -> 0.19 us
    all_to_all x1, waiting for transfers between devices: 8.1 us -> 2.06 us  [per_device(): got = lax.all_to_all(send, FAR, 0, 0, tiled=True)]
    all_to_all x1, starting transfers between devices: 3.87 us -> 7.48 us  [per_device(): spread = lax.all_to_all(spread, FAR, 0, 0, tiled=True)]
    broadcast_in_dim x1 -> x0, local copies, waits for them, and re-layouts: 2.06 us -> none  [per_device(): jnp.broadcast_to(samples[None], (4, 128, 1024))]
    pallas_call x10, Pallas kernels: 13.4 us -> 14.4 us  [call(): pl.pallas_call(kernel, out_shape=tuple((jax.ShapeDtypeStruct(*o) for o in...]
  transfers between devices with their start and end apart: 10 -> 10, of which waited for: 7 -> 9; matrix products, arithmetic and copies ran while one was open for 0% -> 0% of each run, Pallas kernels for 6% -> 5%
where the time goes in v6:
time: 101 us; the launch traced here: 100 us
  starting transfers between devices  51.4 us (51%)
  waiting for transfers between devices  33.4 us (33%)
  Pallas kernels  14.4 us (14%)
    pallas_call x10, Pallas kernels, call(): pl.pallas_call(kernel, out_shape=tuple((jax.ShapeDtypeStruct(*o) for o in...  14.4 us
    all_to_all x1, starting transfers between devices, per_device(): got = lax.all_to_all(send, FAR, 0, 0, tiled=True)  12.6 us
    ppermute x2, waiting for transfers between devices, per_device(): packs.append(lax.ppermute(pack, ('core', 'yh', 'yl'), pairs))  12.1 us
    all_to_all x1, waiting for transfers between devices, per_device(): spread = lax.all_to_all(spread, FAR, 0, 0, tiled=True)  8.1 us
    ppermute x2, starting transfers between devices, per_device(): packs.append(lax.ppermute(pack, ('core', 'yh', 'yl'), pairs))  8.06 us
    all_to_all x1, starting transfers between devices, per_device(): spread = lax.all_to_all(spread, FAR, 0, 0, tiled=True)  7.48 us
    all_to_all x1, starting transfers between devices, per_device(): got = lax.all_to_all(send, NEAR, 0, 0, tiled=True)  7.23 us
    ppermute x1, waiting for transfers between devices, per_device(): home = lax.ppermute(give, 'xl', swap)  4.58 us
  transfers between devices with their start and end apart: 10, of which 9 were waited for; matrix products, arithmetic and copies ran while one was open for 0% of the time, Pallas kernels for 5%

profile of v6, /device:TPU:1, one launch (start us, length us, event | category | flops | bytes accessed | tf_op | source)
XLA Modules:
  0.0 100.2 jit_solution(2305507161974330821)
XLA Ops:
  0.6 2.1 %open.1 = (bf16[64,1408]{1,0:T(8,128)(2,1)}, bf16[4,128,1024]{2,1,0:T(8,128)(2,1)}) custom-call(bf16[128,1024]{1,0:T(8,128)(2,1)} %samples.1, bf16[64,1024]{1,0:T(8,128)(2,1)} %bitcast.17, f32[64,256]{1,0:T(8,128)} %bitcast.16), custom_call_target="tpu_custom_call" | custom-call | tf_op jit(solution)/shard_map/open/pallas_call | solution.py:265
  2.7 0.0 copy-start
  2.7 4.5 %all-to-all-start = ((bf16[4,128,1024]{2,1,0:T(8,128)(2,1)}), bf16[4,128,1024]{2,1,0:T(8,128)(2,1)S(1)}, u32[]{:S(2)}, u32[]{:S(2)}) async-start(bf16[4,128,1024]{2,1,0:T(8,128)(2,1)} %get-tuple-element.26), calls=%async_computation | async-start | bytes 2097152 | tf_op jit(solution)/shard_map/all_to_all | solution.py:298
  7.2 0.0 copy-done
  7.2 6.1 %collective-permute-start = (bf16[64,1408]{1,0:T(8,128)(2,1)S(1)}, bf16[64,1408]{1,0:T(8,128)(2,1)S(1)}, u32[]{:S(2)}, u32[]{:S(2)}) collective-permute-start(bf16[64,1408]{1,0:T(8,128)(2,1)S(1)} %copy-done), channel_id=1, source_target_pairs={{5,0},{4,1},{7,2},{6,3},{1,4},{0,5},{3,6},{2,7},{23,16},{18,17},{1... | collective-permute-start | bytes 540680 | tf_op jit(solution)/shard_map/ppermute | solution.py:297
  13.4 1.9 %collective-permute-start.1 = (bf16[64,1408]{1,0:T(8,128)(2,1)S(1)}, bf16[64,1408]{1,0:T(8,128)(2,1)S(1)}, u32[]{:S(2)}, u32[]{:S(2)}) collective-permute-start(bf16[64,1408]{1,0:T(8,128)(2,1)S(1)} %copy-done), channel_id=1, source_target_pairs={{22,16},{19,17},{16,18},{21,19},{18,20},{23,21},{20,22},{17,23},{3... | collective-permute-start | bytes 540680 | tf_op jit(solution)/shard_map/ppermute | solution.py:297
  15.3 0.1 stack.23.place
  15.4 0.9 collective-permute-done.first
  16.2 11.3 %collective-permute-done.1.second = bf16[64,1408]{1,0:T(8,128)(2,1)S(1)} collective-permute-done((bf16[64,1408]{1,0:T(8,128)(2,1)S(1)}, bf16[64,1408]{1,0:T(8,128)(2,1)S(1)}, u32[]{:S(2)}, u32[]{:S(2)}) %collective-permute-start.1) | collective-permute-done | bytes 180256 | tf_op jit(solution)/shard_map/ppermute | solution.py:297
  27.5 0.7 prepare.1
  28.2 0.0 all-to-all-done
  28.2 1.9 %collective-permute-start.2 = (bf16[512,1024]{1,0:T(8,128)(2,1)S(1)}, bf16[512,1024]{1,0:T(8,128)(2,1)S(1)}, u32[]{:S(2)}, u32[]{:S(2)}) collective-permute-start(bf16[512,1024]{1,0:T(8,128)(2,1)S(1)} %bitcast.13), channel_id=1, source_target_pairs={{0,16},{16,0},{1,17},{17,1},{2,18},{18,2},{3,19},{19,3},{4,20},{20... | collective-permute-start | bytes 3145736 | tf_op jit(solution)/shard_map/ppermute | solution.py:307
  30.1 1.8 %early.1 = (f32[512,256]{1,0:T(8,128)S(1)}, f32[128,1024]{1,0:T(8,128)S(1)}, bf16[4,128,128]{2,1,0:T(8,128)(2,1)S(1)}) custom-call(bf16[512,1024]{1,0:T(8,128)(2,1)S(1)} %bitcast.14, bf16[128,1024]{1,0:T(8,128)(2,1)S(1)} %get-tuple-element.32.turn, bf16[128,512]{1,0:T(8,128)(2,1)S(1)} %get-tuple-element.33.codes_t, bf16[512,256]{1,0:T(8,128)(2,1)S(1)} %get-tuple-element.34.left), custom_call_target="tpu_custom_call" | custom-call | bytes 8000000 | tf_op jit(solution)/shard_map/early/pallas_call | solution.py:265
  32.0 0.8 collective-permute-done.2.samples
  32.8 3.9 %late.1 = (bf16[16,88,128]{2,1,0:T(8,128)(2,1)}, bf16[4,128,128]{2,1,0:T(8,128)(2,1)S(1)}, bf16[4,128,128]{2,1,0:T(8,128)(2,1)S(1)}) custom-call(s32[5]{0:T(128)S(1)} %stack.23.place, bf16[512,1024]{1,0:T(8,128)(2,1)S(1)} %collective-permute-done.2.samples, bf16[128,1024]{1,0:T(8,128)(2,1)S(1)} %get-tuple-element.32.turn, ...), custom_call_target="tpu_custom_call" | custom-call | bytes 8000000 | tf_op jit(solution)/shard_map/late/pallas_call | solution.py:265
  36.6 12.6 %all-to-all-start.1 = ((bf16[16,88,128]{2,1,0:T(8,128)(2,1)}), bf16[16,88,128]{2,1,0:T(8,128)(2,1)S(1)}, u32[]{:S(2)}, u32[]{:S(2)}) async-start(bf16[16,88,128]{2,1,0:T(8,128)(2,1)} %get-tuple-element.38), calls=%async_computation.1 | async-start | bytes 720896 | tf_op jit(solution)/shard_map/all_to_all | solution.py:326
  49.2 2.8 %collective-permute-start.3 = (bf16[4,128,128]{2,1,0:T(8,128)(2,1)S(1)}, bf16[4,128,128]{2,1,0:T(8,128)(2,1)S(1)}, u32[]{:S(2)}, u32[]{:S(2)}) collective-permute-start(bf16[4,128,128]{2,1,0:T(8,128)(2,1)S(1)} %get-tuple-element.40), channel_id=1, source_target_pairs={{0,8},{8,0},{1,9},{9,1},{2,10},{10,2},{3,11},{11,3},{4,12},{12,4},... | collective-permute-start | bytes 393224 | tf_op jit(solution)/shard_map/ppermute | solution.py:323
  51.9 4.6 %collective-permute-done.3.got = bf16[4,128,128]{2,1,0:T(8,128)(2,1)S(1)} collective-permute-done((bf16[4,128,128]{2,1,0:T(8,128)(2,1)S(1)}, bf16[4,128,128]{2,1,0:T(8,128)(2,1)S(1)}, u32[]{:S(2)}, u32[]{:S(2)}) %collective-permute-start.3) | collective-permute-done | bytes 131104 | tf_op jit(solution)/shard_map/ppermute | solution.py:323
  56.5 0.5 second.1
  57.1 3.7 %collective-permute-start.4 = (bf16[4,128,128]{2,1,0:T(8,128)(2,1)S(1)}, bf16[4,128,128]{2,1,0:T(8,128)(2,1)S(1)}, u32[]{:S(2)}, u32[]{:S(2)}) collective-permute-start(bf16[4,128,128]{2,1,0:T(8,128)(2,1)S(1)} %second.1), channel_id=1, source_target_pairs={{0,16},{16,0},{1,17},{17,1},{2,18},{18,2},{3,19},{19,3},{4,20},{20... | collective-permute-start | bytes 393224 | tf_op jit(solution)/shard_map/ppermute | solution.py:325
  60.7 1.0 collective-permute-done.4.got2
  61.7 2.1 %all-to-all-done.1.got = bf16[16,88,128]{2,1,0:T(8,128)(2,1)S(1)} async-done(((bf16[16,88,128]{2,1,0:T(8,128)(2,1)}), bf16[16,88,128]{2,1,0:T(8,128)(2,1)S(1)}, u32[]{:S(2)}, u32[]{:S(2)}) %all-to-all-start.1) | async-done | bytes 360480 | tf_op jit(solution)/shard_map/all_to_all | solution.py:326
  63.8 1.4 %middle.1 = bf16[32,16,128]{2,1,0:T(8,128)(2,1)} custom-call(s32[5]{0:T(128)S(1)} %stack.23.place, bf16[16,88,128]{2,1,0:T(8,128)(2,1)S(1)} %all-to-all-done.1.got), custom_call_target="tpu_custom_call" | custom-call | tf_op jit(solution)/shard_map/middle/pallas_call | solution.py:265
  65.1 7.2 %all-to-all-start.2 = ((bf16[32,16,128]{2,1,0:T(8,128)(2,1)}), bf16[32,16,128]{2,1,0:T(8,128)(2,1)S(1)}, u32[]{:S(2)}, u32[]{:S(2)}) async-start(bf16[32,16,128]{2,1,0:T(8,128)(2,1)} %middle.1), calls=%async_computation.2 | async-start | bytes 262144 | tf_op jit(solution)/shard_map/all_to_all | solution.py:331
  72.4 0.0 copy-start.1
  72.4 0.6 third.1
  73.0 3.3 %collective-permute-start.5 = (bf16[4,128,128]{2,1,0:T(8,128)(2,1)S(1)}, bf16[4,128,128]{2,1,0:T(8,128)(2,1)S(1)}, u32[]{:S(2)}, u32[]{:S(2)}) collective-permute-start(bf16[4,128,128]{2,1,0:T(8,128)(2,1)S(1)} %third.1), channel_id=1, source_target_pairs={{0,1},{1,0},{2,3},{3,2},{4,5},{5,4},{6,7},{7,6},{8,9},{9,8},{10,11... | collective-permute-start | bytes 393224 | tf_op jit(solution)/shard_map/ppermute | solution.py:330
  76.3 0.0 copy-done.1
  76.3 0.1 copy.6
  76.4 4.1 %collective-permute-done.5.got3 = bf16[4,128,128]{2,1,0:T(8,128)(2,1)S(1)} collective-permute-done((bf16[4,128,128]{2,1,0:T(8,128)(2,1)S(1)}, bf16[4,128,128]{2,1,0:T(8,128)(2,1)S(1)}, u32[]{:S(2)}, u32[]{:S(2)}) %collective-permute-start.5) | collective-permute-done | bytes 131104 | tf_op jit(solution)/shard_map/ppermute | solution.py:330
  80.5 0.7 all-to-all-done.2.got
  81.2 1.3 %reduce.1 = (f32[2,1024]{1,0:T(2,128)}, f32[16,8,128]{2,1,0:T(8,128)}) custom-call(s32[5]{0:T(128)S(1)} %stack.23.place, bf16[32,16,128]{2,1,0:T(8,128)(2,1)S(1)} %all-to-all-done.2.got, f32[256,64]{1,0:T(8,128)S(1)} %bitcast.15), custom_call_target="tpu_custom_call" | custom-call | tf_op jit(solution)/shard_map/reduce/pallas_call | solution.py:265
  82.4 7.5 %all-to-all-start.3 = ((f32[16,8,128]{2,1,0:T(8,128)}), f32[16,8,128]{2,1,0:T(8,128)S(1)}, u32[]{:S(2)}, u32[]{:S(2)}) async-start(f32[16,8,128]{2,1,0:T(8,128)} %get-tuple-element.44), calls=%async_computation.3 | async-start | bytes 131072 | tf_op jit(solution)/shard_map/all_to_all | solution.py:339
  89.9 1.4 %home.1 = bf16[128,1024]{1,0:T(8,128)(2,1)} custom-call(s32[5]{0:T(128)S(1)} %stack.23.place, bf16[4,128,128]{2,1,0:T(8,128)(2,1)S(1)} %get-tuple-element.37.early, bf16[4,128,128]{2,1,0:T(8,128)(2,1)S(1)} %collective-permute-done.3.got, bf16[4,128,128]{2,1,0:T(8,128)(2,1)S(1)} %collective-permute-done.4.got2, ...), custom_call_target="tpu_custom_call" | custom-call | tf_op jit(solution)/shard_map/home/pallas_call | solution.py:265
  91.3 8.1 %all-to-all-done.3.got = f32[16,8,128]{2,1,0:T(8,128)S(1)} async-done(((f32[16,8,128]{2,1,0:T(8,128)}), f32[16,8,128]{2,1,0:T(8,128)S(1)}, u32[]{:S(2)}, u32[]{:S(2)}) %all-to-all-start.3) | async-done | bytes 65568 | tf_op jit(solution)/shard_map/all_to_all | solution.py:339
  99.4 0.8 codes.1
Async XLA Ops:
  2.7 4.5 %copy-start = (bf16[64,1408]{1,0:T(8,128)(2,1)S(1)}, bf16[64,1408]{1,0:T(8,128)(2,1)}, u32[]{:S(2)}) copy-start(bf16[64,1408]{1,0:T(8,128)(2,1)} %get-tuple-element.27.pack) | copy-start | bytes 540676
  2.7 25.4 %all-to-all-start = ((bf16[4,128,1024]{2,1,0:T(8,128)(2,1)}), bf16[4,128,1024]{2,1,0:T(8,128)(2,1)S(1)}, u32[]{:S(2)}, u32[]{:S(2)}) async-start(bf16[4,128,1024]{2,1,0:T(8,128)(2,1)} %get-tuple-element.26), calls=%async_computation | async-start | bytes 2097152 | tf_op jit(solution)/shard_map/all_to_all | solution.py:298
  7.2 9.0 %collective-permute-start = (bf16[64,1408]{1,0:T(8,128)(2,1)S(1)}, bf16[64,1408]{1,0:T(8,128)(2,1)S(1)}, u32[]{:S(2)}, u32[]{:S(2)}) collective-permute-start(bf16[64,1408]{1,0:T(8,128)(2,1)S(1)} %copy-done), channel_id=1, source_target_pairs={{5,0},{4,1},{7,2},{6,3},{1,4},{0,5},{3,6},{2,7},{23,16},{18,17},{1... | collective-permute-start | bytes 540680 | tf_op jit(solution)/shard_map/ppermute | solution.py:297
  13.4 14.1 %collective-permute-start.1 = (bf16[64,1408]{1,0:T(8,128)(2,1)S(1)}, bf16[64,1408]{1,0:T(8,128)(2,1)S(1)}, u32[]{:S(2)}, u32[]{:S(2)}) collective-permute-start(bf16[64,1408]{1,0:T(8,128)(2,1)S(1)} %copy-done), channel_id=1, source_target_pairs={{22,16},{19,17},{16,18},{21,19},{18,20},{23,21},{20,22},{17,23},{3... | collective-permute-start | bytes 540680 | tf_op jit(solution)/shard_map/ppermute | solution.py:297
  28.2 4.6 %collective-permute-start.2 = (bf16[512,1024]{1,0:T(8,128)(2,1)S(1)}, bf16[512,1024]{1,0:T(8,128)(2,1)S(1)}, u32[]{:S(2)}, u32[]{:S(2)}) collective-permute-start(bf16[512,1024]{1,0:T(8,128)(2,1)S(1)} %bitcast.13), channel_id=1, source_target_pairs={{0,16},{16,0},{1,17},{17,1},{2,18},{18,2},{3,19},{19,3},{4,20},{20... | collective-permute-start | bytes 3145736 | tf_op jit(solution)/shard_map/ppermute | solution.py:307
  36.6 27.2 %all-to-all-start.1 = ((bf16[16,88,128]{2,1,0:T(8,128)(2,1)}), bf16[16,88,128]{2,1,0:T(8,128)(2,1)S(1)}, u32[]{:S(2)}, u32[]{:S(2)}) async-start(bf16[16,88,128]{2,1,0:T(8,128)(2,1)} %get-tuple-element.38), calls=%async_computation.1 | async-start | bytes 720896 | tf_op jit(solution)/shard_map/all_to_all | solution.py:326
  49.2 7.3 %collective-permute-start.3 = (bf16[4,128,128]{2,1,0:T(8,128)(2,1)S(1)}, bf16[4,128,128]{2,1,0:T(8,128)(2,1)S(1)}, u32[]{:S(2)}, u32[]{:S(2)}) collective-permute-start(bf16[4,128,128]{2,1,0:T(8,128)(2,1)S(1)} %get-tuple-element.40), channel_id=1, source_target_pairs={{0,8},{8,0},{1,9},{9,1},{2,10},{10,2},{3,11},{11,3},{4,12},{12,4},... | collective-permute-start | bytes 393224 | tf_op jit(solution)/shard_map/ppermute | solution.py:323
  57.1 4.6 %collective-permute-start.4 = (bf16[4,128,128]{2,1,0:T(8,128)(2,1)S(1)}, bf16[4,128,128]{2,1,0:T(8,128)(2,1)S(1)}, u32[]{:S(2)}, u32[]{:S(2)}) collective-permute-start(bf16[4,128,128]{2,1,0:T(8,128)(2,1)S(1)} %second.1), channel_id=1, source_target_pairs={{0,16},{16,0},{1,17},{17,1},{2,18},{18,2},{3,19},{19,3},{4,20},{20... | collective-permute-start | bytes 393224 | tf_op jit(solution)/shard_map/ppermute | solution.py:325
  65.1 16.0 %all-to-all-start.2 = ((bf16[32,16,128]{2,1,0:T(8,128)(2,1)}), bf16[32,16,128]{2,1,0:T(8,128)(2,1)S(1)}, u32[]{:S(2)}, u32[]{:S(2)}) async-start(bf16[32,16,128]{2,1,0:T(8,128)(2,1)} %middle.1), calls=%async_computation.2 | async-start | bytes 262144 | tf_op jit(solution)/shard_map/all_to_all | solution.py:331
  72.4 3.9 %copy-start.1 = (f32[1,256,64]{1,2,0:T(8,128)S(1)}, f32[1,256,64]{1,2,0:T(8,128)}, u32[]{:S(2)}) copy-start(f32[1,256,64]{1,2,0:T(8,128)} %param.5) | copy-start | bytes 196612
  73.0 7.5 %collective-permute-start.5 = (bf16[4,128,128]{2,1,0:T(8,128)(2,1)S(1)}, bf16[4,128,128]{2,1,0:T(8,128)(2,1)S(1)}, u32[]{:S(2)}, u32[]{:S(2)}) collective-permute-start(bf16[4,128,128]{2,1,0:T(8,128)(2,1)S(1)} %third.1), channel_id=1, source_target_pairs={{0,1},{1,0},{2,3},{3,2},{4,5},{5,4},{6,7},{7,6},{8,9},{9,8},{10,11... | collective-permute-start | bytes 393224 | tf_op jit(solution)/shard_map/ppermute | solution.py:330
  82.4 17.0 %all-to-all-start.3 = ((f32[16,8,128]{2,1,0:T(8,128)}), f32[16,8,128]{2,1,0:T(8,128)S(1)}, u32[]{:S(2)}, u32[]{:S(2)}) async-start(f32[16,8,128]{2,1,0:T(8,128)} %get-tuple-element.44), calls=%async_computation.3 | async-start | bytes 131072 | tf_op jit(solution)/shard_map/all_to_all | solution.py:339

commit v7 on v6

--- a/solution.py
+++ b/solution.py
@@ -53,8 +53,8 @@
 def prepare_kernel(place, pack, first, second, turn, codes_t, left):
     core, yl = place[0], place[3]
     w0, w1, w2 = pack[...], first[...], second[...]
-    wa = jnp.where(core == 0, w0, jnp.where(yl == 0, w2, w1))
-    wb = jnp.where(core == 0, w1, jnp.where(yl == 0, w1, w2))
+    wa = jnp.where(core == 0, w0, jnp.where(yl == 0, w1, w2))
+    wb = jnp.where(core == 0, w1, jnp.where(yl == 0, w2, w1))
     turn[0:64, :] = wa[:, :1024]
     turn[64:128, :] = wb[:, :1024]
     zero = jnp.zeros((64, 256), BF)
@@ -114,17 +114,18 @@
 
 
 def late_kernel(
-    place, samples, turn, codes_t, left, sums, cross, early, send, recon, give
+    place, samples, turn, codes_t, left, sums, cross, early, send, recon, give_x, give_y, give_xy
 ):
     def put(block, tile):
         recon[block] = tile
 
     sums, cross = assign_rows(samples, turn, codes_t, left, sums[...], cross[...], put)
     cross = cross.astype(BF)
-    xl = place[1]
-    for yl in range(2):
-        give[yl] = early[(1 - xl) * 2 + yl]
-        give[2 + yl] = recon[(1 - xl) * 2 + yl]
+    xl, yl = place[1], place[3]
+    for n, block in enumerate((early, recon)):
+        give_x[n] = block[(1 - xl) * 2 + yl]
+        give_y[n] = block[xl * 2 + 1 - yl]
+        give_xy[n] = block[(1 - xl) * 2 + 1 - yl]
     eye = (
         lax.broadcasted_iota(jnp.int32, (128, 128), 0)
         == lax.broadcasted_iota(jnp.int32, (128, 128), 1)
@@ -187,7 +188,7 @@
     return [jnp.where(low, a, turned), d, jnp.where(low, turned, a), c]
 
 
-def reduce_kernel(place, got, codes, cross, spread):
+def cross_kernel(got, cross):
     low = half_mask((2, 128))
     for xl in range(2):
         total = [jnp.zeros((2, 128), F32)] * 4
@@ -202,6 +203,9 @@
         for p in range(4):
             at = (xl * 4 + p) * 128
             cross[:, at : at + 128] = total[p]
+
+
+def fresh_kernel(place, got, codes, spread):
     my_xl, my_yh, my_yl = place[1], place[2], place[3]
     t = jnp.zeros((16, 128), F32)
     for yh in range(4):
@@ -229,30 +233,23 @@
     codes_t[...] = jnp.concatenate(tiles, axis=0).T[:64]
 
 
-def second_kernel(place, late, got, send):
-    xl = place[1]
-    for yl in range(2):
-        send[yl] = late[xl * 2 + yl]
-        send[2 + yl] = got[2 + yl]
-
-
-def third_kernel(place, early, got, got2, send):
+def second_kernel(place, late, got_x, got_y, got_xy, send):
     xl, yl = place[1], place[3]
-    send[0] = early[xl * 2 + 1 - yl]
-    send[1] = got[1 - yl]
-    send[2] = got2[1 - yl]
-    send[3] = got2[2 + 1 - yl]
-
-
-def home_kernel(place, early, got, got2, got3, recon):
+    send[0] = late[xl * 2 + yl]
+    send[1] = got_y[1]
+    send[2] = got_x[1]
+    send[3] = got_xy[1]
+
+
+def home_kernel(place, early, got_x, got_y, got_xy, got_core, recon):
     core, xl, yh, yl = place[0], place[1], place[2], place[3]
     low = half_mask((128, 128))
-    same = [[early[xl * 2 + yl], got[yl]], [got2[yl], got2[2 + yl]]]
+    here = [[early[xl * 2 + yl], got_y[0]], [got_x[0], got_xy[0]]]
     for across in range(2):
         blocks = []
         for c in range(2):
-            near = jnp.where(core == c, same[0][across], same[1][across])
-            far = jnp.where(core == c, got3[across], got3[2 + across])
+            near = jnp.where(core == c, here[across][0], got_core[across * 2])
+            far = jnp.where(core == c, here[across][1], got_core[across * 2 + 1])
             for y in range(2):
                 blocks.append(jnp.where(yl == y, near, far).astype(F32))
         side = (1 - xl) if across else xl
@@ -287,7 +284,7 @@
         vmem=60,
     )
     packs = []
-    for steps in ((3, 1), (None, 2)):
+    for steps in ((3, 2), (None, 1)):
         pairs = [
             (c * 8 + ((y + step if y & 1 else y - step) & 7), c * 8 + y)
             for c, step in enumerate(steps)
@@ -305,7 +302,7 @@
     mine, *tools = lax.optimization_barrier((mine, *tools))
     swap = [(0, 1), (1, 0)]
     other = lax.ppermute(mine, "core", swap)
-    block = ((4, 128, 128), BF)
+    block, pair = ((4, 128, 128), BF), ((2, 128, 128), BF)
     sums, cross, early = call(
         early_kernel,
         "early",
@@ -313,32 +310,33 @@
         (mine, *tools),
         moved=8_000_000,
     )
-    send, late, give = call(
+    send, late, *gives = call(
         late_kernel,
         "late",
-        [((16, 88, 128), BF), block, block],
+        [((16, 88, 128), BF), block, pair, pair, pair],
         (place, other, *tools, sums, cross, early),
         moved=8_000_000,
     )
-    home = lax.ppermute(give, "xl", swap)
-    (second,) = call(second_kernel, "second", [block], (place, late, home))
-    home2 = lax.ppermute(second, "core", swap)
+    both = [(0, 3), (1, 2), (2, 1), (3, 0)]
+    got_x = lax.ppermute(gives[0], "xl", swap)
+    got_y = lax.ppermute(gives[1], "yl", swap)
+    got_xy = lax.ppermute(gives[2], ("xl", "yl"), both)
     got = lax.all_to_all(send, FAR, 0, 0, tiled=True)
-    got, home2 = lax.optimization_barrier((got, home2))
+    got, got_x, got_y, got_xy = lax.optimization_barrier((got, got_x, got_y, got_xy))
     (send,) = call(middle_kernel, "middle", [((32, 16, 128), BF)], (place, got))
-    (third,) = call(third_kernel, "third", [block], (place, early, home, home2))
-    home3 = lax.ppermute(third, "yl", swap)
+    (other_half,) = call(second_kernel, "second", [block], (place, late, got_x, got_y, got_xy))
+    got_core = lax.ppermute(other_half, "core", swap)
     got = lax.all_to_all(send, NEAR, 0, 0, tiled=True)
-    got, home3 = lax.optimization_barrier((got, home3))
-    cross, spread = call(
-        reduce_kernel,
-        "reduce",
-        [((2, 1024), F32), ((16, 8, 128), F32)],
-        (place, got, codebook[0]),
-    )
+    got, got_core = lax.optimization_barrier((got, got_core))
+    (spread,) = call(
+        fresh_kernel, "fresh", [((16, 8, 128), F32)], (place, got, codebook[0])
+    )
+    (cross,) = call(cross_kernel, "cross", [((2, 1024), F32)], (got,))
     spread = lax.all_to_all(spread, FAR, 0, 0, tiled=True)
-    (recon,) = call(home_kernel, "home", [((128, 1024), BF)], (place, early, home, home2, home3))
-    spread, recon = lax.optimization_barrier((spread, recon))
+    (recon,) = call(
+        home_kernel, "home", [((128, 1024), BF)], (place, early, got_x, got_y, got_xy, got_core)
+    )
+    spread, recon, cross = lax.optimization_barrier((spread, recon, cross))
     (new_codes,) = call(codes_kernel, "codes", [((64, 256), F32)], (spread,))
     return recon, new_codes.T[None], cross
 

time: 101 us -> 100 us (0.990)
  waiting for transfers between devices: 33.4 us -> 30.6 us
  starting transfers between devices: 51.4 us -> 52.6 us
    ppermute x3 -> x4, waiting for transfers between devices: 9.67 us -> 3.6 us  [the longest x1 2.6 us: per_device(): got_xy = lax.ppermute(gives[2], ('xl', 'yl'), both)]
    all_to_all x1, waiting for transfers between devices: 0.67 us -> 4.95 us  [per_device(): got = lax.all_to_all(send, NEAR, 0, 0, tiled=True)]
    ppermute x2, starting transfers between devices: 8.06 us -> 9.91 us  [per_device(): packs.append(lax.ppermute(pack, ('core', 'yh', 'yl'), pairs))]
    ppermute x2, waiting for transfers between devices: 12.1 us -> 10.3 us  [per_device(): packs.append(lax.ppermute(pack, ('core', 'yh', 'yl'), pairs))]
    all_to_all x1, waiting for transfers between devices: 2.06 us -> 3.59 us  [per_device(): got = lax.all_to_all(send, FAR, 0, 0, tiled=True)]
    all_to_all x1, starting transfers between devices: 7.48 us -> 6 us  [per_device(): spread = lax.all_to_all(spread, FAR, 0, 0, tiled=True)]
    ppermute x3 -> x4, starting transfers between devices: 9.71 us -> 10.5 us  [the longest x1 3.7 us: per_device(): got_xy = lax.ppermute(gives[2], ('xl', 'yl'), both)]
  transfers between devices with their start and end apart: 10 -> 11, of which waited for: 9 -> 7; matrix products, arithmetic and copies ran while one was open for 0% -> 0% of each run, Pallas kernels for 5% -> 5%
where the time goes in v7:
time: 100 us; the launch traced here: 98.7 us
  starting transfers between devices  52.6 us (53%)
  waiting for transfers between devices  30.6 us (31%)
  Pallas kernels  14.6 us (15%)
    pallas_call x10, Pallas kernels, call(): pl.pallas_call(kernel, out_shape=tuple((jax.ShapeDtypeStruct(*o) for o in...  14.6 us
    all_to_all x1, starting transfers between devices, per_device(): got = lax.all_to_all(send, FAR, 0, 0, tiled=True)  12.6 us
    ppermute x2, waiting for transfers between devices, per_device(): packs.append(lax.ppermute(pack, ('core', 'yh', 'yl'), pairs))  10.3 us
    ppermute x2, starting transfers between devices, per_device(): packs.append(lax.ppermute(pack, ('core', 'yh', 'yl'), pairs))  9.91 us
    all_to_all x1, waiting for transfers between devices, per_device(): spread = lax.all_to_all(spread, FAR, 0, 0, tiled=True)  7.42 us
    all_to_all x1, starting transfers between devices, per_device(): got = lax.all_to_all(send, NEAR, 0, 0, tiled=True)  7.21 us
    all_to_all x1, starting transfers between devices, per_device(): spread = lax.all_to_all(spread, FAR, 0, 0, tiled=True)  6 us
    all_to_all x1, waiting for transfers between devices, per_device(): got = lax.all_to_all(send, NEAR, 0, 0, tiled=True)  4.95 us
  transfers between devices with their start and end apart: 11, of which 7 were waited for; matrix products, arithmetic and copies ran while one was open for 0% of the time, Pallas kernels for 5%

profile of v7, /device:TPU:1, one launch (start us, length us, event | category | flops | bytes accessed | tf_op | source)
XLA Modules:
  0.0 98.7 jit_solution(6771214570312673400)
XLA Ops:
  0.6 2.1 %open.1 = (bf16[64,1408]{1,0:T(8,128)(2,1)}, bf16[4,128,1024]{2,1,0:T(8,128)(2,1)}) custom-call(bf16[128,1024]{1,0:T(8,128)(2,1)} %samples.1, bf16[64,1024]{1,0:T(8,128)(2,1)} %bitcast.17, f32[64,256]{1,0:T(8,128)} %bitcast.16), custom_call_target="tpu_custom_call" | custom-call | tf_op jit(solution)/shard_map/open/pallas_call | solution.py:262
  2.7 0.0 copy-start
  2.7 4.5 %all-to-all-start = ((bf16[4,128,1024]{2,1,0:T(8,128)(2,1)}), bf16[4,128,1024]{2,1,0:T(8,128)(2,1)S(1)}, u32[]{:S(2)}, u32[]{:S(2)}) async-start(bf16[4,128,1024]{2,1,0:T(8,128)(2,1)} %get-tuple-element.29), calls=%async_computation | async-start | bytes 2097152 | tf_op jit(solution)/shard_map/all_to_all | solution.py:295
  7.2 0.0 copy-done
  7.2 4.3 %collective-permute-start = (bf16[64,1408]{1,0:T(8,128)(2,1)S(1)}, bf16[64,1408]{1,0:T(8,128)(2,1)S(1)}, u32[]{:S(2)}, u32[]{:S(2)}) collective-permute-start(bf16[64,1408]{1,0:T(8,128)(2,1)S(1)} %copy-done), channel_id=1, source_target_pairs={{5,0},{4,1},{7,2},{6,3},{1,4},{0,5},{3,6},{2,7},{22,16},{19,17},{1... | collective-permute-start | bytes 540680 | tf_op jit(solution)/shard_map/ppermute | solution.py:294
  11.5 5.7 %collective-permute-start.1 = (bf16[64,1408]{1,0:T(8,128)(2,1)S(1)}, bf16[64,1408]{1,0:T(8,128)(2,1)S(1)}, u32[]{:S(2)}, u32[]{:S(2)}) collective-permute-start(bf16[64,1408]{1,0:T(8,128)(2,1)S(1)} %copy-done), channel_id=1, source_target_pairs={{23,16},{18,17},{17,18},{20,19},{19,20},{22,21},{21,22},{16,23},{3... | collective-permute-start | bytes 540680 | tf_op jit(solution)/shard_map/ppermute | solution.py:294
  17.1 0.1 stack.23.place
  17.2 10.3 %collective-permute-done.first = bf16[64,1408]{1,0:T(8,128)(2,1)S(1)} collective-permute-done((bf16[64,1408]{1,0:T(8,128)(2,1)S(1)}, bf16[64,1408]{1,0:T(8,128)(2,1)S(1)}, u32[]{:S(2)}, u32[]{:S(2)}) %collective-permute-start) | collective-permute-done | bytes 180256 | tf_op jit(solution)/shard_map/ppermute | solution.py:294
  27.5 0.0 collective-permute-done.1.second
  27.5 0.7 prepare.1
  28.2 0.0 all-to-all-done
  28.2 1.9 %collective-permute-start.2 = (bf16[512,1024]{1,0:T(8,128)(2,1)S(1)}, bf16[512,1024]{1,0:T(8,128)(2,1)S(1)}, u32[]{:S(2)}, u32[]{:S(2)}) collective-permute-start(bf16[512,1024]{1,0:T(8,128)(2,1)S(1)} %bitcast.13), channel_id=1, source_target_pairs={{0,16},{16,0},{1,17},{17,1},{2,18},{18,2},{3,19},{19,3},{4,20},{20... | collective-permute-start | bytes 3145736 | tf_op jit(solution)/shard_map/ppermute | solution.py:304
  30.1 1.8 %early.1 = (f32[512,256]{1,0:T(8,128)S(1)}, f32[128,1024]{1,0:T(8,128)S(1)}, bf16[4,128,128]{2,1,0:T(8,128)(2,1)S(1)}) custom-call(bf16[512,1024]{1,0:T(8,128)(2,1)S(1)} %bitcast.14, bf16[128,1024]{1,0:T(8,128)(2,1)S(1)} %get-tuple-element.35.turn, bf16[128,512]{1,0:T(8,128)(2,1)S(1)} %get-tuple-element.36.codes_t, bf16[512,256]{1,0:T(8,128)(2,1)S(1)} %get-tuple-element.37.left), custom_call_target="tpu_custom_call" | custom-call | bytes 8000000 | tf_op jit(solution)/shard_map/early/pallas_call | solution.py:262
  32.0 0.8 collective-permute-done.2.samples
  32.8 3.8 %late.1 = (bf16[16,88,128]{2,1,0:T(8,128)(2,1)}, bf16[4,128,128]{2,1,0:T(8,128)(2,1)S(1)}, bf16[2,128,128]{2,1,0:T(8,128)(2,1)S(1)}, bf16[2,128,128]{2,1,0:T(8,128)(2,1)S(1)}, bf16[2,128,128]{2,1,0:T(8,128)(2,1)S(1)}) custom-call(s32[5]{0:T(128)S(1)} %stack.23.place, bf16[512,1024]{1,0:T(8,128)(2,1)S(1)} %collective-permute-done.2.samples, ...), custom_call_target="tpu_custom_call" | custom-call | bytes 8000000 | tf_op jit(solution)/shard_map/late/pallas_call | solution.py:262
  36.6 12.6 %all-to-all-start.1 = ((bf16[16,88,128]{2,1,0:T(8,128)(2,1)}), bf16[16,88,128]{2,1,0:T(8,128)(2,1)S(1)}, u32[]{:S(2)}, u32[]{:S(2)}) async-start(bf16[16,88,128]{2,1,0:T(8,128)(2,1)} %get-tuple-element.41), calls=%async_computation.1 | async-start | bytes 720896 | tf_op jit(solution)/shard_map/all_to_all | solution.py:324
  49.2 2.7 %collective-permute-start.3 = (bf16[2,128,128]{2,1,0:T(8,128)(2,1)S(1)}, bf16[2,128,128]{2,1,0:T(8,128)(2,1)S(1)}, u32[]{:S(2)}, u32[]{:S(2)}) collective-permute-start(bf16[2,128,128]{2,1,0:T(8,128)(2,1)S(1)} %get-tuple-element.42), channel_id=1, source_target_pairs={{0,8},{8,0},{1,9},{9,1},{2,10},{10,2},{3,11},{11,3},{4,12},{12,4},... | collective-permute-start | bytes 196616 | tf_op jit(solution)/shard_map/ppermute | solution.py:321
  51.9 1.9 %collective-permute-start.4 = (bf16[2,128,128]{2,1,0:T(8,128)(2,1)S(1)}, bf16[2,128,128]{2,1,0:T(8,128)(2,1)S(1)}, u32[]{:S(2)}, u32[]{:S(2)}) collective-permute-start(bf16[2,128,128]{2,1,0:T(8,128)(2,1)S(1)} %get-tuple-element.43), channel_id=1, source_target_pairs={{0,1},{1,0},{2,3},{3,2},{4,5},{5,4},{6,7},{7,6},{8,9},{9,8},{10,11... | collective-permute-start | bytes 196616 | tf_op jit(solution)/shard_map/ppermute | solution.py:322
  53.9 3.7 %collective-permute-start.5 = (bf16[2,128,128]{2,1,0:T(8,128)(2,1)S(1)}, bf16[2,128,128]{2,1,0:T(8,128)(2,1)S(1)}, u32[]{:S(2)}, u32[]{:S(2)}) collective-permute-start(bf16[2,128,128]{2,1,0:T(8,128)(2,1)S(1)} %get-tuple-element.44), channel_id=1, source_target_pairs={{0,9},{1,8},{8,1},{9,0},{2,11},{3,10},{10,3},{11,2},{4,13},{5,12},... | collective-permute-start | bytes 196616 | tf_op jit(solution)/shard_map/ppermute | solution.py:323
  57.6 0.0 collective-permute-done.3.got_x
  57.6 0.0 collective-permute-done.4.got_y
  57.6 2.6 %collective-permute-done.5.got_xy = bf16[2,128,128]{2,1,0:T(8,128)(2,1)S(1)} collective-permute-done((bf16[2,128,128]{2,1,0:T(8,128)(2,1)S(1)}, bf16[2,128,128]{2,1,0:T(8,128)(2,1)S(1)}, u32[]{:S(2)}, u32[]{:S(2)}) %collective-permute-start.5) | collective-permute-done | bytes 65568 | tf_op jit(solution)/shard_map/ppermute | solution.py:323
  60.2 3.6 %all-to-all-done.1.got = bf16[16,88,128]{2,1,0:T(8,128)(2,1)S(1)} async-done(((bf16[16,88,128]{2,1,0:T(8,128)(2,1)}), bf16[16,88,128]{2,1,0:T(8,128)(2,1)S(1)}, u32[]{:S(2)}, u32[]{:S(2)}) %all-to-all-start.1) | async-done | bytes 360480 | tf_op jit(solution)/shard_map/all_to_all | solution.py:324
  63.8 1.4 %middle.1 = bf16[32,16,128]{2,1,0:T(8,128)(2,1)} custom-call(s32[5]{0:T(128)S(1)} %stack.23.place, bf16[16,88,128]{2,1,0:T(8,128)(2,1)S(1)} %all-to-all-done.1.got), custom_call_target="tpu_custom_call" | custom-call | tf_op jit(solution)/shard_map/middle/pallas_call | solution.py:262
  65.2 7.2 %all-to-all-start.2 = ((bf16[32,16,128]{2,1,0:T(8,128)(2,1)}), bf16[32,16,128]{2,1,0:T(8,128)(2,1)S(1)}, u32[]{:S(2)}, u32[]{:S(2)}) async-start(bf16[32,16,128]{2,1,0:T(8,128)(2,1)} %middle.1), calls=%async_computation.2 | async-start | bytes 262144 | tf_op jit(solution)/shard_map/all_to_all | solution.py:329
  72.4 0.0 copy-start.1
  72.4 0.6 second.1
  73.0 2.1 %collective-permute-start.6 = (bf16[4,128,128]{2,1,0:T(8,128)(2,1)S(1)}, bf16[4,128,128]{2,1,0:T(8,128)(2,1)S(1)}, u32[]{:S(2)}, u32[]{:S(2)}) collective-permute-start(bf16[4,128,128]{2,1,0:T(8,128)(2,1)S(1)} %second.1), channel_id=1, source_target_pairs={{0,16},{16,0},{1,17},{17,1},{2,18},{18,2},{3,19},{19,3},{4,20},{20... | collective-permute-start | bytes 393224 | tf_op jit(solution)/shard_map/ppermute | solution.py:328
  75.1 0.0 copy-done.1
  75.1 0.1 copy.6
  75.2 1.0 %collective-permute-done.6.got_core = bf16[4,128,128]{2,1,0:T(8,128)(2,1)S(1)} collective-permute-done((bf16[4,128,128]{2,1,0:T(8,128)(2,1)S(1)}, bf16[4,128,128]{2,1,0:T(8,128)(2,1)S(1)}, u32[]{:S(2)}, u32[]{:S(2)}) %collective-permute-start.6) | collective-permute-done | bytes 131104 | tf_op jit(solution)/shard_map/ppermute | solution.py:328
  76.2 5.0 %all-to-all-done.2.got = bf16[32,16,128]{2,1,0:T(8,128)(2,1)S(1)} async-done(((bf16[32,16,128]{2,1,0:T(8,128)(2,1)}), bf16[32,16,128]{2,1,0:T(8,128)(2,1)S(1)}, u32[]{:S(2)}, u32[]{:S(2)}) %all-to-all-start.2) | async-done | bytes 131104 | tf_op jit(solution)/shard_map/all_to_all | solution.py:329
  81.2 1.3 %fresh.1 = f32[16,8,128]{2,1,0:T(8,128)} custom-call(s32[5]{0:T(128)S(1)} %stack.23.place, bf16[32,16,128]{2,1,0:T(8,128)(2,1)S(1)} %all-to-all-done.2.got, f32[256,64]{1,0:T(8,128)S(1)} %bitcast.15), custom_call_target="tpu_custom_call" | custom-call | tf_op jit(solution)/shard_map/fresh/pallas_call | solution.py:262
  82.4 6.0 %all-to-all-start.3 = ((f32[16,8,128]{2,1,0:T(8,128)}), f32[16,8,128]{2,1,0:T(8,128)S(1)}, u32[]{:S(2)}, u32[]{:S(2)}) async-start(f32[16,8,128]{2,1,0:T(8,128)} %fresh.1), calls=%async_computation.3 | async-start | bytes 131072 | tf_op jit(solution)/shard_map/all_to_all | solution.py:335
  88.4 0.7 cross.1
  89.1 1.4 %home.1 = bf16[128,1024]{1,0:T(8,128)(2,1)} custom-call(s32[5]{0:T(128)S(1)} %stack.23.place, bf16[4,128,128]{2,1,0:T(8,128)(2,1)S(1)} %get-tuple-element.40.early, bf16[2,128,128]{2,1,0:T(8,128)(2,1)S(1)} %collective-permute-done.3.got_x, bf16[2,128,128]{2,1,0:T(8,128)(2,1)S(1)} %collective-permute-done.4.got_y, ...), custom_call_target="tpu_custom_call" | custom-call | tf_op jit(solution)/shard_map/home/pallas_call | solution.py:262
  90.5 7.4 %all-to-all-done.3.got = f32[16,8,128]{2,1,0:T(8,128)S(1)} async-done(((f32[16,8,128]{2,1,0:T(8,128)}), f32[16,8,128]{2,1,0:T(8,128)S(1)}, u32[]{:S(2)}, u32[]{:S(2)}) %all-to-all-start.3) | async-done | bytes 65568 | tf_op jit(solution)/shard_map/all_to_all | solution.py:335
  98.0 0.8 codes.1
Async XLA Ops:
  2.7 4.5 %copy-start = (bf16[64,1408]{1,0:T(8,128)(2,1)S(1)}, bf16[64,1408]{1,0:T(8,128)(2,1)}, u32[]{:S(2)}) copy-start(bf16[64,1408]{1,0:T(8,128)(2,1)} %get-tuple-element.30.pack) | copy-start | bytes 540676
  2.7 25.4 %all-to-all-start = ((bf16[4,128,1024]{2,1,0:T(8,128)(2,1)}), bf16[4,128,1024]{2,1,0:T(8,128)(2,1)S(1)}, u32[]{:S(2)}, u32[]{:S(2)}) async-start(bf16[4,128,1024]{2,1,0:T(8,128)(2,1)} %get-tuple-element.29), calls=%async_computation | async-start | bytes 2097152 | tf_op jit(solution)/shard_map/all_to_all | solution.py:295
  7.2 20.3 %collective-permute-start = (bf16[64,1408]{1,0:T(8,128)(2,1)S(1)}, bf16[64,1408]{1,0:T(8,128)(2,1)S(1)}, u32[]{:S(2)}, u32[]{:S(2)}) collective-permute-start(bf16[64,1408]{1,0:T(8,128)(2,1)S(1)} %copy-done), channel_id=1, source_target_pairs={{5,0},{4,1},{7,2},{6,3},{1,4},{0,5},{3,6},{2,7},{22,16},{19,17},{1... | collective-permute-start | bytes 540680 | tf_op jit(solution)/shard_map/ppermute | solution.py:294
  11.5 16.0 %collective-permute-start.1 = (bf16[64,1408]{1,0:T(8,128)(2,1)S(1)}, bf16[64,1408]{1,0:T(8,128)(2,1)S(1)}, u32[]{:S(2)}, u32[]{:S(2)}) collective-permute-start(bf16[64,1408]{1,0:T(8,128)(2,1)S(1)} %copy-done), channel_id=1, source_target_pairs={{23,16},{18,17},{17,18},{20,19},{19,20},{22,21},{21,22},{16,23},{3... | collective-permute-start | bytes 540680 | tf_op jit(solution)/shard_map/ppermute | solution.py:294
  28.2 4.6 %collective-permute-start.2 = (bf16[512,1024]{1,0:T(8,128)(2,1)S(1)}, bf16[512,1024]{1,0:T(8,128)(2,1)S(1)}, u32[]{:S(2)}, u32[]{:S(2)}) collective-permute-start(bf16[512,1024]{1,0:T(8,128)(2,1)S(1)} %bitcast.13), channel_id=1, source_target_pairs={{0,16},{16,0},{1,17},{17,1},{2,18},{18,2},{3,19},{19,3},{4,20},{20... | collective-permute-start | bytes 3145736 | tf_op jit(solution)/shard_map/ppermute | solution.py:304
  36.6 27.2 %all-to-all-start.1 = ((bf16[16,88,128]{2,1,0:T(8,128)(2,1)}), bf16[16,88,128]{2,1,0:T(8,128)(2,1)S(1)}, u32[]{:S(2)}, u32[]{:S(2)}) async-start(bf16[16,88,128]{2,1,0:T(8,128)(2,1)} %get-tuple-element.41), calls=%async_computation.1 | async-start | bytes 720896 | tf_op jit(solution)/shard_map/all_to_all | solution.py:324
  49.2 8.4 %collective-permute-start.3 = (bf16[2,128,128]{2,1,0:T(8,128)(2,1)S(1)}, bf16[2,128,128]{2,1,0:T(8,128)(2,1)S(1)}, u32[]{:S(2)}, u32[]{:S(2)}) collective-permute-start(bf16[2,128,128]{2,1,0:T(8,128)(2,1)S(1)} %get-tuple-element.42), channel_id=1, source_target_pairs={{0,8},{8,0},{1,9},{9,1},{2,10},{10,2},{3,11},{11,3},{4,12},{12,4},... | collective-permute-start | bytes 196616 | tf_op jit(solution)/shard_map/ppermute | solution.py:321
  51.9 5.7 %collective-permute-start.4 = (bf16[2,128,128]{2,1,0:T(8,128)(2,1)S(1)}, bf16[2,128,128]{2,1,0:T(8,128)(2,1)S(1)}, u32[]{:S(2)}, u32[]{:S(2)}) collective-permute-start(bf16[2,128,128]{2,1,0:T(8,128)(2,1)S(1)} %get-tuple-element.43), channel_id=1, source_target_pairs={{0,1},{1,0},{2,3},{3,2},{4,5},{5,4},{6,7},{7,6},{8,9},{9,8},{10,11... | collective-permute-start | bytes 196616 | tf_op jit(solution)/shard_map/ppermute | solution.py:322
  53.9 6.3 %collective-permute-start.5 = (bf16[2,128,128]{2,1,0:T(8,128)(2,1)S(1)}, bf16[2,128,128]{2,1,0:T(8,128)(2,1)S(1)}, u32[]{:S(2)}, u32[]{:S(2)}) collective-permute-start(bf16[2,128,128]{2,1,0:T(8,128)(2,1)S(1)} %get-tuple-element.44), channel_id=1, source_target_pairs={{0,9},{1,8},{8,1},{9,0},{2,11},{3,10},{10,3},{11,2},{4,13},{5,12},... | collective-permute-start | bytes 196616 | tf_op jit(solution)/shard_map/ppermute | solution.py:323
  65.2 16.0 %all-to-all-start.2 = ((bf16[32,16,128]{2,1,0:T(8,128)(2,1)}), bf16[32,16,128]{2,1,0:T(8,128)(2,1)S(1)}, u32[]{:S(2)}, u32[]{:S(2)}) async-start(bf16[32,16,128]{2,1,0:T(8,128)(2,1)} %middle.1), calls=%async_computation.2 | async-start | bytes 262144 | tf_op jit(solution)/shard_map/all_to_all | solution.py:329
  72.4 2.7 %copy-start.1 = (f32[1,256,64]{1,2,0:T(8,128)S(1)}, f32[1,256,64]{1,2,0:T(8,128)}, u32[]{:S(2)}) copy-start(f32[1,256,64]{1,2,0:T(8,128)} %param.5) | copy-start | bytes 196612
  73.0 3.2 %collective-permute-start.6 = (bf16[4,128,128]{2,1,0:T(8,128)(2,1)S(1)}, bf16[4,128,128]{2,1,0:T(8,128)(2,1)S(1)}, u32[]{:S(2)}, u32[]{:S(2)}) collective-permute-start(bf16[4,128,128]{2,1,0:T(8,128)(2,1)S(1)} %second.1), channel_id=1, source_target_pairs={{0,16},{16,0},{1,17},{17,1},{2,18},{18,2},{3,19},{19,3},{4,20},{20... | collective-permute-start | bytes 393224 | tf_op jit(solution)/shard_map/ppermute | solution.py:328
  82.4 15.5 %all-to-all-start.3 = ((f32[16,8,128]{2,1,0:T(8,128)}), f32[16,8,128]{2,1,0:T(8,128)S(1)}, u32[]{:S(2)}, u32[]{:S(2)}) async-start(f32[16,8,128]{2,1,0:T(8,128)} %fresh.1), calls=%async_computation.3 | async-start | bytes 131072 | tf_op jit(solution)/shard_map/all_to_all | solution.py:335

commit v8 on v7

v8 whole, which is shorter than its diff:
```python
import functools

import jax
import jax.numpy as jnp
from jax import lax
from jax.experimental import pallas as pl
from jax.experimental.pallas import tpu as pltpu
from jax.sharding import Mesh
from jax.sharding import PartitionSpec as P

SIZES = (8, 2, 2, 2, 4, 2)
NAMES = ("z", "xh", "core", "xl", "yh", "yl")
DP = ("z", "xh", "core")
SUB = ("xl", "yh", "yl")
PLACES = (((0, 5), (1, 4)), ((6, 7), (3, 2)))
FAR = ("z", "xh")
NEAR = ("core", "xl", "yh", "yl")
BF = jnp.bfloat16
F32 = jnp.float32
NT = (((1,), (1,)), ((), ()))
VMEM = pl.BlockSpec(memory_space=pltpu.VMEM)
SMEM = pl.BlockSpec(memory_space=pltpu.SMEM)


def half_mask(shape):
    return lax.broadcasted_iota(jnp.int32, shape, len(shape) - 1) < 64


def swap_halves(x):
    return pltpu.roll(x, 64, 1)


def split(x):
    high = x.astype(BF).astype(F32)
    return high, x - high


def open_kernel(samples, turn_t, codes_t, pack, copies):
    for n in range(4):
        copies[n] = samples[...]
    codes = codes_t[...]
    square = jnp.sum(codes * codes, axis=0, keepdims=True)
    high = square.astype(BF).astype(F32)
    mid = (square - high).astype(BF).astype(F32)
    low = square - high - mid
    squares = jnp.concatenate([high, mid, low, jnp.zeros((13, 256), F32)], axis=0).astype(BF)
    pack[:, 0:1024] = turn_t[...]
    pack[:, 1024:1280] = codes.astype(BF)
    pack[0:16, 1280:] = squares[:, :128]
    pack[16:32, 1280:] = squares[:, 128:]
    pack[32:64, 1280:] = jnp.zeros((32, 128), BF)


def prepare_kernel(place, pack, first, second, turn, codes_t, left):
    core = place[0]
    w0, w1, w2 = pack[...], first[...], second[...]
    wa = jnp.where(core == 0, w0, w1)
    wb = jnp.where(core == 0, w1, w2)
    turn[0:64, :] = wa[:, :1024]
    turn[64:128, :] = wb[:, :1024]
    zero = jnp.zeros((64, 256), BF)
    both = jnp.concatenate(
        [
            jnp.concatenate([wa[:, 1024:1280], zero], axis=1),
            jnp.concatenate([zero, wb[:, 1024:1280]], axis=1),
        ],
        axis=0,
    )
    codes_t[...] = both
    squares = jnp.concatenate(
        [wa[0:16, 1280:], wa[16:32, 1280:], wb[0:16, 1280:], wb[16:32, 1280:]], axis=1
    )
    left[...] = jnp.concatenate([both * BF(-2.0), squares, jnp.zeros((112, 512), BF)], axis=0).T


def assign_rows(samples, turn, codes_t, left, sums, cross, put):
    rows, chunk = 512, 256
    lane = lax.broadcasted_iota(jnp.int32, (chunk, 128), 1)
    three = jnp.where(lane < 3, 1.0, 0.0).astype(BF)
    ones = jnp.ones((chunk, 128), BF)
    row16 = lax.broadcasted_iota(jnp.int32, (16, 256), 0)
    pick = (lax.broadcasted_iota(jnp.int32, (16, 256), 1) & 64) == 0
    pick = jnp.where(pick == (row16 == 0), 1.0, 0.0).astype(BF)
    for c in range(rows // chunk):
        x = samples[c * chunk : (c + 1) * chunk, :]
        rot = lax.dot_general(x, turn[...], NT, preferred_element_type=F32).astype(BF)
        square_high, square_low = split(jnp.square(rot.astype(F32)))
        square = jnp.concatenate([square_high, square_low], axis=1).astype(BF)
        row_square = lax.dot_general(pick, square, NT, preferred_element_type=F32)
        near = lax.dot_general(
            left[...], jnp.concatenate([rot, three], axis=1), NT, preferred_element_type=F32
        )
        parts = []
        for i in range(2):
            logits = -0.125 * (row_square[i : i + 1] + near[i * 256 : (i + 1) * 256])
            e = jnp.exp(logits - jnp.max(logits, axis=0, keepdims=True))
            parts.append((e * (1.0 / jnp.sum(e, axis=0, keepdims=True))).astype(BF))
        weights = jnp.concatenate(parts, axis=0)
        rebuilt = jnp.dot(codes_t[...], weights, preferred_element_type=F32).astype(BF)
        s = jnp.dot(weights, jnp.concatenate([rot, ones], axis=1), preferred_element_type=F32)
        k = jnp.dot(rebuilt, x, preferred_element_type=F32)
        sums = s if sums is None else sums + s
        cross = k if cross is None else cross + k
        back = rebuilt.T
        put(2 * c, back[:128])
        put(2 * c + 1, back[128:])
    return sums, cross


def early_kernel(samples, turn, codes_t, left, sums, cross, recon):
    def put(block, tile):
        recon[block] = tile

    sums[...], cross[...] = assign_rows(samples, turn, codes_t, left, None, None, put)


def late_kernel(samples, turn, codes_t, left, sums, cross, send, recon, sums_a, sums_b):
    def put(block, tile):
        recon[block] = tile

    sums, cross = assign_rows(samples, turn, codes_t, left, sums[...], cross[...], put)
    cross = cross.astype(BF)
    r = lax.broadcasted_iota(jnp.int32, (256, 256), 0)
    wanted = ((r & 4) << 5) | ((r & 2) << 5) | ((r >> 3) << 1) | (r & 1)
    order = jnp.where(lax.broadcasted_iota(jnp.int32, (256, 256), 1) == wanted, 1.0, 0.0).astype(BF)
    pieces = [
        lax.dot_general(order, cross[:, n * 256 : (n + 1) * 256], NT, preferred_element_type=F32)
        for n in range(4)
    ]
    for d in range(32):
        tiles = [piece[8 * d : 8 * d + 8] for piece in pieces]
        send[d] = jnp.concatenate(tiles, axis=0).astype(BF)
    low = half_mask((64, 128))
    diagonal = (
        lax.broadcasted_iota(jnp.int32, (128, 128), 0)
        == lax.broadcasted_iota(jnp.int32, (128, 128), 1)
    )
    for i, out in enumerate((sums_a, sums_b)):
        lines = []
        for h in range(2):
            at = i * 256 + h * 128
            a, b = sums[at : at + 64, :128], sums[at + 64 : at + 128, :128]
            if i == 0:
                tile = jnp.where(low, a, swap_halves(b))
            else:
                tile = jnp.where(low, swap_halves(a), b)
            out[h * 64 : h * 64 + 64, :] = tile.astype(BF)
            count = jnp.where(diagonal, sums[at : at + 128, 128:], 0.0)
            lines += split(jnp.sum(count, axis=0, keepdims=True))
        out[128:144, :] = jnp.concatenate(lines + [jnp.zeros((12, 128), F32)], axis=0).astype(BF)


def half_kernel(place, first, second, keep, give):
    core = place[0]
    both = first[...].astype(F32) + second[...].astype(F32)
    empty = jnp.zeros((14, 128), F32)
    halves = []
    for h in range(2):
        line = both[128 + 2 * h : 129 + 2 * h] + both[129 + 2 * h : 130 + 2 * h]
        halves.append(jnp.concatenate([both[h * 64 : h * 64 + 64], *split(line), empty], axis=0))
    keep[...] = jnp.where(core == 0, halves[0], halves[1])
    give[...] = jnp.where(core == 0, halves[1], halves[0]).astype(BF)


def arrange(low, a, b, c, d):
    turned = swap_halves(b)
    return [jnp.where(low, a, turned), swap_halves(d), jnp.where(low, turned, a), c]


def middle_kernel(got, keep, half, send):
    low = half_mask((32, 128))
    columns = []
    for xl in range(2):
        total = [jnp.zeros((32, 128), F32)] * 4
        for yh in range(4):
            blocks = [got[core * 16 + xl * 8 + yh * 2 + yl].astype(F32) for core in range(2) for yl in range(2)]
            for p, tile in enumerate(arrange(low, *blocks)):
                total[(yh + p) & 3] += tile
        columns += total
    r = lax.broadcasted_iota(jnp.int32, (256, 256), 0)
    wanted = (((r >> 1) & 7) << 5) | ((r >> 4) << 1) | (r & 1)
    order = jnp.where(lax.broadcasted_iota(jnp.int32, (256, 256), 1) == wanted, 1.0, 0.0).astype(BF)
    cross = jnp.dot(
        order, jnp.concatenate(columns, axis=0).astype(BF), preferred_element_type=F32
    ).astype(BF)
    both = keep[...] + half[...].astype(F32)
    line = both[64:65] + both[65:66]
    both = jnp.concatenate([both[:64], *split(line), jnp.zeros((6, 128), F32)], axis=0).astype(BF)
    for q in range(16):
        send[q, 0:16, :] = cross[q * 16 : q * 16 + 16]
        send[q, 16:88, :] = both


def finish_kernel(place, got, codes_t, cross, fresh):
    total = jnp.sum(got[...].astype(F32), axis=0)
    for n in range(8):
        cross[:, n * 128 : (n + 1) * 128] = total[2 * n : 2 * n + 2]
    sums, count = total[16:80], total[80:81] + total[81:82]
    sums = jnp.concatenate([sums, swap_halves(sums)], axis=0).T[:64]
    own = jnp.where(place[0] == 0, codes_t[:, :128], codes_t[:, 128:])
    fresh[...] = (sums + own) / (count + 1.0)


def codes_kernel(place, mine, other, codes_t):
    a, b = mine[...], other[...]
    codes_t[:, :128] = jnp.where(place[0] == 0, a, b)
    codes_t[:, 128:] = jnp.where(place[0] == 0, b, a)


def second_kernel(place, early, got_core, give_x, give_y, give_xy):
    xl, yl = place[1], place[3]
    for n, block in enumerate((early, got_core)):
        give_x[n] = block[(1 - xl) * 2 + yl]
        give_y[n] = block[xl * 2 + 1 - yl]
        give_xy[n] = block[(1 - xl) * 2 + 1 - yl]


def home_kernel(place, early, got_core, got_x, got_y, got_xy, recon):
    core, xl, yh, yl = place[0], place[1], place[2], place[3]
    low = half_mask((128, 128))
    own = [early[xl * 2 + yl], got_core[xl * 2 + yl]]
    for across, (same, far) in enumerate(((own, got_y), (got_x, got_xy))):
        blocks = []
        for c in range(2):
            near_c = jnp.where(core == c, same[0], same[1])
            far_c = jnp.where(core == c, far[0], far[1])
            for y in range(2):
                blocks.append(jnp.where(yl == y, near_c, far_c).astype(F32))
        side = (1 - xl) if across else xl
        for p, tile in enumerate(arrange(low, *blocks)):
            at = pl.multiple_of((side * 4 + ((yh + p) & 3)) * 128, 128)
            recon[:, pl.ds(at, 128)] = tile.astype(BF)


def call(kernel, name, outs, args, flops=0, moved=0, scratch=(), vmem=40):
    return pl.pallas_call(
        kernel,
        out_shape=tuple(jax.ShapeDtypeStruct(*o) for o in outs),
        in_specs=[SMEM if a.ndim == 1 else VMEM for a in args],
        out_specs=(VMEM,) * len(outs),
        scratch_shapes=list(scratch),
        compiler_params=pltpu.CompilerParams(vmem_limit_bytes=vmem * 1024 * 1024),
        cost_estimate=pl.CostEstimate(flops=flops, bytes_accessed=moved, transcendentals=0),
        name=name,
    )(*args)


def per_device(samples, rotation, codebook):
    core, xl = lax.axis_index("core"), lax.axis_index("xl")
    yh, yl = lax.axis_index("yh"), lax.axis_index("yl")
    chunk = lax.axis_index("z") * 2 + lax.axis_index("xh")
    place = jnp.stack([core, xl, yh, yl, chunk]).astype(jnp.int32)
    pack, copies = call(
        open_kernel,
        "open",
        [((64, 1408), BF), ((4, 128, 1024), BF)],
        (samples, rotation.T, codebook[0].T),
        vmem=60,
    )
    packs = []
    for steps in ((3, 2), (None, 1)):
        pairs = [
            (c * 8 + ((y + step if y & 1 else y - step) & 7), c * 8 + y)
            for c, step in enumerate(steps)
            for y in range(8)
            if step is not None
        ]
        packs.append(lax.ppermute(pack, ("core", "yh", "yl"), pairs))
    mine = lax.all_to_all(copies, ("xl", "yl"), 0, 0, tiled=True).reshape(512, 1024)
    tools = call(
        prepare_kernel,
        "prepare",
        [((128, 1024), BF), ((128, 512), BF), ((512, 256), BF)],
        (place, pack, *packs),
    )
    mine, *tools = lax.optimization_barrier((mine, *tools))
    swap = [(0, 1), (1, 0)]
    other = lax.ppermute(mine, "core", swap)
    block, pair = ((4, 128, 128), BF), ((2, 128, 128), BF)
    sums, cross, early = call(
        early_kernel,
        "early",
        [((512, 256), F32), ((128, 1024), F32), block],
        (mine, *tools),
        moved=8_000_000,
    )
    send, late, *totals = call(
        late_kernel,
        "late",
        [((32, 32, 128), BF), block, ((144, 128), BF), ((144, 128), BF)],
        (other, *tools, sums, cross),
        moved=8_000_000,
    )
    moved = []
    for i in range(2):
        pairs = [
            (c * 8 + y, c * 8 + (((y & 6) + PLACES[c][y & 1][i]) & 7)) for c in range(2) for y in range(8)
        ]
        moved.append(lax.ppermute(totals[i], ("core", "yh", "yl"), pairs))
    got_core = lax.ppermute(late, "core", swap)
    keep, give = call(half_kernel, "half", [((80, 128), F32), ((80, 128), BF)], (place, *moved))
    half = lax.ppermute(give, "core", swap)
    got = lax.all_to_all(send, NEAR, 0, 0, tiled=True)
    got, half, got_core = lax.optimization_barrier((got, half, got_core))
    (send,) = call(middle_kernel, "middle", [((16, 88, 128), BF)], (got, keep, half))
    gives = call(second_kernel, "second", [pair, pair, pair], (place, early, got_core))
    got_x = lax.ppermute(gives[0], "xl", swap)
    got_y = lax.ppermute(gives[1], "yl", swap)
    got_xy = lax.ppermute(gives[2], ("xl", "yl"), [(0, 3), (1, 2), (2, 1), (3, 0)])
    got = lax.all_to_all(send, FAR, 0, 0, tiled=True)
    got, got_x, got_y, got_xy = lax.optimization_barrier((got, got_x, got_y, got_xy))
    cross, fresh = call(
        finish_kernel,
        "finish",
        [((2, 1024), F32), ((64, 128), F32)],
        (place, got, codebook[0].T),
    )
    fresh_other = lax.ppermute(fresh, "core", swap)
    (recon,) = call(
        home_kernel, "home", [((128, 1024), BF)], (place, early, got_core, got_x, got_y, got_xy)
    )
    fresh_other, recon = lax.optimization_barrier((fresh_other, recon))
    (new_codes,) = call(codes_kernel, "codes", [((64, 256), F32)], (place, fresh, fresh_other))
    return recon, new_codes.T[None], cross


def solution(mesh):
    fine = Mesh(mesh.devices.reshape(SIZES), NAMES)
    rows = P(DP + SUB, None)
    return jax.shard_map(
        per_device,
        mesh=fine,
        in_specs=(rows, P(None, SUB), P(SUB, None, None)),
        out_specs=(rows, P(SUB, None, None), rows),
        check_vma=False,
    )
```

time: 100 us -> 95.8 us (0.958)
  waiting for transfers between devices: 30.6 us -> 23.5 us
  starting transfers between devices: 52.6 us -> 56.8 us
    ppermute x2 -> x6, starting transfers between devices: 5.84 us -> 19.6 us  [the longest x2 7.72 us: per_device(): moved.append(lax.ppermute(totals[i], ('core', 'yh', 'yl'), pairs))]
    all_to_all x1 -> x0, waiting for transfers between devices: 7.42 us -> none  [per_device(): spread = lax.all_to_all(spread, FAR, 0, 0, tiled=True)]
    all_to_all x1 -> x0, starting transfers between devices: 6 us -> none  [per_device(): spread = lax.all_to_all(spread, FAR, 0, 0, tiled=True)]
    all_to_all x1, waiting for transfers between devices: 4.95 us -> 0.01 us  [per_device(): got = lax.all_to_all(send, NEAR, 0, 0, tiled=True)]
    ppermute x2 -> x6, waiting for transfers between devices: 3.59 us -> 7.29 us  [the longest x2 3.71 us: per_device(): moved.append(lax.ppermute(totals[i], ('core', 'yh', 'yl'), pairs))]
    ppermute x2, starting transfers between devices: 9.91 us -> 8.06 us  [per_device(): packs.append(lax.ppermute(pack, ('core', 'yh', 'yl'), pairs))]
    ppermute x2, waiting for transfers between devices: 10.3 us -> 12.1 us  [per_device(): packs.append(lax.ppermute(pack, ('core', 'yh', 'yl'), pairs))]
    all_to_all x1, starting transfers between devices: 7.21 us -> 5.79 us  [per_device(): got = lax.all_to_all(send, NEAR, 0, 0, tiled=True)]
  transfers between devices with their start and end apart: 11 -> 14, of which waited for: 7 -> 7; matrix products, arithmetic and copies ran while one was open for 0% -> 0% of each run, Pallas kernels for 5% -> 5%
where the time goes in v8:
time: 95.8 us; the launch traced here: 95.2 us
  starting transfers between devices  56.8 us (59%)
  waiting for transfers between devices  23.5 us (25%)
  Pallas kernels  13.9 us (15%)
    pallas_call x10, Pallas kernels, call(): pl.pallas_call(kernel, out_shape=tuple((jax.ShapeDtypeStruct(*o) for o in...  13.9 us
    all_to_all x1, starting transfers between devices, per_device(): got = lax.all_to_all(send, FAR, 0, 0, tiled=True)  12.6 us
    ppermute x2, waiting for transfers between devices, per_device(): packs.append(lax.ppermute(pack, ('core', 'yh', 'yl'), pairs))  12.1 us
    ppermute x2, starting transfers between devices, per_device(): packs.append(lax.ppermute(pack, ('core', 'yh', 'yl'), pairs))  8.06 us
    ppermute x2, starting transfers between devices, per_device(): moved.append(lax.ppermute(totals[i], ('core', 'yh', 'yl'), pairs))  7.72 us
    all_to_all x1, starting transfers between devices, per_device(): got = lax.all_to_all(send, NEAR, 0, 0, tiled=True)  5.79 us
    all_to_all x1, starting transfers between devices, per_device(): lax.all_to_all(copies, ('xl', 'yl'), 0, 0, tiled=True).reshape(512, 1024)  4.45 us
    ppermute x1, starting transfers between devices, per_device(): lax.ppermute(gives[2], ('xl', 'yl'), [(0, 3), (1, 2), (2, 1), (3, 0)])  3.96 us
  transfers between devices with their start and end apart: 14, of which 7 were waited for; matrix products, arithmetic and copies ran while one was open for 0% of the time, Pallas kernels for 5%

profile of v8, /device:TPU:1, one launch (start us, length us, event | category | flops | bytes accessed | tf_op | source)
XLA Modules:
  0.0 95.2 jit_solution(16799120023281361337)
XLA Ops:
  0.6 2.1 %open.1 = (bf16[64,1408]{1,0:T(8,128)(2,1)}, bf16[4,128,1024]{2,1,0:T(8,128)(2,1)}) custom-call(bf16[128,1024]{1,0:T(8,128)(2,1)} %samples.1, bf16[64,1024]{1,0:T(8,128)(2,1)} %bitcast.17, f32[64,256]{1,0:T(8,128)} %bitcast.15), custom_call_target="tpu_custom_call" | custom-call | tf_op jit(solution)/shard_map/open/pallas_call | solution.py:236
  2.7 0.0 copy-start.1
  2.7 4.5 %all-to-all-start = ((bf16[4,128,1024]{2,1,0:T(8,128)(2,1)}), bf16[4,128,1024]{2,1,0:T(8,128)(2,1)S(1)}, u32[]{:S(2)}, u32[]{:S(2)}) async-start(bf16[4,128,1024]{2,1,0:T(8,128)(2,1)} %get-tuple-element.35), calls=%async_computation | async-start | bytes 2097152 | tf_op jit(solution)/shard_map/all_to_all | solution.py:269
  7.2 0.0 copy-done.1
  7.2 6.1 %collective-permute-start.1 = (bf16[64,1408]{1,0:T(8,128)(2,1)S(1)}, bf16[64,1408]{1,0:T(8,128)(2,1)S(1)}, u32[]{:S(2)}, u32[]{:S(2)}) collective-permute-start(bf16[64,1408]{1,0:T(8,128)(2,1)S(1)} %copy-done.1), channel_id=1, source_target_pairs={{23,16},{18,17},{17,18},{20,19},{19,20},{22,21},{21,22},{16,23},{3... | collective-permute-start | bytes 540680 | tf_op jit(solution)/shard_map/ppermute | solution.py:268
  13.4 1.9 %collective-permute-start = (bf16[64,1408]{1,0:T(8,128)(2,1)S(1)}, bf16[64,1408]{1,0:T(8,128)(2,1)S(1)}, u32[]{:S(2)}, u32[]{:S(2)}) collective-permute-start(bf16[64,1408]{1,0:T(8,128)(2,1)S(1)} %copy-done.1), channel_id=1, source_target_pairs={{5,0},{4,1},{7,2},{6,3},{1,4},{0,5},{3,6},{2,7},{22,16},{19,17},{1... | collective-permute-start | bytes 540680 | tf_op jit(solution)/shard_map/ppermute | solution.py:268
  15.3 0.1 stack.23.place
  15.4 0.8 collective-permute-done.1.second
  16.2 11.3 %collective-permute-done.first = bf16[64,1408]{1,0:T(8,128)(2,1)S(1)} collective-permute-done((bf16[64,1408]{1,0:T(8,128)(2,1)S(1)}, bf16[64,1408]{1,0:T(8,128)(2,1)S(1)}, u32[]{:S(2)}, u32[]{:S(2)}) %collective-permute-start) | collective-permute-done | bytes 180256 | tf_op jit(solution)/shard_map/ppermute | solution.py:268
  27.5 0.7 prepare.1
  28.2 0.0 all-to-all-done
  28.2 1.9 %collective-permute-start.2 = (bf16[512,1024]{1,0:T(8,128)(2,1)S(1)}, bf16[512,1024]{1,0:T(8,128)(2,1)S(1)}, u32[]{:S(2)}, u32[]{:S(2)}) collective-permute-start(bf16[512,1024]{1,0:T(8,128)(2,1)S(1)} %bitcast.13), channel_id=1, source_target_pairs={{0,16},{16,0},{1,17},{17,1},{2,18},{18,2},{3,19},{19,3},{4,20},{20... | collective-permute-start | bytes 3145736 | tf_op jit(solution)/shard_map/ppermute | solution.py:278
  30.1 1.8 %early.1 = (f32[512,256]{1,0:T(8,128)S(1)}, f32[128,1024]{1,0:T(8,128)S(1)}, bf16[4,128,128]{2,1,0:T(8,128)(2,1)S(1)}) custom-call(bf16[512,1024]{1,0:T(8,128)(2,1)S(1)} %bitcast.14, bf16[128,1024]{1,0:T(8,128)(2,1)S(1)} %get-tuple-element.41.turn, bf16[128,512]{1,0:T(8,128)(2,1)S(1)} %get-tuple-element.42.codes_t, bf16[512,256]{1,0:T(8,128)(2,1)S(1)} %get-tuple-element.43.left), custom_call_target="tpu_custom_call" | custom-call | bytes 8000000 | tf_op jit(solution)/shard_map/early/pallas_call | solution.py:236
  31.9 0.8 collective-permute-done.2.samples
  32.7 3.3 %late.1 = (bf16[32,32,128]{2,1,0:T(8,128)(2,1)}, bf16[4,128,128]{2,1,0:T(8,128)(2,1)S(1)}, bf16[144,128]{1,0:T(8,128)(2,1)S(1)}, bf16[144,128]{1,0:T(8,128)(2,1)S(1)}) custom-call(bf16[512,1024]{1,0:T(8,128)(2,1)S(1)} %collective-permute-done.2.samples, bf16[128,1024]{1,0:T(8,128)(2,1)S(1)} %get-tuple-element.41.turn, ...), custom_call_target="tpu_custom_call" | custom-call | bytes 8000000 | tf_op jit(solution)/shard_map/late/pallas_call | solution.py:236
  36.0 5.8 %all-to-all-start.1 = ((bf16[32,32,128]{2,1,0:T(8,128)(2,1)}), bf16[32,32,128]{2,1,0:T(8,128)(2,1)S(1)}, u32[]{:S(2)}, u32[]{:S(2)}) async-start(bf16[32,32,128]{2,1,0:T(8,128)(2,1)} %get-tuple-element.46), calls=%async_computation.1 | async-start | bytes 524288 | tf_op jit(solution)/shard_map/all_to_all | solution.py:303
  41.8 2.1 %collective-permute-start.6 = (bf16[4,128,128]{2,1,0:T(8,128)(2,1)S(1)}, bf16[4,128,128]{2,1,0:T(8,128)(2,1)S(1)}, u32[]{:S(2)}, u32[]{:S(2)}) collective-permute-start(bf16[4,128,128]{2,1,0:T(8,128)(2,1)S(1)} %get-tuple-element.50), channel_id=1, source_target_pairs={{0,16},{16,0},{1,17},{17,1},{2,18},{18,2},{3,19},{19,3},{4,20},{20... | collective-permute-start | bytes 393224 | tf_op jit(solution)/shard_map/ppermute | solution.py:300
  44.0 5.5 %collective-permute-start.3 = (bf16[144,128]{1,0:T(8,128)(2,1)S(1)}, bf16[144,128]{1,0:T(8,128)(2,1)S(1)}, u32[]{:S(2)}, u32[]{:S(2)}) collective-permute-start(bf16[144,128]{1,0:T(8,128)(2,1)S(1)} %get-tuple-element.47), channel_id=1, source_target_pairs={{0,0},{1,1},{2,2},{3,3},{4,4},{5,5},{6,6},{7,7},{16,22},{17,19},{1... | collective-permute-start | bytes 110600 | tf_op jit(solution)/shard_map/ppermute | solution.py:299
  49.5 2.2 %collective-permute-start.4 = (bf16[144,128]{1,0:T(8,128)(2,1)S(1)}, bf16[144,128]{1,0:T(8,128)(2,1)S(1)}, u32[]{:S(2)}, u32[]{:S(2)}) collective-permute-start(bf16[144,128]{1,0:T(8,128)(2,1)S(1)} %get-tuple-element.48), channel_id=1, source_target_pairs={{0,5},{1,4},{2,7},{3,6},{4,1},{5,0},{6,3},{7,2},{16,23},{17,18},{1... | collective-permute-start | bytes 110600 | tf_op jit(solution)/shard_map/ppermute | solution.py:299
  51.7 0.0 collective-permute-done.3.first
  51.7 3.7 %collective-permute-done.4.second = bf16[144,128]{1,0:T(8,128)(2,1)S(1)} collective-permute-done((bf16[144,128]{1,0:T(8,128)(2,1)S(1)}, bf16[144,128]{1,0:T(8,128)(2,1)S(1)}, u32[]{:S(2)}, u32[]{:S(2)}) %collective-permute-start.4) | collective-permute-done | bytes 36896 | tf_op jit(solution)/shard_map/ppermute | solution.py:299
  55.4 0.6 half.1
  56.0 1.9 %collective-permute-start.5 = (bf16[80,128]{1,0:T(8,128)(2,1)S(1)}, bf16[80,128]{1,0:T(8,128)(2,1)S(1)}, u32[]{:S(2)}, u32[]{:S(2)}) collective-permute-start(bf16[80,128]{1,0:T(8,128)(2,1)S(1)} %get-tuple-element.49), channel_id=1, source_target_pairs={{0,16},{16,0},{1,17},{17,1},{2,18},{18,2},{3,19},{19,3},{4,20},{20... | collective-permute-start | bytes 61448 | tf_op jit(solution)/shard_map/ppermute | solution.py:302
  57.9 1.2 %collective-permute-done.5.half = bf16[80,128]{1,0:T(8,128)(2,1)S(1)} collective-permute-done((bf16[80,128]{1,0:T(8,128)(2,1)S(1)}, bf16[80,128]{1,0:T(8,128)(2,1)S(1)}, u32[]{:S(2)}, u32[]{:S(2)}) %collective-permute-start.5) | collective-permute-done | bytes 20512 | tf_op jit(solution)/shard_map/ppermute | solution.py:302
  59.1 0.0 collective-permute-done.6.got_core
  59.1 0.0 all-to-all-done.1.got
  59.1 1.0 %middle.1 = bf16[16,88,128]{2,1,0:T(8,128)(2,1)} custom-call(bf16[32,32,128]{2,1,0:T(8,128)(2,1)S(1)} %all-to-all-done.1.got, f32[80,128]{1,0:T(8,128)S(1)} %get-tuple-element.52.keep, bf16[80,128]{1,0:T(8,128)(2,1)S(1)} %collective-permute-done.5.half), custom_call_target="tpu_custom_call" | custom-call | tf_op jit(solution)/shard_map/middle/pallas_call | solution.py:236
  60.1 12.6 %all-to-all-start.2 = ((bf16[16,88,128]{2,1,0:T(8,128)(2,1)}), bf16[16,88,128]{2,1,0:T(8,128)(2,1)S(1)}, u32[]{:S(2)}, u32[]{:S(2)}) async-start(bf16[16,88,128]{2,1,0:T(8,128)(2,1)} %middle.1), calls=%async_computation.2 | async-start | bytes 720896 | tf_op jit(solution)/shard_map/all_to_all | solution.py:310
  72.7 0.0 copy-start
  72.7 0.6 second.1
  73.3 2.5 %collective-permute-start.7 = (bf16[2,128,128]{2,1,0:T(8,128)(2,1)S(1)}, bf16[2,128,128]{2,1,0:T(8,128)(2,1)S(1)}, u32[]{:S(2)}, u32[]{:S(2)}) collective-permute-start(bf16[2,128,128]{2,1,0:T(8,128)(2,1)S(1)} %get-tuple-element.56), channel_id=1, source_target_pairs={{0,8},{8,0},{1,9},{9,1},{2,10},{10,2},{3,11},{11,3},{4,12},{12,4},... | collective-permute-start | bytes 196616 | tf_op jit(solution)/shard_map/ppermute | solution.py:307
  75.8 1.9 %collective-permute-start.8 = (bf16[2,128,128]{2,1,0:T(8,128)(2,1)S(1)}, bf16[2,128,128]{2,1,0:T(8,128)(2,1)S(1)}, u32[]{:S(2)}, u32[]{:S(2)}) collective-permute-start(bf16[2,128,128]{2,1,0:T(8,128)(2,1)S(1)} %get-tuple-element.57), channel_id=1, source_target_pairs={{0,1},{1,0},{2,3},{3,2},{4,5},{5,4},{6,7},{7,6},{8,9},{9,8},{10,11... | collective-permute-start | bytes 196616 | tf_op jit(solution)/shard_map/ppermute | solution.py:308
  77.7 4.0 %collective-permute-start.9 = (bf16[2,128,128]{2,1,0:T(8,128)(2,1)S(1)}, bf16[2,128,128]{2,1,0:T(8,128)(2,1)S(1)}, u32[]{:S(2)}, u32[]{:S(2)}) collective-permute-start(bf16[2,128,128]{2,1,0:T(8,128)(2,1)S(1)} %get-tuple-element.58), channel_id=1, source_target_pairs={{0,9},{1,8},{8,1},{9,0},{2,11},{3,10},{10,3},{11,2},{4,13},{5,12},... | collective-permute-start | bytes 196616 | tf_op jit(solution)/shard_map/ppermute | solution.py:309
  81.7 0.0 collective-permute-done.7.got_x
  81.7 0.0 collective-permute-done.8.got_y
  81.7 2.4 %collective-permute-done.9.got_xy = bf16[2,128,128]{2,1,0:T(8,128)(2,1)S(1)} collective-permute-done((bf16[2,128,128]{2,1,0:T(8,128)(2,1)S(1)}, bf16[2,128,128]{2,1,0:T(8,128)(2,1)S(1)}, u32[]{:S(2)}, u32[]{:S(2)}) %collective-permute-start.9) | collective-permute-done | bytes 65568 | tf_op jit(solution)/shard_map/ppermute | solution.py:309
  84.1 3.4 %all-to-all-done.2.got = bf16[16,88,128]{2,1,0:T(8,128)(2,1)S(1)} async-done(((bf16[16,88,128]{2,1,0:T(8,128)(2,1)}), bf16[16,88,128]{2,1,0:T(8,128)(2,1)S(1)}, u32[]{:S(2)}, u32[]{:S(2)}) %all-to-all-start.2) | async-done | bytes 360480 | tf_op jit(solution)/shard_map/all_to_all | solution.py:310
  87.5 0.0 copy-done
  87.5 1.2 %finish.1 = (f32[2,1024]{1,0:T(2,128)}, f32[64,128]{1,0:T(8,128)S(1)}) custom-call(s32[5]{0:T(128)S(1)} %stack.23.place, bf16[16,88,128]{2,1,0:T(8,128)(2,1)S(1)} %all-to-all-done.2.got, f32[64,256]{1,0:T(8,128)S(1)} %bitcast.16), custom_call_target="tpu_custom_call" | custom-call | tf_op jit(solution)/shard_map/finish/pallas_call | solution.py:236
  88.7 3.9 %collective-permute-start.10 = (f32[64,128]{1,0:T(8,128)S(1)}, f32[64,128]{1,0:T(8,128)S(1)}, u32[]{:S(2)}, u32[]{:S(2)}) collective-permute-start(f32[64,128]{1,0:T(8,128)S(1)} %get-tuple-element.60.mine), channel_id=1, source_target_pairs={{0,16},{16,0},{1,17},{17,1},{2,18},{18,2},{3,19},{19,3},{4,20},{20... | collective-permute-start | bytes 98312 | tf_op jit(solution)/shard_map/ppermute | solution.py:318
  92.6 1.4 %home.1 = bf16[128,1024]{1,0:T(8,128)(2,1)} custom-call(s32[5]{0:T(128)S(1)} %stack.23.place, bf16[4,128,128]{2,1,0:T(8,128)(2,1)S(1)} %get-tuple-element.54.early, bf16[4,128,128]{2,1,0:T(8,128)(2,1)S(1)} %collective-permute-done.6.got_core, bf16[2,128,128]{2,1,0:T(8,128)(2,1)S(1)} %collective-permute-done.7.got_x, ...), custom_call_target="tpu_custom_call" | custom-call | tf_op jit(solution)/shard_map/home/pallas_call | solution.py:236
  94.0 0.0 collective-permute-done.10.other
  94.0 1.2 %codes.1 = f32[64,256]{1,0:T(8,128)} custom-call(s32[5]{0:T(128)S(1)} %stack.23.place, f32[64,128]{1,0:T(8,128)S(1)} %get-tuple-element.60.mine, f32[64,128]{1,0:T(8,128)S(1)} %collective-permute-done.10.other), custom_call_target="tpu_custom_call" | custom-call | tf_op jit(solution)/shard_map/codes/pallas_call | solution.py:236
Async XLA Ops:
  2.7 4.5 %copy-start.1 = (bf16[64,1408]{1,0:T(8,128)(2,1)S(1)}, bf16[64,1408]{1,0:T(8,128)(2,1)}, u32[]{:S(2)}) copy-start(bf16[64,1408]{1,0:T(8,128)(2,1)} %get-tuple-element.36.pack) | copy-start | bytes 540676
  2.7 25.4 %all-to-all-start = ((bf16[4,128,1024]{2,1,0:T(8,128)(2,1)}), bf16[4,128,1024]{2,1,0:T(8,128)(2,1)S(1)}, u32[]{:S(2)}, u32[]{:S(2)}) async-start(bf16[4,128,1024]{2,1,0:T(8,128)(2,1)} %get-tuple-element.35), calls=%async_computation | async-start | bytes 2097152 | tf_op jit(solution)/shard_map/all_to_all | solution.py:269
  7.2 9.0 %collective-permute-start.1 = (bf16[64,1408]{1,0:T(8,128)(2,1)S(1)}, bf16[64,1408]{1,0:T(8,128)(2,1)S(1)}, u32[]{:S(2)}, u32[]{:S(2)}) collective-permute-start(bf16[64,1408]{1,0:T(8,128)(2,1)S(1)} %copy-done.1), channel_id=1, source_target_pairs={{23,16},{18,17},{17,18},{20,19},{19,20},{22,21},{21,22},{16,23},{3... | collective-permute-start | bytes 540680 | tf_op jit(solution)/shard_map/ppermute | solution.py:268
  13.4 14.1 %collective-permute-start = (bf16[64,1408]{1,0:T(8,128)(2,1)S(1)}, bf16[64,1408]{1,0:T(8,128)(2,1)S(1)}, u32[]{:S(2)}, u32[]{:S(2)}) collective-permute-start(bf16[64,1408]{1,0:T(8,128)(2,1)S(1)} %copy-done.1), channel_id=1, source_target_pairs={{5,0},{4,1},{7,2},{6,3},{1,4},{0,5},{3,6},{2,7},{22,16},{19,17},{1... | collective-permute-start | bytes 540680 | tf_op jit(solution)/shard_map/ppermute | solution.py:268
  28.2 4.6 %collective-permute-start.2 = (bf16[512,1024]{1,0:T(8,128)(2,1)S(1)}, bf16[512,1024]{1,0:T(8,128)(2,1)S(1)}, u32[]{:S(2)}, u32[]{:S(2)}) collective-permute-start(bf16[512,1024]{1,0:T(8,128)(2,1)S(1)} %bitcast.13), channel_id=1, source_target_pairs={{0,16},{16,0},{1,17},{17,1},{2,18},{18,2},{3,19},{19,3},{4,20},{20... | collective-permute-start | bytes 3145736 | tf_op jit(solution)/shard_map/ppermute | solution.py:278
  36.0 23.1 %all-to-all-start.1 = ((bf16[32,32,128]{2,1,0:T(8,128)(2,1)}), bf16[32,32,128]{2,1,0:T(8,128)(2,1)S(1)}, u32[]{:S(2)}, u32[]{:S(2)}) async-start(bf16[32,32,128]{2,1,0:T(8,128)(2,1)} %get-tuple-element.46), calls=%async_computation.1 | async-start | bytes 524288 | tf_op jit(solution)/shard_map/all_to_all | solution.py:303
  41.8 17.2 %collective-permute-start.6 = (bf16[4,128,128]{2,1,0:T(8,128)(2,1)S(1)}, bf16[4,128,128]{2,1,0:T(8,128)(2,1)S(1)}, u32[]{:S(2)}, u32[]{:S(2)}) collective-permute-start(bf16[4,128,128]{2,1,0:T(8,128)(2,1)S(1)} %get-tuple-element.50), channel_id=1, source_target_pairs={{0,16},{16,0},{1,17},{17,1},{2,18},{18,2},{3,19},{19,3},{4,20},{20... | collective-permute-start | bytes 393224 | tf_op jit(solution)/shard_map/ppermute | solution.py:300
  44.0 7.7 %collective-permute-start.3 = (bf16[144,128]{1,0:T(8,128)(2,1)S(1)}, bf16[144,128]{1,0:T(8,128)(2,1)S(1)}, u32[]{:S(2)}, u32[]{:S(2)}) collective-permute-start(bf16[144,128]{1,0:T(8,128)(2,1)S(1)} %get-tuple-element.47), channel_id=1, source_target_pairs={{0,0},{1,1},{2,2},{3,3},{4,4},{5,5},{6,6},{7,7},{16,22},{17,19},{1... | collective-permute-start | bytes 110600 | tf_op jit(solution)/shard_map/ppermute | solution.py:299
  49.5 5.9 %collective-permute-start.4 = (bf16[144,128]{1,0:T(8,128)(2,1)S(1)}, bf16[144,128]{1,0:T(8,128)(2,1)S(1)}, u32[]{:S(2)}, u32[]{:S(2)}) collective-permute-start(bf16[144,128]{1,0:T(8,128)(2,1)S(1)} %get-tuple-element.48), channel_id=1, source_target_pairs={{0,5},{1,4},{2,7},{3,6},{4,1},{5,0},{6,3},{7,2},{16,23},{17,18},{1... | collective-permute-start | bytes 110600 | tf_op jit(solution)/shard_map/ppermute | solution.py:299
  56.0 3.1 %collective-permute-start.5 = (bf16[80,128]{1,0:T(8,128)(2,1)S(1)}, bf16[80,128]{1,0:T(8,128)(2,1)S(1)}, u32[]{:S(2)}, u32[]{:S(2)}) collective-permute-start(bf16[80,128]{1,0:T(8,128)(2,1)S(1)} %get-tuple-element.49), channel_id=1, source_target_pairs={{0,16},{16,0},{1,17},{17,1},{2,18},{18,2},{3,19},{19,3},{4,20},{20... | collective-permute-start | bytes 61448 | tf_op jit(solution)/shard_map/ppermute | solution.py:302
  60.1 27.4 %all-to-all-start.2 = ((bf16[16,88,128]{2,1,0:T(8,128)(2,1)}), bf16[16,88,128]{2,1,0:T(8,128)(2,1)S(1)}, u32[]{:S(2)}, u32[]{:S(2)}) async-start(bf16[16,88,128]{2,1,0:T(8,128)(2,1)} %middle.1), calls=%async_computation.2 | async-start | bytes 720896 | tf_op jit(solution)/shard_map/all_to_all | solution.py:310
  72.7 14.8 %copy-start = (f32[1,256,64]{1,2,0:T(8,128)S(1)}, f32[1,256,64]{1,2,0:T(8,128)}, u32[]{:S(2)}) copy-start(f32[1,256,64]{1,2,0:T(8,128)} %param.5) | copy-start | bytes 196612
  73.3 8.4 %collective-permute-start.7 = (bf16[2,128,128]{2,1,0:T(8,128)(2,1)S(1)}, bf16[2,128,128]{2,1,0:T(8,128)(2,1)S(1)}, u32[]{:S(2)}, u32[]{:S(2)}) collective-permute-start(bf16[2,128,128]{2,1,0:T(8,128)(2,1)S(1)} %get-tuple-element.56), channel_id=1, source_target_pairs={{0,8},{8,0},{1,9},{9,1},{2,10},{10,2},{3,11},{11,3},{4,12},{12,4},... | collective-permute-start | bytes 196616 | tf_op jit(solution)/shard_map/ppermute | solution.py:307
  75.8 5.9 %collective-permute-start.8 = (bf16[2,128,128]{2,1,0:T(8,128)(2,1)S(1)}, bf16[2,128,128]{2,1,0:T(8,128)(2,1)S(1)}, u32[]{:S(2)}, u32[]{:S(2)}) collective-permute-start(bf16[2,128,128]{2,1,0:T(8,128)(2,1)S(1)} %get-tuple-element.57), channel_id=1, source_target_pairs={{0,1},{1,0},{2,3},{3,2},{4,5},{5,4},{6,7},{7,6},{8,9},{9,8},{10,11... | collective-permute-start | bytes 196616 | tf_op jit(solution)/shard_map/ppermute | solution.py:308
  77.7 6.4 %collective-permute-start.9 = (bf16[2,128,128]{2,1,0:T(8,128)(2,1)S(1)}, bf16[2,128,128]{2,1,0:T(8,128)(2,1)S(1)}, u32[]{:S(2)}, u32[]{:S(2)}) collective-permute-start(bf16[2,128,128]{2,1,0:T(8,128)(2,1)S(1)} %get-tuple-element.58), channel_id=1, source_target_pairs={{0,9},{1,8},{8,1},{9,0},{2,11},{3,10},{10,3},{11,2},{4,13},{5,12},... | collective-permute-start | bytes 196616 | tf_op jit(solution)/shard_map/ppermute | solution.py:309
  88.7 5.3 %collective-permute-start.10 = (f32[64,128]{1,0:T(8,128)S(1)}, f32[64,128]{1,0:T(8,128)S(1)}, u32[]{:S(2)}, u32[]{:S(2)}) collective-permute-start(f32[64,128]{1,0:T(8,128)S(1)} %get-tuple-element.60.mine), channel_id=1, source_target_pairs={{0,16},{16,0},{1,17},{17,1},{2,18},{18,2},{3,19},{19,3},{4,20},{20... | collective-permute-start | bytes 98312 | tf_op jit(solution)/shard_map/ppermute | solution.py:318

commit v9 on v8

--- a/solution.py
+++ b/solution.py
@@ -19,7 +19,7 @@
 F32 = jnp.float32
 NT = (((1,), (1,)), ((), ()))
 VMEM = pl.BlockSpec(memory_space=pltpu.VMEM)
-SMEM = pl.BlockSpec(memory_space=pltpu.SMEM)
+ANY = pl.BlockSpec(memory_space=pl.ANY)
 
 
 def half_mask(shape):
@@ -35,9 +35,10 @@
     return high, x - high
 
 
-def open_kernel(samples, turn_t, codes_t, pack, copies):
-    for n in range(4):
-        copies[n] = samples[...]
+def open_kernel(samples, turn_t, codes_t, pack, copies, done):
+    moves = [pltpu.make_async_copy(samples, copies.at[n], done.at[n]) for n in range(4)]
+    for move in moves:
+        move.start()
     codes = codes_t[...]
     square = jnp.sum(codes * codes, axis=0, keepdims=True)
     high = square.astype(BF).astype(F32)
@@ -49,10 +50,12 @@
     pack[0:16, 1280:] = squares[:, :128]
     pack[16:32, 1280:] = squares[:, 128:]
     pack[32:64, 1280:] = jnp.zeros((32, 128), BF)
-
-
-def prepare_kernel(place, pack, first, second, turn, codes_t, left):
-    core = place[0]
+    for move in moves:
+        move.wait()
+
+
+def prepare_kernel(pack, first, second, turn, codes_t, left):
+    core = lax.axis_index("core")
     w0, w1, w2 = pack[...], first[...], second[...]
     wa = jnp.where(core == 0, w0, w1)
     wb = jnp.where(core == 0, w1, w2)
@@ -150,8 +153,8 @@
         out[128:144, :] = jnp.concatenate(lines + [jnp.zeros((12, 128), F32)], axis=0).astype(BF)
 
 
-def half_kernel(place, first, second, keep, give):
-    core = place[0]
+def half_kernel(first, second, keep, give):
+    core = lax.axis_index("core")
     both = first[...].astype(F32) + second[...].astype(F32)
     empty = jnp.zeros((14, 128), F32)
     halves = []
@@ -191,32 +194,33 @@
         send[q, 16:88, :] = both
 
 
-def finish_kernel(place, got, codes_t, cross, fresh):
+def finish_kernel(got, codes_t, cross, fresh):
     total = jnp.sum(got[...].astype(F32), axis=0)
     for n in range(8):
         cross[:, n * 128 : (n + 1) * 128] = total[2 * n : 2 * n + 2]
     sums, count = total[16:80], total[80:81] + total[81:82]
     sums = jnp.concatenate([sums, swap_halves(sums)], axis=0).T[:64]
-    own = jnp.where(place[0] == 0, codes_t[:, :128], codes_t[:, 128:])
+    own = jnp.where(lax.axis_index("core") == 0, codes_t[:, :128], codes_t[:, 128:])
     fresh[...] = (sums + own) / (count + 1.0)
 
 
-def codes_kernel(place, mine, other, codes_t):
+def codes_kernel(mine, other, codes_t):
     a, b = mine[...], other[...]
-    codes_t[:, :128] = jnp.where(place[0] == 0, a, b)
-    codes_t[:, 128:] = jnp.where(place[0] == 0, b, a)
-
-
-def second_kernel(place, early, got_core, give_x, give_y, give_xy):
-    xl, yl = place[1], place[3]
+    codes_t[:, :128] = jnp.where(lax.axis_index("core") == 0, a, b)
+    codes_t[:, 128:] = jnp.where(lax.axis_index("core") == 0, b, a)
+
+
+def second_kernel(early, got_core, give_x, give_y, give_xy):
+    xl, yl = lax.axis_index("xl"), lax.axis_index("yl")
     for n, block in enumerate((early, got_core)):
         give_x[n] = block[(1 - xl) * 2 + yl]
         give_y[n] = block[xl * 2 + 1 - yl]
         give_xy[n] = block[(1 - xl) * 2 + 1 - yl]
 
 
-def home_kernel(place, early, got_core, got_x, got_y, got_xy, recon):
-    core, xl, yh, yl = place[0], place[1], place[2], place[3]
+def home_kernel(early, got_core, got_x, got_y, got_xy, recon):
+    core, xl = lax.axis_index("core"), lax.axis_index("xl")
+    yh, yl = lax.axis_index("yh"), lax.axis_index("yl")
     low = half_mask((128, 128))
     own = [early[xl * 2 + yl], got_core[xl * 2 + yl]]
     for across, (same, far) in enumerate(((own, got_y), (got_x, got_xy))):
@@ -232,31 +236,31 @@
             recon[:, pl.ds(at, 128)] = tile.astype(BF)
 
 
-def call(kernel, name, outs, args, flops=0, moved=0, scratch=(), vmem=40):
+def call(kernel, name, outs, args, flops=0, moved=0):
     return pl.pallas_call(
         kernel,
         out_shape=tuple(jax.ShapeDtypeStruct(*o) for o in outs),
-        in_specs=[SMEM if a.ndim == 1 else VMEM for a in args],
+        in_specs=[VMEM] * len(args),
         out_specs=(VMEM,) * len(outs),
-        scratch_shapes=list(scratch),
-        compiler_params=pltpu.CompilerParams(vmem_limit_bytes=vmem * 1024 * 1024),
+        compiler_params=pltpu.CompilerParams(vmem_limit_bytes=40 * 1024 * 1024),
         cost_estimate=pl.CostEstimate(flops=flops, bytes_accessed=moved, transcendentals=0),
         name=name,
     )(*args)
 
 
 def per_device(samples, rotation, codebook):
-    core, xl = lax.axis_index("core"), lax.axis_index("xl")
-    yh, yl = lax.axis_index("yh"), lax.axis_index("yl")
-    chunk = lax.axis_index("z") * 2 + lax.axis_index("xh")
-    place = jnp.stack([core, xl, yh, yl, chunk]).astype(jnp.int32)
-    pack, copies = call(
+    pack, copies = pl.pallas_call(
         open_kernel,
-        "open",
-        [((64, 1408), BF), ((4, 128, 1024), BF)],
-        (samples, rotation.T, codebook[0].T),
-        vmem=60,
-    )
+        out_shape=(
+            jax.ShapeDtypeStruct((64, 1408), BF),
+            jax.ShapeDtypeStruct((4, 128, 1024), BF),
+        ),
+        in_specs=[ANY, VMEM, VMEM],
+        out_specs=(VMEM, ANY),
+        scratch_shapes=[pltpu.SemaphoreType.DMA((4,))],
+        compiler_params=pltpu.CompilerParams(vmem_limit_bytes=60 * 1024 * 1024),
+        name="open",
+    )(samples, rotation.T, codebook[0].T)
     packs = []
     for steps in ((3, 2), (None, 1)):
         pairs = [
@@ -271,7 +275,7 @@
         prepare_kernel,
         "prepare",
         [((128, 1024), BF), ((128, 512), BF), ((512, 256), BF)],
-        (place, pack, *packs),
+        (pack, *packs),
     )
     mine, *tools = lax.optimization_barrier((mine, *tools))
     swap = [(0, 1), (1, 0)]
@@ -298,12 +302,14 @@
         ]
         moved.append(lax.ppermute(totals[i], ("core", "yh", "yl"), pairs))
     got_core = lax.ppermute(late, "core", swap)
-    keep, give = call(half_kernel, "half", [((80, 128), F32), ((80, 128), BF)], (place, *moved))
+    keep, give = call(
+        half_kernel, "half", [((80, 128), F32), ((80, 128), BF)], tuple(moved), flops=2 * 10**9
+    )
     half = lax.ppermute(give, "core", swap)
     got = lax.all_to_all(send, NEAR, 0, 0, tiled=True)
     got, half, got_core = lax.optimization_barrier((got, half, got_core))
     (send,) = call(middle_kernel, "middle", [((16, 88, 128), BF)], (got, keep, half))
-    gives = call(second_kernel, "second", [pair, pair, pair], (place, early, got_core))
+    gives = call(second_kernel, "second", [pair, pair, pair], (early, got_core))
     got_x = lax.ppermute(gives[0], "xl", swap)
     got_y = lax.ppermute(gives[1], "yl", swap)
     got_xy = lax.ppermute(gives[2], ("xl", "yl"), [(0, 3), (1, 2), (2, 1), (3, 0)])
@@ -313,14 +319,14 @@
         finish_kernel,
         "finish",
         [((2, 1024), F32), ((64, 128), F32)],
-        (place, got, codebook[0].T),
+        (got, codebook[0].T),
     )
     fresh_other = lax.ppermute(fresh, "core", swap)
     (recon,) = call(
-        home_kernel, "home", [((128, 1024), BF)], (place, early, got_core, got_x, got_y, got_xy)
+        home_kernel, "home", [((128, 1024), BF)], (early, got_core, got_x, got_y, got_xy)
     )
     fresh_other, recon = lax.optimization_barrier((fresh_other, recon))
-    (new_codes,) = call(codes_kernel, "codes", [((64, 256), F32)], (place, fresh, fresh_other))
+    (new_codes,) = call(codes_kernel, "codes", [((64, 256), F32)], (fresh, fresh_other))
     return recon, new_codes.T[None], cross
 
 

time: 95.8 us -> 123 us (1.28)
  Pallas kernels: 13.9 us -> 43 us
  waiting for transfers between devices: 23.5 us -> 21.1 us
    pallas_call x0 -> x1, Pallas kernels: none -> 34.5 us  [per_device(): pl.pallas_call(open_kernel, out_shape=(jax.ShapeDtypeStruct((64, 1408), B...]
    pallas_call x10 -> x9, Pallas kernels: 13.9 us -> 8.48 us  [call(): pl.pallas_call(kernel, out_shape=tuple((jax.ShapeDtypeStruct(*o) for o in...]
    ppermute x1, starting transfers between devices: 1.92 us -> 4.21 us  [per_device(): got_y = lax.ppermute(gives[1], 'yl', swap)]
    all_to_all x1, waiting for transfers between devices: 3.36 us -> 1.44 us  [per_device(): got = lax.all_to_all(send, FAR, 0, 0, tiled=True)]
    ppermute x2, waiting for transfers between devices: 3.71 us -> 2.13 us  [per_device(): moved.append(lax.ppermute(totals[i], ('core', 'yh', 'yl'), pairs))]
    ppermute x1, starting transfers between devices: 3.96 us -> 2.44 us  [per_device(): lax.ppermute(gives[2], ('xl', 'yl'), [(0, 3), (1, 2), (2, 1), (3, 0)])]
    ppermute x1, waiting for transfers between devices: 2.42 us -> 3.73 us  [per_device(): lax.ppermute(gives[2], ('xl', 'yl'), [(0, 3), (1, 2), (2, 1), (3, 0)])]
  transfers between devices with their start and end apart: 14 -> 14, of which waited for: 7 -> 7; matrix products, arithmetic and copies ran while one was open for 0% -> 0% of each run, Pallas kernels for 5% -> 2%
where the time goes in v9:
time: 123 us; the launch traced here: 122 us
  starting transfers between devices  57.4 us (47%)
  Pallas kernels  43 us (35%)
  waiting for transfers between devices  21.1 us (17%)
    pallas_call x1, Pallas kernels, per_device(): pl.pallas_call(open_kernel, out_shape=(jax.ShapeDtypeStruct((64, 1408), B...  34.5 us
    all_to_all x1, starting transfers between devices, per_device(): got = lax.all_to_all(send, FAR, 0, 0, tiled=True)  12.6 us
    ppermute x2, waiting for transfers between devices, per_device(): packs.append(lax.ppermute(pack, ('core', 'yh', 'yl'), pairs))  12.2 us
    pallas_call x9, Pallas kernels, call(): pl.pallas_call(kernel, out_shape=tuple((jax.ShapeDtypeStruct(*o) for o in...  8.48 us
    ppermute x2, starting transfers between devices, per_device(): packs.append(lax.ppermute(pack, ('core', 'yh', 'yl'), pairs))  8.06 us
    ppermute x2, starting transfers between devices, per_device(): moved.append(lax.ppermute(totals[i], ('core', 'yh', 'yl'), pairs))  7.59 us
    all_to_all x1, starting transfers between devices, per_device(): got = lax.all_to_all(send, NEAR, 0, 0, tiled=True)  5.8 us
    all_to_all x1, starting transfers between devices, per_device(): lax.all_to_all(copies, ('xl', 'yl'), 0, 0, tiled=True).reshape(512, 1024)  4.47 us
  transfers between devices with their start and end apart: 14, of which 7 were waited for; matrix products, arithmetic and copies ran while one was open for 0% of the time, Pallas kernels for 2%

profile of v9, /device:TPU:1, one launch (start us, length us, event | category | flops | bytes accessed | tf_op | source)
XLA Modules:
  0.0 122.3 jit_solution(3276416530269802587)
XLA Ops:
  0.6 34.5 %open.1 = (bf16[64,1408]{1,0:T(8,128)(2,1)}, bf16[4,128,1024]{2,1,0:T(8,128)(2,1)}) custom-call(bf16[128,1024]{1,0:T(8,128)(2,1)} %samples.1, bf16[64,1024]{1,0:T(8,128)(2,1)} %bitcast.12, f32[64,256]{1,0:T(8,128)} %bitcast.10), custom_call_target="tpu_custom_call" | custom-call | tf_op jit(solution)/shard_map/open/pallas_call | solution.py:252
  35.1 0.0 copy-start.1
  35.1 4.5 %all-to-all-start = ((bf16[4,128,1024]{2,1,0:T(8,128)(2,1)}), bf16[4,128,1024]{2,1,0:T(8,128)(2,1)S(1)}, u32[]{:S(2)}, u32[]{:S(2)}) async-start(bf16[4,128,1024]{2,1,0:T(8,128)(2,1)} %get-tuple-element.35), calls=%async_computation | async-start | bytes 2097152 | tf_op jit(solution)/shard_map/all_to_all | solution.py:273
  39.6 0.0 copy-done.1
  39.6 6.1 %collective-permute-start.1 = (bf16[64,1408]{1,0:T(8,128)(2,1)S(1)}, bf16[64,1408]{1,0:T(8,128)(2,1)S(1)}, u32[]{:S(2)}, u32[]{:S(2)}) collective-permute-start(bf16[64,1408]{1,0:T(8,128)(2,1)S(1)} %copy-done.1), channel_id=1, source_target_pairs={{23,16},{18,17},{17,18},{20,19},{19,20},{22,21},{21,22},{16,23},{3... | collective-permute-start | bytes 540680 | tf_op jit(solution)/shard_map/ppermute | solution.py:272
  45.7 1.9 %collective-permute-start = (bf16[64,1408]{1,0:T(8,128)(2,1)S(1)}, bf16[64,1408]{1,0:T(8,128)(2,1)S(1)}, u32[]{:S(2)}, u32[]{:S(2)}) collective-permute-start(bf16[64,1408]{1,0:T(8,128)(2,1)S(1)} %copy-done.1), channel_id=1, source_target_pairs={{5,0},{4,1},{7,2},{6,3},{1,4},{0,5},{3,6},{2,7},{22,16},{19,17},{1... | collective-permute-start | bytes 540680 | tf_op jit(solution)/shard_map/ppermute | solution.py:272
  47.7 0.9 collective-permute-done.1.second
  48.6 11.3 %collective-permute-done.first = bf16[64,1408]{1,0:T(8,128)(2,1)S(1)} collective-permute-done((bf16[64,1408]{1,0:T(8,128)(2,1)S(1)}, bf16[64,1408]{1,0:T(8,128)(2,1)S(1)}, u32[]{:S(2)}, u32[]{:S(2)}) %collective-permute-start) | collective-permute-done | bytes 180256 | tf_op jit(solution)/shard_map/ppermute | solution.py:272
  59.9 0.1 prepare.1
  60.0 0.0 all-to-all-done
  60.0 1.9 %collective-permute-start.2 = (bf16[512,1024]{1,0:T(8,128)(2,1)S(1)}, bf16[512,1024]{1,0:T(8,128)(2,1)S(1)}, u32[]{:S(2)}, u32[]{:S(2)}) collective-permute-start(bf16[512,1024]{1,0:T(8,128)(2,1)S(1)} %bitcast.8), channel_id=1, source_target_pairs={{0,16},{16,0},{1,17},{17,1},{2,18},{18,2},{3,19},{19,3},{4,20},{20... | collective-permute-start | bytes 3145736 | tf_op jit(solution)/shard_map/ppermute | solution.py:282
  62.0 1.8 %early.1 = (f32[512,256]{1,0:T(8,128)S(1)}, f32[128,1024]{1,0:T(8,128)S(1)}, bf16[4,128,128]{2,1,0:T(8,128)(2,1)S(1)}) custom-call(bf16[512,1024]{1,0:T(8,128)(2,1)S(1)} %bitcast.9, bf16[128,1024]{1,0:T(8,128)(2,1)S(1)} %get-tuple-element.41.turn, bf16[128,512]{1,0:T(8,128)(2,1)S(1)} %get-tuple-element.42.codes_t, bf16[512,256]{1,0:T(8,128)(2,1)S(1)} %get-tuple-element.43.left), custom_call_target="tpu_custom_call" | custom-call | bytes 8000000 | tf_op jit(solution)/shard_map/early/pallas_call | solution.py:240
  63.8 0.8 collective-permute-done.2.samples
  64.6 3.3 %late.1 = (bf16[32,32,128]{2,1,0:T(8,128)(2,1)}, bf16[4,128,128]{2,1,0:T(8,128)(2,1)S(1)}, bf16[144,128]{1,0:T(8,128)(2,1)S(1)}, bf16[144,128]{1,0:T(8,128)(2,1)S(1)}) custom-call(bf16[512,1024]{1,0:T(8,128)(2,1)S(1)} %collective-permute-done.2.samples, bf16[128,1024]{1,0:T(8,128)(2,1)S(1)} %get-tuple-element.41.turn, ...), custom_call_target="tpu_custom_call" | custom-call | bytes 8000000 | tf_op jit(solution)/shard_map/late/pallas_call | solution.py:240
  67.9 5.8 %all-to-all-start.1 = ((bf16[32,32,128]{2,1,0:T(8,128)(2,1)}), bf16[32,32,128]{2,1,0:T(8,128)(2,1)S(1)}, u32[]{:S(2)}, u32[]{:S(2)}) async-start(bf16[32,32,128]{2,1,0:T(8,128)(2,1)} %get-tuple-element.46), calls=%async_computation.1 | async-start | bytes 524288 | tf_op jit(solution)/shard_map/all_to_all | solution.py:309
  73.7 5.4 %collective-permute-start.3 = (bf16[144,128]{1,0:T(8,128)(2,1)S(1)}, bf16[144,128]{1,0:T(8,128)(2,1)S(1)}, u32[]{:S(2)}, u32[]{:S(2)}) collective-permute-start(bf16[144,128]{1,0:T(8,128)(2,1)S(1)} %get-tuple-element.47), channel_id=1, source_target_pairs={{0,0},{1,1},{2,2},{3,3},{4,4},{5,5},{6,6},{7,7},{16,22},{17,19},{1... | collective-permute-start | bytes 110600 | tf_op jit(solution)/shard_map/ppermute | solution.py:303
  79.1 2.2 %collective-permute-start.4 = (bf16[144,128]{1,0:T(8,128)(2,1)S(1)}, bf16[144,128]{1,0:T(8,128)(2,1)S(1)}, u32[]{:S(2)}, u32[]{:S(2)}) collective-permute-start(bf16[144,128]{1,0:T(8,128)(2,1)S(1)} %get-tuple-element.48), channel_id=1, source_target_pairs={{0,5},{1,4},{2,7},{3,6},{4,1},{5,0},{6,3},{7,2},{16,23},{17,18},{1... | collective-permute-start | bytes 110600 | tf_op jit(solution)/shard_map/ppermute | solution.py:303
  81.3 1.9 %collective-permute-start.6 = (bf16[4,128,128]{2,1,0:T(8,128)(2,1)S(1)}, bf16[4,128,128]{2,1,0:T(8,128)(2,1)S(1)}, u32[]{:S(2)}, u32[]{:S(2)}) collective-permute-start(bf16[4,128,128]{2,1,0:T(8,128)(2,1)S(1)} %get-tuple-element.50), channel_id=1, source_target_pairs={{0,16},{16,0},{1,17},{17,1},{2,18},{18,2},{3,19},{19,3},{4,20},{20... | collective-permute-start | bytes 393224 | tf_op jit(solution)/shard_map/ppermute | solution.py:304
  83.2 0.0 collective-permute-done.3.first
  83.2 2.1 %collective-permute-done.4.second = bf16[144,128]{1,0:T(8,128)(2,1)S(1)} collective-permute-done((bf16[144,128]{1,0:T(8,128)(2,1)S(1)}, bf16[144,128]{1,0:T(8,128)(2,1)S(1)}, u32[]{:S(2)}, u32[]{:S(2)}) %collective-permute-start.4) | collective-permute-done | bytes 36896 | tf_op jit(solution)/shard_map/ppermute | solution.py:303
  85.4 2.3 %collective-permute-start.5 = (bf16[80,128]{1,0:T(8,128)(2,1)S(1)}, bf16[80,128]{1,0:T(8,128)(2,1)S(1)}, u32[]{:S(2)}, u32[]{:S(2)}) collective-permute-start(bf16[80,128]{1,0:T(8,128)(2,1)S(1)} %get-tuple-element.49), channel_id=1, source_target_pairs={{0,16},{16,0},{1,17},{17,1},{2,18},{18,2},{3,19},{19,3},{4,20},{20... | collective-permute-start | bytes 61448 | tf_op jit(solution)/shard_map/ppermute | solution.py:308
  87.6 0.8 collective-permute-done.5.half
  88.5 0.0 collective-permute-done.6.got_core
  88.5 0.0 all-to-all-done.1.got
  88.5 1.0 middle.1
  89.5 12.6 %all-to-all-start.2 = ((bf16[16,88,128]{2,1,0:T(8,128)(2,1)}), bf16[16,88,128]{2,1,0:T(8,128)(2,1)S(1)}, u32[]{:S(2)}, u32[]{:S(2)}) async-start(bf16[16,88,128]{2,1,0:T(8,128)(2,1)} %middle.1), calls=%async_computation.2 | async-start | bytes 720896 | tf_op jit(solution)/shard_map/all_to_all | solution.py:316
  102.1 0.0 copy-start
  102.1 2.6 %collective-permute-start.7 = (bf16[2,128,128]{2,1,0:T(8,128)(2,1)S(1)}, bf16[2,128,128]{2,1,0:T(8,128)(2,1)S(1)}, u32[]{:S(2)}, u32[]{:S(2)}) collective-permute-start(bf16[2,128,128]{2,1,0:T(8,128)(2,1)S(1)} %get-tuple-element.56), channel_id=1, source_target_pairs={{0,8},{8,0},{1,9},{9,1},{2,10},{10,2},{3,11},{11,3},{4,12},{12,4},... | collective-permute-start | bytes 196616 | tf_op jit(solution)/shard_map/ppermute | solution.py:313
  104.7 4.2 %collective-permute-start.8 = (bf16[2,128,128]{2,1,0:T(8,128)(2,1)S(1)}, bf16[2,128,128]{2,1,0:T(8,128)(2,1)S(1)}, u32[]{:S(2)}, u32[]{:S(2)}) collective-permute-start(bf16[2,128,128]{2,1,0:T(8,128)(2,1)S(1)} %get-tuple-element.57), channel_id=1, source_target_pairs={{0,1},{1,0},{2,3},{3,2},{4,5},{5,4},{6,7},{7,6},{8,9},{9,8},{10,11... | collective-permute-start | bytes 196616 | tf_op jit(solution)/shard_map/ppermute | solution.py:314
  108.9 2.4 %collective-permute-start.9 = (bf16[2,128,128]{2,1,0:T(8,128)(2,1)S(1)}, bf16[2,128,128]{2,1,0:T(8,128)(2,1)S(1)}, u32[]{:S(2)}, u32[]{:S(2)}) collective-permute-start(bf16[2,128,128]{2,1,0:T(8,128)(2,1)S(1)} %get-tuple-element.58), channel_id=1, source_target_pairs={{0,9},{1,8},{8,1},{9,0},{2,11},{3,10},{10,3},{11,2},{4,13},{5,12},... | collective-permute-start | bytes 196616 | tf_op jit(solution)/shard_map/ppermute | solution.py:315
  111.4 0.0 collective-permute-done.7.got_x
  111.4 0.0 collective-permute-done.8.got_y
  111.4 3.7 %collective-permute-done.9.got_xy = bf16[2,128,128]{2,1,0:T(8,128)(2,1)S(1)} collective-permute-done((bf16[2,128,128]{2,1,0:T(8,128)(2,1)S(1)}, bf16[2,128,128]{2,1,0:T(8,128)(2,1)S(1)}, u32[]{:S(2)}, u32[]{:S(2)}) %collective-permute-start.9) | collective-permute-done | bytes 65568 | tf_op jit(solution)/shard_map/ppermute | solution.py:315
  115.1 1.4 %all-to-all-done.2.got = bf16[16,88,128]{2,1,0:T(8,128)(2,1)S(1)} async-done(((bf16[16,88,128]{2,1,0:T(8,128)(2,1)}), bf16[16,88,128]{2,1,0:T(8,128)(2,1)S(1)}, u32[]{:S(2)}, u32[]{:S(2)}) %all-to-all-start.2) | async-done | bytes 360480 | tf_op jit(solution)/shard_map/all_to_all | solution.py:316
  116.6 0.0 copy-done
  116.6 0.7 finish.1
  117.3 3.6 %collective-permute-start.10 = (f32[64,128]{1,0:T(8,128)S(1)}, f32[64,128]{1,0:T(8,128)S(1)}, u32[]{:S(2)}, u32[]{:S(2)}) collective-permute-start(f32[64,128]{1,0:T(8,128)S(1)} %get-tuple-element.60.mine), channel_id=1, source_target_pairs={{0,16},{16,0},{1,17},{17,1},{2,18},{18,2},{3,19},{19,3},{4,20},{20... | collective-permute-start | bytes 98312 | tf_op jit(solution)/shard_map/ppermute | solution.py:324
  120.8 0.9 home.1
  121.7 0.0 collective-permute-done.10.other
  121.7 0.6 codes.1
  (2 shorter events, 0.0 us)
Async XLA Ops:
  35.1 4.5 %copy-start.1 = (bf16[64,1408]{1,0:T(8,128)(2,1)S(1)}, bf16[64,1408]{1,0:T(8,128)(2,1)}, u32[]{:S(2)}) copy-start(bf16[64,1408]{1,0:T(8,128)(2,1)} %get-tuple-element.36.pack) | copy-start | bytes 540676
  35.1 24.9 %all-to-all-start = ((bf16[4,128,1024]{2,1,0:T(8,128)(2,1)}), bf16[4,128,1024]{2,1,0:T(8,128)(2,1)S(1)}, u32[]{:S(2)}, u32[]{:S(2)}) async-start(bf16[4,128,1024]{2,1,0:T(8,128)(2,1)} %get-tuple-element.35), calls=%async_computation | async-start | bytes 2097152 | tf_op jit(solution)/shard_map/all_to_all | solution.py:273
  39.6 9.0 %collective-permute-start.1 = (bf16[64,1408]{1,0:T(8,128)(2,1)S(1)}, bf16[64,1408]{1,0:T(8,128)(2,1)S(1)}, u32[]{:S(2)}, u32[]{:S(2)}) collective-permute-start(bf16[64,1408]{1,0:T(8,128)(2,1)S(1)} %copy-done.1), channel_id=1, source_target_pairs={{23,16},{18,17},{17,18},{20,19},{19,20},{22,21},{21,22},{16,23},{3... | collective-permute-start | bytes 540680 | tf_op jit(solution)/shard_map/ppermute | solution.py:272
  45.7 14.1 %collective-permute-start = (bf16[64,1408]{1,0:T(8,128)(2,1)S(1)}, bf16[64,1408]{1,0:T(8,128)(2,1)S(1)}, u32[]{:S(2)}, u32[]{:S(2)}) collective-permute-start(bf16[64,1408]{1,0:T(8,128)(2,1)S(1)} %copy-done.1), channel_id=1, source_target_pairs={{5,0},{4,1},{7,2},{6,3},{1,4},{0,5},{3,6},{2,7},{22,16},{19,17},{1... | collective-permute-start | bytes 540680 | tf_op jit(solution)/shard_map/ppermute | solution.py:272
  60.0 4.6 %collective-permute-start.2 = (bf16[512,1024]{1,0:T(8,128)(2,1)S(1)}, bf16[512,1024]{1,0:T(8,128)(2,1)S(1)}, u32[]{:S(2)}, u32[]{:S(2)}) collective-permute-start(bf16[512,1024]{1,0:T(8,128)(2,1)S(1)} %bitcast.8), channel_id=1, source_target_pairs={{0,16},{16,0},{1,17},{17,1},{2,18},{18,2},{3,19},{19,3},{4,20},{20... | collective-permute-start | bytes 3145736 | tf_op jit(solution)/shard_map/ppermute | solution.py:282
  67.9 20.6 %all-to-all-start.1 = ((bf16[32,32,128]{2,1,0:T(8,128)(2,1)}), bf16[32,32,128]{2,1,0:T(8,128)(2,1)S(1)}, u32[]{:S(2)}, u32[]{:S(2)}) async-start(bf16[32,32,128]{2,1,0:T(8,128)(2,1)} %get-tuple-element.46), calls=%async_computation.1 | async-start | bytes 524288 | tf_op jit(solution)/shard_map/all_to_all | solution.py:309
  73.7 9.5 %collective-permute-start.3 = (bf16[144,128]{1,0:T(8,128)(2,1)S(1)}, bf16[144,128]{1,0:T(8,128)(2,1)S(1)}, u32[]{:S(2)}, u32[]{:S(2)}) collective-permute-start(bf16[144,128]{1,0:T(8,128)(2,1)S(1)} %get-tuple-element.47), channel_id=1, source_target_pairs={{0,0},{1,1},{2,2},{3,3},{4,4},{5,5},{6,6},{7,7},{16,22},{17,19},{1... | collective-permute-start | bytes 110600 | tf_op jit(solution)/shard_map/ppermute | solution.py:303
  79.1 6.3 %collective-permute-start.4 = (bf16[144,128]{1,0:T(8,128)(2,1)S(1)}, bf16[144,128]{1,0:T(8,128)(2,1)S(1)}, u32[]{:S(2)}, u32[]{:S(2)}) collective-permute-start(bf16[144,128]{1,0:T(8,128)(2,1)S(1)} %get-tuple-element.48), channel_id=1, source_target_pairs={{0,5},{1,4},{2,7},{3,6},{4,1},{5,0},{6,3},{7,2},{16,23},{17,18},{1... | collective-permute-start | bytes 110600 | tf_op jit(solution)/shard_map/ppermute | solution.py:303
  81.3 7.2 %collective-permute-start.6 = (bf16[4,128,128]{2,1,0:T(8,128)(2,1)S(1)}, bf16[4,128,128]{2,1,0:T(8,128)(2,1)S(1)}, u32[]{:S(2)}, u32[]{:S(2)}) collective-permute-start(bf16[4,128,128]{2,1,0:T(8,128)(2,1)S(1)} %get-tuple-element.50), channel_id=1, source_target_pairs={{0,16},{16,0},{1,17},{17,1},{2,18},{18,2},{3,19},{19,3},{4,20},{20... | collective-permute-start | bytes 393224 | tf_op jit(solution)/shard_map/ppermute | solution.py:304
  85.4 3.1 %collective-permute-start.5 = (bf16[80,128]{1,0:T(8,128)(2,1)S(1)}, bf16[80,128]{1,0:T(8,128)(2,1)S(1)}, u32[]{:S(2)}, u32[]{:S(2)}) collective-permute-start(bf16[80,128]{1,0:T(8,128)(2,1)S(1)} %get-tuple-element.49), channel_id=1, source_target_pairs={{0,16},{16,0},{1,17},{17,1},{2,18},{18,2},{3,19},{19,3},{4,20},{20... | collective-permute-start | bytes 61448 | tf_op jit(solution)/shard_map/ppermute | solution.py:308
  89.5 27.1 %all-to-all-start.2 = ((bf16[16,88,128]{2,1,0:T(8,128)(2,1)}), bf16[16,88,128]{2,1,0:T(8,128)(2,1)S(1)}, u32[]{:S(2)}, u32[]{:S(2)}) async-start(bf16[16,88,128]{2,1,0:T(8,128)(2,1)} %middle.1), calls=%async_computation.2 | async-start | bytes 720896 | tf_op jit(solution)/shard_map/all_to_all | solution.py:316
  102.1 14.5 %copy-start = (f32[1,256,64]{1,2,0:T(8,128)S(1)}, f32[1,256,64]{1,2,0:T(8,128)}, u32[]{:S(2)}) copy-start(f32[1,256,64]{1,2,0:T(8,128)} %param.5) | copy-start | bytes 196612
  102.1 9.3 %collective-permute-start.7 = (bf16[2,128,128]{2,1,0:T(8,128)(2,1)S(1)}, bf16[2,128,128]{2,1,0:T(8,128)(2,1)S(1)}, u32[]{:S(2)}, u32[]{:S(2)}) collective-permute-start(bf16[2,128,128]{2,1,0:T(8,128)(2,1)S(1)} %get-tuple-element.56), channel_id=1, source_target_pairs={{0,8},{8,0},{1,9},{9,1},{2,10},{10,2},{3,11},{11,3},{4,12},{12,4},... | collective-permute-start | bytes 196616 | tf_op jit(solution)/shard_map/ppermute | solution.py:313
  104.7 6.7 %collective-permute-start.8 = (bf16[2,128,128]{2,1,0:T(8,128)(2,1)S(1)}, bf16[2,128,128]{2,1,0:T(8,128)(2,1)S(1)}, u32[]{:S(2)}, u32[]{:S(2)}) collective-permute-start(bf16[2,128,128]{2,1,0:T(8,128)(2,1)S(1)} %get-tuple-element.57), channel_id=1, source_target_pairs={{0,1},{1,0},{2,3},{3,2},{4,5},{5,4},{6,7},{7,6},{8,9},{9,8},{10,11... | collective-permute-start | bytes 196616 | tf_op jit(solution)/shard_map/ppermute | solution.py:314
  108.9 6.2 %collective-permute-start.9 = (bf16[2,128,128]{2,1,0:T(8,128)(2,1)S(1)}, bf16[2,128,128]{2,1,0:T(8,128)(2,1)S(1)}, u32[]{:S(2)}, u32[]{:S(2)}) collective-permute-start(bf16[2,128,128]{2,1,0:T(8,128)(2,1)S(1)} %get-tuple-element.58), channel_id=1, source_target_pairs={{0,9},{1,8},{8,1},{9,0},{2,11},{3,10},{10,3},{11,2},{4,13},{5,12},... | collective-permute-start | bytes 196616 | tf_op jit(solution)/shard_map/ppermute | solution.py:315
  117.3 4.4 %collective-permute-start.10 = (f32[64,128]{1,0:T(8,128)S(1)}, f32[64,128]{1,0:T(8,128)S(1)}, u32[]{:S(2)}, u32[]{:S(2)}) collective-permute-start(f32[64,128]{1,0:T(8,128)S(1)} %get-tuple-element.60.mine), channel_id=1, source_target_pairs={{0,16},{16,0},{1,17},{17,1},{2,18},{18,2},{3,19},{19,3},{4,20},{20... | collective-permute-start | bytes 98312 | tf_op jit(solution)/shard_map/ppermute | solution.py:324

commit v10 on v9

--- a/solution.py
+++ b/solution.py
@@ -255,7 +255,7 @@
             jax.ShapeDtypeStruct((64, 1408), BF),
             jax.ShapeDtypeStruct((4, 128, 1024), BF),
         ),
-        in_specs=[ANY, VMEM, VMEM],
+        in_specs=[VMEM, VMEM, VMEM],
         out_specs=(VMEM, ANY),
         scratch_shapes=[pltpu.SemaphoreType.DMA((4,))],
         compiler_params=pltpu.CompilerParams(vmem_limit_bytes=60 * 1024 * 1024),

time: 123 us -> 91.4 us (0.74)
  Pallas kernels: 43 us -> 11.2 us
    pallas_call x1, Pallas kernels: 34.5 us -> 2.73 us  [per_device(): pl.pallas_call(open_kernel, out_shape=(jax.ShapeDtypeStruct((64, 1408), B...]
  transfers between devices with their start and end apart: 14 -> 14, of which waited for: 7 -> 7; matrix products, arithmetic and copies ran while one was open for 0% -> 0% of each run, Pallas kernels for 2% -> 3%
where the time goes in v10:
time: 91.4 us; the launch traced here: 90.6 us
  starting transfers between devices  57.4 us (63%)
  waiting for transfers between devices  21.1 us (23%)
  Pallas kernels  11.2 us (12%)
    all_to_all x1, starting transfers between devices, per_device(): got = lax.all_to_all(send, FAR, 0, 0, tiled=True)  12.6 us
    ppermute x2, waiting for transfers between devices, per_device(): packs.append(lax.ppermute(pack, ('core', 'yh', 'yl'), pairs))  12.2 us
    pallas_call x9, Pallas kernels, call(): pl.pallas_call(kernel, out_shape=tuple((jax.ShapeDtypeStruct(*o) for o in...  8.49 us
    ppermute x2, starting transfers between devices, per_device(): packs.append(lax.ppermute(pack, ('core', 'yh', 'yl'), pairs))  8.06 us
    ppermute x2, starting transfers between devices, per_device(): moved.append(lax.ppermute(totals[i], ('core', 'yh', 'yl'), pairs))  7.59 us
    all_to_all x1, starting transfers between devices, per_device(): got = lax.all_to_all(send, NEAR, 0, 0, tiled=True)  5.79 us
    all_to_all x1, starting transfers between devices, per_device(): lax.all_to_all(copies, ('xl', 'yl'), 0, 0, tiled=True).reshape(512, 1024)  4.47 us
    ppermute x1, starting transfers between devices, per_device(): got_y = lax.ppermute(gives[1], 'yl', swap)  4.21 us
  transfers between devices with their start and end apart: 14, of which 7 were waited for; matrix products, arithmetic and copies ran while one was open for 0% of the time, Pallas kernels for 3%

profile of v10, /device:TPU:1, one launch (start us, length us, event | category | flops | bytes accessed | tf_op | source)
XLA Modules:
  0.0 90.6 jit_solution(16948926905807936909)
XLA Ops:
  0.6 2.7 %open.1 = (bf16[64,1408]{1,0:T(8,128)(2,1)}, bf16[4,128,1024]{2,1,0:T(8,128)(2,1)}) custom-call(bf16[128,1024]{1,0:T(8,128)(2,1)} %samples.1, bf16[64,1024]{1,0:T(8,128)(2,1)} %bitcast.12, f32[64,256]{1,0:T(8,128)} %bitcast.10), custom_call_target="tpu_custom_call" | custom-call | tf_op jit(solution)/shard_map/open/pallas_call | solution.py:252
  3.4 0.0 copy-start.1
  3.4 4.5 %all-to-all-start = ((bf16[4,128,1024]{2,1,0:T(8,128)(2,1)}), bf16[4,128,1024]{2,1,0:T(8,128)(2,1)S(1)}, u32[]{:S(2)}, u32[]{:S(2)}) async-start(bf16[4,128,1024]{2,1,0:T(8,128)(2,1)} %get-tuple-element.35), calls=%async_computation | async-start | bytes 2097152 | tf_op jit(solution)/shard_map/all_to_all | solution.py:273
  7.8 0.0 copy-done.1
  7.9 6.1 %collective-permute-start.1 = (bf16[64,1408]{1,0:T(8,128)(2,1)S(1)}, bf16[64,1408]{1,0:T(8,128)(2,1)S(1)}, u32[]{:S(2)}, u32[]{:S(2)}) collective-permute-start(bf16[64,1408]{1,0:T(8,128)(2,1)S(1)} %copy-done.1), channel_id=1, source_target_pairs={{23,16},{18,17},{17,18},{20,19},{19,20},{22,21},{21,22},{16,23},{3... | collective-permute-start | bytes 540680 | tf_op jit(solution)/shard_map/ppermute | solution.py:272
  14.0 1.9 %collective-permute-start = (bf16[64,1408]{1,0:T(8,128)(2,1)S(1)}, bf16[64,1408]{1,0:T(8,128)(2,1)S(1)}, u32[]{:S(2)}, u32[]{:S(2)}) collective-permute-start(bf16[64,1408]{1,0:T(8,128)(2,1)S(1)} %copy-done.1), channel_id=1, source_target_pairs={{5,0},{4,1},{7,2},{6,3},{1,4},{0,5},{3,6},{2,7},{22,16},{19,17},{1... | collective-permute-start | bytes 540680 | tf_op jit(solution)/shard_map/ppermute | solution.py:272
  15.9 0.9 %collective-permute-done.1.second = bf16[64,1408]{1,0:T(8,128)(2,1)S(1)} collective-permute-done((bf16[64,1408]{1,0:T(8,128)(2,1)S(1)}, bf16[64,1408]{1,0:T(8,128)(2,1)S(1)}, u32[]{:S(2)}, u32[]{:S(2)}) %collective-permute-start.1) | collective-permute-done | bytes 180256 | tf_op jit(solution)/shard_map/ppermute | solution.py:272
  16.9 11.3 %collective-permute-done.first = bf16[64,1408]{1,0:T(8,128)(2,1)S(1)} collective-permute-done((bf16[64,1408]{1,0:T(8,128)(2,1)S(1)}, bf16[64,1408]{1,0:T(8,128)(2,1)S(1)}, u32[]{:S(2)}, u32[]{:S(2)}) %collective-permute-start) | collective-permute-done | bytes 180256 | tf_op jit(solution)/shard_map/ppermute | solution.py:272
  28.1 0.1 prepare.1
  28.3 0.0 all-to-all-done
  28.3 1.9 %collective-permute-start.2 = (bf16[512,1024]{1,0:T(8,128)(2,1)S(1)}, bf16[512,1024]{1,0:T(8,128)(2,1)S(1)}, u32[]{:S(2)}, u32[]{:S(2)}) collective-permute-start(bf16[512,1024]{1,0:T(8,128)(2,1)S(1)} %bitcast.8), channel_id=1, source_target_pairs={{0,16},{16,0},{1,17},{17,1},{2,18},{18,2},{3,19},{19,3},{4,20},{20... | collective-permute-start | bytes 3145736 | tf_op jit(solution)/shard_map/ppermute | solution.py:282
  30.2 1.8 %early.1 = (f32[512,256]{1,0:T(8,128)S(1)}, f32[128,1024]{1,0:T(8,128)S(1)}, bf16[4,128,128]{2,1,0:T(8,128)(2,1)S(1)}) custom-call(bf16[512,1024]{1,0:T(8,128)(2,1)S(1)} %bitcast.9, bf16[128,1024]{1,0:T(8,128)(2,1)S(1)} %get-tuple-element.41.turn, bf16[128,512]{1,0:T(8,128)(2,1)S(1)} %get-tuple-element.42.codes_t, bf16[512,256]{1,0:T(8,128)(2,1)S(1)} %get-tuple-element.43.left), custom_call_target="tpu_custom_call" | custom-call | bytes 8000000 | tf_op jit(solution)/shard_map/early/pallas_call | solution.py:240
  32.0 0.8 collective-permute-done.2.samples
  32.8 3.3 %late.1 = (bf16[32,32,128]{2,1,0:T(8,128)(2,1)}, bf16[4,128,128]{2,1,0:T(8,128)(2,1)S(1)}, bf16[144,128]{1,0:T(8,128)(2,1)S(1)}, bf16[144,128]{1,0:T(8,128)(2,1)S(1)}) custom-call(bf16[512,1024]{1,0:T(8,128)(2,1)S(1)} %collective-permute-done.2.samples, bf16[128,1024]{1,0:T(8,128)(2,1)S(1)} %get-tuple-element.41.turn, ...), custom_call_target="tpu_custom_call" | custom-call | bytes 8000000 | tf_op jit(solution)/shard_map/late/pallas_call | solution.py:240
  36.1 5.8 %all-to-all-start.1 = ((bf16[32,32,128]{2,1,0:T(8,128)(2,1)}), bf16[32,32,128]{2,1,0:T(8,128)(2,1)S(1)}, u32[]{:S(2)}, u32[]{:S(2)}) async-start(bf16[32,32,128]{2,1,0:T(8,128)(2,1)} %get-tuple-element.46), calls=%async_computation.1 | async-start | bytes 524288 | tf_op jit(solution)/shard_map/all_to_all | solution.py:309
  41.9 5.4 %collective-permute-start.3 = (bf16[144,128]{1,0:T(8,128)(2,1)S(1)}, bf16[144,128]{1,0:T(8,128)(2,1)S(1)}, u32[]{:S(2)}, u32[]{:S(2)}) collective-permute-start(bf16[144,128]{1,0:T(8,128)(2,1)S(1)} %get-tuple-element.47), channel_id=1, source_target_pairs={{0,0},{1,1},{2,2},{3,3},{4,4},{5,5},{6,6},{7,7},{16,22},{17,19},{1... | collective-permute-start | bytes 110600 | tf_op jit(solution)/shard_map/ppermute | solution.py:303
  47.3 2.2 %collective-permute-start.4 = (bf16[144,128]{1,0:T(8,128)(2,1)S(1)}, bf16[144,128]{1,0:T(8,128)(2,1)S(1)}, u32[]{:S(2)}, u32[]{:S(2)}) collective-permute-start(bf16[144,128]{1,0:T(8,128)(2,1)S(1)} %get-tuple-element.48), channel_id=1, source_target_pairs={{0,5},{1,4},{2,7},{3,6},{4,1},{5,0},{6,3},{7,2},{16,23},{17,18},{1... | collective-permute-start | bytes 110600 | tf_op jit(solution)/shard_map/ppermute | solution.py:303
  49.5 1.9 %collective-permute-start.6 = (bf16[4,128,128]{2,1,0:T(8,128)(2,1)S(1)}, bf16[4,128,128]{2,1,0:T(8,128)(2,1)S(1)}, u32[]{:S(2)}, u32[]{:S(2)}) collective-permute-start(bf16[4,128,128]{2,1,0:T(8,128)(2,1)S(1)} %get-tuple-element.50), channel_id=1, source_target_pairs={{0,16},{16,0},{1,17},{17,1},{2,18},{18,2},{3,19},{19,3},{4,20},{20... | collective-permute-start | bytes 393224 | tf_op jit(solution)/shard_map/ppermute | solution.py:304
  51.5 0.0 collective-permute-done.3.first
  51.5 2.1 %collective-permute-done.4.second = bf16[144,128]{1,0:T(8,128)(2,1)S(1)} collective-permute-done((bf16[144,128]{1,0:T(8,128)(2,1)S(1)}, bf16[144,128]{1,0:T(8,128)(2,1)S(1)}, u32[]{:S(2)}, u32[]{:S(2)}) %collective-permute-start.4) | collective-permute-done | bytes 36896 | tf_op jit(solution)/shard_map/ppermute | solution.py:303
  53.6 2.3 %collective-permute-start.5 = (bf16[80,128]{1,0:T(8,128)(2,1)S(1)}, bf16[80,128]{1,0:T(8,128)(2,1)S(1)}, u32[]{:S(2)}, u32[]{:S(2)}) collective-permute-start(bf16[80,128]{1,0:T(8,128)(2,1)S(1)} %get-tuple-element.49), channel_id=1, source_target_pairs={{0,16},{16,0},{1,17},{17,1},{2,18},{18,2},{3,19},{19,3},{4,20},{20... | collective-permute-start | bytes 61448 | tf_op jit(solution)/shard_map/ppermute | solution.py:308
  55.9 0.8 collective-permute-done.5.half
  56.7 0.0 collective-permute-done.6.got_core
  56.7 0.0 all-to-all-done.1.got
  56.7 1.0 %middle.1 = bf16[16,88,128]{2,1,0:T(8,128)(2,1)} custom-call(bf16[32,32,128]{2,1,0:T(8,128)(2,1)S(1)} %all-to-all-done.1.got, f32[80,128]{1,0:T(8,128)S(1)} %get-tuple-element.52.keep, bf16[80,128]{1,0:T(8,128)(2,1)S(1)} %collective-permute-done.5.half), custom_call_target="tpu_custom_call" | custom-call | tf_op jit(solution)/shard_map/middle/pallas_call | solution.py:240
  57.7 12.6 %all-to-all-start.2 = ((bf16[16,88,128]{2,1,0:T(8,128)(2,1)}), bf16[16,88,128]{2,1,0:T(8,128)(2,1)S(1)}, u32[]{:S(2)}, u32[]{:S(2)}) async-start(bf16[16,88,128]{2,1,0:T(8,128)(2,1)} %middle.1), calls=%async_computation.2 | async-start | bytes 720896 | tf_op jit(solution)/shard_map/all_to_all | solution.py:316
  70.3 0.0 copy-start
  70.4 2.6 %collective-permute-start.7 = (bf16[2,128,128]{2,1,0:T(8,128)(2,1)S(1)}, bf16[2,128,128]{2,1,0:T(8,128)(2,1)S(1)}, u32[]{:S(2)}, u32[]{:S(2)}) collective-permute-start(bf16[2,128,128]{2,1,0:T(8,128)(2,1)S(1)} %get-tuple-element.56), channel_id=1, source_target_pairs={{0,8},{8,0},{1,9},{9,1},{2,10},{10,2},{3,11},{11,3},{4,12},{12,4},... | collective-permute-start | bytes 196616 | tf_op jit(solution)/shard_map/ppermute | solution.py:313
  73.0 4.2 %collective-permute-start.8 = (bf16[2,128,128]{2,1,0:T(8,128)(2,1)S(1)}, bf16[2,128,128]{2,1,0:T(8,128)(2,1)S(1)}, u32[]{:S(2)}, u32[]{:S(2)}) collective-permute-start(bf16[2,128,128]{2,1,0:T(8,128)(2,1)S(1)} %get-tuple-element.57), channel_id=1, source_target_pairs={{0,1},{1,0},{2,3},{3,2},{4,5},{5,4},{6,7},{7,6},{8,9},{9,8},{10,11... | collective-permute-start | bytes 196616 | tf_op jit(solution)/shard_map/ppermute | solution.py:314
  77.2 2.4 %collective-permute-start.9 = (bf16[2,128,128]{2,1,0:T(8,128)(2,1)S(1)}, bf16[2,128,128]{2,1,0:T(8,128)(2,1)S(1)}, u32[]{:S(2)}, u32[]{:S(2)}) collective-permute-start(bf16[2,128,128]{2,1,0:T(8,128)(2,1)S(1)} %get-tuple-element.58), channel_id=1, source_target_pairs={{0,9},{1,8},{8,1},{9,0},{2,11},{3,10},{10,3},{11,2},{4,13},{5,12},... | collective-permute-start | bytes 196616 | tf_op jit(solution)/shard_map/ppermute | solution.py:315
  79.6 0.0 collective-permute-done.7.got_x
  79.7 0.0 collective-permute-done.8.got_y
  79.7 3.7 %collective-permute-done.9.got_xy = bf16[2,128,128]{2,1,0:T(8,128)(2,1)S(1)} collective-permute-done((bf16[2,128,128]{2,1,0:T(8,128)(2,1)S(1)}, bf16[2,128,128]{2,1,0:T(8,128)(2,1)S(1)}, u32[]{:S(2)}, u32[]{:S(2)}) %collective-permute-start.9) | collective-permute-done | bytes 65568 | tf_op jit(solution)/shard_map/ppermute | solution.py:315
  83.4 1.4 %all-to-all-done.2.got = bf16[16,88,128]{2,1,0:T(8,128)(2,1)S(1)} async-done(((bf16[16,88,128]{2,1,0:T(8,128)(2,1)}), bf16[16,88,128]{2,1,0:T(8,128)(2,1)S(1)}, u32[]{:S(2)}, u32[]{:S(2)}) %all-to-all-start.2) | async-done | bytes 360480 | tf_op jit(solution)/shard_map/all_to_all | solution.py:316
  84.8 0.0 copy-done
  84.8 0.7 finish.1
  85.5 3.6 %collective-permute-start.10 = (f32[64,128]{1,0:T(8,128)S(1)}, f32[64,128]{1,0:T(8,128)S(1)}, u32[]{:S(2)}, u32[]{:S(2)}) collective-permute-start(f32[64,128]{1,0:T(8,128)S(1)} %get-tuple-element.60.mine), channel_id=1, source_target_pairs={{0,16},{16,0},{1,17},{17,1},{2,18},{18,2},{3,19},{19,3},{4,20},{20... | collective-permute-start | bytes 98312 | tf_op jit(solution)/shard_map/ppermute | solution.py:324
  89.1 0.9 home.1
  89.9 0.0 collective-permute-done.10.other
  89.9 0.6 codes.1
  (2 shorter events, 0.0 us)
Async XLA Ops:
  3.4 4.5 %copy-start.1 = (bf16[64,1408]{1,0:T(8,128)(2,1)S(1)}, bf16[64,1408]{1,0:T(8,128)(2,1)}, u32[]{:S(2)}) copy-start(bf16[64,1408]{1,0:T(8,128)(2,1)} %get-tuple-element.36.pack) | copy-start | bytes 540676
  3.4 24.9 %all-to-all-start = ((bf16[4,128,1024]{2,1,0:T(8,128)(2,1)}), bf16[4,128,1024]{2,1,0:T(8,128)(2,1)S(1)}, u32[]{:S(2)}, u32[]{:S(2)}) async-start(bf16[4,128,1024]{2,1,0:T(8,128)(2,1)} %get-tuple-element.35), calls=%async_computation | async-start | bytes 2097152 | tf_op jit(solution)/shard_map/all_to_all | solution.py:273
  7.9 9.0 %collective-permute-start.1 = (bf16[64,1408]{1,0:T(8,128)(2,1)S(1)}, bf16[64,1408]{1,0:T(8,128)(2,1)S(1)}, u32[]{:S(2)}, u32[]{:S(2)}) collective-permute-start(bf16[64,1408]{1,0:T(8,128)(2,1)S(1)} %copy-done.1), channel_id=1, source_target_pairs={{23,16},{18,17},{17,18},{20,19},{19,20},{22,21},{21,22},{16,23},{3... | collective-permute-start | bytes 540680 | tf_op jit(solution)/shard_map/ppermute | solution.py:272
  14.0 14.1 %collective-permute-start = (bf16[64,1408]{1,0:T(8,128)(2,1)S(1)}, bf16[64,1408]{1,0:T(8,128)(2,1)S(1)}, u32[]{:S(2)}, u32[]{:S(2)}) collective-permute-start(bf16[64,1408]{1,0:T(8,128)(2,1)S(1)} %copy-done.1), channel_id=1, source_target_pairs={{5,0},{4,1},{7,2},{6,3},{1,4},{0,5},{3,6},{2,7},{22,16},{19,17},{1... | collective-permute-start | bytes 540680 | tf_op jit(solution)/shard_map/ppermute | solution.py:272
  28.3 4.6 %collective-permute-start.2 = (bf16[512,1024]{1,0:T(8,128)(2,1)S(1)}, bf16[512,1024]{1,0:T(8,128)(2,1)S(1)}, u32[]{:S(2)}, u32[]{:S(2)}) collective-permute-start(bf16[512,1024]{1,0:T(8,128)(2,1)S(1)} %bitcast.8), channel_id=1, source_target_pairs={{0,16},{16,0},{1,17},{17,1},{2,18},{18,2},{3,19},{19,3},{4,20},{20... | collective-permute-start | bytes 3145736 | tf_op jit(solution)/shard_map/ppermute | solution.py:282
  36.1 20.6 %all-to-all-start.1 = ((bf16[32,32,128]{2,1,0:T(8,128)(2,1)}), bf16[32,32,128]{2,1,0:T(8,128)(2,1)S(1)}, u32[]{:S(2)}, u32[]{:S(2)}) async-start(bf16[32,32,128]{2,1,0:T(8,128)(2,1)} %get-tuple-element.46), calls=%async_computation.1 | async-start | bytes 524288 | tf_op jit(solution)/shard_map/all_to_all | solution.py:309
  41.9 9.5 %collective-permute-start.3 = (bf16[144,128]{1,0:T(8,128)(2,1)S(1)}, bf16[144,128]{1,0:T(8,128)(2,1)S(1)}, u32[]{:S(2)}, u32[]{:S(2)}) collective-permute-start(bf16[144,128]{1,0:T(8,128)(2,1)S(1)} %get-tuple-element.47), channel_id=1, source_target_pairs={{0,0},{1,1},{2,2},{3,3},{4,4},{5,5},{6,6},{7,7},{16,22},{17,19},{1... | collective-permute-start | bytes 110600 | tf_op jit(solution)/shard_map/ppermute | solution.py:303
  47.3 6.3 %collective-permute-start.4 = (bf16[144,128]{1,0:T(8,128)(2,1)S(1)}, bf16[144,128]{1,0:T(8,128)(2,1)S(1)}, u32[]{:S(2)}, u32[]{:S(2)}) collective-permute-start(bf16[144,128]{1,0:T(8,128)(2,1)S(1)} %get-tuple-element.48), channel_id=1, source_target_pairs={{0,5},{1,4},{2,7},{3,6},{4,1},{5,0},{6,3},{7,2},{16,23},{17,18},{1... | collective-permute-start | bytes 110600 | tf_op jit(solution)/shard_map/ppermute | solution.py:303
  49.5 7.2 %collective-permute-start.6 = (bf16[4,128,128]{2,1,0:T(8,128)(2,1)S(1)}, bf16[4,128,128]{2,1,0:T(8,128)(2,1)S(1)}, u32[]{:S(2)}, u32[]{:S(2)}) collective-permute-start(bf16[4,128,128]{2,1,0:T(8,128)(2,1)S(1)} %get-tuple-element.50), channel_id=1, source_target_pairs={{0,16},{16,0},{1,17},{17,1},{2,18},{18,2},{3,19},{19,3},{4,20},{20... | collective-permute-start | bytes 393224 | tf_op jit(solution)/shard_map/ppermute | solution.py:304
  53.6 3.1 %collective-permute-start.5 = (bf16[80,128]{1,0:T(8,128)(2,1)S(1)}, bf16[80,128]{1,0:T(8,128)(2,1)S(1)}, u32[]{:S(2)}, u32[]{:S(2)}) collective-permute-start(bf16[80,128]{1,0:T(8,128)(2,1)S(1)} %get-tuple-element.49), channel_id=1, source_target_pairs={{0,16},{16,0},{1,17},{17,1},{2,18},{18,2},{3,19},{19,3},{4,20},{20... | collective-permute-start | bytes 61448 | tf_op jit(solution)/shard_map/ppermute | solution.py:308
  57.7 27.1 %all-to-all-start.2 = ((bf16[16,88,128]{2,1,0:T(8,128)(2,1)}), bf16[16,88,128]{2,1,0:T(8,128)(2,1)S(1)}, u32[]{:S(2)}, u32[]{:S(2)}) async-start(bf16[16,88,128]{2,1,0:T(8,128)(2,1)} %middle.1), calls=%async_computation.2 | async-start | bytes 720896 | tf_op jit(solution)/shard_map/all_to_all | solution.py:316
  70.3 14.5 %copy-start = (f32[1,256,64]{1,2,0:T(8,128)S(1)}, f32[1,256,64]{1,2,0:T(8,128)}, u32[]{:S(2)}) copy-start(f32[1,256,64]{1,2,0:T(8,128)} %param.5) | copy-start | bytes 196612
  70.4 9.3 %collective-permute-start.7 = (bf16[2,128,128]{2,1,0:T(8,128)(2,1)S(1)}, bf16[2,128,128]{2,1,0:T(8,128)(2,1)S(1)}, u32[]{:S(2)}, u32[]{:S(2)}) collective-permute-start(bf16[2,128,128]{2,1,0:T(8,128)(2,1)S(1)} %get-tuple-element.56), channel_id=1, source_target_pairs={{0,8},{8,0},{1,9},{9,1},{2,10},{10,2},{3,11},{11,3},{4,12},{12,4},... | collective-permute-start | bytes 196616 | tf_op jit(solution)/shard_map/ppermute | solution.py:313
  73.0 6.7 %collective-permute-start.8 = (bf16[2,128,128]{2,1,0:T(8,128)(2,1)S(1)}, bf16[2,128,128]{2,1,0:T(8,128)(2,1)S(1)}, u32[]{:S(2)}, u32[]{:S(2)}) collective-permute-start(bf16[2,128,128]{2,1,0:T(8,128)(2,1)S(1)} %get-tuple-element.57), channel_id=1, source_target_pairs={{0,1},{1,0},{2,3},{3,2},{4,5},{5,4},{6,7},{7,6},{8,9},{9,8},{10,11... | collective-permute-start | bytes 196616 | tf_op jit(solution)/shard_map/ppermute | solution.py:314
  77.2 6.2 %collective-permute-start.9 = (bf16[2,128,128]{2,1,0:T(8,128)(2,1)S(1)}, bf16[2,128,128]{2,1,0:T(8,128)(2,1)S(1)}, u32[]{:S(2)}, u32[]{:S(2)}) collective-permute-start(bf16[2,128,128]{2,1,0:T(8,128)(2,1)S(1)} %get-tuple-element.58), channel_id=1, source_target_pairs={{0,9},{1,8},{8,1},{9,0},{2,11},{3,10},{10,3},{11,2},{4,13},{5,12},... | collective-permute-start | bytes 196616 | tf_op jit(solution)/shard_map/ppermute | solution.py:315
  85.5 4.4 %collective-permute-start.10 = (f32[64,128]{1,0:T(8,128)S(1)}, f32[64,128]{1,0:T(8,128)S(1)}, u32[]{:S(2)}, u32[]{:S(2)}) collective-permute-start(f32[64,128]{1,0:T(8,128)S(1)} %get-tuple-element.60.mine), channel_id=1, source_target_pairs={{0,16},{16,0},{1,17},{17,1},{2,18},{18,2},{3,19},{19,3},{4,20},{20... | collective-permute-start | bytes 98312 | tf_op jit(solution)/shard_map/ppermute | solution.py:324

commit v11 on v10

--- a/solution.py
+++ b/solution.py
@@ -8,18 +8,18 @@
 from jax.sharding import Mesh
 from jax.sharding import PartitionSpec as P
 
-SIZES = (8, 2, 2, 2, 4, 2)
-NAMES = ("z", "xh", "core", "xl", "yh", "yl")
-DP = ("z", "xh", "core")
-SUB = ("xl", "yh", "yl")
-PLACES = (((0, 5), (1, 4)), ((6, 7), (3, 2)))
-FAR = ("z", "xh")
-NEAR = ("core", "xl", "yh", "yl")
+SIZES = (4, 2, 2, 2, 2, 8)
+NAMES = ("zh", "zl", "xh", "core", "xl", "y")
+DP = ("zh", "zl", "xh", "core")
+SUB = ("xl", "y")
+OFFSETS = (((0, -1), (4, 1)), ((2, -3), (-2, 3)))
+FAR = ("zh", "zl", "xh")
+NEAR = ("core", "xl", "y")
+LINE = ("zl", "core", "y")
 BF = jnp.bfloat16
 F32 = jnp.float32
 NT = (((1,), (1,)), ((), ()))
 VMEM = pl.BlockSpec(memory_space=pltpu.VMEM)
-ANY = pl.BlockSpec(memory_space=pl.ANY)
 
 
 def half_mask(shape):
@@ -35,10 +35,9 @@
     return high, x - high
 
 
-def open_kernel(samples, turn_t, codes_t, pack, copies, done):
-    moves = [pltpu.make_async_copy(samples, copies.at[n], done.at[n]) for n in range(4)]
-    for move in moves:
-        move.start()
+def open_kernel(samples, turn_t, codes_t, pack, copies):
+    for n in range(4):
+        copies[n] = samples[...]
     codes = codes_t[...]
     square = jnp.sum(codes * codes, axis=0, keepdims=True)
     high = square.astype(BF).astype(F32)
@@ -50,15 +49,12 @@
     pack[0:16, 1280:] = squares[:, :128]
     pack[16:32, 1280:] = squares[:, 128:]
     pack[32:64, 1280:] = jnp.zeros((32, 128), BF)
-    for move in moves:
-        move.wait()
 
 
 def prepare_kernel(pack, first, second, turn, codes_t, left):
-    core = lax.axis_index("core")
-    w0, w1, w2 = pack[...], first[...], second[...]
-    wa = jnp.where(core == 0, w0, w1)
-    wb = jnp.where(core == 0, w1, w2)
+    near = lax.axis_index("zl") + lax.axis_index("core")
+    wa = jnp.where(near == 0, pack[...], first[...])
+    wb = second[...]
     turn[0:64, :] = wa[:, :1024]
     turn[64:128, :] = wb[:, :1024]
     zero = jnp.zeros((64, 256), BF)
@@ -165,26 +161,33 @@
     give[...] = jnp.where(core == 0, halves[1], halves[0]).astype(BF)
 
 
-def arrange(low, a, b, c, d):
-    turned = swap_halves(b)
-    return [jnp.where(low, a, turned), swap_halves(d), jnp.where(low, turned, a), c]
-
-
-def middle_kernel(got, keep, half, send):
+def middle_kernel(got, keep, half, send, columns):
     low = half_mask((32, 128))
-    columns = []
-    for xl in range(2):
-        total = [jnp.zeros((32, 128), F32)] * 4
-        for yh in range(4):
-            blocks = [got[core * 16 + xl * 8 + yh * 2 + yl].astype(F32) for core in range(2) for yl in range(2)]
-            for p, tile in enumerate(arrange(low, *blocks)):
-                total[(yh + p) & 3] += tile
-        columns += total
+    for zl in range(2):
+
+        @pl.when(lax.axis_index("zl") == zl)
+        def _():
+            for xl in range(2):
+                even = [None] * 4
+                odd = [None] * 4
+                for y in range(8):
+                    for core in range(2):
+                        block = got[core * 16 + xl * 8 + y].astype(F32)
+                        ends = [((y + step) & 7) >> 1 for step in OFFSETS[zl][core]]
+                        if y & 1:
+                            block = swap_halves(block)
+                            ends.reverse()
+                        for sums, p in zip((even, odd), ends):
+                            sums[p] = block if sums[p] is None else sums[p] + block
+                for p in range(4):
+                    at = (xl * 4 + p) * 32
+                    columns[at : at + 32, :] = jnp.where(low, even[p], odd[p])
+
     r = lax.broadcasted_iota(jnp.int32, (256, 256), 0)
     wanted = (((r >> 1) & 7) << 5) | ((r >> 4) << 1) | (r & 1)
     order = jnp.where(lax.broadcasted_iota(jnp.int32, (256, 256), 1) == wanted, 1.0, 0.0).astype(BF)
     cross = jnp.dot(
-        order, jnp.concatenate(columns, axis=0).astype(BF), preferred_element_type=F32
+        order, columns[...].astype(BF), preferred_element_type=F32
     ).astype(BF)
     both = keep[...] + half[...].astype(F32)
     line = both[64:65] + both[65:66]
@@ -210,38 +213,50 @@
     codes_t[:, 128:] = jnp.where(lax.axis_index("core") == 0, b, a)
 
 
-def second_kernel(early, got_core, give_x, give_y, give_xy):
-    xl, yl = lax.axis_index("xl"), lax.axis_index("yl")
+def second_kernel(early, got_core, give_x, give_z, give_xz):
+    zl, xl = lax.axis_index("zl"), lax.axis_index("xl")
     for n, block in enumerate((early, got_core)):
-        give_x[n] = block[(1 - xl) * 2 + yl]
-        give_y[n] = block[xl * 2 + 1 - yl]
-        give_xy[n] = block[(1 - xl) * 2 + 1 - yl]
-
-
-def home_kernel(early, got_core, got_x, got_y, got_xy, recon):
-    core, xl = lax.axis_index("core"), lax.axis_index("xl")
-    yh, yl = lax.axis_index("yh"), lax.axis_index("yl")
+        give_x[n] = block[zl * 2 + 1 - xl]
+        give_z[n] = block[(1 - zl) * 2 + xl]
+        give_xz[n] = block[(1 - zl) * 2 + 1 - xl]
+
+
+def home_kernel(early, got_core, got_x, got_z, got_xz, recon):
+    zl, core = lax.axis_index("zl"), lax.axis_index("core")
+    xl, y = lax.axis_index("xl"), lax.axis_index("y")
     low = half_mask((128, 128))
-    own = [early[xl * 2 + yl], got_core[xl * 2 + yl]]
-    for across, (same, far) in enumerate(((own, got_y), (got_x, got_xy))):
+    is_odd = (y & 1) == 1
+    own = [early[zl * 2 + xl], got_core[zl * 2 + xl]]
+    for across, (same, far) in enumerate(((own, got_z), (got_x, got_xz))):
         blocks = []
-        for c in range(2):
-            near_c = jnp.where(core == c, same[0], same[1])
-            far_c = jnp.where(core == c, far[0], far[1])
-            for y in range(2):
-                blocks.append(jnp.where(yl == y, near_c, far_c).astype(F32))
+        for z in range(2):
+            for c in range(2):
+                near_c = jnp.where(core == c, same[0], same[1])
+                far_c = jnp.where(core == c, far[0], far[1])
+                block = jnp.where(zl == z, near_c, far_c).astype(F32)
+                blocks.append(jnp.where(is_odd, swap_halves(block), block))
         side = (1 - xl) if across else xl
-        for p, tile in enumerate(arrange(low, *blocks)):
-            at = pl.multiple_of((side * 4 + ((yh + p) & 3)) * 128, 128)
-            recon[:, pl.ds(at, 128)] = tile.astype(BF)
-
-
-def call(kernel, name, outs, args, flops=0, moved=0):
+        for p in range(4):
+            ends = []
+            for i in range(2):
+                found = []
+                for parity in range(2):
+                    for n in range(4):
+                        step = OFFSETS[n >> 1][n & 1][i ^ parity]
+                        if ((parity + step) & 7) >> 1 == p:
+                            found.append(blocks[n])
+                ends.append(found[0] if found[0] is found[1] else jnp.where(is_odd, found[1], found[0]))
+            at = pl.multiple_of((side * 4 + (((y >> 1) + p) & 3)) * 128, 128)
+            recon[:, pl.ds(at, 128)] = jnp.where(low, *ends).astype(BF)
+
+
+def call(kernel, name, outs, args, flops=0, moved=0, scratch=()):
     return pl.pallas_call(
         kernel,
         out_shape=tuple(jax.ShapeDtypeStruct(*o) for o in outs),
         in_specs=[VMEM] * len(args),
         out_specs=(VMEM,) * len(outs),
+        scratch_shapes=list(scratch),
         compiler_params=pltpu.CompilerParams(vmem_limit_bytes=40 * 1024 * 1024),
         cost_estimate=pl.CostEstimate(flops=flops, bytes_accessed=moved, transcendentals=0),
         name=name,
@@ -256,21 +271,22 @@
             jax.ShapeDtypeStruct((4, 128, 1024), BF),
         ),
         in_specs=[VMEM, VMEM, VMEM],
-        out_specs=(VMEM, ANY),
-        scratch_shapes=[pltpu.SemaphoreType.DMA((4,))],
+        out_specs=(VMEM, VMEM),
         compiler_params=pltpu.CompilerParams(vmem_limit_bytes=60 * 1024 * 1024),
         name="open",
     )(samples, rotation.T, codebook[0].T)
-    packs = []
-    for steps in ((3, 2), (None, 1)):
-        pairs = [
-            (c * 8 + ((y + step if y & 1 else y - step) & 7), c * 8 + y)
-            for c, step in enumerate(steps)
-            for y in range(8)
-            if step is not None
-        ]
-        packs.append(lax.ppermute(pack, ("core", "yh", "yl"), pairs))
-    mine = lax.all_to_all(copies, ("xl", "yl"), 0, 0, tiled=True).reshape(512, 1024)
+    packs, lines = [], []
+    for i in range(2):
+        lines.append(
+            [
+                (at + y, at + ((y + OFFSETS[at >> 4][(at >> 3) & 1][i]) & 7))
+                for at in range(0, 32, 8)
+                for y in range(8)
+            ]
+        )
+        pairs = [(b, a) for a, b in lines[i] if i == 1 or a >= 8]
+        packs.append(lax.ppermute(pack, LINE, pairs))
+    mine = lax.all_to_all(copies, ("zl", "xl"), 0, 0, tiled=True).reshape(512, 1024)
     tools = call(
         prepare_kernel,
         "prepare",
@@ -295,12 +311,7 @@
         (other, *tools, sums, cross),
         moved=8_000_000,
     )
-    moved = []
-    for i in range(2):
-        pairs = [
-            (c * 8 + y, c * 8 + (((y & 6) + PLACES[c][y & 1][i]) & 7)) for c in range(2) for y in range(8)
-        ]
-        moved.append(lax.ppermute(totals[i], ("core", "yh", "yl"), pairs))
+    moved = [lax.ppermute(totals[i], LINE, lines[i]) for i in range(2)]
     got_core = lax.ppermute(late, "core", swap)
     keep, give = call(
         half_kernel, "half", [((80, 128), F32), ((80, 128), BF)], tuple(moved), flops=2 * 10**9
@@ -308,13 +319,19 @@
     half = lax.ppermute(give, "core", swap)
     got = lax.all_to_all(send, NEAR, 0, 0, tiled=True)
     got, half, got_core = lax.optimization_barrier((got, half, got_core))
-    (send,) = call(middle_kernel, "middle", [((16, 88, 128), BF)], (got, keep, half))
+    (send,) = call(
+        middle_kernel,
+        "middle",
+        [((16, 88, 128), BF)],
+        (got, keep, half),
+        scratch=[pltpu.VMEM((256, 128), F32)],
+    )
     gives = call(second_kernel, "second", [pair, pair, pair], (early, got_core))
     got_x = lax.ppermute(gives[0], "xl", swap)
-    got_y = lax.ppermute(gives[1], "yl", swap)
-    got_xy = lax.ppermute(gives[2], ("xl", "yl"), [(0, 3), (1, 2), (2, 1), (3, 0)])
+    got_z = lax.ppermute(gives[1], "zl", swap)
+    got_xz = lax.ppermute(gives[2], ("zl", "xl"), [(0, 3), (1, 2), (2, 1), (3, 0)])
     got = lax.all_to_all(send, FAR, 0, 0, tiled=True)
-    got, got_x, got_y, got_xy = lax.optimization_barrier((got, got_x, got_y, got_xy))
+    got, got_x, got_z, got_xz = lax.optimization_barrier((got, got_x, got_z, got_xz))
     cross, fresh = call(
         finish_kernel,
         "finish",
@@ -323,7 +340,7 @@
     )
     fresh_other = lax.ppermute(fresh, "core", swap)
     (recon,) = call(
-        home_kernel, "home", [((128, 1024), BF)], (early, got_core, got_x, got_y, got_xy)
+        home_kernel, "home", [((128, 1024), BF)], (early, got_core, got_x, got_z, got_xz)
     )
     fresh_other, recon = lax.optimization_barrier((fresh_other, recon))
     (new_codes,) = call(codes_kernel, "codes", [((64, 256), F32)], (fresh, fresh_other))

time: 91.4 us -> 93.8 us (1.026)
  starting transfers between devices: 57.4 us -> 63.9 us
  waiting for transfers between devices: 21.1 us -> 17.6 us
    ppermute x6, waiting for transfers between devices: 18.1 us -> 13.8 us  [the longest x2 7.63 us: per_device(): packs.append(lax.ppermute(pack, LINE, pairs))]
    all_to_all x1, starting transfers between devices: 12.6 us -> 15.4 us  [per_device(): got = lax.all_to_all(send, FAR, 0, 0, tiled=True)]
    ppermute x6, starting transfers between devices: 22.3 us -> 24.8 us  [the longest x2 9.52 us: per_device(): packs.append(lax.ppermute(pack, LINE, pairs))]
    ppermute x1, starting transfers between devices: 3.57 us -> 4.52 us  [per_device(): fresh_other = lax.ppermute(fresh, 'core', swap)]
  transfers between devices with their start and end apart: 14 -> 14, of which waited for: 7 -> 8; matrix products, arithmetic and copies ran while one was open for 0% -> 0% of each run, Pallas kernels for 3% -> 3%
where the time goes in v11:
time: 93.8 us; the launch traced here: 93 us
  starting transfers between devices  63.9 us (68%)
  waiting for transfers between devices  17.6 us (19%)
  Pallas kernels  10.7 us (11%)
    all_to_all x1, starting transfers between devices, per_device(): got = lax.all_to_all(send, FAR, 0, 0, tiled=True)  15.4 us
    ppermute x2, starting transfers between devices, per_device(): packs.append(lax.ppermute(pack, LINE, pairs))  9.52 us
    ppermute x2, starting transfers between devices, per_device(): moved = [lax.ppermute(totals[i], LINE, lines[i]) for i in range(2)]  9.39 us
    pallas_call x9, Pallas kernels, call(): pl.pallas_call(kernel, out_shape=tuple((jax.ShapeDtypeStruct(*o) for o in...  8.54 us
    ppermute x2, waiting for transfers between devices, per_device(): packs.append(lax.ppermute(pack, LINE, pairs))  7.63 us
    all_to_all x1, starting transfers between devices, per_device(): got = lax.all_to_all(send, NEAR, 0, 0, tiled=True)  5.69 us
    all_to_all x1, starting transfers between devices, per_device(): lax.all_to_all(copies, ('zl', 'xl'), 0, 0, tiled=True).reshape(512, 1024)  5.25 us
    ppermute x1, starting transfers between devices, per_device(): fresh_other = lax.ppermute(fresh, 'core', swap)  4.52 us
  transfers between devices with their start and end apart: 14, of which 8 were waited for; matrix products, arithmetic and copies ran while one was open for 0% of the time, Pallas kernels for 3%

profile of v11, /device:TPU:1, one launch (start us, length us, event | category | flops | bytes accessed | tf_op | source)
XLA Modules:
  0.0 93.0 jit_solution(3502466499618793705)
XLA Ops:
  0.6 2.1 %open.1 = (bf16[64,1408]{1,0:T(8,128)(2,1)}, bf16[4,128,1024]{2,1,0:T(8,128)(2,1)}) custom-call(bf16[128,1024]{1,0:T(8,128)(2,1)} %samples.1, bf16[64,1024]{1,0:T(8,128)(2,1)} %bitcast.12, f32[64,256]{1,0:T(8,128)} %bitcast.10), custom_call_target="tpu_custom_call" | custom-call | tf_op jit(solution)/shard_map/open/pallas_call | solution.py:267
  2.7 0.0 copy-start.1
  2.7 5.2 %all-to-all-start = ((bf16[4,128,1024]{2,1,0:T(8,128)(2,1)}), bf16[4,128,1024]{2,1,0:T(8,128)(2,1)S(1)}, u32[]{:S(2)}, u32[]{:S(2)}) async-start(bf16[4,128,1024]{2,1,0:T(8,128)(2,1)} %get-tuple-element.35), calls=%async_computation | async-start | bytes 2097152 | tf_op jit(solution)/shard_map/all_to_all | solution.py:289
  8.0 0.0 copy-done.1
  8.0 5.1 %collective-permute-start.1 = (bf16[64,1408]{1,0:T(8,128)(2,1)S(1)}, bf16[64,1408]{1,0:T(8,128)(2,1)S(1)}, u32[]{:S(2)}, u32[]{:S(2)}) collective-permute-start(bf16[64,1408]{1,0:T(8,128)(2,1)S(1)} %copy-done.1), channel_id=1, source_target_pairs={{7,0},{0,1},{1,2},{2,3},{3,4},{4,5},{5,6},{6,7},{17,16},{18,17},{1... | collective-permute-start | bytes 540680 | tf_op jit(solution)/shard_map/ppermute | solution.py:288
  13.1 4.4 %collective-permute-start = (bf16[64,1408]{1,0:T(8,128)(2,1)S(1)}, bf16[64,1408]{1,0:T(8,128)(2,1)S(1)}, u32[]{:S(2)}, u32[]{:S(2)}) collective-permute-start(bf16[64,1408]{1,0:T(8,128)(2,1)S(1)} %copy-done.1), channel_id=1, source_target_pairs={{20,16},{21,17},{22,18},{23,19},{16,20},{17,21},{18,22},{19,23},{6... | collective-permute-start | bytes 540680 | tf_op jit(solution)/shard_map/ppermute | solution.py:288
  17.5 0.0 collective-permute-done.1.second
  17.5 7.6 %collective-permute-done.first = bf16[64,1408]{1,0:T(8,128)(2,1)S(1)} collective-permute-done((bf16[64,1408]{1,0:T(8,128)(2,1)S(1)}, bf16[64,1408]{1,0:T(8,128)(2,1)S(1)}, u32[]{:S(2)}, u32[]{:S(2)}) %collective-permute-start) | collective-permute-done | bytes 180256 | tf_op jit(solution)/shard_map/ppermute | solution.py:288
  25.2 0.1 prepare.1
  25.3 0.0 all-to-all-done
  25.3 1.9 %collective-permute-start.2 = (bf16[512,1024]{1,0:T(8,128)(2,1)S(1)}, bf16[512,1024]{1,0:T(8,128)(2,1)S(1)}, u32[]{:S(2)}, u32[]{:S(2)}) collective-permute-start(bf16[512,1024]{1,0:T(8,128)(2,1)S(1)} %bitcast.8), channel_id=1, source_target_pairs={{0,16},{16,0},{1,17},{17,1},{2,18},{18,2},{3,19},{19,3},{4,20},{20... | collective-permute-start | bytes 3145736 | tf_op jit(solution)/shard_map/ppermute | solution.py:298
  27.2 1.8 %early.1 = (f32[512,256]{1,0:T(8,128)S(1)}, f32[128,1024]{1,0:T(8,128)S(1)}, bf16[4,128,128]{2,1,0:T(8,128)(2,1)S(1)}) custom-call(bf16[512,1024]{1,0:T(8,128)(2,1)S(1)} %bitcast.9, bf16[128,1024]{1,0:T(8,128)(2,1)S(1)} %get-tuple-element.41.turn, bf16[128,512]{1,0:T(8,128)(2,1)S(1)} %get-tuple-element.42.codes_t, bf16[512,256]{1,0:T(8,128)(2,1)S(1)} %get-tuple-element.43.left), custom_call_target="tpu_custom_call" | custom-call | bytes 8000000 | tf_op jit(solution)/shard_map/early/pallas_call | solution.py:254
  29.1 0.8 collective-permute-done.2.samples
  29.9 3.3 %late.1 = (bf16[32,32,128]{2,1,0:T(8,128)(2,1)}, bf16[4,128,128]{2,1,0:T(8,128)(2,1)S(1)}, bf16[144,128]{1,0:T(8,128)(2,1)S(1)}, bf16[144,128]{1,0:T(8,128)(2,1)S(1)}) custom-call(bf16[512,1024]{1,0:T(8,128)(2,1)S(1)} %collective-permute-done.2.samples, bf16[128,1024]{1,0:T(8,128)(2,1)S(1)} %get-tuple-element.41.turn, ...), custom_call_target="tpu_custom_call" | custom-call | bytes 8000000 | tf_op jit(solution)/shard_map/late/pallas_call | solution.py:254
  33.2 5.7 %all-to-all-start.1 = ((bf16[32,32,128]{2,1,0:T(8,128)(2,1)}), bf16[32,32,128]{2,1,0:T(8,128)(2,1)S(1)}, u32[]{:S(2)}, u32[]{:S(2)}) async-start(bf16[32,32,128]{2,1,0:T(8,128)(2,1)} %get-tuple-element.46), calls=%async_computation.1 | async-start | bytes 524288 | tf_op jit(solution)/shard_map/all_to_all | solution.py:320
  38.8 7.2 %collective-permute-start.3 = (bf16[144,128]{1,0:T(8,128)(2,1)S(1)}, bf16[144,128]{1,0:T(8,128)(2,1)S(1)}, u32[]{:S(2)}, u32[]{:S(2)}) collective-permute-start(bf16[144,128]{1,0:T(8,128)(2,1)S(1)} %get-tuple-element.47), channel_id=1, source_target_pairs={{0,0},{1,1},{2,2},{3,3},{4,4},{5,5},{6,6},{7,7},{16,20},{17,21},{1... | collective-permute-start | bytes 110600 | tf_op jit(solution)/shard_map/ppermute | solution.py:314
  46.0 2.2 %collective-permute-start.4 = (bf16[144,128]{1,0:T(8,128)(2,1)S(1)}, bf16[144,128]{1,0:T(8,128)(2,1)S(1)}, u32[]{:S(2)}, u32[]{:S(2)}) collective-permute-start(bf16[144,128]{1,0:T(8,128)(2,1)S(1)} %get-tuple-element.48), channel_id=1, source_target_pairs={{0,7},{1,0},{2,1},{3,2},{4,3},{5,4},{6,5},{7,6},{16,17},{17,18},{1... | collective-permute-start | bytes 110600 | tf_op jit(solution)/shard_map/ppermute | solution.py:314
  48.3 1.9 %collective-permute-start.6 = (bf16[4,128,128]{2,1,0:T(8,128)(2,1)S(1)}, bf16[4,128,128]{2,1,0:T(8,128)(2,1)S(1)}, u32[]{:S(2)}, u32[]{:S(2)}) collective-permute-start(bf16[4,128,128]{2,1,0:T(8,128)(2,1)S(1)} %get-tuple-element.50), channel_id=1, source_target_pairs={{0,16},{16,0},{1,17},{17,1},{2,18},{18,2},{3,19},{19,3},{4,20},{20... | collective-permute-start | bytes 393224 | tf_op jit(solution)/shard_map/ppermute | solution.py:315
  50.2 1.4 %collective-permute-done.3.first = bf16[144,128]{1,0:T(8,128)(2,1)S(1)} collective-permute-done((bf16[144,128]{1,0:T(8,128)(2,1)S(1)}, bf16[144,128]{1,0:T(8,128)(2,1)S(1)}, u32[]{:S(2)}, u32[]{:S(2)}) %collective-permute-start.3) | collective-permute-done | bytes 36896 | tf_op jit(solution)/shard_map/ppermute | solution.py:314
  51.6 0.4 collective-permute-done.4.second
  52.0 1.9 %collective-permute-start.5 = (bf16[80,128]{1,0:T(8,128)(2,1)S(1)}, bf16[80,128]{1,0:T(8,128)(2,1)S(1)}, u32[]{:S(2)}, u32[]{:S(2)}) collective-permute-start(bf16[80,128]{1,0:T(8,128)(2,1)S(1)} %get-tuple-element.49), channel_id=1, source_target_pairs={{0,16},{16,0},{1,17},{17,1},{2,18},{18,2},{3,19},{19,3},{4,20},{20... | collective-permute-start | bytes 61448 | tf_op jit(solution)/shard_map/ppermute | solution.py:319
  54.0 1.2 %collective-permute-done.5.half = bf16[80,128]{1,0:T(8,128)(2,1)S(1)} collective-permute-done((bf16[80,128]{1,0:T(8,128)(2,1)S(1)}, bf16[80,128]{1,0:T(8,128)(2,1)S(1)}, u32[]{:S(2)}, u32[]{:S(2)}) %collective-permute-start.5) | collective-permute-done | bytes 20512 | tf_op jit(solution)/shard_map/ppermute | solution.py:319
  55.1 0.0 collective-permute-done.6.got_core
  55.1 0.0 all-to-all-done.1.got
  55.1 1.1 %middle.1 = bf16[16,88,128]{2,1,0:T(8,128)(2,1)} custom-call(bf16[32,32,128]{2,1,0:T(8,128)(2,1)S(1)} %all-to-all-done.1.got, f32[80,128]{1,0:T(8,128)S(1)} %get-tuple-element.52.keep, bf16[80,128]{1,0:T(8,128)(2,1)S(1)} %collective-permute-done.5.half), custom_call_target="tpu_custom_call" | custom-call | tf_op jit(solution)/shard_map/middle/pallas_call | solution.py:254
  56.2 15.4 %all-to-all-start.2 = ((bf16[16,88,128]{2,1,0:T(8,128)(2,1)}), bf16[16,88,128]{2,1,0:T(8,128)(2,1)S(1)}, u32[]{:S(2)}, u32[]{:S(2)}) async-start(bf16[16,88,128]{2,1,0:T(8,128)(2,1)} %middle.1), calls=%async_computation.2 | async-start | bytes 720896 | tf_op jit(solution)/shard_map/all_to_all | solution.py:333
  71.6 0.0 copy-start
  71.7 2.5 %collective-permute-start.7 = (bf16[2,128,128]{2,1,0:T(8,128)(2,1)S(1)}, bf16[2,128,128]{2,1,0:T(8,128)(2,1)S(1)}, u32[]{:S(2)}, u32[]{:S(2)}) collective-permute-start(bf16[2,128,128]{2,1,0:T(8,128)(2,1)S(1)} %get-tuple-element.56), channel_id=1, source_target_pairs={{0,8},{8,0},{1,9},{9,1},{2,10},{10,2},{3,11},{11,3},{4,12},{12,4},... | collective-permute-start | bytes 196616 | tf_op jit(solution)/shard_map/ppermute | solution.py:330
  74.2 3.3 %collective-permute-start.8 = (bf16[2,128,128]{2,1,0:T(8,128)(2,1)S(1)}, bf16[2,128,128]{2,1,0:T(8,128)(2,1)S(1)}, u32[]{:S(2)}, u32[]{:S(2)}) collective-permute-start(bf16[2,128,128]{2,1,0:T(8,128)(2,1)S(1)} %get-tuple-element.57), channel_id=1, source_target_pairs={{0,64},{64,0},{1,65},{65,1},{2,66},{66,2},{3,67},{67,3},{4,68},{68... | collective-permute-start | bytes 196616 | tf_op jit(solution)/shard_map/ppermute | solution.py:331
  77.5 2.6 %collective-permute-start.9 = (bf16[2,128,128]{2,1,0:T(8,128)(2,1)S(1)}, bf16[2,128,128]{2,1,0:T(8,128)(2,1)S(1)}, u32[]{:S(2)}, u32[]{:S(2)}) collective-permute-start(bf16[2,128,128]{2,1,0:T(8,128)(2,1)S(1)} %get-tuple-element.58), channel_id=1, source_target_pairs={{0,72},{8,64},{64,8},{72,0},{1,73},{9,65},{65,9},{73,1},{2,74},{10... | collective-permute-start | bytes 196616 | tf_op jit(solution)/shard_map/ppermute | solution.py:332
  80.1 0.0 collective-permute-done.7.got_x
  80.1 2.6 %collective-permute-done.8.got_z = bf16[2,128,128]{2,1,0:T(8,128)(2,1)S(1)} collective-permute-done((bf16[2,128,128]{2,1,0:T(8,128)(2,1)S(1)}, bf16[2,128,128]{2,1,0:T(8,128)(2,1)S(1)}, u32[]{:S(2)}, u32[]{:S(2)}) %collective-permute-start.8) | collective-permute-done | bytes 65568 | tf_op jit(solution)/shard_map/ppermute | solution.py:331
  82.7 1.7 %collective-permute-done.9.got_xz = bf16[2,128,128]{2,1,0:T(8,128)(2,1)S(1)} collective-permute-done((bf16[2,128,128]{2,1,0:T(8,128)(2,1)S(1)}, bf16[2,128,128]{2,1,0:T(8,128)(2,1)S(1)}, u32[]{:S(2)}, u32[]{:S(2)}) %collective-permute-start.9) | collective-permute-done | bytes 65568 | tf_op jit(solution)/shard_map/ppermute | solution.py:332
  84.4 1.8 %all-to-all-done.2.got = bf16[16,88,128]{2,1,0:T(8,128)(2,1)S(1)} async-done(((bf16[16,88,128]{2,1,0:T(8,128)(2,1)}), bf16[16,88,128]{2,1,0:T(8,128)(2,1)S(1)}, u32[]{:S(2)}, u32[]{:S(2)}) %all-to-all-start.2) | async-done | bytes 360480 | tf_op jit(solution)/shard_map/all_to_all | solution.py:333
  86.2 0.0 copy-done
  86.2 0.7 finish.1
  86.9 4.5 %collective-permute-start.10 = (f32[64,128]{1,0:T(8,128)S(1)}, f32[64,128]{1,0:T(8,128)S(1)}, u32[]{:S(2)}, u32[]{:S(2)}) collective-permute-start(f32[64,128]{1,0:T(8,128)S(1)} %get-tuple-element.60.mine), channel_id=1, source_target_pairs={{0,16},{16,0},{1,17},{17,1},{2,18},{18,2},{3,19},{19,3},{4,20},{20... | collective-permute-start | bytes 98312 | tf_op jit(solution)/shard_map/ppermute | solution.py:341
  91.4 0.9 home.1
  92.3 0.0 collective-permute-done.10.other
  92.3 0.6 codes.1
  (2 shorter events, 0.0 us)
Async XLA Ops:
  2.7 5.3 %copy-start.1 = (bf16[64,1408]{1,0:T(8,128)(2,1)S(1)}, bf16[64,1408]{1,0:T(8,128)(2,1)}, u32[]{:S(2)}) copy-start(bf16[64,1408]{1,0:T(8,128)(2,1)} %get-tuple-element.36.pack) | copy-start | bytes 540676
  2.7 22.6 %all-to-all-start = ((bf16[4,128,1024]{2,1,0:T(8,128)(2,1)}), bf16[4,128,1024]{2,1,0:T(8,128)(2,1)S(1)}, u32[]{:S(2)}, u32[]{:S(2)}) async-start(bf16[4,128,1024]{2,1,0:T(8,128)(2,1)} %get-tuple-element.35), calls=%async_computation | async-start | bytes 2097152 | tf_op jit(solution)/shard_map/all_to_all | solution.py:289
  8.0 9.5 %collective-permute-start.1 = (bf16[64,1408]{1,0:T(8,128)(2,1)S(1)}, bf16[64,1408]{1,0:T(8,128)(2,1)S(1)}, u32[]{:S(2)}, u32[]{:S(2)}) collective-permute-start(bf16[64,1408]{1,0:T(8,128)(2,1)S(1)} %copy-done.1), channel_id=1, source_target_pairs={{7,0},{0,1},{1,2},{2,3},{3,4},{4,5},{5,6},{6,7},{17,16},{18,17},{1... | collective-permute-start | bytes 540680 | tf_op jit(solution)/shard_map/ppermute | solution.py:288
  13.1 12.1 %collective-permute-start = (bf16[64,1408]{1,0:T(8,128)(2,1)S(1)}, bf16[64,1408]{1,0:T(8,128)(2,1)S(1)}, u32[]{:S(2)}, u32[]{:S(2)}) collective-permute-start(bf16[64,1408]{1,0:T(8,128)(2,1)S(1)} %copy-done.1), channel_id=1, source_target_pairs={{20,16},{21,17},{22,18},{23,19},{16,20},{17,21},{18,22},{19,23},{6... | collective-permute-start | bytes 540680 | tf_op jit(solution)/shard_map/ppermute | solution.py:288
  25.3 4.6 %collective-permute-start.2 = (bf16[512,1024]{1,0:T(8,128)(2,1)S(1)}, bf16[512,1024]{1,0:T(8,128)(2,1)S(1)}, u32[]{:S(2)}, u32[]{:S(2)}) collective-permute-start(bf16[512,1024]{1,0:T(8,128)(2,1)S(1)} %bitcast.8), channel_id=1, source_target_pairs={{0,16},{16,0},{1,17},{17,1},{2,18},{18,2},{3,19},{19,3},{4,20},{20... | collective-permute-start | bytes 3145736 | tf_op jit(solution)/shard_map/ppermute | solution.py:298
  33.2 22.0 %all-to-all-start.1 = ((bf16[32,32,128]{2,1,0:T(8,128)(2,1)}), bf16[32,32,128]{2,1,0:T(8,128)(2,1)S(1)}, u32[]{:S(2)}, u32[]{:S(2)}) async-start(bf16[32,32,128]{2,1,0:T(8,128)(2,1)} %get-tuple-element.46), calls=%async_computation.1 | async-start | bytes 524288 | tf_op jit(solution)/shard_map/all_to_all | solution.py:320
  38.8 12.8 %collective-permute-start.3 = (bf16[144,128]{1,0:T(8,128)(2,1)S(1)}, bf16[144,128]{1,0:T(8,128)(2,1)S(1)}, u32[]{:S(2)}, u32[]{:S(2)}) collective-permute-start(bf16[144,128]{1,0:T(8,128)(2,1)S(1)} %get-tuple-element.47), channel_id=1, source_target_pairs={{0,0},{1,1},{2,2},{3,3},{4,4},{5,5},{6,6},{7,7},{16,20},{17,21},{1... | collective-permute-start | bytes 110600 | tf_op jit(solution)/shard_map/ppermute | solution.py:314
  46.0 6.0 %collective-permute-start.4 = (bf16[144,128]{1,0:T(8,128)(2,1)S(1)}, bf16[144,128]{1,0:T(8,128)(2,1)S(1)}, u32[]{:S(2)}, u32[]{:S(2)}) collective-permute-start(bf16[144,128]{1,0:T(8,128)(2,1)S(1)} %get-tuple-element.48), channel_id=1, source_target_pairs={{0,7},{1,0},{2,1},{3,2},{4,3},{5,4},{6,5},{7,6},{16,17},{17,18},{1... | collective-permute-start | bytes 110600 | tf_op jit(solution)/shard_map/ppermute | solution.py:314
  48.3 6.9 %collective-permute-start.6 = (bf16[4,128,128]{2,1,0:T(8,128)(2,1)S(1)}, bf16[4,128,128]{2,1,0:T(8,128)(2,1)S(1)}, u32[]{:S(2)}, u32[]{:S(2)}) collective-permute-start(bf16[4,128,128]{2,1,0:T(8,128)(2,1)S(1)} %get-tuple-element.50), channel_id=1, source_target_pairs={{0,16},{16,0},{1,17},{17,1},{2,18},{18,2},{3,19},{19,3},{4,20},{20... | collective-permute-start | bytes 393224 | tf_op jit(solution)/shard_map/ppermute | solution.py:315
  52.0 3.1 %collective-permute-start.5 = (bf16[80,128]{1,0:T(8,128)(2,1)S(1)}, bf16[80,128]{1,0:T(8,128)(2,1)S(1)}, u32[]{:S(2)}, u32[]{:S(2)}) collective-permute-start(bf16[80,128]{1,0:T(8,128)(2,1)S(1)} %get-tuple-element.49), channel_id=1, source_target_pairs={{0,16},{16,0},{1,17},{17,1},{2,18},{18,2},{3,19},{19,3},{4,20},{20... | collective-permute-start | bytes 61448 | tf_op jit(solution)/shard_map/ppermute | solution.py:319
  56.2 30.0 %all-to-all-start.2 = ((bf16[16,88,128]{2,1,0:T(8,128)(2,1)}), bf16[16,88,128]{2,1,0:T(8,128)(2,1)S(1)}, u32[]{:S(2)}, u32[]{:S(2)}) async-start(bf16[16,88,128]{2,1,0:T(8,128)(2,1)} %middle.1), calls=%async_computation.2 | async-start | bytes 720896 | tf_op jit(solution)/shard_map/all_to_all | solution.py:333
  71.6 14.6 %copy-start = (f32[1,256,64]{1,2,0:T(8,128)S(1)}, f32[1,256,64]{1,2,0:T(8,128)}, u32[]{:S(2)}) copy-start(f32[1,256,64]{1,2,0:T(8,128)} %param.5) | copy-start | bytes 196612
  71.7 8.4 %collective-permute-start.7 = (bf16[2,128,128]{2,1,0:T(8,128)(2,1)S(1)}, bf16[2,128,128]{2,1,0:T(8,128)(2,1)S(1)}, u32[]{:S(2)}, u32[]{:S(2)}) collective-permute-start(bf16[2,128,128]{2,1,0:T(8,128)(2,1)S(1)} %get-tuple-element.56), channel_id=1, source_target_pairs={{0,8},{8,0},{1,9},{9,1},{2,10},{10,2},{3,11},{11,3},{4,12},{12,4},... | collective-permute-start | bytes 196616 | tf_op jit(solution)/shard_map/ppermute | solution.py:330
  74.2 8.5 %collective-permute-start.8 = (bf16[2,128,128]{2,1,0:T(8,128)(2,1)S(1)}, bf16[2,128,128]{2,1,0:T(8,128)(2,1)S(1)}, u32[]{:S(2)}, u32[]{:S(2)}) collective-permute-start(bf16[2,128,128]{2,1,0:T(8,128)(2,1)S(1)} %get-tuple-element.57), channel_id=1, source_target_pairs={{0,64},{64,0},{1,65},{65,1},{2,66},{66,2},{3,67},{67,3},{4,68},{68... | collective-permute-start | bytes 196616 | tf_op jit(solution)/shard_map/ppermute | solution.py:331
  77.5 6.9 %collective-permute-start.9 = (bf16[2,128,128]{2,1,0:T(8,128)(2,1)S(1)}, bf16[2,128,128]{2,1,0:T(8,128)(2,1)S(1)}, u32[]{:S(2)}, u32[]{:S(2)}) collective-permute-start(bf16[2,128,128]{2,1,0:T(8,128)(2,1)S(1)} %get-tuple-element.58), channel_id=1, source_target_pairs={{0,72},{8,64},{64,8},{72,0},{1,73},{9,65},{65,9},{73,1},{2,74},{10... | collective-permute-start | bytes 196616 | tf_op jit(solution)/shard_map/ppermute | solution.py:332
  86.9 5.4 %collective-permute-start.10 = (f32[64,128]{1,0:T(8,128)S(1)}, f32[64,128]{1,0:T(8,128)S(1)}, u32[]{:S(2)}, u32[]{:S(2)}) collective-permute-start(f32[64,128]{1,0:T(8,128)S(1)} %get-tuple-element.60.mine), channel_id=1, source_target_pairs={{0,16},{16,0},{1,17},{17,1},{2,18},{18,2},{3,19},{19,3},{4,20},{20... | collective-permute-start | bytes 98312 | tf_op jit(solution)/shard_map/ppermute | solution.py:341

commit v12 on v10

--- a/solution.py
+++ b/solution.py
@@ -19,7 +19,6 @@
 F32 = jnp.float32
 NT = (((1,), (1,)), ((), ()))
 VMEM = pl.BlockSpec(memory_space=pltpu.VMEM)
-ANY = pl.BlockSpec(memory_space=pl.ANY)
 
 
 def half_mask(shape):
@@ -35,10 +34,9 @@
     return high, x - high
 
 
-def open_kernel(samples, turn_t, codes_t, pack, copies, done):
-    moves = [pltpu.make_async_copy(samples, copies.at[n], done.at[n]) for n in range(4)]
-    for move in moves:
-        move.start()
+def open_kernel(samples, turn_t, codes_t, pack, copies):
+    for n in range(4):
+        copies[n] = samples[...]
     codes = codes_t[...]
     square = jnp.sum(codes * codes, axis=0, keepdims=True)
     high = square.astype(BF).astype(F32)
@@ -50,8 +48,6 @@
     pack[0:16, 1280:] = squares[:, :128]
     pack[16:32, 1280:] = squares[:, 128:]
     pack[32:64, 1280:] = jnp.zeros((32, 128), BF)
-    for move in moves:
-        move.wait()
 
 
 def prepare_kernel(pack, first, second, turn, codes_t, left):
@@ -256,8 +252,7 @@
             jax.ShapeDtypeStruct((4, 128, 1024), BF),
         ),
         in_specs=[VMEM, VMEM, VMEM],
-        out_specs=(VMEM, ANY),
-        scratch_shapes=[pltpu.SemaphoreType.DMA((4,))],
+        out_specs=(VMEM, VMEM),
         compiler_params=pltpu.CompilerParams(vmem_limit_bytes=60 * 1024 * 1024),
         name="open",
     )(samples, rotation.T, codebook[0].T)

time: 91.4 us -> 90.8 us (level)
  no operation moved by 1% of the time
where the time goes in v12:
time: 90.8 us; the launch traced here: 89.9 us
  starting transfers between devices  57.4 us (63%)
  waiting for transfers between devices  21.1 us (23%)
  Pallas kernels  10.6 us (12%)
    all_to_all x1, starting transfers between devices, per_device(): got = lax.all_to_all(send, FAR, 0, 0, tiled=True)  12.6 us
    ppermute x2, waiting for transfers between devices, per_device(): packs.append(lax.ppermute(pack, ('core', 'yh', 'yl'), pairs))  12.2 us
    pallas_call x9, Pallas kernels, call(): pl.pallas_call(kernel, out_shape=tuple((jax.ShapeDtypeStruct(*o) for o in...  8.48 us
    ppermute x2, starting transfers between devices, per_device(): packs.append(lax.ppermute(pack, ('core', 'yh', 'yl'), pairs))  8.06 us
    ppermute x2, starting transfers between devices, per_device(): moved.append(lax.ppermute(totals[i], ('core', 'yh', 'yl'), pairs))  7.59 us
    all_to_all x1, starting transfers between devices, per_device(): got = lax.all_to_all(send, NEAR, 0, 0, tiled=True)  5.79 us
    all_to_all x1, starting transfers between devices, per_device(): lax.all_to_all(copies, ('xl', 'yl'), 0, 0, tiled=True).reshape(512, 1024)  4.45 us
    ppermute x1, starting transfers between devices, per_device(): got_y = lax.ppermute(gives[1], 'yl', swap)  4.21 us
  transfers between devices with their start and end apart: 14, of which 7 were waited for; matrix products, arithmetic and copies ran while one was open for 0% of the time, Pallas kernels for 3%

profile of v12, /device:TPU:1, one launch (start us, length us, event | category | flops | bytes accessed | tf_op | source)
XLA Modules:
  0.0 89.9 jit_solution(16064643693950606271)
XLA Ops:
  0.6 2.1 %open.1 = (bf16[64,1408]{1,0:T(8,128)(2,1)}, bf16[4,128,1024]{2,1,0:T(8,128)(2,1)}) custom-call(bf16[128,1024]{1,0:T(8,128)(2,1)} %samples.1, bf16[64,1024]{1,0:T(8,128)(2,1)} %bitcast.12, f32[64,256]{1,0:T(8,128)} %bitcast.10), custom_call_target="tpu_custom_call" | custom-call | tf_op jit(solution)/shard_map/open/pallas_call | solution.py:248
  2.7 0.0 copy-start.1
  2.7 4.5 %all-to-all-start = ((bf16[4,128,1024]{2,1,0:T(8,128)(2,1)}), bf16[4,128,1024]{2,1,0:T(8,128)(2,1)S(1)}, u32[]{:S(2)}, u32[]{:S(2)}) async-start(bf16[4,128,1024]{2,1,0:T(8,128)(2,1)} %get-tuple-element.35), calls=%async_computation | async-start | bytes 2097152 | tf_op jit(solution)/shard_map/all_to_all | solution.py:268
  7.2 0.0 copy-done.1
  7.2 6.1 %collective-permute-start.1 = (bf16[64,1408]{1,0:T(8,128)(2,1)S(1)}, bf16[64,1408]{1,0:T(8,128)(2,1)S(1)}, u32[]{:S(2)}, u32[]{:S(2)}) collective-permute-start(bf16[64,1408]{1,0:T(8,128)(2,1)S(1)} %copy-done.1), channel_id=1, source_target_pairs={{23,16},{18,17},{17,18},{20,19},{19,20},{22,21},{21,22},{16,23},{3... | collective-permute-start | bytes 540680 | tf_op jit(solution)/shard_map/ppermute | solution.py:267
  13.4 1.9 %collective-permute-start = (bf16[64,1408]{1,0:T(8,128)(2,1)S(1)}, bf16[64,1408]{1,0:T(8,128)(2,1)S(1)}, u32[]{:S(2)}, u32[]{:S(2)}) collective-permute-start(bf16[64,1408]{1,0:T(8,128)(2,1)S(1)} %copy-done.1), channel_id=1, source_target_pairs={{5,0},{4,1},{7,2},{6,3},{1,4},{0,5},{3,6},{2,7},{22,16},{19,17},{1... | collective-permute-start | bytes 540680 | tf_op jit(solution)/shard_map/ppermute | solution.py:267
  15.3 0.9 %collective-permute-done.1.second = bf16[64,1408]{1,0:T(8,128)(2,1)S(1)} collective-permute-done((bf16[64,1408]{1,0:T(8,128)(2,1)S(1)}, bf16[64,1408]{1,0:T(8,128)(2,1)S(1)}, u32[]{:S(2)}, u32[]{:S(2)}) %collective-permute-start.1) | collective-permute-done | bytes 180256 | tf_op jit(solution)/shard_map/ppermute | solution.py:267
  16.2 11.3 %collective-permute-done.first = bf16[64,1408]{1,0:T(8,128)(2,1)S(1)} collective-permute-done((bf16[64,1408]{1,0:T(8,128)(2,1)S(1)}, bf16[64,1408]{1,0:T(8,128)(2,1)S(1)}, u32[]{:S(2)}, u32[]{:S(2)}) %collective-permute-start) | collective-permute-done | bytes 180256 | tf_op jit(solution)/shard_map/ppermute | solution.py:267
  27.5 0.1 prepare.1
  27.6 0.0 all-to-all-done
  27.6 1.9 %collective-permute-start.2 = (bf16[512,1024]{1,0:T(8,128)(2,1)S(1)}, bf16[512,1024]{1,0:T(8,128)(2,1)S(1)}, u32[]{:S(2)}, u32[]{:S(2)}) collective-permute-start(bf16[512,1024]{1,0:T(8,128)(2,1)S(1)} %bitcast.8), channel_id=1, source_target_pairs={{0,16},{16,0},{1,17},{17,1},{2,18},{18,2},{3,19},{19,3},{4,20},{20... | collective-permute-start | bytes 3145736 | tf_op jit(solution)/shard_map/ppermute | solution.py:277
  29.6 1.8 %early.1 = (f32[512,256]{1,0:T(8,128)S(1)}, f32[128,1024]{1,0:T(8,128)S(1)}, bf16[4,128,128]{2,1,0:T(8,128)(2,1)S(1)}) custom-call(bf16[512,1024]{1,0:T(8,128)(2,1)S(1)} %bitcast.9, bf16[128,1024]{1,0:T(8,128)(2,1)S(1)} %get-tuple-element.41.turn, bf16[128,512]{1,0:T(8,128)(2,1)S(1)} %get-tuple-element.42.codes_t, bf16[512,256]{1,0:T(8,128)(2,1)S(1)} %get-tuple-element.43.left), custom_call_target="tpu_custom_call" | custom-call | bytes 8000000 | tf_op jit(solution)/shard_map/early/pallas_call | solution.py:236
  31.4 0.8 collective-permute-done.2.samples
  32.2 3.3 %late.1 = (bf16[32,32,128]{2,1,0:T(8,128)(2,1)}, bf16[4,128,128]{2,1,0:T(8,128)(2,1)S(1)}, bf16[144,128]{1,0:T(8,128)(2,1)S(1)}, bf16[144,128]{1,0:T(8,128)(2,1)S(1)}) custom-call(bf16[512,1024]{1,0:T(8,128)(2,1)S(1)} %collective-permute-done.2.samples, bf16[128,1024]{1,0:T(8,128)(2,1)S(1)} %get-tuple-element.41.turn, ...), custom_call_target="tpu_custom_call" | custom-call | bytes 8000000 | tf_op jit(solution)/shard_map/late/pallas_call | solution.py:236
  35.5 5.8 %all-to-all-start.1 = ((bf16[32,32,128]{2,1,0:T(8,128)(2,1)}), bf16[32,32,128]{2,1,0:T(8,128)(2,1)S(1)}, u32[]{:S(2)}, u32[]{:S(2)}) async-start(bf16[32,32,128]{2,1,0:T(8,128)(2,1)} %get-tuple-element.46), calls=%async_computation.1 | async-start | bytes 524288 | tf_op jit(solution)/shard_map/all_to_all | solution.py:304
  41.3 5.4 %collective-permute-start.3 = (bf16[144,128]{1,0:T(8,128)(2,1)S(1)}, bf16[144,128]{1,0:T(8,128)(2,1)S(1)}, u32[]{:S(2)}, u32[]{:S(2)}) collective-permute-start(bf16[144,128]{1,0:T(8,128)(2,1)S(1)} %get-tuple-element.47), channel_id=1, source_target_pairs={{0,0},{1,1},{2,2},{3,3},{4,4},{5,5},{6,6},{7,7},{16,22},{17,19},{1... | collective-permute-start | bytes 110600 | tf_op jit(solution)/shard_map/ppermute | solution.py:298
  46.7 2.2 %collective-permute-start.4 = (bf16[144,128]{1,0:T(8,128)(2,1)S(1)}, bf16[144,128]{1,0:T(8,128)(2,1)S(1)}, u32[]{:S(2)}, u32[]{:S(2)}) collective-permute-start(bf16[144,128]{1,0:T(8,128)(2,1)S(1)} %get-tuple-element.48), channel_id=1, source_target_pairs={{0,5},{1,4},{2,7},{3,6},{4,1},{5,0},{6,3},{7,2},{16,23},{17,18},{1... | collective-permute-start | bytes 110600 | tf_op jit(solution)/shard_map/ppermute | solution.py:298
  48.9 1.9 %collective-permute-start.6 = (bf16[4,128,128]{2,1,0:T(8,128)(2,1)S(1)}, bf16[4,128,128]{2,1,0:T(8,128)(2,1)S(1)}, u32[]{:S(2)}, u32[]{:S(2)}) collective-permute-start(bf16[4,128,128]{2,1,0:T(8,128)(2,1)S(1)} %get-tuple-element.50), channel_id=1, source_target_pairs={{0,16},{16,0},{1,17},{17,1},{2,18},{18,2},{3,19},{19,3},{4,20},{20... | collective-permute-start | bytes 393224 | tf_op jit(solution)/shard_map/ppermute | solution.py:299
  50.8 0.0 collective-permute-done.3.first
  50.8 2.1 %collective-permute-done.4.second = bf16[144,128]{1,0:T(8,128)(2,1)S(1)} collective-permute-done((bf16[144,128]{1,0:T(8,128)(2,1)S(1)}, bf16[144,128]{1,0:T(8,128)(2,1)S(1)}, u32[]{:S(2)}, u32[]{:S(2)}) %collective-permute-start.4) | collective-permute-done | bytes 36896 | tf_op jit(solution)/shard_map/ppermute | solution.py:298
  53.0 2.3 %collective-permute-start.5 = (bf16[80,128]{1,0:T(8,128)(2,1)S(1)}, bf16[80,128]{1,0:T(8,128)(2,1)S(1)}, u32[]{:S(2)}, u32[]{:S(2)}) collective-permute-start(bf16[80,128]{1,0:T(8,128)(2,1)S(1)} %get-tuple-element.49), channel_id=1, source_target_pairs={{0,16},{16,0},{1,17},{17,1},{2,18},{18,2},{3,19},{19,3},{4,20},{20... | collective-permute-start | bytes 61448 | tf_op jit(solution)/shard_map/ppermute | solution.py:303
  55.2 0.8 collective-permute-done.5.half
  56.1 0.0 collective-permute-done.6.got_core
  56.1 0.0 all-to-all-done.1.got
  56.1 1.0 %middle.1 = bf16[16,88,128]{2,1,0:T(8,128)(2,1)} custom-call(bf16[32,32,128]{2,1,0:T(8,128)(2,1)S(1)} %all-to-all-done.1.got, f32[80,128]{1,0:T(8,128)S(1)} %get-tuple-element.52.keep, bf16[80,128]{1,0:T(8,128)(2,1)S(1)} %collective-permute-done.5.half), custom_call_target="tpu_custom_call" | custom-call | tf_op jit(solution)/shard_map/middle/pallas_call | solution.py:236
  57.1 12.6 %all-to-all-start.2 = ((bf16[16,88,128]{2,1,0:T(8,128)(2,1)}), bf16[16,88,128]{2,1,0:T(8,128)(2,1)S(1)}, u32[]{:S(2)}, u32[]{:S(2)}) async-start(bf16[16,88,128]{2,1,0:T(8,128)(2,1)} %middle.1), calls=%async_computation.2 | async-start | bytes 720896 | tf_op jit(solution)/shard_map/all_to_all | solution.py:311
  69.7 0.0 copy-start
  69.7 2.6 %collective-permute-start.7 = (bf16[2,128,128]{2,1,0:T(8,128)(2,1)S(1)}, bf16[2,128,128]{2,1,0:T(8,128)(2,1)S(1)}, u32[]{:S(2)}, u32[]{:S(2)}) collective-permute-start(bf16[2,128,128]{2,1,0:T(8,128)(2,1)S(1)} %get-tuple-element.56), channel_id=1, source_target_pairs={{0,8},{8,0},{1,9},{9,1},{2,10},{10,2},{3,11},{11,3},{4,12},{12,4},... | collective-permute-start | bytes 196616 | tf_op jit(solution)/shard_map/ppermute | solution.py:308
  72.3 4.2 %collective-permute-start.8 = (bf16[2,128,128]{2,1,0:T(8,128)(2,1)S(1)}, bf16[2,128,128]{2,1,0:T(8,128)(2,1)S(1)}, u32[]{:S(2)}, u32[]{:S(2)}) collective-permute-start(bf16[2,128,128]{2,1,0:T(8,128)(2,1)S(1)} %get-tuple-element.57), channel_id=1, source_target_pairs={{0,1},{1,0},{2,3},{3,2},{4,5},{5,4},{6,7},{7,6},{8,9},{9,8},{10,11... | collective-permute-start | bytes 196616 | tf_op jit(solution)/shard_map/ppermute | solution.py:309
  76.5 2.4 %collective-permute-start.9 = (bf16[2,128,128]{2,1,0:T(8,128)(2,1)S(1)}, bf16[2,128,128]{2,1,0:T(8,128)(2,1)S(1)}, u32[]{:S(2)}, u32[]{:S(2)}) collective-permute-start(bf16[2,128,128]{2,1,0:T(8,128)(2,1)S(1)} %get-tuple-element.58), channel_id=1, source_target_pairs={{0,9},{1,8},{8,1},{9,0},{2,11},{3,10},{10,3},{11,2},{4,13},{5,12},... | collective-permute-start | bytes 196616 | tf_op jit(solution)/shard_map/ppermute | solution.py:310
  79.0 0.0 collective-permute-done.7.got_x
  79.0 0.0 collective-permute-done.8.got_y
  79.0 3.7 %collective-permute-done.9.got_xy = bf16[2,128,128]{2,1,0:T(8,128)(2,1)S(1)} collective-permute-done((bf16[2,128,128]{2,1,0:T(8,128)(2,1)S(1)}, bf16[2,128,128]{2,1,0:T(8,128)(2,1)S(1)}, u32[]{:S(2)}, u32[]{:S(2)}) %collective-permute-start.9) | collective-permute-done | bytes 65568 | tf_op jit(solution)/shard_map/ppermute | solution.py:310
  82.7 1.5 %all-to-all-done.2.got = bf16[16,88,128]{2,1,0:T(8,128)(2,1)S(1)} async-done(((bf16[16,88,128]{2,1,0:T(8,128)(2,1)}), bf16[16,88,128]{2,1,0:T(8,128)(2,1)S(1)}, u32[]{:S(2)}, u32[]{:S(2)}) %all-to-all-start.2) | async-done | bytes 360480 | tf_op jit(solution)/shard_map/all_to_all | solution.py:311
  84.2 0.0 copy-done
  84.2 0.7 finish.1
  84.9 3.6 %collective-permute-start.10 = (f32[64,128]{1,0:T(8,128)S(1)}, f32[64,128]{1,0:T(8,128)S(1)}, u32[]{:S(2)}, u32[]{:S(2)}) collective-permute-start(f32[64,128]{1,0:T(8,128)S(1)} %get-tuple-element.60.mine), channel_id=1, source_target_pairs={{0,16},{16,0},{1,17},{17,1},{2,18},{18,2},{3,19},{19,3},{4,20},{20... | collective-permute-start | bytes 98312 | tf_op jit(solution)/shard_map/ppermute | solution.py:319
  88.4 0.9 home.1
  89.3 0.0 collective-permute-done.10.other
  89.3 0.6 codes.1
  (2 shorter events, 0.0 us)
Async XLA Ops:
  2.7 4.5 %copy-start.1 = (bf16[64,1408]{1,0:T(8,128)(2,1)S(1)}, bf16[64,1408]{1,0:T(8,128)(2,1)}, u32[]{:S(2)}) copy-start(bf16[64,1408]{1,0:T(8,128)(2,1)} %get-tuple-element.36.pack) | copy-start | bytes 540676
  2.7 24.9 %all-to-all-start = ((bf16[4,128,1024]{2,1,0:T(8,128)(2,1)}), bf16[4,128,1024]{2,1,0:T(8,128)(2,1)S(1)}, u32[]{:S(2)}, u32[]{:S(2)}) async-start(bf16[4,128,1024]{2,1,0:T(8,128)(2,1)} %get-tuple-element.35), calls=%async_computation | async-start | bytes 2097152 | tf_op jit(solution)/shard_map/all_to_all | solution.py:268
  7.2 9.0 %collective-permute-start.1 = (bf16[64,1408]{1,0:T(8,128)(2,1)S(1)}, bf16[64,1408]{1,0:T(8,128)(2,1)S(1)}, u32[]{:S(2)}, u32[]{:S(2)}) collective-permute-start(bf16[64,1408]{1,0:T(8,128)(2,1)S(1)} %copy-done.1), channel_id=1, source_target_pairs={{23,16},{18,17},{17,18},{20,19},{19,20},{22,21},{21,22},{16,23},{3... | collective-permute-start | bytes 540680 | tf_op jit(solution)/shard_map/ppermute | solution.py:267
  13.4 14.1 %collective-permute-start = (bf16[64,1408]{1,0:T(8,128)(2,1)S(1)}, bf16[64,1408]{1,0:T(8,128)(2,1)S(1)}, u32[]{:S(2)}, u32[]{:S(2)}) collective-permute-start(bf16[64,1408]{1,0:T(8,128)(2,1)S(1)} %copy-done.1), channel_id=1, source_target_pairs={{5,0},{4,1},{7,2},{6,3},{1,4},{0,5},{3,6},{2,7},{22,16},{19,17},{1... | collective-permute-start | bytes 540680 | tf_op jit(solution)/shard_map/ppermute | solution.py:267
  27.6 4.6 %collective-permute-start.2 = (bf16[512,1024]{1,0:T(8,128)(2,1)S(1)}, bf16[512,1024]{1,0:T(8,128)(2,1)S(1)}, u32[]{:S(2)}, u32[]{:S(2)}) collective-permute-start(bf16[512,1024]{1,0:T(8,128)(2,1)S(1)} %bitcast.8), channel_id=1, source_target_pairs={{0,16},{16,0},{1,17},{17,1},{2,18},{18,2},{3,19},{19,3},{4,20},{20... | collective-permute-start | bytes 3145736 | tf_op jit(solution)/shard_map/ppermute | solution.py:277
  35.5 20.6 %all-to-all-start.1 = ((bf16[32,32,128]{2,1,0:T(8,128)(2,1)}), bf16[32,32,128]{2,1,0:T(8,128)(2,1)S(1)}, u32[]{:S(2)}, u32[]{:S(2)}) async-start(bf16[32,32,128]{2,1,0:T(8,128)(2,1)} %get-tuple-element.46), calls=%async_computation.1 | async-start | bytes 524288 | tf_op jit(solution)/shard_map/all_to_all | solution.py:304
  41.3 9.5 %collective-permute-start.3 = (bf16[144,128]{1,0:T(8,128)(2,1)S(1)}, bf16[144,128]{1,0:T(8,128)(2,1)S(1)}, u32[]{:S(2)}, u32[]{:S(2)}) collective-permute-start(bf16[144,128]{1,0:T(8,128)(2,1)S(1)} %get-tuple-element.47), channel_id=1, source_target_pairs={{0,0},{1,1},{2,2},{3,3},{4,4},{5,5},{6,6},{7,7},{16,22},{17,19},{1... | collective-permute-start | bytes 110600 | tf_op jit(solution)/shard_map/ppermute | solution.py:298
  46.7 6.3 %collective-permute-start.4 = (bf16[144,128]{1,0:T(8,128)(2,1)S(1)}, bf16[144,128]{1,0:T(8,128)(2,1)S(1)}, u32[]{:S(2)}, u32[]{:S(2)}) collective-permute-start(bf16[144,128]{1,0:T(8,128)(2,1)S(1)} %get-tuple-element.48), channel_id=1, source_target_pairs={{0,5},{1,4},{2,7},{3,6},{4,1},{5,0},{6,3},{7,2},{16,23},{17,18},{1... | collective-permute-start | bytes 110600 | tf_op jit(solution)/shard_map/ppermute | solution.py:298
  48.9 7.2 %collective-permute-start.6 = (bf16[4,128,128]{2,1,0:T(8,128)(2,1)S(1)}, bf16[4,128,128]{2,1,0:T(8,128)(2,1)S(1)}, u32[]{:S(2)}, u32[]{:S(2)}) collective-permute-start(bf16[4,128,128]{2,1,0:T(8,128)(2,1)S(1)} %get-tuple-element.50), channel_id=1, source_target_pairs={{0,16},{16,0},{1,17},{17,1},{2,18},{18,2},{3,19},{19,3},{4,20},{20... | collective-permute-start | bytes 393224 | tf_op jit(solution)/shard_map/ppermute | solution.py:299
  53.0 3.1 %collective-permute-start.5 = (bf16[80,128]{1,0:T(8,128)(2,1)S(1)}, bf16[80,128]{1,0:T(8,128)(2,1)S(1)}, u32[]{:S(2)}, u32[]{:S(2)}) collective-permute-start(bf16[80,128]{1,0:T(8,128)(2,1)S(1)} %get-tuple-element.49), channel_id=1, source_target_pairs={{0,16},{16,0},{1,17},{17,1},{2,18},{18,2},{3,19},{19,3},{4,20},{20... | collective-permute-start | bytes 61448 | tf_op jit(solution)/shard_map/ppermute | solution.py:303
  57.1 27.1 %all-to-all-start.2 = ((bf16[16,88,128]{2,1,0:T(8,128)(2,1)}), bf16[16,88,128]{2,1,0:T(8,128)(2,1)S(1)}, u32[]{:S(2)}, u32[]{:S(2)}) async-start(bf16[16,88,128]{2,1,0:T(8,128)(2,1)} %middle.1), calls=%async_computation.2 | async-start | bytes 720896 | tf_op jit(solution)/shard_map/all_to_all | solution.py:311
  69.7 14.5 %copy-start = (f32[1,256,64]{1,2,0:T(8,128)S(1)}, f32[1,256,64]{1,2,0:T(8,128)}, u32[]{:S(2)}) copy-start(f32[1,256,64]{1,2,0:T(8,128)} %param.5) | copy-start | bytes 196612
  69.7 9.3 %collective-permute-start.7 = (bf16[2,128,128]{2,1,0:T(8,128)(2,1)S(1)}, bf16[2,128,128]{2,1,0:T(8,128)(2,1)S(1)}, u32[]{:S(2)}, u32[]{:S(2)}) collective-permute-start(bf16[2,128,128]{2,1,0:T(8,128)(2,1)S(1)} %get-tuple-element.56), channel_id=1, source_target_pairs={{0,8},{8,0},{1,9},{9,1},{2,10},{10,2},{3,11},{11,3},{4,12},{12,4},... | collective-permute-start | bytes 196616 | tf_op jit(solution)/shard_map/ppermute | solution.py:308
  72.3 6.7 %collective-permute-start.8 = (bf16[2,128,128]{2,1,0:T(8,128)(2,1)S(1)}, bf16[2,128,128]{2,1,0:T(8,128)(2,1)S(1)}, u32[]{:S(2)}, u32[]{:S(2)}) collective-permute-start(bf16[2,128,128]{2,1,0:T(8,128)(2,1)S(1)} %get-tuple-element.57), channel_id=1, source_target_pairs={{0,1},{1,0},{2,3},{3,2},{4,5},{5,4},{6,7},{7,6},{8,9},{9,8},{10,11... | collective-permute-start | bytes 196616 | tf_op jit(solution)/shard_map/ppermute | solution.py:309
  76.5 6.2 %collective-permute-start.9 = (bf16[2,128,128]{2,1,0:T(8,128)(2,1)S(1)}, bf16[2,128,128]{2,1,0:T(8,128)(2,1)S(1)}, u32[]{:S(2)}, u32[]{:S(2)}) collective-permute-start(bf16[2,128,128]{2,1,0:T(8,128)(2,1)S(1)} %get-tuple-element.58), channel_id=1, source_target_pairs={{0,9},{1,8},{8,1},{9,0},{2,11},{3,10},{10,3},{11,2},{4,13},{5,12},... | collective-permute-start | bytes 196616 | tf_op jit(solution)/shard_map/ppermute | solution.py:310
  84.9 4.4 %collective-permute-start.10 = (f32[64,128]{1,0:T(8,128)S(1)}, f32[64,128]{1,0:T(8,128)S(1)}, u32[]{:S(2)}, u32[]{:S(2)}) collective-permute-start(f32[64,128]{1,0:T(8,128)S(1)} %get-tuple-element.60.mine), channel_id=1, source_target_pairs={{0,16},{16,0},{1,17},{17,1},{2,18},{18,2},{3,19},{19,3},{4,20},{20... | collective-permute-start | bytes 98312 | tf_op jit(solution)/shard_map/ppermute | solution.py:319

commit v13 on v12

--- a/solution.py
+++ b/solution.py
@@ -271,8 +271,8 @@
         "prepare",
         [((128, 1024), BF), ((128, 512), BF), ((512, 256), BF)],
         (pack, *packs),
-    )
-    mine, *tools = lax.optimization_barrier((mine, *tools))
+        flops=16 * 10**9,
+    )
     swap = [(0, 1), (1, 0)]
     other = lax.ppermute(mine, "core", swap)
     block, pair = ((4, 128, 128), BF), ((2, 128, 128), BF)

time: 90.8 us -> 90.3 us (level)
  waiting for transfers between devices: 21.1 us -> 8.59 us
  starting transfers between devices: 57.4 us -> 69.5 us
    ppermute x2, waiting for transfers between devices: 12.2 us -> 0.01 us  [per_device(): packs.append(lax.ppermute(pack, ('core', 'yh', 'yl'), pairs))]
    ppermute x1, starting transfers between devices: 1.92 us -> 13 us  [per_device(): other = lax.ppermute(mine, 'core', swap)]
    all_to_all x1, starting transfers between devices: 5.79 us -> 6.82 us  [per_device(): got = lax.all_to_all(send, NEAR, 0, 0, tiled=True)]
  transfers between devices with their start and end apart: 14 -> 14, of which waited for: 7 -> 6; matrix products, arithmetic and copies ran while one was open for 0% -> 0% of each run, Pallas kernels for 3% -> 3%
where the time goes in v13:
time: 90.3 us; the launch traced here: 89.5 us
  starting transfers between devices  69.5 us (77%)
  Pallas kernels  10.6 us (12%)
  waiting for transfers between devices  8.59 us (10%)
    ppermute x1, starting transfers between devices, per_device(): other = lax.ppermute(mine, 'core', swap)  13 us
    all_to_all x1, starting transfers between devices, per_device(): got = lax.all_to_all(send, FAR, 0, 0, tiled=True)  12.6 us
    pallas_call x9, Pallas kernels, call(): pl.pallas_call(kernel, out_shape=tuple((jax.ShapeDtypeStruct(*o) for o in...  8.5 us
    ppermute x2, starting transfers between devices, per_device(): packs.append(lax.ppermute(pack, ('core', 'yh', 'yl'), pairs))  8.06 us
    ppermute x2, starting transfers between devices, per_device(): moved.append(lax.ppermute(totals[i], ('core', 'yh', 'yl'), pairs))  7.59 us
    all_to_all x1, starting transfers between devices, per_device(): got = lax.all_to_all(send, NEAR, 0, 0, tiled=True)  6.82 us
    all_to_all x1, starting transfers between devices, per_device(): lax.all_to_all(copies, ('xl', 'yl'), 0, 0, tiled=True).reshape(512, 1024)  4.45 us
    ppermute x1, starting transfers between devices, per_device(): got_y = lax.ppermute(gives[1], 'yl', swap)  4.21 us
  transfers between devices with their start and end apart: 14, of which 6 were waited for; matrix products, arithmetic and copies ran while one was open for 0% of the time, Pallas kernels for 3%

profile of v13, /device:TPU:1, one launch (start us, length us, event | category | flops | bytes accessed | tf_op | source)
XLA Modules:
  0.0 89.5 jit_solution(5399889027051694555)
XLA Ops:
  0.6 2.1 %open.1 = (bf16[64,1408]{1,0:T(8,128)(2,1)}, bf16[4,128,1024]{2,1,0:T(8,128)(2,1)}) custom-call(bf16[128,1024]{1,0:T(8,128)(2,1)} %samples.1, bf16[64,1024]{1,0:T(8,128)(2,1)} %bitcast.12, f32[64,256]{1,0:T(8,128)} %bitcast.10), custom_call_target="tpu_custom_call" | custom-call | tf_op jit(solution)/shard_map/open/pallas_call | solution.py:248
  2.7 0.0 copy-start.1
  2.7 4.5 %all-to-all-start = ((bf16[4,128,1024]{2,1,0:T(8,128)(2,1)}), bf16[4,128,1024]{2,1,0:T(8,128)(2,1)S(1)}, u32[]{:S(2)}, u32[]{:S(2)}) async-start(bf16[4,128,1024]{2,1,0:T(8,128)(2,1)} %get-tuple-element.31), calls=%async_computation | async-start | bytes 2097152 | tf_op jit(solution)/shard_map/all_to_all | solution.py:268
  7.2 0.0 copy-done.1
  7.2 6.1 %collective-permute-start.2 = (bf16[64,1408]{1,0:T(8,128)(2,1)S(1)}, bf16[64,1408]{1,0:T(8,128)(2,1)S(1)}, u32[]{:S(2)}, u32[]{:S(2)}) collective-permute-start(bf16[64,1408]{1,0:T(8,128)(2,1)S(1)} %copy-done.1), channel_id=1, source_target_pairs={{23,16},{18,17},{17,18},{20,19},{19,20},{22,21},{21,22},{16,23},{3... | collective-permute-start | bytes 540680 | tf_op jit(solution)/shard_map/ppermute | solution.py:267
  13.4 1.9 %collective-permute-start.1 = (bf16[64,1408]{1,0:T(8,128)(2,1)S(1)}, bf16[64,1408]{1,0:T(8,128)(2,1)S(1)}, u32[]{:S(2)}, u32[]{:S(2)}) collective-permute-start(bf16[64,1408]{1,0:T(8,128)(2,1)S(1)} %copy-done.1), channel_id=1, source_target_pairs={{5,0},{4,1},{7,2},{6,3},{1,4},{0,5},{3,6},{2,7},{22,16},{19,17},{1... | collective-permute-start | bytes 540680 | tf_op jit(solution)/shard_map/ppermute | solution.py:267
  15.3 0.2 all-to-all-done
  15.5 13.0 %collective-permute-start = (bf16[512,1024]{1,0:T(8,128)(2,1)S(1)}, bf16[512,1024]{1,0:T(8,128)(2,1)S(1)}, u32[]{:S(2)}, u32[]{:S(2)}) collective-permute-start(bf16[512,1024]{1,0:T(8,128)(2,1)S(1)} %bitcast.8), channel_id=1, source_target_pairs={{0,16},{16,0},{1,17},{17,1},{2,18},{18,2},{3,19},{19,3},{4,20},{20... | collective-permute-start | bytes 3145736 | tf_op jit(solution)/shard_map/ppermute | solution.py:277
  28.4 0.0 collective-permute-done.2.second
  28.5 0.0 collective-permute-done.1.first
  28.5 0.1 prepare.1
  28.6 1.8 %early.1 = (f32[512,256]{1,0:T(8,128)S(1)}, f32[128,1024]{1,0:T(8,128)S(1)}, bf16[4,128,128]{2,1,0:T(8,128)(2,1)S(1)}) custom-call(bf16[512,1024]{1,0:T(8,128)(2,1)S(1)} %bitcast.9, bf16[128,1024]{1,0:T(8,128)(2,1)S(1)} %get-tuple-element.33.turn, bf16[128,512]{1,0:T(8,128)(2,1)S(1)} %get-tuple-element.34.codes_t, bf16[512,256]{1,0:T(8,128)(2,1)S(1)} %get-tuple-element.35.left), custom_call_target="tpu_custom_call" | custom-call | bytes 8000000 | tf_op jit(solution)/shard_map/early/pallas_call | solution.py:236
  30.5 0.2 collective-permute-done.samples
  30.7 3.3 %late.1 = (bf16[32,32,128]{2,1,0:T(8,128)(2,1)}, bf16[4,128,128]{2,1,0:T(8,128)(2,1)S(1)}, bf16[144,128]{1,0:T(8,128)(2,1)S(1)}, bf16[144,128]{1,0:T(8,128)(2,1)S(1)}) custom-call(bf16[512,1024]{1,0:T(8,128)(2,1)S(1)} %collective-permute-done.samples, bf16[128,1024]{1,0:T(8,128)(2,1)S(1)} %get-tuple-element.33.turn, ...), custom_call_target="tpu_custom_call" | custom-call | bytes 8000000 | tf_op jit(solution)/shard_map/late/pallas_call | solution.py:236
  34.0 6.8 %all-to-all-start.1 = ((bf16[32,32,128]{2,1,0:T(8,128)(2,1)}), bf16[32,32,128]{2,1,0:T(8,128)(2,1)S(1)}, u32[]{:S(2)}, u32[]{:S(2)}) async-start(bf16[32,32,128]{2,1,0:T(8,128)(2,1)} %get-tuple-element.38), calls=%async_computation.1 | async-start | bytes 524288 | tf_op jit(solution)/shard_map/all_to_all | solution.py:304
  40.8 5.4 %collective-permute-start.3 = (bf16[144,128]{1,0:T(8,128)(2,1)S(1)}, bf16[144,128]{1,0:T(8,128)(2,1)S(1)}, u32[]{:S(2)}, u32[]{:S(2)}) collective-permute-start(bf16[144,128]{1,0:T(8,128)(2,1)S(1)} %get-tuple-element.39), channel_id=1, source_target_pairs={{0,0},{1,1},{2,2},{3,3},{4,4},{5,5},{6,6},{7,7},{16,22},{17,19},{1... | collective-permute-start | bytes 110600 | tf_op jit(solution)/shard_map/ppermute | solution.py:298
  46.2 2.2 %collective-permute-start.4 = (bf16[144,128]{1,0:T(8,128)(2,1)S(1)}, bf16[144,128]{1,0:T(8,128)(2,1)S(1)}, u32[]{:S(2)}, u32[]{:S(2)}) collective-permute-start(bf16[144,128]{1,0:T(8,128)(2,1)S(1)} %get-tuple-element.40), channel_id=1, source_target_pairs={{0,5},{1,4},{2,7},{3,6},{4,1},{5,0},{6,3},{7,2},{16,23},{17,18},{1... | collective-permute-start | bytes 110600 | tf_op jit(solution)/shard_map/ppermute | solution.py:298
  48.4 1.9 %collective-permute-start.6 = (bf16[4,128,128]{2,1,0:T(8,128)(2,1)S(1)}, bf16[4,128,128]{2,1,0:T(8,128)(2,1)S(1)}, u32[]{:S(2)}, u32[]{:S(2)}) collective-permute-start(bf16[4,128,128]{2,1,0:T(8,128)(2,1)S(1)} %get-tuple-element.42), channel_id=1, source_target_pairs={{0,16},{16,0},{1,17},{17,1},{2,18},{18,2},{3,19},{19,3},{4,20},{20... | collective-permute-start | bytes 393224 | tf_op jit(solution)/shard_map/ppermute | solution.py:299
  50.4 0.0 collective-permute-done.3.first
  50.4 2.1 %collective-permute-done.4.second = bf16[144,128]{1,0:T(8,128)(2,1)S(1)} collective-permute-done((bf16[144,128]{1,0:T(8,128)(2,1)S(1)}, bf16[144,128]{1,0:T(8,128)(2,1)S(1)}, u32[]{:S(2)}, u32[]{:S(2)}) %collective-permute-start.4) | collective-permute-done | bytes 36896 | tf_op jit(solution)/shard_map/ppermute | solution.py:298
  52.5 2.3 %collective-permute-start.5 = (bf16[80,128]{1,0:T(8,128)(2,1)S(1)}, bf16[80,128]{1,0:T(8,128)(2,1)S(1)}, u32[]{:S(2)}, u32[]{:S(2)}) collective-permute-start(bf16[80,128]{1,0:T(8,128)(2,1)S(1)} %get-tuple-element.41), channel_id=1, source_target_pairs={{0,16},{16,0},{1,17},{17,1},{2,18},{18,2},{3,19},{19,3},{4,20},{20... | collective-permute-start | bytes 61448 | tf_op jit(solution)/shard_map/ppermute | solution.py:303
  54.8 0.8 collective-permute-done.5.half
  55.6 0.0 collective-permute-done.6.got_core
  55.6 0.0 all-to-all-done.1.got
  55.6 1.0 %middle.1 = bf16[16,88,128]{2,1,0:T(8,128)(2,1)} custom-call(bf16[32,32,128]{2,1,0:T(8,128)(2,1)S(1)} %all-to-all-done.1.got, f32[80,128]{1,0:T(8,128)S(1)} %get-tuple-element.44.keep, bf16[80,128]{1,0:T(8,128)(2,1)S(1)} %collective-permute-done.5.half), custom_call_target="tpu_custom_call" | custom-call | tf_op jit(solution)/shard_map/middle/pallas_call | solution.py:236
  56.6 12.6 %all-to-all-start.2 = ((bf16[16,88,128]{2,1,0:T(8,128)(2,1)}), bf16[16,88,128]{2,1,0:T(8,128)(2,1)S(1)}, u32[]{:S(2)}, u32[]{:S(2)}) async-start(bf16[16,88,128]{2,1,0:T(8,128)(2,1)} %middle.1), calls=%async_computation.2 | async-start | bytes 720896 | tf_op jit(solution)/shard_map/all_to_all | solution.py:311
  69.2 0.0 copy-start
  69.3 2.6 %collective-permute-start.7 = (bf16[2,128,128]{2,1,0:T(8,128)(2,1)S(1)}, bf16[2,128,128]{2,1,0:T(8,128)(2,1)S(1)}, u32[]{:S(2)}, u32[]{:S(2)}) collective-permute-start(bf16[2,128,128]{2,1,0:T(8,128)(2,1)S(1)} %get-tuple-element.48), channel_id=1, source_target_pairs={{0,8},{8,0},{1,9},{9,1},{2,10},{10,2},{3,11},{11,3},{4,12},{12,4},... | collective-permute-start | bytes 196616 | tf_op jit(solution)/shard_map/ppermute | solution.py:308
  71.9 4.2 %collective-permute-start.8 = (bf16[2,128,128]{2,1,0:T(8,128)(2,1)S(1)}, bf16[2,128,128]{2,1,0:T(8,128)(2,1)S(1)}, u32[]{:S(2)}, u32[]{:S(2)}) collective-permute-start(bf16[2,128,128]{2,1,0:T(8,128)(2,1)S(1)} %get-tuple-element.49), channel_id=1, source_target_pairs={{0,1},{1,0},{2,3},{3,2},{4,5},{5,4},{6,7},{7,6},{8,9},{9,8},{10,11... | collective-permute-start | bytes 196616 | tf_op jit(solution)/shard_map/ppermute | solution.py:309
  76.1 2.4 %collective-permute-start.9 = (bf16[2,128,128]{2,1,0:T(8,128)(2,1)S(1)}, bf16[2,128,128]{2,1,0:T(8,128)(2,1)S(1)}, u32[]{:S(2)}, u32[]{:S(2)}) collective-permute-start(bf16[2,128,128]{2,1,0:T(8,128)(2,1)S(1)} %get-tuple-element.50), channel_id=1, source_target_pairs={{0,9},{1,8},{8,1},{9,0},{2,11},{3,10},{10,3},{11,2},{4,13},{5,12},... | collective-permute-start | bytes 196616 | tf_op jit(solution)/shard_map/ppermute | solution.py:310
  78.5 0.0 collective-permute-done.7.got_x
  78.5 0.0 collective-permute-done.8.got_y
  78.6 3.7 %collective-permute-done.9.got_xy = bf16[2,128,128]{2,1,0:T(8,128)(2,1)S(1)} collective-permute-done((bf16[2,128,128]{2,1,0:T(8,128)(2,1)S(1)}, bf16[2,128,128]{2,1,0:T(8,128)(2,1)S(1)}, u32[]{:S(2)}, u32[]{:S(2)}) %collective-permute-start.9) | collective-permute-done | bytes 65568 | tf_op jit(solution)/shard_map/ppermute | solution.py:310
  82.3 1.4 %all-to-all-done.2.got = bf16[16,88,128]{2,1,0:T(8,128)(2,1)S(1)} async-done(((bf16[16,88,128]{2,1,0:T(8,128)(2,1)}), bf16[16,88,128]{2,1,0:T(8,128)(2,1)S(1)}, u32[]{:S(2)}, u32[]{:S(2)}) %all-to-all-start.2) | async-done | bytes 360480 | tf_op jit(solution)/shard_map/all_to_all | solution.py:311
  83.7 0.0 copy-done
  83.7 0.7 finish.1
  84.4 3.6 %collective-permute-start.10 = (f32[64,128]{1,0:T(8,128)S(1)}, f32[64,128]{1,0:T(8,128)S(1)}, u32[]{:S(2)}, u32[]{:S(2)}) collective-permute-start(f32[64,128]{1,0:T(8,128)S(1)} %get-tuple-element.52.mine), channel_id=1, source_target_pairs={{0,16},{16,0},{1,17},{17,1},{2,18},{18,2},{3,19},{19,3},{4,20},{20... | collective-permute-start | bytes 98312 | tf_op jit(solution)/shard_map/ppermute | solution.py:319
  88.0 0.9 home.1
  88.8 0.0 collective-permute-done.10.other
  88.8 0.6 codes.1
  (2 shorter events, 0.0 us)
Async XLA Ops:
  2.7 4.5 %copy-start.1 = (bf16[64,1408]{1,0:T(8,128)(2,1)S(1)}, bf16[64,1408]{1,0:T(8,128)(2,1)}, u32[]{:S(2)}) copy-start(bf16[64,1408]{1,0:T(8,128)(2,1)} %get-tuple-element.32.pack) | copy-start | bytes 540676
  2.7 12.7 %all-to-all-start = ((bf16[4,128,1024]{2,1,0:T(8,128)(2,1)}), bf16[4,128,1024]{2,1,0:T(8,128)(2,1)S(1)}, u32[]{:S(2)}, u32[]{:S(2)}) async-start(bf16[4,128,1024]{2,1,0:T(8,128)(2,1)} %get-tuple-element.31), calls=%async_computation | async-start | bytes 2097152 | tf_op jit(solution)/shard_map/all_to_all | solution.py:268
  7.2 21.2 %collective-permute-start.2 = (bf16[64,1408]{1,0:T(8,128)(2,1)S(1)}, bf16[64,1408]{1,0:T(8,128)(2,1)S(1)}, u32[]{:S(2)}, u32[]{:S(2)}) collective-permute-start(bf16[64,1408]{1,0:T(8,128)(2,1)S(1)} %copy-done.1), channel_id=1, source_target_pairs={{23,16},{18,17},{17,18},{20,19},{19,20},{22,21},{21,22},{16,23},{3... | collective-permute-start | bytes 540680 | tf_op jit(solution)/shard_map/ppermute | solution.py:267
  13.4 15.1 %collective-permute-start.1 = (bf16[64,1408]{1,0:T(8,128)(2,1)S(1)}, bf16[64,1408]{1,0:T(8,128)(2,1)S(1)}, u32[]{:S(2)}, u32[]{:S(2)}) collective-permute-start(bf16[64,1408]{1,0:T(8,128)(2,1)S(1)} %copy-done.1), channel_id=1, source_target_pairs={{5,0},{4,1},{7,2},{6,3},{1,4},{0,5},{3,6},{2,7},{22,16},{19,17},{1... | collective-permute-start | bytes 540680 | tf_op jit(solution)/shard_map/ppermute | solution.py:267
  15.5 15.2 %collective-permute-start = (bf16[512,1024]{1,0:T(8,128)(2,1)S(1)}, bf16[512,1024]{1,0:T(8,128)(2,1)S(1)}, u32[]{:S(2)}, u32[]{:S(2)}) collective-permute-start(bf16[512,1024]{1,0:T(8,128)(2,1)S(1)} %bitcast.8), channel_id=1, source_target_pairs={{0,16},{16,0},{1,17},{17,1},{2,18},{18,2},{3,19},{19,3},{4,20},{20... | collective-permute-start | bytes 3145736 | tf_op jit(solution)/shard_map/ppermute | solution.py:277
  34.0 21.6 %all-to-all-start.1 = ((bf16[32,32,128]{2,1,0:T(8,128)(2,1)}), bf16[32,32,128]{2,1,0:T(8,128)(2,1)S(1)}, u32[]{:S(2)}, u32[]{:S(2)}) async-start(bf16[32,32,128]{2,1,0:T(8,128)(2,1)} %get-tuple-element.38), calls=%async_computation.1 | async-start | bytes 524288 | tf_op jit(solution)/shard_map/all_to_all | solution.py:304
  40.8 9.5 %collective-permute-start.3 = (bf16[144,128]{1,0:T(8,128)(2,1)S(1)}, bf16[144,128]{1,0:T(8,128)(2,1)S(1)}, u32[]{:S(2)}, u32[]{:S(2)}) collective-permute-start(bf16[144,128]{1,0:T(8,128)(2,1)S(1)} %get-tuple-element.39), channel_id=1, source_target_pairs={{0,0},{1,1},{2,2},{3,3},{4,4},{5,5},{6,6},{7,7},{16,22},{17,19},{1... | collective-permute-start | bytes 110600 | tf_op jit(solution)/shard_map/ppermute | solution.py:298
  46.2 6.3 %collective-permute-start.4 = (bf16[144,128]{1,0:T(8,128)(2,1)S(1)}, bf16[144,128]{1,0:T(8,128)(2,1)S(1)}, u32[]{:S(2)}, u32[]{:S(2)}) collective-permute-start(bf16[144,128]{1,0:T(8,128)(2,1)S(1)} %get-tuple-element.40), channel_id=1, source_target_pairs={{0,5},{1,4},{2,7},{3,6},{4,1},{5,0},{6,3},{7,2},{16,23},{17,18},{1... | collective-permute-start | bytes 110600 | tf_op jit(solution)/shard_map/ppermute | solution.py:298
  48.4 7.2 %collective-permute-start.6 = (bf16[4,128,128]{2,1,0:T(8,128)(2,1)S(1)}, bf16[4,128,128]{2,1,0:T(8,128)(2,1)S(1)}, u32[]{:S(2)}, u32[]{:S(2)}) collective-permute-start(bf16[4,128,128]{2,1,0:T(8,128)(2,1)S(1)} %get-tuple-element.42), channel_id=1, source_target_pairs={{0,16},{16,0},{1,17},{17,1},{2,18},{18,2},{3,19},{19,3},{4,20},{20... | collective-permute-start | bytes 393224 | tf_op jit(solution)/shard_map/ppermute | solution.py:299
  52.5 3.1 %collective-permute-start.5 = (bf16[80,128]{1,0:T(8,128)(2,1)S(1)}, bf16[80,128]{1,0:T(8,128)(2,1)S(1)}, u32[]{:S(2)}, u32[]{:S(2)}) collective-permute-start(bf16[80,128]{1,0:T(8,128)(2,1)S(1)} %get-tuple-element.41), channel_id=1, source_target_pairs={{0,16},{16,0},{1,17},{17,1},{2,18},{18,2},{3,19},{19,3},{4,20},{20... | collective-permute-start | bytes 61448 | tf_op jit(solution)/shard_map/ppermute | solution.py:303
  56.6 27.1 %all-to-all-start.2 = ((bf16[16,88,128]{2,1,0:T(8,128)(2,1)}), bf16[16,88,128]{2,1,0:T(8,128)(2,1)S(1)}, u32[]{:S(2)}, u32[]{:S(2)}) async-start(bf16[16,88,128]{2,1,0:T(8,128)(2,1)} %middle.1), calls=%async_computation.2 | async-start | bytes 720896 | tf_op jit(solution)/shard_map/all_to_all | solution.py:311
  69.2 14.5 %copy-start = (f32[1,256,64]{1,2,0:T(8,128)S(1)}, f32[1,256,64]{1,2,0:T(8,128)}, u32[]{:S(2)}) copy-start(f32[1,256,64]{1,2,0:T(8,128)} %param.5) | copy-start | bytes 196612
  69.3 9.3 %collective-permute-start.7 = (bf16[2,128,128]{2,1,0:T(8,128)(2,1)S(1)}, bf16[2,128,128]{2,1,0:T(8,128)(2,1)S(1)}, u32[]{:S(2)}, u32[]{:S(2)}) collective-permute-start(bf16[2,128,128]{2,1,0:T(8,128)(2,1)S(1)} %get-tuple-element.48), channel_id=1, source_target_pairs={{0,8},{8,0},{1,9},{9,1},{2,10},{10,2},{3,11},{11,3},{4,12},{12,4},... | collective-permute-start | bytes 196616 | tf_op jit(solution)/shard_map/ppermute | solution.py:308
  71.9 6.7 %collective-permute-start.8 = (bf16[2,128,128]{2,1,0:T(8,128)(2,1)S(1)}, bf16[2,128,128]{2,1,0:T(8,128)(2,1)S(1)}, u32[]{:S(2)}, u32[]{:S(2)}) collective-permute-start(bf16[2,128,128]{2,1,0:T(8,128)(2,1)S(1)} %get-tuple-element.49), channel_id=1, source_target_pairs={{0,1},{1,0},{2,3},{3,2},{4,5},{5,4},{6,7},{7,6},{8,9},{9,8},{10,11... | collective-permute-start | bytes 196616 | tf_op jit(solution)/shard_map/ppermute | solution.py:309
  76.1 6.2 %collective-permute-start.9 = (bf16[2,128,128]{2,1,0:T(8,128)(2,1)S(1)}, bf16[2,128,128]{2,1,0:T(8,128)(2,1)S(1)}, u32[]{:S(2)}, u32[]{:S(2)}) collective-permute-start(bf16[2,128,128]{2,1,0:T(8,128)(2,1)S(1)} %get-tuple-element.50), channel_id=1, source_target_pairs={{0,9},{1,8},{8,1},{9,0},{2,11},{3,10},{10,3},{11,2},{4,13},{5,12},... | collective-permute-start | bytes 196616 | tf_op jit(solution)/shard_map/ppermute | solution.py:310
  84.4 4.4 %collective-permute-start.10 = (f32[64,128]{1,0:T(8,128)S(1)}, f32[64,128]{1,0:T(8,128)S(1)}, u32[]{:S(2)}, u32[]{:S(2)}) collective-permute-start(f32[64,128]{1,0:T(8,128)S(1)} %get-tuple-element.52.mine), channel_id=1, source_target_pairs={{0,16},{16,0},{1,17},{17,1},{2,18},{18,2},{3,19},{19,3},{4,20},{20... | collective-permute-start | bytes 98312 | tf_op jit(solution)/shard_map/ppermute | solution.py:319

commit v14 on v13

--- a/solution.py
+++ b/solution.py
@@ -73,7 +73,7 @@
 
 
 def assign_rows(samples, turn, codes_t, left, sums, cross, put):
-    rows, chunk = 512, 256
+    rows, chunk = 512, 512
     lane = lax.broadcasted_iota(jnp.int32, (chunk, 128), 1)
     three = jnp.where(lane < 3, 1.0, 0.0).astype(BF)
     ones = jnp.ones((chunk, 128), BF)
@@ -101,8 +101,8 @@
         sums = s if sums is None else sums + s
         cross = k if cross is None else cross + k
         back = rebuilt.T
-        put(2 * c, back[:128])
-        put(2 * c + 1, back[128:])
+        for n in range(chunk // 128):
+            put(chunk // 128 * c + n, back[n * 128 : (n + 1) * 128])
     return sums, cross
 
 

time: 90.3 us -> 89.8 us (level)
  no operation moved by 1% of the time
where the time goes in v14:
time: 89.8 us; the launch traced here: 88.9 us
  starting transfers between devices  69.5 us (77%)
  Pallas kernels  10 us (11%)
  waiting for transfers between devices  8.62 us (10%)
    ppermute x1, starting transfers between devices, per_device(): other = lax.ppermute(mine, 'core', swap)  13 us
    all_to_all x1, starting transfers between devices, per_device(): got = lax.all_to_all(send, FAR, 0, 0, tiled=True)  12.6 us
    ppermute x2, starting transfers between devices, per_device(): packs.append(lax.ppermute(pack, ('core', 'yh', 'yl'), pairs))  8.06 us
    pallas_call x9, Pallas kernels, call(): pl.pallas_call(kernel, out_shape=tuple((jax.ShapeDtypeStruct(*o) for o in...  7.89 us
    ppermute x2, starting transfers between devices, per_device(): moved.append(lax.ppermute(totals[i], ('core', 'yh', 'yl'), pairs))  7.59 us
    all_to_all x1, starting transfers between devices, per_device(): got = lax.all_to_all(send, NEAR, 0, 0, tiled=True)  6.82 us
    all_to_all x1, starting transfers between devices, per_device(): lax.all_to_all(copies, ('xl', 'yl'), 0, 0, tiled=True).reshape(512, 1024)  4.45 us
    ppermute x1, starting transfers between devices, per_device(): got_y = lax.ppermute(gives[1], 'yl', swap)  4.21 us
  transfers between devices with their start and end apart: 14, of which 6 were waited for; matrix products, arithmetic and copies ran while one was open for 0% of the time, Pallas kernels for 3%

profile of v14, /device:TPU:1, one launch (start us, length us, event | category | flops | bytes accessed | tf_op | source)
XLA Modules:
  0.0 88.9 jit_solution(15333121906467596130)
XLA Ops:
  0.6 2.1 %open.1 = (bf16[64,1408]{1,0:T(8,128)(2,1)}, bf16[4,128,1024]{2,1,0:T(8,128)(2,1)}) custom-call(bf16[128,1024]{1,0:T(8,128)(2,1)} %samples.1, bf16[64,1024]{1,0:T(8,128)(2,1)} %bitcast.12, f32[64,256]{1,0:T(8,128)} %bitcast.10), custom_call_target="tpu_custom_call" | custom-call | tf_op jit(solution)/shard_map/open/pallas_call | solution.py:248
  2.7 0.0 copy-start.1
  2.7 4.5 %all-to-all-start = ((bf16[4,128,1024]{2,1,0:T(8,128)(2,1)}), bf16[4,128,1024]{2,1,0:T(8,128)(2,1)S(1)}, u32[]{:S(2)}, u32[]{:S(2)}) async-start(bf16[4,128,1024]{2,1,0:T(8,128)(2,1)} %get-tuple-element.31), calls=%async_computation | async-start | bytes 2097152 | tf_op jit(solution)/shard_map/all_to_all | solution.py:268
  7.2 0.0 copy-done.1
  7.2 6.1 %collective-permute-start.2 = (bf16[64,1408]{1,0:T(8,128)(2,1)S(1)}, bf16[64,1408]{1,0:T(8,128)(2,1)S(1)}, u32[]{:S(2)}, u32[]{:S(2)}) collective-permute-start(bf16[64,1408]{1,0:T(8,128)(2,1)S(1)} %copy-done.1), channel_id=1, source_target_pairs={{23,16},{18,17},{17,18},{20,19},{19,20},{22,21},{21,22},{16,23},{3... | collective-permute-start | bytes 540680 | tf_op jit(solution)/shard_map/ppermute | solution.py:267
  13.4 1.9 %collective-permute-start.1 = (bf16[64,1408]{1,0:T(8,128)(2,1)S(1)}, bf16[64,1408]{1,0:T(8,128)(2,1)S(1)}, u32[]{:S(2)}, u32[]{:S(2)}) collective-permute-start(bf16[64,1408]{1,0:T(8,128)(2,1)S(1)} %copy-done.1), channel_id=1, source_target_pairs={{5,0},{4,1},{7,2},{6,3},{1,4},{0,5},{3,6},{2,7},{22,16},{19,17},{1... | collective-permute-start | bytes 540680 | tf_op jit(solution)/shard_map/ppermute | solution.py:267
  15.3 0.2 all-to-all-done
  15.5 13.0 %collective-permute-start = (bf16[512,1024]{1,0:T(8,128)(2,1)S(1)}, bf16[512,1024]{1,0:T(8,128)(2,1)S(1)}, u32[]{:S(2)}, u32[]{:S(2)}) collective-permute-start(bf16[512,1024]{1,0:T(8,128)(2,1)S(1)} %bitcast.8), channel_id=1, source_target_pairs={{0,16},{16,0},{1,17},{17,1},{2,18},{18,2},{3,19},{19,3},{4,20},{20... | collective-permute-start | bytes 3145736 | tf_op jit(solution)/shard_map/ppermute | solution.py:277
  28.4 0.0 collective-permute-done.2.second
  28.5 0.0 collective-permute-done.1.first
  28.5 0.1 prepare.1
  28.6 1.8 %early.1 = (f32[512,256]{1,0:T(8,128)S(1)}, f32[128,1024]{1,0:T(8,128)S(1)}, bf16[4,128,128]{2,1,0:T(8,128)(2,1)S(1)}) custom-call(bf16[512,1024]{1,0:T(8,128)(2,1)S(1)} %bitcast.9, bf16[128,1024]{1,0:T(8,128)(2,1)S(1)} %get-tuple-element.33.turn, bf16[128,512]{1,0:T(8,128)(2,1)S(1)} %get-tuple-element.34.codes_t, bf16[512,256]{1,0:T(8,128)(2,1)S(1)} %get-tuple-element.35.left), custom_call_target="tpu_custom_call" | custom-call | bytes 8000000 | tf_op jit(solution)/shard_map/early/pallas_call | solution.py:236
  30.4 0.3 collective-permute-done.samples
  30.7 2.7 %late.1 = (bf16[32,32,128]{2,1,0:T(8,128)(2,1)}, bf16[4,128,128]{2,1,0:T(8,128)(2,1)S(1)}, bf16[144,128]{1,0:T(8,128)(2,1)S(1)}, bf16[144,128]{1,0:T(8,128)(2,1)S(1)}) custom-call(bf16[512,1024]{1,0:T(8,128)(2,1)S(1)} %collective-permute-done.samples, bf16[128,1024]{1,0:T(8,128)(2,1)S(1)} %get-tuple-element.33.turn, ...), custom_call_target="tpu_custom_call" | custom-call | bytes 8000000 | tf_op jit(solution)/shard_map/late/pallas_call | solution.py:236
  33.4 6.8 %all-to-all-start.1 = ((bf16[32,32,128]{2,1,0:T(8,128)(2,1)}), bf16[32,32,128]{2,1,0:T(8,128)(2,1)S(1)}, u32[]{:S(2)}, u32[]{:S(2)}) async-start(bf16[32,32,128]{2,1,0:T(8,128)(2,1)} %get-tuple-element.38), calls=%async_computation.1 | async-start | bytes 524288 | tf_op jit(solution)/shard_map/all_to_all | solution.py:304
  40.2 5.4 %collective-permute-start.3 = (bf16[144,128]{1,0:T(8,128)(2,1)S(1)}, bf16[144,128]{1,0:T(8,128)(2,1)S(1)}, u32[]{:S(2)}, u32[]{:S(2)}) collective-permute-start(bf16[144,128]{1,0:T(8,128)(2,1)S(1)} %get-tuple-element.39), channel_id=1, source_target_pairs={{0,0},{1,1},{2,2},{3,3},{4,4},{5,5},{6,6},{7,7},{16,22},{17,19},{1... | collective-permute-start | bytes 110600 | tf_op jit(solution)/shard_map/ppermute | solution.py:298
  45.7 2.2 %collective-permute-start.4 = (bf16[144,128]{1,0:T(8,128)(2,1)S(1)}, bf16[144,128]{1,0:T(8,128)(2,1)S(1)}, u32[]{:S(2)}, u32[]{:S(2)}) collective-permute-start(bf16[144,128]{1,0:T(8,128)(2,1)S(1)} %get-tuple-element.40), channel_id=1, source_target_pairs={{0,5},{1,4},{2,7},{3,6},{4,1},{5,0},{6,3},{7,2},{16,23},{17,18},{1... | collective-permute-start | bytes 110600 | tf_op jit(solution)/shard_map/ppermute | solution.py:298
  47.8 1.9 %collective-permute-start.6 = (bf16[4,128,128]{2,1,0:T(8,128)(2,1)S(1)}, bf16[4,128,128]{2,1,0:T(8,128)(2,1)S(1)}, u32[]{:S(2)}, u32[]{:S(2)}) collective-permute-start(bf16[4,128,128]{2,1,0:T(8,128)(2,1)S(1)} %get-tuple-element.42), channel_id=1, source_target_pairs={{0,16},{16,0},{1,17},{17,1},{2,18},{18,2},{3,19},{19,3},{4,20},{20... | collective-permute-start | bytes 393224 | tf_op jit(solution)/shard_map/ppermute | solution.py:299
  49.8 0.0 collective-permute-done.3.first
  49.8 2.1 %collective-permute-done.4.second = bf16[144,128]{1,0:T(8,128)(2,1)S(1)} collective-permute-done((bf16[144,128]{1,0:T(8,128)(2,1)S(1)}, bf16[144,128]{1,0:T(8,128)(2,1)S(1)}, u32[]{:S(2)}, u32[]{:S(2)}) %collective-permute-start.4) | collective-permute-done | bytes 36896 | tf_op jit(solution)/shard_map/ppermute | solution.py:298
  51.9 2.3 %collective-permute-start.5 = (bf16[80,128]{1,0:T(8,128)(2,1)S(1)}, bf16[80,128]{1,0:T(8,128)(2,1)S(1)}, u32[]{:S(2)}, u32[]{:S(2)}) collective-permute-start(bf16[80,128]{1,0:T(8,128)(2,1)S(1)} %get-tuple-element.41), channel_id=1, source_target_pairs={{0,16},{16,0},{1,17},{17,1},{2,18},{18,2},{3,19},{19,3},{4,20},{20... | collective-permute-start | bytes 61448 | tf_op jit(solution)/shard_map/ppermute | solution.py:303
  54.2 0.8 collective-permute-done.5.half
  55.0 0.0 collective-permute-done.6.got_core
  55.0 0.0 all-to-all-done.1.got
  55.0 1.0 %middle.1 = bf16[16,88,128]{2,1,0:T(8,128)(2,1)} custom-call(bf16[32,32,128]{2,1,0:T(8,128)(2,1)S(1)} %all-to-all-done.1.got, f32[80,128]{1,0:T(8,128)S(1)} %get-tuple-element.44.keep, bf16[80,128]{1,0:T(8,128)(2,1)S(1)} %collective-permute-done.5.half), custom_call_target="tpu_custom_call" | custom-call | tf_op jit(solution)/shard_map/middle/pallas_call | solution.py:236
  56.0 12.6 %all-to-all-start.2 = ((bf16[16,88,128]{2,1,0:T(8,128)(2,1)}), bf16[16,88,128]{2,1,0:T(8,128)(2,1)S(1)}, u32[]{:S(2)}, u32[]{:S(2)}) async-start(bf16[16,88,128]{2,1,0:T(8,128)(2,1)} %middle.1), calls=%async_computation.2 | async-start | bytes 720896 | tf_op jit(solution)/shard_map/all_to_all | solution.py:311
  68.7 0.0 copy-start
  68.7 2.6 %collective-permute-start.7 = (bf16[2,128,128]{2,1,0:T(8,128)(2,1)S(1)}, bf16[2,128,128]{2,1,0:T(8,128)(2,1)S(1)}, u32[]{:S(2)}, u32[]{:S(2)}) collective-permute-start(bf16[2,128,128]{2,1,0:T(8,128)(2,1)S(1)} %get-tuple-element.48), channel_id=1, source_target_pairs={{0,8},{8,0},{1,9},{9,1},{2,10},{10,2},{3,11},{11,3},{4,12},{12,4},... | collective-permute-start | bytes 196616 | tf_op jit(solution)/shard_map/ppermute | solution.py:308
  71.3 4.2 %collective-permute-start.8 = (bf16[2,128,128]{2,1,0:T(8,128)(2,1)S(1)}, bf16[2,128,128]{2,1,0:T(8,128)(2,1)S(1)}, u32[]{:S(2)}, u32[]{:S(2)}) collective-permute-start(bf16[2,128,128]{2,1,0:T(8,128)(2,1)S(1)} %get-tuple-element.49), channel_id=1, source_target_pairs={{0,1},{1,0},{2,3},{3,2},{4,5},{5,4},{6,7},{7,6},{8,9},{9,8},{10,11... | collective-permute-start | bytes 196616 | tf_op jit(solution)/shard_map/ppermute | solution.py:309
  75.5 2.4 %collective-permute-start.9 = (bf16[2,128,128]{2,1,0:T(8,128)(2,1)S(1)}, bf16[2,128,128]{2,1,0:T(8,128)(2,1)S(1)}, u32[]{:S(2)}, u32[]{:S(2)}) collective-permute-start(bf16[2,128,128]{2,1,0:T(8,128)(2,1)S(1)} %get-tuple-element.50), channel_id=1, source_target_pairs={{0,9},{1,8},{8,1},{9,0},{2,11},{3,10},{10,3},{11,2},{4,13},{5,12},... | collective-permute-start | bytes 196616 | tf_op jit(solution)/shard_map/ppermute | solution.py:310
  78.0 0.0 collective-permute-done.7.got_x
  78.0 0.0 collective-permute-done.8.got_y
  78.0 3.7 %collective-permute-done.9.got_xy = bf16[2,128,128]{2,1,0:T(8,128)(2,1)S(1)} collective-permute-done((bf16[2,128,128]{2,1,0:T(8,128)(2,1)S(1)}, bf16[2,128,128]{2,1,0:T(8,128)(2,1)S(1)}, u32[]{:S(2)}, u32[]{:S(2)}) %collective-permute-start.9) | collective-permute-done | bytes 65568 | tf_op jit(solution)/shard_map/ppermute | solution.py:310
  81.7 1.4 %all-to-all-done.2.got = bf16[16,88,128]{2,1,0:T(8,128)(2,1)S(1)} async-done(((bf16[16,88,128]{2,1,0:T(8,128)(2,1)}), bf16[16,88,128]{2,1,0:T(8,128)(2,1)S(1)}, u32[]{:S(2)}, u32[]{:S(2)}) %all-to-all-start.2) | async-done | bytes 360480 | tf_op jit(solution)/shard_map/all_to_all | solution.py:311
  83.2 0.0 copy-done
  83.2 0.7 finish.1
  83.8 3.6 %collective-permute-start.10 = (f32[64,128]{1,0:T(8,128)S(1)}, f32[64,128]{1,0:T(8,128)S(1)}, u32[]{:S(2)}, u32[]{:S(2)}) collective-permute-start(f32[64,128]{1,0:T(8,128)S(1)} %get-tuple-element.52.mine), channel_id=1, source_target_pairs={{0,16},{16,0},{1,17},{17,1},{2,18},{18,2},{3,19},{19,3},{4,20},{20... | collective-permute-start | bytes 98312 | tf_op jit(solution)/shard_map/ppermute | solution.py:319
  87.4 0.9 home.1
  88.3 0.0 collective-permute-done.10.other
  88.3 0.6 codes.1
  (2 shorter events, 0.0 us)
Async XLA Ops:
  2.7 4.5 %copy-start.1 = (bf16[64,1408]{1,0:T(8,128)(2,1)S(1)}, bf16[64,1408]{1,0:T(8,128)(2,1)}, u32[]{:S(2)}) copy-start(bf16[64,1408]{1,0:T(8,128)(2,1)} %get-tuple-element.32.pack) | copy-start | bytes 540676
  2.7 12.7 %all-to-all-start = ((bf16[4,128,1024]{2,1,0:T(8,128)(2,1)}), bf16[4,128,1024]{2,1,0:T(8,128)(2,1)S(1)}, u32[]{:S(2)}, u32[]{:S(2)}) async-start(bf16[4,128,1024]{2,1,0:T(8,128)(2,1)} %get-tuple-element.31), calls=%async_computation | async-start | bytes 2097152 | tf_op jit(solution)/shard_map/all_to_all | solution.py:268
  7.2 21.2 %collective-permute-start.2 = (bf16[64,1408]{1,0:T(8,128)(2,1)S(1)}, bf16[64,1408]{1,0:T(8,128)(2,1)S(1)}, u32[]{:S(2)}, u32[]{:S(2)}) collective-permute-start(bf16[64,1408]{1,0:T(8,128)(2,1)S(1)} %copy-done.1), channel_id=1, source_target_pairs={{23,16},{18,17},{17,18},{20,19},{19,20},{22,21},{21,22},{16,23},{3... | collective-permute-start | bytes 540680 | tf_op jit(solution)/shard_map/ppermute | solution.py:267
  13.4 15.1 %collective-permute-start.1 = (bf16[64,1408]{1,0:T(8,128)(2,1)S(1)}, bf16[64,1408]{1,0:T(8,128)(2,1)S(1)}, u32[]{:S(2)}, u32[]{:S(2)}) collective-permute-start(bf16[64,1408]{1,0:T(8,128)(2,1)S(1)} %copy-done.1), channel_id=1, source_target_pairs={{5,0},{4,1},{7,2},{6,3},{1,4},{0,5},{3,6},{2,7},{22,16},{19,17},{1... | collective-permute-start | bytes 540680 | tf_op jit(solution)/shard_map/ppermute | solution.py:267
  15.5 15.2 %collective-permute-start = (bf16[512,1024]{1,0:T(8,128)(2,1)S(1)}, bf16[512,1024]{1,0:T(8,128)(2,1)S(1)}, u32[]{:S(2)}, u32[]{:S(2)}) collective-permute-start(bf16[512,1024]{1,0:T(8,128)(2,1)S(1)} %bitcast.8), channel_id=1, source_target_pairs={{0,16},{16,0},{1,17},{17,1},{2,18},{18,2},{3,19},{19,3},{4,20},{20... | collective-permute-start | bytes 3145736 | tf_op jit(solution)/shard_map/ppermute | solution.py:277
  33.4 21.6 %all-to-all-start.1 = ((bf16[32,32,128]{2,1,0:T(8,128)(2,1)}), bf16[32,32,128]{2,1,0:T(8,128)(2,1)S(1)}, u32[]{:S(2)}, u32[]{:S(2)}) async-start(bf16[32,32,128]{2,1,0:T(8,128)(2,1)} %get-tuple-element.38), calls=%async_computation.1 | async-start | bytes 524288 | tf_op jit(solution)/shard_map/all_to_all | solution.py:304
  40.2 9.5 %collective-permute-start.3 = (bf16[144,128]{1,0:T(8,128)(2,1)S(1)}, bf16[144,128]{1,0:T(8,128)(2,1)S(1)}, u32[]{:S(2)}, u32[]{:S(2)}) collective-permute-start(bf16[144,128]{1,0:T(8,128)(2,1)S(1)} %get-tuple-element.39), channel_id=1, source_target_pairs={{0,0},{1,1},{2,2},{3,3},{4,4},{5,5},{6,6},{7,7},{16,22},{17,19},{1... | collective-permute-start | bytes 110600 | tf_op jit(solution)/shard_map/ppermute | solution.py:298
  45.7 6.3 %collective-permute-start.4 = (bf16[144,128]{1,0:T(8,128)(2,1)S(1)}, bf16[144,128]{1,0:T(8,128)(2,1)S(1)}, u32[]{:S(2)}, u32[]{:S(2)}) collective-permute-start(bf16[144,128]{1,0:T(8,128)(2,1)S(1)} %get-tuple-element.40), channel_id=1, source_target_pairs={{0,5},{1,4},{2,7},{3,6},{4,1},{5,0},{6,3},{7,2},{16,23},{17,18},{1... | collective-permute-start | bytes 110600 | tf_op jit(solution)/shard_map/ppermute | solution.py:298
  47.8 7.2 %collective-permute-start.6 = (bf16[4,128,128]{2,1,0:T(8,128)(2,1)S(1)}, bf16[4,128,128]{2,1,0:T(8,128)(2,1)S(1)}, u32[]{:S(2)}, u32[]{:S(2)}) collective-permute-start(bf16[4,128,128]{2,1,0:T(8,128)(2,1)S(1)} %get-tuple-element.42), channel_id=1, source_target_pairs={{0,16},{16,0},{1,17},{17,1},{2,18},{18,2},{3,19},{19,3},{4,20},{20... | collective-permute-start | bytes 393224 | tf_op jit(solution)/shard_map/ppermute | solution.py:299
  51.9 3.1 %collective-permute-start.5 = (bf16[80,128]{1,0:T(8,128)(2,1)S(1)}, bf16[80,128]{1,0:T(8,128)(2,1)S(1)}, u32[]{:S(2)}, u32[]{:S(2)}) collective-permute-start(bf16[80,128]{1,0:T(8,128)(2,1)S(1)} %get-tuple-element.41), channel_id=1, source_target_pairs={{0,16},{16,0},{1,17},{17,1},{2,18},{18,2},{3,19},{19,3},{4,20},{20... | collective-permute-start | bytes 61448 | tf_op jit(solution)/shard_map/ppermute | solution.py:303
  56.0 27.1 %all-to-all-start.2 = ((bf16[16,88,128]{2,1,0:T(8,128)(2,1)}), bf16[16,88,128]{2,1,0:T(8,128)(2,1)S(1)}, u32[]{:S(2)}, u32[]{:S(2)}) async-start(bf16[16,88,128]{2,1,0:T(8,128)(2,1)} %middle.1), calls=%async_computation.2 | async-start | bytes 720896 | tf_op jit(solution)/shard_map/all_to_all | solution.py:311
  68.7 14.5 %copy-start = (f32[1,256,64]{1,2,0:T(8,128)S(1)}, f32[1,256,64]{1,2,0:T(8,128)}, u32[]{:S(2)}) copy-start(f32[1,256,64]{1,2,0:T(8,128)} %param.5) | copy-start | bytes 196612
  68.7 9.3 %collective-permute-start.7 = (bf16[2,128,128]{2,1,0:T(8,128)(2,1)S(1)}, bf16[2,128,128]{2,1,0:T(8,128)(2,1)S(1)}, u32[]{:S(2)}, u32[]{:S(2)}) collective-permute-start(bf16[2,128,128]{2,1,0:T(8,128)(2,1)S(1)} %get-tuple-element.48), channel_id=1, source_target_pairs={{0,8},{8,0},{1,9},{9,1},{2,10},{10,2},{3,11},{11,3},{4,12},{12,4},... | collective-permute-start | bytes 196616 | tf_op jit(solution)/shard_map/ppermute | solution.py:308
  71.3 6.7 %collective-permute-start.8 = (bf16[2,128,128]{2,1,0:T(8,128)(2,1)S(1)}, bf16[2,128,128]{2,1,0:T(8,128)(2,1)S(1)}, u32[]{:S(2)}, u32[]{:S(2)}) collective-permute-start(bf16[2,128,128]{2,1,0:T(8,128)(2,1)S(1)} %get-tuple-element.49), channel_id=1, source_target_pairs={{0,1},{1,0},{2,3},{3,2},{4,5},{5,4},{6,7},{7,6},{8,9},{9,8},{10,11... | collective-permute-start | bytes 196616 | tf_op jit(solution)/shard_map/ppermute | solution.py:309
  75.5 6.2 %collective-permute-start.9 = (bf16[2,128,128]{2,1,0:T(8,128)(2,1)S(1)}, bf16[2,128,128]{2,1,0:T(8,128)(2,1)S(1)}, u32[]{:S(2)}, u32[]{:S(2)}) collective-permute-start(bf16[2,128,128]{2,1,0:T(8,128)(2,1)S(1)} %get-tuple-element.50), channel_id=1, source_target_pairs={{0,9},{1,8},{8,1},{9,0},{2,11},{3,10},{10,3},{11,2},{4,13},{5,12},... | collective-permute-start | bytes 196616 | tf_op jit(solution)/shard_map/ppermute | solution.py:310
  83.8 4.4 %collective-permute-start.10 = (f32[64,128]{1,0:T(8,128)S(1)}, f32[64,128]{1,0:T(8,128)S(1)}, u32[]{:S(2)}, u32[]{:S(2)}) collective-permute-start(f32[64,128]{1,0:T(8,128)S(1)} %get-tuple-element.52.mine), channel_id=1, source_target_pairs={{0,16},{16,0},{1,17},{17,1},{2,18},{18,2},{3,19},{19,3},{4,20},{20... | collective-permute-start | bytes 98312 | tf_op jit(solution)/shard_map/ppermute | solution.py:319

commit v15 on v14

--- a/solution.py
+++ b/solution.py
@@ -305,11 +305,11 @@
     got, half, got_core = lax.optimization_barrier((got, half, got_core))
     (send,) = call(middle_kernel, "middle", [((16, 88, 128), BF)], (got, keep, half))
     gives = call(second_kernel, "second", [pair, pair, pair], (early, got_core))
+    got_xy = lax.ppermute(gives[2], ("xl", "yl"), [(0, 3), (1, 2), (2, 1), (3, 0)])
     got_x = lax.ppermute(gives[0], "xl", swap)
     got_y = lax.ppermute(gives[1], "yl", swap)
-    got_xy = lax.ppermute(gives[2], ("xl", "yl"), [(0, 3), (1, 2), (2, 1), (3, 0)])
     got = lax.all_to_all(send, FAR, 0, 0, tiled=True)
-    got, got_x, got_y, got_xy = lax.optimization_barrier((got, got_x, got_y, got_xy))
+    got, got_xy, got_x, got_y = lax.optimization_barrier((got, got_xy, got_x, got_y))
     cross, fresh = call(
         finish_kernel,
         "finish",

time: 89.8 us -> 89.8 us (level)
    ppermute x1, waiting for transfers between devices: 3.73 us -> 0.01 us  [per_device(): lax.ppermute(gives[2], ('xl', 'yl'), [(0, 3), (1, 2), (2, 1), (3, 0)])]
    ppermute x1, waiting for transfers between devices: 0.01 us -> 2.33 us  [per_device(): got_y = lax.ppermute(gives[1], 'yl', swap)]
    ppermute x1, starting transfers between devices: 4.21 us -> 1.92 us  [per_device(): got_y = lax.ppermute(gives[1], 'yl', swap)]
    ppermute x1, starting transfers between devices: 2.44 us -> 4.59 us  [per_device(): lax.ppermute(gives[2], ('xl', 'yl'), [(0, 3), (1, 2), (2, 1), (3, 0)])]
    ppermute x1, waiting for transfers between devices: 0.01 us -> 1.04 us  [per_device(): got_x = lax.ppermute(gives[0], 'xl', swap)]
  transfers between devices with their start and end apart: 14 -> 14, of which waited for: 6 -> 7; matrix products, arithmetic and copies ran while one was open for 0% -> 0% of each run, Pallas kernels for 3% -> 3%
where the time goes in v15:
time: 89.8 us; the launch traced here: 88.9 us
  starting transfers between devices  69.5 us (77%)
  Pallas kernels  10 us (11%)
  waiting for transfers between devices  8.57 us (10%)
    ppermute x1, starting transfers between devices, per_device(): other = lax.ppermute(mine, 'core', swap)  13 us
    all_to_all x1, starting transfers between devices, per_device(): got = lax.all_to_all(send, FAR, 0, 0, tiled=True)  12.6 us
    ppermute x2, starting transfers between devices, per_device(): packs.append(lax.ppermute(pack, ('core', 'yh', 'yl'), pairs))  8.06 us
    pallas_call x9, Pallas kernels, call(): pl.pallas_call(kernel, out_shape=tuple((jax.ShapeDtypeStruct(*o) for o in...  7.89 us
    ppermute x2, starting transfers between devices, per_device(): moved.append(lax.ppermute(totals[i], ('core', 'yh', 'yl'), pairs))  7.59 us
    all_to_all x1, starting transfers between devices, per_device(): got = lax.all_to_all(send, NEAR, 0, 0, tiled=True)  6.82 us
    ppermute x1, starting transfers between devices, per_device(): lax.ppermute(gives[2], ('xl', 'yl'), [(0, 3), (1, 2), (2, 1), (3, 0)])  4.59 us
    all_to_all x1, starting transfers between devices, per_device(): lax.all_to_all(copies, ('xl', 'yl'), 0, 0, tiled=True).reshape(512, 1024)  4.45 us
  transfers between devices with their start and end apart: 14, of which 7 were waited for; matrix products, arithmetic and copies ran while one was open for 0% of the time, Pallas kernels for 3%

profile of v15, /device:TPU:1, one launch (start us, length us, event | category | flops | bytes accessed | tf_op | source)
XLA Modules:
  0.0 88.9 jit_solution(4855347790719467498)
XLA Ops:
  0.6 2.1 %open.1 = (bf16[64,1408]{1,0:T(8,128)(2,1)}, bf16[4,128,1024]{2,1,0:T(8,128)(2,1)}) custom-call(bf16[128,1024]{1,0:T(8,128)(2,1)} %samples.1, bf16[64,1024]{1,0:T(8,128)(2,1)} %bitcast.12, f32[64,256]{1,0:T(8,128)} %bitcast.10), custom_call_target="tpu_custom_call" | custom-call | tf_op jit(solution)/shard_map/open/pallas_call | solution.py:248
  2.7 0.0 copy-start.1
  2.7 4.5 %all-to-all-start = ((bf16[4,128,1024]{2,1,0:T(8,128)(2,1)}), bf16[4,128,1024]{2,1,0:T(8,128)(2,1)S(1)}, u32[]{:S(2)}, u32[]{:S(2)}) async-start(bf16[4,128,1024]{2,1,0:T(8,128)(2,1)} %get-tuple-element.31), calls=%async_computation | async-start | bytes 2097152 | tf_op jit(solution)/shard_map/all_to_all | solution.py:268
  7.2 0.0 copy-done.1
  7.2 6.1 %collective-permute-start.2 = (bf16[64,1408]{1,0:T(8,128)(2,1)S(1)}, bf16[64,1408]{1,0:T(8,128)(2,1)S(1)}, u32[]{:S(2)}, u32[]{:S(2)}) collective-permute-start(bf16[64,1408]{1,0:T(8,128)(2,1)S(1)} %copy-done.1), channel_id=1, source_target_pairs={{23,16},{18,17},{17,18},{20,19},{19,20},{22,21},{21,22},{16,23},{3... | collective-permute-start | bytes 540680 | tf_op jit(solution)/shard_map/ppermute | solution.py:267
  13.4 1.9 %collective-permute-start.1 = (bf16[64,1408]{1,0:T(8,128)(2,1)S(1)}, bf16[64,1408]{1,0:T(8,128)(2,1)S(1)}, u32[]{:S(2)}, u32[]{:S(2)}) collective-permute-start(bf16[64,1408]{1,0:T(8,128)(2,1)S(1)} %copy-done.1), channel_id=1, source_target_pairs={{5,0},{4,1},{7,2},{6,3},{1,4},{0,5},{3,6},{2,7},{22,16},{19,17},{1... | collective-permute-start | bytes 540680 | tf_op jit(solution)/shard_map/ppermute | solution.py:267
  15.3 0.2 all-to-all-done
  15.5 13.0 %collective-permute-start = (bf16[512,1024]{1,0:T(8,128)(2,1)S(1)}, bf16[512,1024]{1,0:T(8,128)(2,1)S(1)}, u32[]{:S(2)}, u32[]{:S(2)}) collective-permute-start(bf16[512,1024]{1,0:T(8,128)(2,1)S(1)} %bitcast.8), channel_id=1, source_target_pairs={{0,16},{16,0},{1,17},{17,1},{2,18},{18,2},{3,19},{19,3},{4,20},{20... | collective-permute-start | bytes 3145736 | tf_op jit(solution)/shard_map/ppermute | solution.py:277
  28.4 0.0 collective-permute-done.2.second
  28.5 0.0 collective-permute-done.1.first
  28.5 0.1 prepare.1
  28.6 1.8 %early.1 = (f32[512,256]{1,0:T(8,128)S(1)}, f32[128,1024]{1,0:T(8,128)S(1)}, bf16[4,128,128]{2,1,0:T(8,128)(2,1)S(1)}) custom-call(bf16[512,1024]{1,0:T(8,128)(2,1)S(1)} %bitcast.9, bf16[128,1024]{1,0:T(8,128)(2,1)S(1)} %get-tuple-element.33.turn, bf16[128,512]{1,0:T(8,128)(2,1)S(1)} %get-tuple-element.34.codes_t, bf16[512,256]{1,0:T(8,128)(2,1)S(1)} %get-tuple-element.35.left), custom_call_target="tpu_custom_call" | custom-call | bytes 8000000 | tf_op jit(solution)/shard_map/early/pallas_call | solution.py:236
  30.4 0.3 collective-permute-done.samples
  30.7 2.7 %late.1 = (bf16[32,32,128]{2,1,0:T(8,128)(2,1)}, bf16[4,128,128]{2,1,0:T(8,128)(2,1)S(1)}, bf16[144,128]{1,0:T(8,128)(2,1)S(1)}, bf16[144,128]{1,0:T(8,128)(2,1)S(1)}) custom-call(bf16[512,1024]{1,0:T(8,128)(2,1)S(1)} %collective-permute-done.samples, bf16[128,1024]{1,0:T(8,128)(2,1)S(1)} %get-tuple-element.33.turn, ...), custom_call_target="tpu_custom_call" | custom-call | bytes 8000000 | tf_op jit(solution)/shard_map/late/pallas_call | solution.py:236
  33.4 6.8 %all-to-all-start.1 = ((bf16[32,32,128]{2,1,0:T(8,128)(2,1)}), bf16[32,32,128]{2,1,0:T(8,128)(2,1)S(1)}, u32[]{:S(2)}, u32[]{:S(2)}) async-start(bf16[32,32,128]{2,1,0:T(8,128)(2,1)} %get-tuple-element.38), calls=%async_computation.1 | async-start | bytes 524288 | tf_op jit(solution)/shard_map/all_to_all | solution.py:304
  40.2 5.4 %collective-permute-start.3 = (bf16[144,128]{1,0:T(8,128)(2,1)S(1)}, bf16[144,128]{1,0:T(8,128)(2,1)S(1)}, u32[]{:S(2)}, u32[]{:S(2)}) collective-permute-start(bf16[144,128]{1,0:T(8,128)(2,1)S(1)} %get-tuple-element.39), channel_id=1, source_target_pairs={{0,0},{1,1},{2,2},{3,3},{4,4},{5,5},{6,6},{7,7},{16,22},{17,19},{1... | collective-permute-start | bytes 110600 | tf_op jit(solution)/shard_map/ppermute | solution.py:298
  45.7 2.2 %collective-permute-start.4 = (bf16[144,128]{1,0:T(8,128)(2,1)S(1)}, bf16[144,128]{1,0:T(8,128)(2,1)S(1)}, u32[]{:S(2)}, u32[]{:S(2)}) collective-permute-start(bf16[144,128]{1,0:T(8,128)(2,1)S(1)} %get-tuple-element.40), channel_id=1, source_target_pairs={{0,5},{1,4},{2,7},{3,6},{4,1},{5,0},{6,3},{7,2},{16,23},{17,18},{1... | collective-permute-start | bytes 110600 | tf_op jit(solution)/shard_map/ppermute | solution.py:298
  47.8 1.9 %collective-permute-start.6 = (bf16[4,128,128]{2,1,0:T(8,128)(2,1)S(1)}, bf16[4,128,128]{2,1,0:T(8,128)(2,1)S(1)}, u32[]{:S(2)}, u32[]{:S(2)}) collective-permute-start(bf16[4,128,128]{2,1,0:T(8,128)(2,1)S(1)} %get-tuple-element.42), channel_id=1, source_target_pairs={{0,16},{16,0},{1,17},{17,1},{2,18},{18,2},{3,19},{19,3},{4,20},{20... | collective-permute-start | bytes 393224 | tf_op jit(solution)/shard_map/ppermute | solution.py:299
  49.8 0.0 collective-permute-done.3.first
  49.8 2.1 %collective-permute-done.4.second = bf16[144,128]{1,0:T(8,128)(2,1)S(1)} collective-permute-done((bf16[144,128]{1,0:T(8,128)(2,1)S(1)}, bf16[144,128]{1,0:T(8,128)(2,1)S(1)}, u32[]{:S(2)}, u32[]{:S(2)}) %collective-permute-start.4) | collective-permute-done | bytes 36896 | tf_op jit(solution)/shard_map/ppermute | solution.py:298
  51.9 2.3 %collective-permute-start.5 = (bf16[80,128]{1,0:T(8,128)(2,1)S(1)}, bf16[80,128]{1,0:T(8,128)(2,1)S(1)}, u32[]{:S(2)}, u32[]{:S(2)}) collective-permute-start(bf16[80,128]{1,0:T(8,128)(2,1)S(1)} %get-tuple-element.41), channel_id=1, source_target_pairs={{0,16},{16,0},{1,17},{17,1},{2,18},{18,2},{3,19},{19,3},{4,20},{20... | collective-permute-start | bytes 61448 | tf_op jit(solution)/shard_map/ppermute | solution.py:303
  54.2 0.8 collective-permute-done.5.half
  55.0 0.0 collective-permute-done.6.got_core
  55.0 0.0 all-to-all-done.1.got
  55.0 1.0 %middle.1 = bf16[16,88,128]{2,1,0:T(8,128)(2,1)} custom-call(bf16[32,32,128]{2,1,0:T(8,128)(2,1)S(1)} %all-to-all-done.1.got, f32[80,128]{1,0:T(8,128)S(1)} %get-tuple-element.44.keep, bf16[80,128]{1,0:T(8,128)(2,1)S(1)} %collective-permute-done.5.half), custom_call_target="tpu_custom_call" | custom-call | tf_op jit(solution)/shard_map/middle/pallas_call | solution.py:236
  56.0 12.6 %all-to-all-start.2 = ((bf16[16,88,128]{2,1,0:T(8,128)(2,1)}), bf16[16,88,128]{2,1,0:T(8,128)(2,1)S(1)}, u32[]{:S(2)}, u32[]{:S(2)}) async-start(bf16[16,88,128]{2,1,0:T(8,128)(2,1)} %middle.1), calls=%async_computation.2 | async-start | bytes 720896 | tf_op jit(solution)/shard_map/all_to_all | solution.py:311
  68.7 0.0 copy-start
  68.7 4.6 %collective-permute-start.7 = (bf16[2,128,128]{2,1,0:T(8,128)(2,1)S(1)}, bf16[2,128,128]{2,1,0:T(8,128)(2,1)S(1)}, u32[]{:S(2)}, u32[]{:S(2)}) collective-permute-start(bf16[2,128,128]{2,1,0:T(8,128)(2,1)S(1)} %get-tuple-element.48), channel_id=1, source_target_pairs={{0,9},{1,8},{8,1},{9,0},{2,11},{3,10},{10,3},{11,2},{4,13},{5,12},... | collective-permute-start | bytes 196616 | tf_op jit(solution)/shard_map/ppermute | solution.py:308
  73.3 2.7 %collective-permute-start.8 = (bf16[2,128,128]{2,1,0:T(8,128)(2,1)S(1)}, bf16[2,128,128]{2,1,0:T(8,128)(2,1)S(1)}, u32[]{:S(2)}, u32[]{:S(2)}) collective-permute-start(bf16[2,128,128]{2,1,0:T(8,128)(2,1)S(1)} %get-tuple-element.49), channel_id=1, source_target_pairs={{0,8},{8,0},{1,9},{9,1},{2,10},{10,2},{3,11},{11,3},{4,12},{12,4},... | collective-permute-start | bytes 196616 | tf_op jit(solution)/shard_map/ppermute | solution.py:309
  76.0 1.9 %collective-permute-start.9 = (bf16[2,128,128]{2,1,0:T(8,128)(2,1)S(1)}, bf16[2,128,128]{2,1,0:T(8,128)(2,1)S(1)}, u32[]{:S(2)}, u32[]{:S(2)}) collective-permute-start(bf16[2,128,128]{2,1,0:T(8,128)(2,1)S(1)} %get-tuple-element.50), channel_id=1, source_target_pairs={{0,1},{1,0},{2,3},{3,2},{4,5},{5,4},{6,7},{7,6},{8,9},{9,8},{10,11... | collective-permute-start | bytes 196616 | tf_op jit(solution)/shard_map/ppermute | solution.py:310
  78.0 0.0 collective-permute-done.7.got_xy
  78.0 1.0 %collective-permute-done.8.got_x = bf16[2,128,128]{2,1,0:T(8,128)(2,1)S(1)} collective-permute-done((bf16[2,128,128]{2,1,0:T(8,128)(2,1)S(1)}, bf16[2,128,128]{2,1,0:T(8,128)(2,1)S(1)}, u32[]{:S(2)}, u32[]{:S(2)}) %collective-permute-start.8) | collective-permute-done | bytes 65568 | tf_op jit(solution)/shard_map/ppermute | solution.py:309
  79.0 2.3 %collective-permute-done.9.got_y = bf16[2,128,128]{2,1,0:T(8,128)(2,1)S(1)} collective-permute-done((bf16[2,128,128]{2,1,0:T(8,128)(2,1)S(1)}, bf16[2,128,128]{2,1,0:T(8,128)(2,1)S(1)}, u32[]{:S(2)}, u32[]{:S(2)}) %collective-permute-start.9) | collective-permute-done | bytes 65568 | tf_op jit(solution)/shard_map/ppermute | solution.py:310
  81.3 1.8 %all-to-all-done.2.got = bf16[16,88,128]{2,1,0:T(8,128)(2,1)S(1)} async-done(((bf16[16,88,128]{2,1,0:T(8,128)(2,1)}), bf16[16,88,128]{2,1,0:T(8,128)(2,1)S(1)}, u32[]{:S(2)}, u32[]{:S(2)}) %all-to-all-start.2) | async-done | bytes 360480 | tf_op jit(solution)/shard_map/all_to_all | solution.py:311
  83.1 0.0 copy-done
  83.1 0.7 finish.1
  83.8 3.6 %collective-permute-start.10 = (f32[64,128]{1,0:T(8,128)S(1)}, f32[64,128]{1,0:T(8,128)S(1)}, u32[]{:S(2)}, u32[]{:S(2)}) collective-permute-start(f32[64,128]{1,0:T(8,128)S(1)} %get-tuple-element.52.mine), channel_id=1, source_target_pairs={{0,16},{16,0},{1,17},{17,1},{2,18},{18,2},{3,19},{19,3},{4,20},{20... | collective-permute-start | bytes 98312 | tf_op jit(solution)/shard_map/ppermute | solution.py:319
  87.4 0.9 home.1
  88.3 0.0 collective-permute-done.10.other
  88.3 0.6 codes.1
  (2 shorter events, 0.0 us)
Async XLA Ops:
  2.7 4.5 %copy-start.1 = (bf16[64,1408]{1,0:T(8,128)(2,1)S(1)}, bf16[64,1408]{1,0:T(8,128)(2,1)}, u32[]{:S(2)}) copy-start(bf16[64,1408]{1,0:T(8,128)(2,1)} %get-tuple-element.32.pack) | copy-start | bytes 540676
  2.7 12.7 %all-to-all-start = ((bf16[4,128,1024]{2,1,0:T(8,128)(2,1)}), bf16[4,128,1024]{2,1,0:T(8,128)(2,1)S(1)}, u32[]{:S(2)}, u32[]{:S(2)}) async-start(bf16[4,128,1024]{2,1,0:T(8,128)(2,1)} %get-tuple-element.31), calls=%async_computation | async-start | bytes 2097152 | tf_op jit(solution)/shard_map/all_to_all | solution.py:268
  7.2 21.2 %collective-permute-start.2 = (bf16[64,1408]{1,0:T(8,128)(2,1)S(1)}, bf16[64,1408]{1,0:T(8,128)(2,1)S(1)}, u32[]{:S(2)}, u32[]{:S(2)}) collective-permute-start(bf16[64,1408]{1,0:T(8,128)(2,1)S(1)} %copy-done.1), channel_id=1, source_target_pairs={{23,16},{18,17},{17,18},{20,19},{19,20},{22,21},{21,22},{16,23},{3... | collective-permute-start | bytes 540680 | tf_op jit(solution)/shard_map/ppermute | solution.py:267
  13.4 15.1 %collective-permute-start.1 = (bf16[64,1408]{1,0:T(8,128)(2,1)S(1)}, bf16[64,1408]{1,0:T(8,128)(2,1)S(1)}, u32[]{:S(2)}, u32[]{:S(2)}) collective-permute-start(bf16[64,1408]{1,0:T(8,128)(2,1)S(1)} %copy-done.1), channel_id=1, source_target_pairs={{5,0},{4,1},{7,2},{6,3},{1,4},{0,5},{3,6},{2,7},{22,16},{19,17},{1... | collective-permute-start | bytes 540680 | tf_op jit(solution)/shard_map/ppermute | solution.py:267
  15.5 15.2 %collective-permute-start = (bf16[512,1024]{1,0:T(8,128)(2,1)S(1)}, bf16[512,1024]{1,0:T(8,128)(2,1)S(1)}, u32[]{:S(2)}, u32[]{:S(2)}) collective-permute-start(bf16[512,1024]{1,0:T(8,128)(2,1)S(1)} %bitcast.8), channel_id=1, source_target_pairs={{0,16},{16,0},{1,17},{17,1},{2,18},{18,2},{3,19},{19,3},{4,20},{20... | collective-permute-start | bytes 3145736 | tf_op jit(solution)/shard_map/ppermute | solution.py:277
  33.4 21.6 %all-to-all-start.1 = ((bf16[32,32,128]{2,1,0:T(8,128)(2,1)}), bf16[32,32,128]{2,1,0:T(8,128)(2,1)S(1)}, u32[]{:S(2)}, u32[]{:S(2)}) async-start(bf16[32,32,128]{2,1,0:T(8,128)(2,1)} %get-tuple-element.38), calls=%async_computation.1 | async-start | bytes 524288 | tf_op jit(solution)/shard_map/all_to_all | solution.py:304
  40.2 9.5 %collective-permute-start.3 = (bf16[144,128]{1,0:T(8,128)(2,1)S(1)}, bf16[144,128]{1,0:T(8,128)(2,1)S(1)}, u32[]{:S(2)}, u32[]{:S(2)}) collective-permute-start(bf16[144,128]{1,0:T(8,128)(2,1)S(1)} %get-tuple-element.39), channel_id=1, source_target_pairs={{0,0},{1,1},{2,2},{3,3},{4,4},{5,5},{6,6},{7,7},{16,22},{17,19},{1... | collective-permute-start | bytes 110600 | tf_op jit(solution)/shard_map/ppermute | solution.py:298
  45.7 6.3 %collective-permute-start.4 = (bf16[144,128]{1,0:T(8,128)(2,1)S(1)}, bf16[144,128]{1,0:T(8,128)(2,1)S(1)}, u32[]{:S(2)}, u32[]{:S(2)}) collective-permute-start(bf16[144,128]{1,0:T(8,128)(2,1)S(1)} %get-tuple-element.40), channel_id=1, source_target_pairs={{0,5},{1,4},{2,7},{3,6},{4,1},{5,0},{6,3},{7,2},{16,23},{17,18},{1... | collective-permute-start | bytes 110600 | tf_op jit(solution)/shard_map/ppermute | solution.py:298
  47.8 7.2 %collective-permute-start.6 = (bf16[4,128,128]{2,1,0:T(8,128)(2,1)S(1)}, bf16[4,128,128]{2,1,0:T(8,128)(2,1)S(1)}, u32[]{:S(2)}, u32[]{:S(2)}) collective-permute-start(bf16[4,128,128]{2,1,0:T(8,128)(2,1)S(1)} %get-tuple-element.42), channel_id=1, source_target_pairs={{0,16},{16,0},{1,17},{17,1},{2,18},{18,2},{3,19},{19,3},{4,20},{20... | collective-permute-start | bytes 393224 | tf_op jit(solution)/shard_map/ppermute | solution.py:299
  51.9 3.1 %collective-permute-start.5 = (bf16[80,128]{1,0:T(8,128)(2,1)S(1)}, bf16[80,128]{1,0:T(8,128)(2,1)S(1)}, u32[]{:S(2)}, u32[]{:S(2)}) collective-permute-start(bf16[80,128]{1,0:T(8,128)(2,1)S(1)} %get-tuple-element.41), channel_id=1, source_target_pairs={{0,16},{16,0},{1,17},{17,1},{2,18},{18,2},{3,19},{19,3},{4,20},{20... | collective-permute-start | bytes 61448 | tf_op jit(solution)/shard_map/ppermute | solution.py:303
  56.0 27.0 %all-to-all-start.2 = ((bf16[16,88,128]{2,1,0:T(8,128)(2,1)}), bf16[16,88,128]{2,1,0:T(8,128)(2,1)S(1)}, u32[]{:S(2)}, u32[]{:S(2)}) async-start(bf16[16,88,128]{2,1,0:T(8,128)(2,1)} %middle.1), calls=%async_computation.2 | async-start | bytes 720896 | tf_op jit(solution)/shard_map/all_to_all | solution.py:311
  68.7 14.4 %copy-start = (f32[1,256,64]{1,2,0:T(8,128)S(1)}, f32[1,256,64]{1,2,0:T(8,128)}, u32[]{:S(2)}) copy-start(f32[1,256,64]{1,2,0:T(8,128)} %param.5) | copy-start | bytes 196612
  68.7 9.3 %collective-permute-start.7 = (bf16[2,128,128]{2,1,0:T(8,128)(2,1)S(1)}, bf16[2,128,128]{2,1,0:T(8,128)(2,1)S(1)}, u32[]{:S(2)}, u32[]{:S(2)}) collective-permute-start(bf16[2,128,128]{2,1,0:T(8,128)(2,1)S(1)} %get-tuple-element.48), channel_id=1, source_target_pairs={{0,9},{1,8},{8,1},{9,0},{2,11},{3,10},{10,3},{11,2},{4,13},{5,12},... | collective-permute-start | bytes 196616 | tf_op jit(solution)/shard_map/ppermute | solution.py:308
  73.3 5.7 %collective-permute-start.8 = (bf16[2,128,128]{2,1,0:T(8,128)(2,1)S(1)}, bf16[2,128,128]{2,1,0:T(8,128)(2,1)S(1)}, u32[]{:S(2)}, u32[]{:S(2)}) collective-permute-start(bf16[2,128,128]{2,1,0:T(8,128)(2,1)S(1)} %get-tuple-element.49), channel_id=1, source_target_pairs={{0,8},{8,0},{1,9},{9,1},{2,10},{10,2},{3,11},{11,3},{4,12},{12,4},... | collective-permute-start | bytes 196616 | tf_op jit(solution)/shard_map/ppermute | solution.py:309
  76.0 5.3 %collective-permute-start.9 = (bf16[2,128,128]{2,1,0:T(8,128)(2,1)S(1)}, bf16[2,128,128]{2,1,0:T(8,128)(2,1)S(1)}, u32[]{:S(2)}, u32[]{:S(2)}) collective-permute-start(bf16[2,128,128]{2,1,0:T(8,128)(2,1)S(1)} %get-tuple-element.50), channel_id=1, source_target_pairs={{0,1},{1,0},{2,3},{3,2},{4,5},{5,4},{6,7},{7,6},{8,9},{9,8},{10,11... | collective-permute-start | bytes 196616 | tf_op jit(solution)/shard_map/ppermute | solution.py:310
  83.8 4.5 %collective-permute-start.10 = (f32[64,128]{1,0:T(8,128)S(1)}, f32[64,128]{1,0:T(8,128)S(1)}, u32[]{:S(2)}, u32[]{:S(2)}) collective-permute-start(f32[64,128]{1,0:T(8,128)S(1)} %get-tuple-element.52.mine), channel_id=1, source_target_pairs={{0,16},{16,0},{1,17},{17,1},{2,18},{18,2},{3,19},{19,3},{4,20},{20... | collective-permute-start | bytes 98312 | tf_op jit(solution)/shard_map/ppermute | solution.py:319

commit v16 on v15

--- a/solution.py
+++ b/solution.py
@@ -14,7 +14,7 @@
 SUB = ("xl", "yh", "yl")
 PLACES = (((0, 5), (1, 4)), ((6, 7), (3, 2)))
 FAR = ("z", "xh")
-NEAR = ("core", "xl", "yh", "yl")
+NEAR = ("xl", "yh", "yl")
 BF = jnp.bfloat16
 F32 = jnp.float32
 NT = (((1,), (1,)), ((), ()))
@@ -128,7 +128,7 @@
     ]
     for d in range(32):
         tiles = [piece[8 * d : 8 * d + 8] for piece in pieces]
-        send[d] = jnp.concatenate(tiles, axis=0).astype(BF)
+        send[d & 15, (d >> 4) * 32 : (d >> 4) * 32 + 32, :] = jnp.concatenate(tiles, axis=0).astype(BF)
     low = half_mask((64, 128))
     diagonal = (
         lax.broadcasted_iota(jnp.int32, (128, 128), 0)
@@ -166,44 +166,65 @@
     return [jnp.where(low, a, turned), swap_halves(d), jnp.where(low, turned, a), c]
 
 
-def middle_kernel(got, keep, half, send):
-    low = half_mask((32, 128))
-    columns = []
-    for xl in range(2):
-        total = [jnp.zeros((32, 128), F32)] * 4
-        for yh in range(4):
-            blocks = [got[core * 16 + xl * 8 + yh * 2 + yl].astype(F32) for core in range(2) for yl in range(2)]
-            for p, tile in enumerate(arrange(low, *blocks)):
-                total[(yh + p) & 3] += tile
-        columns += total
+def middle_kernel(got, keep, half, send, columns):
+    low = half_mask((64, 128))
+    for core in range(2):
+
+        @pl.when(lax.axis_index("core") == core)
+        def _():
+            for xl in range(2):
+                total = [None] * 4
+                for yh in range(4):
+                    a, b = (got[xl * 8 + yh * 2 + yl].astype(F32) for yl in range(2))
+                    b = swap_halves(b)
+                    if core == 0:
+                        tiles = ((0, jnp.where(low, a, b)), (2, jnp.where(low, b, a)))
+                    else:
+                        tiles = ((1, b), (3, a))
+                    for p, tile in tiles:
+                        p = (yh + p) & 3
+                        total[p] = tile if total[p] is None else total[p] + tile
+                for p in range(4):
+                    at = (xl * 4 + p) * 32
+                    columns[0, at : at + 32, :] = total[p][:32]
+                    columns[1, at : at + 32, :] = total[p][32:]
+
     r = lax.broadcasted_iota(jnp.int32, (256, 256), 0)
     wanted = (((r >> 1) & 7) << 5) | ((r >> 4) << 1) | (r & 1)
     order = jnp.where(lax.broadcasted_iota(jnp.int32, (256, 256), 1) == wanted, 1.0, 0.0).astype(BF)
-    cross = jnp.dot(
-        order, jnp.concatenate(columns, axis=0).astype(BF), preferred_element_type=F32
-    ).astype(BF)
+    cross = [
+        jnp.dot(order, columns[c].astype(BF), preferred_element_type=F32).astype(BF) for c in range(2)
+    ]
     both = keep[...] + half[...].astype(F32)
     line = both[64:65] + both[65:66]
     both = jnp.concatenate([both[:64], *split(line), jnp.zeros((6, 128), F32)], axis=0).astype(BF)
     for q in range(16):
-        send[q, 0:16, :] = cross[q * 16 : q * 16 + 16]
-        send[q, 16:88, :] = both
-
-
-def finish_kernel(got, codes_t, cross, fresh):
+        for c in range(2):
+            send[q, c * 16 : c * 16 + 16, :] = cross[c][q * 16 : q * 16 + 16]
+        send[q, 32:104, :] = both
+
+
+def finish_kernel(got, codes_t, keep, give):
+    first = lax.axis_index("core") == 0
     total = jnp.sum(got[...].astype(F32), axis=0)
+    keep[64:80, :] = jnp.where(first, total[:16], total[16:32])
+    give[64:80, :] = jnp.where(first, total[16:32], total[:16])
+    sums, count = total[32:96], total[96:97] + total[97:98]
+    sums = jnp.concatenate([sums, swap_halves(sums)], axis=0).T[:64]
+    own = jnp.where(first, codes_t[:, :128], codes_t[:, 128:])
+    fresh = (sums + own) / (count + 1.0)
+    keep[0:64, :] = fresh
+    give[0:64, :] = fresh
+
+
+def codes_kernel(mine, other, codes_t, cross):
+    first = lax.axis_index("core") == 0
+    a, b = mine[0:64, :], other[0:64, :]
+    codes_t[:, :128] = jnp.where(first, a, b)
+    codes_t[:, 128:] = jnp.where(first, b, a)
+    total = mine[64:80, :] + other[64:80, :]
     for n in range(8):
         cross[:, n * 128 : (n + 1) * 128] = total[2 * n : 2 * n + 2]
-    sums, count = total[16:80], total[80:81] + total[81:82]
-    sums = jnp.concatenate([sums, swap_halves(sums)], axis=0).T[:64]
-    own = jnp.where(lax.axis_index("core") == 0, codes_t[:, :128], codes_t[:, 128:])
-    fresh[...] = (sums + own) / (count + 1.0)
-
-
-def codes_kernel(mine, other, codes_t):
-    a, b = mine[...], other[...]
-    codes_t[:, :128] = jnp.where(lax.axis_index("core") == 0, a, b)
-    codes_t[:, 128:] = jnp.where(lax.axis_index("core") == 0, b, a)
 
 
 def second_kernel(early, got_core, give_x, give_y, give_xy):
@@ -232,12 +253,13 @@
             recon[:, pl.ds(at, 128)] = tile.astype(BF)
 
 
-def call(kernel, name, outs, args, flops=0, moved=0):
+def call(kernel, name, outs, args, flops=0, moved=0, scratch=()):
     return pl.pallas_call(
         kernel,
         out_shape=tuple(jax.ShapeDtypeStruct(*o) for o in outs),
         in_specs=[VMEM] * len(args),
         out_specs=(VMEM,) * len(outs),
+        scratch_shapes=list(scratch),
         compiler_params=pltpu.CompilerParams(vmem_limit_bytes=40 * 1024 * 1024),
         cost_estimate=pl.CostEstimate(flops=flops, bytes_accessed=moved, transcendentals=0),
         name=name,
@@ -286,7 +308,7 @@
     send, late, *totals = call(
         late_kernel,
         "late",
-        [((32, 32, 128), BF), block, ((144, 128), BF), ((144, 128), BF)],
+        [((16, 64, 128), BF), block, ((144, 128), BF), ((144, 128), BF)],
         (other, *tools, sums, cross),
         moved=8_000_000,
     )
@@ -303,25 +325,29 @@
     half = lax.ppermute(give, "core", swap)
     got = lax.all_to_all(send, NEAR, 0, 0, tiled=True)
     got, half, got_core = lax.optimization_barrier((got, half, got_core))
-    (send,) = call(middle_kernel, "middle", [((16, 88, 128), BF)], (got, keep, half))
+    (send,) = call(
+        middle_kernel,
+        "middle",
+        [((16, 104, 128), BF)],
+        (got, keep, half),
+        scratch=[pltpu.VMEM((2, 256, 128), F32)],
+    )
     gives = call(second_kernel, "second", [pair, pair, pair], (early, got_core))
     got_xy = lax.ppermute(gives[2], ("xl", "yl"), [(0, 3), (1, 2), (2, 1), (3, 0)])
     got_x = lax.ppermute(gives[0], "xl", swap)
     got_y = lax.ppermute(gives[1], "yl", swap)
     got = lax.all_to_all(send, FAR, 0, 0, tiled=True)
     got, got_xy, got_x, got_y = lax.optimization_barrier((got, got_xy, got_x, got_y))
-    cross, fresh = call(
-        finish_kernel,
-        "finish",
-        [((2, 1024), F32), ((64, 128), F32)],
-        (got, codebook[0].T),
-    )
-    fresh_other = lax.ppermute(fresh, "core", swap)
+    ends = [((80, 128), F32)] * 2
+    mine, give = call(finish_kernel, "finish", ends, (got, codebook[0].T))
+    other = lax.ppermute(give, "core", swap)
     (recon,) = call(
         home_kernel, "home", [((128, 1024), BF)], (early, got_core, got_x, got_y, got_xy)
     )
-    fresh_other, recon = lax.optimization_barrier((fresh_other, recon))
-    (new_codes,) = call(codes_kernel, "codes", [((64, 256), F32)], (fresh, fresh_other))
+    other, recon = lax.optimization_barrier((other, recon))
+    new_codes, cross = call(
+        codes_kernel, "codes", [((64, 256), F32), ((2, 1024), F32)], (mine, other)
+    )
     return recon, new_codes.T[None], cross
 
 

time: 89.8 us -> 90.5 us (level)
  waiting for transfers between devices: 8.57 us -> 9.54 us
    all_to_all x1, waiting for transfers between devices: 1.76 us -> 3.05 us  [per_device(): got = lax.all_to_all(send, FAR, 0, 0, tiled=True)]
where the time goes in v16:
time: 90.5 us; the launch traced here: 89.8 us
  starting transfers between devices  69.9 us (77%)
  Pallas kernels  9.59 us (11%)
  waiting for transfers between devices  9.54 us (11%)
    ppermute x1, starting transfers between devices, per_device(): other = lax.ppermute(mine, 'core', swap)  13 us
    all_to_all x1, starting transfers between devices, per_device(): got = lax.all_to_all(send, FAR, 0, 0, tiled=True)  12.6 us
    ppermute x2, starting transfers between devices, per_device(): packs.append(lax.ppermute(pack, ('core', 'yh', 'yl'), pairs))  8.06 us
    ppermute x2, starting transfers between devices, per_device(): moved.append(lax.ppermute(totals[i], ('core', 'yh', 'yl'), pairs))  7.56 us
    pallas_call x9, Pallas kernels, call(): pl.pallas_call(kernel, out_shape=tuple((jax.ShapeDtypeStruct(*o) for o in...  7.48 us
    all_to_all x1, starting transfers between devices, per_device(): got = lax.all_to_all(send, NEAR, 0, 0, tiled=True)  6.11 us
    all_to_all x1, starting transfers between devices, per_device(): lax.all_to_all(copies, ('xl', 'yl'), 0, 0, tiled=True).reshape(512, 1024)  4.45 us
    ppermute x1, starting transfers between devices, per_device(): lax.ppermute(gives[2], ('xl', 'yl'), [(0, 3), (1, 2), (2, 1), (3, 0)])  4.28 us
  transfers between devices with their start and end apart: 14, of which 7 were waited for; matrix products, arithmetic and copies ran while one was open for 0% of the time, Pallas kernels for 3%

profile of v16, /device:TPU:1, one launch (start us, length us, event | category | flops | bytes accessed | tf_op | source)
XLA Modules:
  0.0 89.8 jit_solution(4749182717855252798)
XLA Ops:
  0.6 2.1 %open.1 = (bf16[64,1408]{1,0:T(8,128)(2,1)}, bf16[4,128,1024]{2,1,0:T(8,128)(2,1)}) custom-call(bf16[128,1024]{1,0:T(8,128)(2,1)} %samples.1, bf16[64,1024]{1,0:T(8,128)(2,1)} %bitcast.12, f32[64,256]{1,0:T(8,128)} %bitcast.10), custom_call_target="tpu_custom_call" | custom-call | tf_op jit(solution)/shard_map/open/pallas_call | solution.py:270
  2.7 0.0 copy-start.1
  2.7 4.5 %all-to-all-start = ((bf16[4,128,1024]{2,1,0:T(8,128)(2,1)}), bf16[4,128,1024]{2,1,0:T(8,128)(2,1)S(1)}, u32[]{:S(2)}, u32[]{:S(2)}) async-start(bf16[4,128,1024]{2,1,0:T(8,128)(2,1)} %get-tuple-element.33), calls=%async_computation | async-start | bytes 2097152 | tf_op jit(solution)/shard_map/all_to_all | solution.py:290
  7.2 0.0 copy-done.1
  7.2 6.1 %collective-permute-start.2 = (bf16[64,1408]{1,0:T(8,128)(2,1)S(1)}, bf16[64,1408]{1,0:T(8,128)(2,1)S(1)}, u32[]{:S(2)}, u32[]{:S(2)}) collective-permute-start(bf16[64,1408]{1,0:T(8,128)(2,1)S(1)} %copy-done.1), channel_id=1, source_target_pairs={{23,16},{18,17},{17,18},{20,19},{19,20},{22,21},{21,22},{16,23},{3... | collective-permute-start | bytes 540680 | tf_op jit(solution)/shard_map/ppermute | solution.py:289
  13.4 1.9 %collective-permute-start.1 = (bf16[64,1408]{1,0:T(8,128)(2,1)S(1)}, bf16[64,1408]{1,0:T(8,128)(2,1)S(1)}, u32[]{:S(2)}, u32[]{:S(2)}) collective-permute-start(bf16[64,1408]{1,0:T(8,128)(2,1)S(1)} %copy-done.1), channel_id=1, source_target_pairs={{5,0},{4,1},{7,2},{6,3},{1,4},{0,5},{3,6},{2,7},{22,16},{19,17},{1... | collective-permute-start | bytes 540680 | tf_op jit(solution)/shard_map/ppermute | solution.py:289
  15.3 0.2 all-to-all-done
  15.5 13.0 %collective-permute-start = (bf16[512,1024]{1,0:T(8,128)(2,1)S(1)}, bf16[512,1024]{1,0:T(8,128)(2,1)S(1)}, u32[]{:S(2)}, u32[]{:S(2)}) collective-permute-start(bf16[512,1024]{1,0:T(8,128)(2,1)S(1)} %bitcast.8), channel_id=1, source_target_pairs={{0,16},{16,0},{1,17},{17,1},{2,18},{18,2},{3,19},{19,3},{4,20},{20... | collective-permute-start | bytes 3145736 | tf_op jit(solution)/shard_map/ppermute | solution.py:299
  28.4 0.0 collective-permute-done.2.second
  28.5 0.0 collective-permute-done.1.first
  28.5 0.1 prepare.1
  28.6 1.8 %early.1 = (f32[512,256]{1,0:T(8,128)S(1)}, f32[128,1024]{1,0:T(8,128)S(1)}, bf16[4,128,128]{2,1,0:T(8,128)(2,1)S(1)}) custom-call(bf16[512,1024]{1,0:T(8,128)(2,1)S(1)} %bitcast.9, bf16[128,1024]{1,0:T(8,128)(2,1)S(1)} %get-tuple-element.35.turn, bf16[128,512]{1,0:T(8,128)(2,1)S(1)} %get-tuple-element.36.codes_t, bf16[512,256]{1,0:T(8,128)(2,1)S(1)} %get-tuple-element.37.left), custom_call_target="tpu_custom_call" | custom-call | bytes 8000000 | tf_op jit(solution)/shard_map/early/pallas_call | solution.py:257
  30.4 0.3 collective-permute-done.samples
  30.7 2.7 %late.1 = (bf16[16,64,128]{2,1,0:T(8,128)(2,1)}, bf16[4,128,128]{2,1,0:T(8,128)(2,1)S(1)}, bf16[144,128]{1,0:T(8,128)(2,1)S(1)}, bf16[144,128]{1,0:T(8,128)(2,1)S(1)}) custom-call(bf16[512,1024]{1,0:T(8,128)(2,1)S(1)} %collective-permute-done.samples, bf16[128,1024]{1,0:T(8,128)(2,1)S(1)} %get-tuple-element.35.turn, ...), custom_call_target="tpu_custom_call" | custom-call | bytes 8000000 | tf_op jit(solution)/shard_map/late/pallas_call | solution.py:257
  33.4 6.1 %all-to-all-start.1 = ((bf16[16,64,128]{2,1,0:T(8,128)(2,1)}), bf16[16,64,128]{2,1,0:T(8,128)(2,1)S(1)}, u32[]{:S(2)}, u32[]{:S(2)}) async-start(bf16[16,64,128]{2,1,0:T(8,128)(2,1)} %get-tuple-element.40), calls=%async_computation.1 | async-start | bytes 524288 | tf_op jit(solution)/shard_map/all_to_all | solution.py:326
  39.5 5.4 %collective-permute-start.3 = (bf16[144,128]{1,0:T(8,128)(2,1)S(1)}, bf16[144,128]{1,0:T(8,128)(2,1)S(1)}, u32[]{:S(2)}, u32[]{:S(2)}) collective-permute-start(bf16[144,128]{1,0:T(8,128)(2,1)S(1)} %get-tuple-element.41), channel_id=1, source_target_pairs={{0,0},{1,1},{2,2},{3,3},{4,4},{5,5},{6,6},{7,7},{16,22},{17,19},{1... | collective-permute-start | bytes 110600 | tf_op jit(solution)/shard_map/ppermute | solution.py:320
  44.9 2.2 %collective-permute-start.4 = (bf16[144,128]{1,0:T(8,128)(2,1)S(1)}, bf16[144,128]{1,0:T(8,128)(2,1)S(1)}, u32[]{:S(2)}, u32[]{:S(2)}) collective-permute-start(bf16[144,128]{1,0:T(8,128)(2,1)S(1)} %get-tuple-element.42), channel_id=1, source_target_pairs={{0,5},{1,4},{2,7},{3,6},{4,1},{5,0},{6,3},{7,2},{16,23},{17,18},{1... | collective-permute-start | bytes 110600 | tf_op jit(solution)/shard_map/ppermute | solution.py:320
  47.1 2.5 %collective-permute-start.6 = (bf16[4,128,128]{2,1,0:T(8,128)(2,1)S(1)}, bf16[4,128,128]{2,1,0:T(8,128)(2,1)S(1)}, u32[]{:S(2)}, u32[]{:S(2)}) collective-permute-start(bf16[4,128,128]{2,1,0:T(8,128)(2,1)S(1)} %get-tuple-element.44), channel_id=1, source_target_pairs={{0,16},{16,0},{1,17},{17,1},{2,18},{18,2},{3,19},{19,3},{4,20},{20... | collective-permute-start | bytes 393224 | tf_op jit(solution)/shard_map/ppermute | solution.py:321
  49.6 0.0 collective-permute-done.3.first
  49.6 1.8 %collective-permute-done.4.second = bf16[144,128]{1,0:T(8,128)(2,1)S(1)} collective-permute-done((bf16[144,128]{1,0:T(8,128)(2,1)S(1)}, bf16[144,128]{1,0:T(8,128)(2,1)S(1)}, u32[]{:S(2)}, u32[]{:S(2)}) %collective-permute-start.4) | collective-permute-done | bytes 36896 | tf_op jit(solution)/shard_map/ppermute | solution.py:320
  51.4 2.3 %collective-permute-start.5 = (bf16[80,128]{1,0:T(8,128)(2,1)S(1)}, bf16[80,128]{1,0:T(8,128)(2,1)S(1)}, u32[]{:S(2)}, u32[]{:S(2)}) collective-permute-start(bf16[80,128]{1,0:T(8,128)(2,1)S(1)} %get-tuple-element.43), channel_id=1, source_target_pairs={{0,16},{16,0},{1,17},{17,1},{2,18},{18,2},{3,19},{19,3},{4,20},{20... | collective-permute-start | bytes 61448 | tf_op jit(solution)/shard_map/ppermute | solution.py:325
  53.8 0.8 collective-permute-done.5.half
  54.6 0.0 collective-permute-done.6.got_core
  54.6 0.0 all-to-all-done.1.got
  54.6 1.1 %middle.1 = bf16[16,104,128]{2,1,0:T(8,128)(2,1)} custom-call(bf16[16,64,128]{2,1,0:T(8,128)(2,1)S(1)} %all-to-all-done.1.got, f32[80,128]{1,0:T(8,128)S(1)} %get-tuple-element.46.keep, bf16[80,128]{1,0:T(8,128)(2,1)S(1)} %collective-permute-done.5.half), custom_call_target="tpu_custom_call" | custom-call | tf_op jit(solution)/shard_map/middle/pallas_call | solution.py:257
  55.7 12.6 %all-to-all-start.2 = ((bf16[16,104,128]{2,1,0:T(8,128)(2,1)}), bf16[16,104,128]{2,1,0:T(8,128)(2,1)S(1)}, u32[]{:S(2)}, u32[]{:S(2)}) async-start(bf16[16,104,128]{2,1,0:T(8,128)(2,1)} %middle.1), calls=%async_computation.2 | async-start | bytes 851968 | tf_op jit(solution)/shard_map/all_to_all | solution.py:339
  68.3 0.0 copy-start
  68.3 4.3 %collective-permute-start.7 = (bf16[2,128,128]{2,1,0:T(8,128)(2,1)S(1)}, bf16[2,128,128]{2,1,0:T(8,128)(2,1)S(1)}, u32[]{:S(2)}, u32[]{:S(2)}) collective-permute-start(bf16[2,128,128]{2,1,0:T(8,128)(2,1)S(1)} %get-tuple-element.50), channel_id=1, source_target_pairs={{0,9},{1,8},{8,1},{9,0},{2,11},{3,10},{10,3},{11,2},{4,13},{5,12},... | collective-permute-start | bytes 196616 | tf_op jit(solution)/shard_map/ppermute | solution.py:336
  72.6 2.9 %collective-permute-start.8 = (bf16[2,128,128]{2,1,0:T(8,128)(2,1)S(1)}, bf16[2,128,128]{2,1,0:T(8,128)(2,1)S(1)}, u32[]{:S(2)}, u32[]{:S(2)}) collective-permute-start(bf16[2,128,128]{2,1,0:T(8,128)(2,1)S(1)} %get-tuple-element.51), channel_id=1, source_target_pairs={{0,8},{8,0},{1,9},{9,1},{2,10},{10,2},{3,11},{11,3},{4,12},{12,4},... | collective-permute-start | bytes 196616 | tf_op jit(solution)/shard_map/ppermute | solution.py:337
  75.5 1.9 %collective-permute-start.9 = (bf16[2,128,128]{2,1,0:T(8,128)(2,1)S(1)}, bf16[2,128,128]{2,1,0:T(8,128)(2,1)S(1)}, u32[]{:S(2)}, u32[]{:S(2)}) collective-permute-start(bf16[2,128,128]{2,1,0:T(8,128)(2,1)S(1)} %get-tuple-element.52), channel_id=1, source_target_pairs={{0,1},{1,0},{2,3},{3,2},{4,5},{5,4},{6,7},{7,6},{8,9},{9,8},{10,11... | collective-permute-start | bytes 196616 | tf_op jit(solution)/shard_map/ppermute | solution.py:338
  77.4 0.0 collective-permute-done.7.got_xy
  77.4 1.5 %collective-permute-done.8.got_x = bf16[2,128,128]{2,1,0:T(8,128)(2,1)S(1)} collective-permute-done((bf16[2,128,128]{2,1,0:T(8,128)(2,1)S(1)}, bf16[2,128,128]{2,1,0:T(8,128)(2,1)S(1)}, u32[]{:S(2)}, u32[]{:S(2)}) %collective-permute-start.8) | collective-permute-done | bytes 65568 | tf_op jit(solution)/shard_map/ppermute | solution.py:337
  78.9 1.9 %collective-permute-done.9.got_y = bf16[2,128,128]{2,1,0:T(8,128)(2,1)S(1)} collective-permute-done((bf16[2,128,128]{2,1,0:T(8,128)(2,1)S(1)}, bf16[2,128,128]{2,1,0:T(8,128)(2,1)S(1)}, u32[]{:S(2)}, u32[]{:S(2)}) %collective-permute-start.9) | collective-permute-done | bytes 65568 | tf_op jit(solution)/shard_map/ppermute | solution.py:338
  80.8 3.0 %all-to-all-done.2.got = bf16[16,104,128]{2,1,0:T(8,128)(2,1)S(1)} async-done(((bf16[16,104,128]{2,1,0:T(8,128)(2,1)}), bf16[16,104,128]{2,1,0:T(8,128)(2,1)S(1)}, u32[]{:S(2)}, u32[]{:S(2)}) %all-to-all-start.2) | async-done | bytes 426016 | tf_op jit(solution)/shard_map/all_to_all | solution.py:339
  83.9 0.0 copy-done
  83.9 0.2 finish.1
  84.0 4.2 %collective-permute-start.10 = (f32[80,128]{1,0:T(8,128)S(1)}, f32[80,128]{1,0:T(8,128)S(1)}, u32[]{:S(2)}, u32[]{:S(2)}) collective-permute-start(f32[80,128]{1,0:T(8,128)S(1)} %get-tuple-element.54), channel_id=1, source_target_pairs={{0,16},{16,0},{1,17},{17,1},{2,18},{18,2},{3,19},{19,3},{4,20},{20... | collective-permute-start | bytes 122888 | tf_op jit(solution)/shard_map/ppermute | solution.py:343
  88.3 0.9 home.1
  89.2 0.0 collective-permute-done.10.other
  89.2 0.6 codes.1
  (2 shorter events, 0.0 us)
Async XLA Ops:
  2.7 4.5 %copy-start.1 = (bf16[64,1408]{1,0:T(8,128)(2,1)S(1)}, bf16[64,1408]{1,0:T(8,128)(2,1)}, u32[]{:S(2)}) copy-start(bf16[64,1408]{1,0:T(8,128)(2,1)} %get-tuple-element.34.pack) | copy-start | bytes 540676
  2.7 12.7 %all-to-all-start = ((bf16[4,128,1024]{2,1,0:T(8,128)(2,1)}), bf16[4,128,1024]{2,1,0:T(8,128)(2,1)S(1)}, u32[]{:S(2)}, u32[]{:S(2)}) async-start(bf16[4,128,1024]{2,1,0:T(8,128)(2,1)} %get-tuple-element.33), calls=%async_computation | async-start | bytes 2097152 | tf_op jit(solution)/shard_map/all_to_all | solution.py:290
  7.2 21.2 %collective-permute-start.2 = (bf16[64,1408]{1,0:T(8,128)(2,1)S(1)}, bf16[64,1408]{1,0:T(8,128)(2,1)S(1)}, u32[]{:S(2)}, u32[]{:S(2)}) collective-permute-start(bf16[64,1408]{1,0:T(8,128)(2,1)S(1)} %copy-done.1), channel_id=1, source_target_pairs={{23,16},{18,17},{17,18},{20,19},{19,20},{22,21},{21,22},{16,23},{3... | collective-permute-start | bytes 540680 | tf_op jit(solution)/shard_map/ppermute | solution.py:289
  13.4 15.1 %collective-permute-start.1 = (bf16[64,1408]{1,0:T(8,128)(2,1)S(1)}, bf16[64,1408]{1,0:T(8,128)(2,1)S(1)}, u32[]{:S(2)}, u32[]{:S(2)}) collective-permute-start(bf16[64,1408]{1,0:T(8,128)(2,1)S(1)} %copy-done.1), channel_id=1, source_target_pairs={{5,0},{4,1},{7,2},{6,3},{1,4},{0,5},{3,6},{2,7},{22,16},{19,17},{1... | collective-permute-start | bytes 540680 | tf_op jit(solution)/shard_map/ppermute | solution.py:289
  15.5 15.2 %collective-permute-start = (bf16[512,1024]{1,0:T(8,128)(2,1)S(1)}, bf16[512,1024]{1,0:T(8,128)(2,1)S(1)}, u32[]{:S(2)}, u32[]{:S(2)}) collective-permute-start(bf16[512,1024]{1,0:T(8,128)(2,1)S(1)} %bitcast.8), channel_id=1, source_target_pairs={{0,16},{16,0},{1,17},{17,1},{2,18},{18,2},{3,19},{19,3},{4,20},{20... | collective-permute-start | bytes 3145736 | tf_op jit(solution)/shard_map/ppermute | solution.py:299
  33.4 21.2 %all-to-all-start.1 = ((bf16[16,64,128]{2,1,0:T(8,128)(2,1)}), bf16[16,64,128]{2,1,0:T(8,128)(2,1)S(1)}, u32[]{:S(2)}, u32[]{:S(2)}) async-start(bf16[16,64,128]{2,1,0:T(8,128)(2,1)} %get-tuple-element.40), calls=%async_computation.1 | async-start | bytes 524288 | tf_op jit(solution)/shard_map/all_to_all | solution.py:326
  39.5 10.1 %collective-permute-start.3 = (bf16[144,128]{1,0:T(8,128)(2,1)S(1)}, bf16[144,128]{1,0:T(8,128)(2,1)S(1)}, u32[]{:S(2)}, u32[]{:S(2)}) collective-permute-start(bf16[144,128]{1,0:T(8,128)(2,1)S(1)} %get-tuple-element.41), channel_id=1, source_target_pairs={{0,0},{1,1},{2,2},{3,3},{4,4},{5,5},{6,6},{7,7},{16,22},{17,19},{1... | collective-permute-start | bytes 110600 | tf_op jit(solution)/shard_map/ppermute | solution.py:320
  44.9 6.5 %collective-permute-start.4 = (bf16[144,128]{1,0:T(8,128)(2,1)S(1)}, bf16[144,128]{1,0:T(8,128)(2,1)S(1)}, u32[]{:S(2)}, u32[]{:S(2)}) collective-permute-start(bf16[144,128]{1,0:T(8,128)(2,1)S(1)} %get-tuple-element.42), channel_id=1, source_target_pairs={{0,5},{1,4},{2,7},{3,6},{4,1},{5,0},{6,3},{7,2},{16,23},{17,18},{1... | collective-permute-start | bytes 110600 | tf_op jit(solution)/shard_map/ppermute | solution.py:320
  47.1 7.5 %collective-permute-start.6 = (bf16[4,128,128]{2,1,0:T(8,128)(2,1)S(1)}, bf16[4,128,128]{2,1,0:T(8,128)(2,1)S(1)}, u32[]{:S(2)}, u32[]{:S(2)}) collective-permute-start(bf16[4,128,128]{2,1,0:T(8,128)(2,1)S(1)} %get-tuple-element.44), channel_id=1, source_target_pairs={{0,16},{16,0},{1,17},{17,1},{2,18},{18,2},{3,19},{19,3},{4,20},{20... | collective-permute-start | bytes 393224 | tf_op jit(solution)/shard_map/ppermute | solution.py:321
  51.4 3.1 %collective-permute-start.5 = (bf16[80,128]{1,0:T(8,128)(2,1)S(1)}, bf16[80,128]{1,0:T(8,128)(2,1)S(1)}, u32[]{:S(2)}, u32[]{:S(2)}) collective-permute-start(bf16[80,128]{1,0:T(8,128)(2,1)S(1)} %get-tuple-element.43), channel_id=1, source_target_pairs={{0,16},{16,0},{1,17},{17,1},{2,18},{18,2},{3,19},{19,3},{4,20},{20... | collective-permute-start | bytes 61448 | tf_op jit(solution)/shard_map/ppermute | solution.py:325
  55.7 28.2 %all-to-all-start.2 = ((bf16[16,104,128]{2,1,0:T(8,128)(2,1)}), bf16[16,104,128]{2,1,0:T(8,128)(2,1)S(1)}, u32[]{:S(2)}, u32[]{:S(2)}) async-start(bf16[16,104,128]{2,1,0:T(8,128)(2,1)} %middle.1), calls=%async_computation.2 | async-start | bytes 851968 | tf_op jit(solution)/shard_map/all_to_all | solution.py:339
  68.3 15.6 %copy-start = (f32[1,256,64]{1,2,0:T(8,128)S(1)}, f32[1,256,64]{1,2,0:T(8,128)}, u32[]{:S(2)}) copy-start(f32[1,256,64]{1,2,0:T(8,128)} %param.5) | copy-start | bytes 196612
  68.3 9.1 %collective-permute-start.7 = (bf16[2,128,128]{2,1,0:T(8,128)(2,1)S(1)}, bf16[2,128,128]{2,1,0:T(8,128)(2,1)S(1)}, u32[]{:S(2)}, u32[]{:S(2)}) collective-permute-start(bf16[2,128,128]{2,1,0:T(8,128)(2,1)S(1)} %get-tuple-element.50), channel_id=1, source_target_pairs={{0,9},{1,8},{8,1},{9,0},{2,11},{3,10},{10,3},{11,2},{4,13},{5,12},... | collective-permute-start | bytes 196616 | tf_op jit(solution)/shard_map/ppermute | solution.py:336
  72.6 6.3 %collective-permute-start.8 = (bf16[2,128,128]{2,1,0:T(8,128)(2,1)S(1)}, bf16[2,128,128]{2,1,0:T(8,128)(2,1)S(1)}, u32[]{:S(2)}, u32[]{:S(2)}) collective-permute-start(bf16[2,128,128]{2,1,0:T(8,128)(2,1)S(1)} %get-tuple-element.51), channel_id=1, source_target_pairs={{0,8},{8,0},{1,9},{9,1},{2,10},{10,2},{3,11},{11,3},{4,12},{12,4},... | collective-permute-start | bytes 196616 | tf_op jit(solution)/shard_map/ppermute | solution.py:337
  75.5 5.3 %collective-permute-start.9 = (bf16[2,128,128]{2,1,0:T(8,128)(2,1)S(1)}, bf16[2,128,128]{2,1,0:T(8,128)(2,1)S(1)}, u32[]{:S(2)}, u32[]{:S(2)}) collective-permute-start(bf16[2,128,128]{2,1,0:T(8,128)(2,1)S(1)} %get-tuple-element.52), channel_id=1, source_target_pairs={{0,1},{1,0},{2,3},{3,2},{4,5},{5,4},{6,7},{7,6},{8,9},{9,8},{10,11... | collective-permute-start | bytes 196616 | tf_op jit(solution)/shard_map/ppermute | solution.py:338
  84.0 5.1 %collective-permute-start.10 = (f32[80,128]{1,0:T(8,128)S(1)}, f32[80,128]{1,0:T(8,128)S(1)}, u32[]{:S(2)}, u32[]{:S(2)}) collective-permute-start(f32[80,128]{1,0:T(8,128)S(1)} %get-tuple-element.54), channel_id=1, source_target_pairs={{0,16},{16,0},{1,17},{17,1},{2,18},{18,2},{3,19},{19,3},{4,20},{20... | collective-permute-start | bytes 122888 | tf_op jit(solution)/shard_map/ppermute | solution.py:343

commit v17 on v15

--- a/solution.py
+++ b/solution.py
@@ -12,7 +12,7 @@
 NAMES = ("z", "xh", "core", "xl", "yh", "yl")
 DP = ("z", "xh", "core")
 SUB = ("xl", "yh", "yl")
-PLACES = (((0, 5), (1, 4)), ((6, 7), (3, 2)))
+PLACES = (((0, 6), (1, 3)), ((7, 5), (2, 4)))
 FAR = ("z", "xh")
 NEAR = ("core", "xl", "yh", "yl")
 BF = jnp.bfloat16
@@ -162,8 +162,8 @@
 
 
 def arrange(low, a, b, c, d):
-    turned = swap_halves(b)
-    return [jnp.where(low, a, turned), swap_halves(d), jnp.where(low, turned, a), c]
+    e, f, g, h = (swap_halves(x) for x in (a, b, c, d))
+    return [jnp.where(low, a, f), jnp.where(low, d, b), jnp.where(low, h, c), jnp.where(low, e, g)]
 
 
 def middle_kernel(got, keep, half, send):
@@ -257,7 +257,7 @@
         name="open",
     )(samples, rotation.T, codebook[0].T)
     packs = []
-    for steps in ((3, 2), (None, 1)):
+    for steps in ((2, 1), (None, 3)):
         pairs = [
             (c * 8 + ((y + step if y & 1 else y - step) & 7), c * 8 + y)
             for c, step in enumerate(steps)
@@ -291,7 +291,7 @@
         moved=8_000_000,
     )
     moved = []
-    for i in range(2):
+    for i in (1, 0):
         pairs = [
             (c * 8 + y, c * 8 + (((y & 6) + PLACES[c][y & 1][i]) & 7)) for c in range(2) for y in range(8)
         ]

time: 89.8 us -> 89.7 us (level)
    ppermute x1, starting transfers between devices: 13 us -> 9.59 us  [per_device(): other = lax.ppermute(mine, 'core', swap)]
    all_to_all x1, waiting for transfers between devices: 1.76 us -> 3.37 us  [per_device(): got = lax.all_to_all(send, FAR, 0, 0, tiled=True)]
    ppermute x2, starting transfers between devices: 8.06 us -> 9.63 us  [per_device(): packs.append(lax.ppermute(pack, ('core', 'yh', 'yl'), pairs))]
    ppermute x1, starting transfers between devices: 4.59 us -> 3.17 us  [per_device(): lax.ppermute(gives[2], ('xl', 'yl'), [(0, 3), (1, 2), (2, 1), (3, 0)])]
    all_to_all x1, starting transfers between devices: 6.82 us -> 7.74 us  [per_device(): got = lax.all_to_all(send, NEAR, 0, 0, tiled=True)]
    ppermute x2, starting transfers between devices: 7.59 us -> 8.49 us  [per_device(): moved.append(lax.ppermute(totals[i], ('core', 'yh', 'yl'), pairs))]
where the time goes in v17:
time: 89.7 us; the launch traced here: 89 us
  starting transfers between devices  68.8 us (77%)
  Pallas kernels  10 us (11%)
  waiting for transfers between devices  9.39 us (10%)
    all_to_all x1, starting transfers between devices, per_device(): got = lax.all_to_all(send, FAR, 0, 0, tiled=True)  12.6 us
    ppermute x2, starting transfers between devices, per_device(): packs.append(lax.ppermute(pack, ('core', 'yh', 'yl'), pairs))  9.63 us
    ppermute x1, starting transfers between devices, per_device(): other = lax.ppermute(mine, 'core', swap)  9.59 us
    ppermute x2, starting transfers between devices, per_device(): moved.append(lax.ppermute(totals[i], ('core', 'yh', 'yl'), pairs))  8.49 us
    pallas_call x9, Pallas kernels, call(): pl.pallas_call(kernel, out_shape=tuple((jax.ShapeDtypeStruct(*o) for o in...  7.93 us
    all_to_all x1, starting transfers between devices, per_device(): got = lax.all_to_all(send, NEAR, 0, 0, tiled=True)  7.74 us
    all_to_all x1, starting transfers between devices, per_device(): lax.all_to_all(copies, ('xl', 'yl'), 0, 0, tiled=True).reshape(512, 1024)  4.45 us
    ppermute x1, starting transfers between devices, per_device(): fresh_other = lax.ppermute(fresh, 'core', swap)  4.03 us
  transfers between devices with their start and end apart: 14, of which 7 were waited for; matrix products, arithmetic and copies ran while one was open for 0% of the time, Pallas kernels for 3%

profile of v17, /device:TPU:1, one launch (start us, length us, event | category | flops | bytes accessed | tf_op | source)
XLA Modules:
  0.0 89.0 jit_solution(16201206526190151494)
XLA Ops:
  0.6 2.1 %open.1 = (bf16[64,1408]{1,0:T(8,128)(2,1)}, bf16[4,128,1024]{2,1,0:T(8,128)(2,1)}) custom-call(bf16[128,1024]{1,0:T(8,128)(2,1)} %samples.1, bf16[64,1024]{1,0:T(8,128)(2,1)} %bitcast.12, f32[64,256]{1,0:T(8,128)} %bitcast.10), custom_call_target="tpu_custom_call" | custom-call | tf_op jit(solution)/shard_map/open/pallas_call | solution.py:248
  2.7 0.0 copy-start.1
  2.7 4.5 %all-to-all-start = ((bf16[4,128,1024]{2,1,0:T(8,128)(2,1)}), bf16[4,128,1024]{2,1,0:T(8,128)(2,1)S(1)}, u32[]{:S(2)}, u32[]{:S(2)}) async-start(bf16[4,128,1024]{2,1,0:T(8,128)(2,1)} %get-tuple-element.31), calls=%async_computation | async-start | bytes 2097152 | tf_op jit(solution)/shard_map/all_to_all | solution.py:268
  7.2 0.0 copy-done.1
  7.2 7.7 %collective-permute-start.2 = (bf16[64,1408]{1,0:T(8,128)(2,1)S(1)}, bf16[64,1408]{1,0:T(8,128)(2,1)S(1)}, u32[]{:S(2)}, u32[]{:S(2)}) collective-permute-start(bf16[64,1408]{1,0:T(8,128)(2,1)S(1)} %copy-done.1), channel_id=1, source_target_pairs={{21,16},{20,17},{23,18},{22,19},{17,20},{16,21},{19,22},{18,23},{2... | collective-permute-start | bytes 540680 | tf_op jit(solution)/shard_map/ppermute | solution.py:267
  14.9 1.9 %collective-permute-start.1 = (bf16[64,1408]{1,0:T(8,128)(2,1)S(1)}, bf16[64,1408]{1,0:T(8,128)(2,1)S(1)}, u32[]{:S(2)}, u32[]{:S(2)}) collective-permute-start(bf16[64,1408]{1,0:T(8,128)(2,1)S(1)} %copy-done.1), channel_id=1, source_target_pairs={{6,0},{3,1},{0,2},{5,3},{2,4},{7,5},{4,6},{1,7},{23,16},{18,17},{1... | collective-permute-start | bytes 540680 | tf_op jit(solution)/shard_map/ppermute | solution.py:267
  16.9 0.0 all-to-all-done
  16.9 9.6 %collective-permute-start = (bf16[512,1024]{1,0:T(8,128)(2,1)S(1)}, bf16[512,1024]{1,0:T(8,128)(2,1)S(1)}, u32[]{:S(2)}, u32[]{:S(2)}) collective-permute-start(bf16[512,1024]{1,0:T(8,128)(2,1)S(1)} %bitcast.8), channel_id=1, source_target_pairs={{0,16},{16,0},{1,17},{17,1},{2,18},{18,2},{3,19},{19,3},{4,20},{20... | collective-permute-start | bytes 3145736 | tf_op jit(solution)/shard_map/ppermute | solution.py:277
  26.5 0.0 collective-permute-done.2.second
  26.5 0.0 collective-permute-done.1.first
  26.5 0.1 prepare.1
  26.6 1.8 %early.1 = (f32[512,256]{1,0:T(8,128)S(1)}, f32[128,1024]{1,0:T(8,128)S(1)}, bf16[4,128,128]{2,1,0:T(8,128)(2,1)S(1)}) custom-call(bf16[512,1024]{1,0:T(8,128)(2,1)S(1)} %bitcast.9, bf16[128,1024]{1,0:T(8,128)(2,1)S(1)} %get-tuple-element.33.turn, bf16[128,512]{1,0:T(8,128)(2,1)S(1)} %get-tuple-element.34.codes_t, bf16[512,256]{1,0:T(8,128)(2,1)S(1)} %get-tuple-element.35.left), custom_call_target="tpu_custom_call" | custom-call | bytes 8000000 | tf_op jit(solution)/shard_map/early/pallas_call | solution.py:236
  28.4 0.3 collective-permute-done.samples
  28.7 2.7 %late.1 = (bf16[32,32,128]{2,1,0:T(8,128)(2,1)}, bf16[4,128,128]{2,1,0:T(8,128)(2,1)S(1)}, bf16[144,128]{1,0:T(8,128)(2,1)S(1)}, bf16[144,128]{1,0:T(8,128)(2,1)S(1)}) custom-call(bf16[512,1024]{1,0:T(8,128)(2,1)S(1)} %collective-permute-done.samples, bf16[128,1024]{1,0:T(8,128)(2,1)S(1)} %get-tuple-element.33.turn, ...), custom_call_target="tpu_custom_call" | custom-call | bytes 8000000 | tf_op jit(solution)/shard_map/late/pallas_call | solution.py:236
  31.4 7.7 %all-to-all-start.1 = ((bf16[32,32,128]{2,1,0:T(8,128)(2,1)}), bf16[32,32,128]{2,1,0:T(8,128)(2,1)S(1)}, u32[]{:S(2)}, u32[]{:S(2)}) async-start(bf16[32,32,128]{2,1,0:T(8,128)(2,1)} %get-tuple-element.38), calls=%async_computation.1 | async-start | bytes 524288 | tf_op jit(solution)/shard_map/all_to_all | solution.py:304
  39.2 6.3 %collective-permute-start.3 = (bf16[144,128]{1,0:T(8,128)(2,1)S(1)}, bf16[144,128]{1,0:T(8,128)(2,1)S(1)}, u32[]{:S(2)}, u32[]{:S(2)}) collective-permute-start(bf16[144,128]{1,0:T(8,128)(2,1)S(1)} %get-tuple-element.39), channel_id=1, source_target_pairs={{0,6},{1,3},{2,0},{3,5},{4,2},{5,7},{6,4},{7,1},{16,21},{17,20},{1... | collective-permute-start | bytes 110600 | tf_op jit(solution)/shard_map/ppermute | solution.py:298
  45.5 2.2 %collective-permute-start.4 = (bf16[144,128]{1,0:T(8,128)(2,1)S(1)}, bf16[144,128]{1,0:T(8,128)(2,1)S(1)}, u32[]{:S(2)}, u32[]{:S(2)}) collective-permute-start(bf16[144,128]{1,0:T(8,128)(2,1)S(1)} %get-tuple-element.40), channel_id=1, source_target_pairs={{0,0},{1,1},{2,2},{3,3},{4,4},{5,5},{6,6},{7,7},{16,23},{17,18},{1... | collective-permute-start | bytes 110600 | tf_op jit(solution)/shard_map/ppermute | solution.py:298
  47.7 1.9 %collective-permute-start.6 = (bf16[4,128,128]{2,1,0:T(8,128)(2,1)S(1)}, bf16[4,128,128]{2,1,0:T(8,128)(2,1)S(1)}, u32[]{:S(2)}, u32[]{:S(2)}) collective-permute-start(bf16[4,128,128]{2,1,0:T(8,128)(2,1)S(1)} %get-tuple-element.42), channel_id=1, source_target_pairs={{0,16},{16,0},{1,17},{17,1},{2,18},{18,2},{3,19},{19,3},{4,20},{20... | collective-permute-start | bytes 393224 | tf_op jit(solution)/shard_map/ppermute | solution.py:299
  49.6 0.4 collective-permute-done.3.first
  50.0 1.4 %collective-permute-done.4.second = bf16[144,128]{1,0:T(8,128)(2,1)S(1)} collective-permute-done((bf16[144,128]{1,0:T(8,128)(2,1)S(1)}, bf16[144,128]{1,0:T(8,128)(2,1)S(1)}, u32[]{:S(2)}, u32[]{:S(2)}) %collective-permute-start.4) | collective-permute-done | bytes 36896 | tf_op jit(solution)/shard_map/ppermute | solution.py:298
  51.4 1.9 %collective-permute-start.5 = (bf16[80,128]{1,0:T(8,128)(2,1)S(1)}, bf16[80,128]{1,0:T(8,128)(2,1)S(1)}, u32[]{:S(2)}, u32[]{:S(2)}) collective-permute-start(bf16[80,128]{1,0:T(8,128)(2,1)S(1)} %get-tuple-element.41), channel_id=1, source_target_pairs={{0,16},{16,0},{1,17},{17,1},{2,18},{18,2},{3,19},{19,3},{4,20},{20... | collective-permute-start | bytes 61448 | tf_op jit(solution)/shard_map/ppermute | solution.py:303
  53.3 1.2 %collective-permute-done.5.half = bf16[80,128]{1,0:T(8,128)(2,1)S(1)} collective-permute-done((bf16[80,128]{1,0:T(8,128)(2,1)S(1)}, bf16[80,128]{1,0:T(8,128)(2,1)S(1)}, u32[]{:S(2)}, u32[]{:S(2)}) %collective-permute-start.5) | collective-permute-done | bytes 20512 | tf_op jit(solution)/shard_map/ppermute | solution.py:303
  54.5 0.0 collective-permute-done.6.got_core
  54.5 0.0 all-to-all-done.1.got
  54.5 1.0 %middle.1 = bf16[16,88,128]{2,1,0:T(8,128)(2,1)} custom-call(bf16[32,32,128]{2,1,0:T(8,128)(2,1)S(1)} %all-to-all-done.1.got, f32[80,128]{1,0:T(8,128)S(1)} %get-tuple-element.44.keep, bf16[80,128]{1,0:T(8,128)(2,1)S(1)} %collective-permute-done.5.half), custom_call_target="tpu_custom_call" | custom-call | tf_op jit(solution)/shard_map/middle/pallas_call | solution.py:236
  55.6 12.6 %all-to-all-start.2 = ((bf16[16,88,128]{2,1,0:T(8,128)(2,1)}), bf16[16,88,128]{2,1,0:T(8,128)(2,1)S(1)}, u32[]{:S(2)}, u32[]{:S(2)}) async-start(bf16[16,88,128]{2,1,0:T(8,128)(2,1)} %middle.1), calls=%async_computation.2 | async-start | bytes 720896 | tf_op jit(solution)/shard_map/all_to_all | solution.py:311
  68.2 0.0 copy-start
  68.2 3.2 %collective-permute-start.7 = (bf16[2,128,128]{2,1,0:T(8,128)(2,1)S(1)}, bf16[2,128,128]{2,1,0:T(8,128)(2,1)S(1)}, u32[]{:S(2)}, u32[]{:S(2)}) collective-permute-start(bf16[2,128,128]{2,1,0:T(8,128)(2,1)S(1)} %get-tuple-element.48), channel_id=1, source_target_pairs={{0,9},{1,8},{8,1},{9,0},{2,11},{3,10},{10,3},{11,2},{4,13},{5,12},... | collective-permute-start | bytes 196616 | tf_op jit(solution)/shard_map/ppermute | solution.py:308
  71.4 2.7 %collective-permute-start.8 = (bf16[2,128,128]{2,1,0:T(8,128)(2,1)S(1)}, bf16[2,128,128]{2,1,0:T(8,128)(2,1)S(1)}, u32[]{:S(2)}, u32[]{:S(2)}) collective-permute-start(bf16[2,128,128]{2,1,0:T(8,128)(2,1)S(1)} %get-tuple-element.49), channel_id=1, source_target_pairs={{0,8},{8,0},{1,9},{9,1},{2,10},{10,2},{3,11},{11,3},{4,12},{12,4},... | collective-permute-start | bytes 196616 | tf_op jit(solution)/shard_map/ppermute | solution.py:309
  74.1 2.5 %collective-permute-start.9 = (bf16[2,128,128]{2,1,0:T(8,128)(2,1)S(1)}, bf16[2,128,128]{2,1,0:T(8,128)(2,1)S(1)}, u32[]{:S(2)}, u32[]{:S(2)}) collective-permute-start(bf16[2,128,128]{2,1,0:T(8,128)(2,1)S(1)} %get-tuple-element.50), channel_id=1, source_target_pairs={{0,1},{1,0},{2,3},{3,2},{4,5},{5,4},{6,7},{7,6},{8,9},{9,8},{10,11... | collective-permute-start | bytes 196616 | tf_op jit(solution)/shard_map/ppermute | solution.py:310
  76.6 0.0 collective-permute-done.7.got_xy
  76.6 1.1 %collective-permute-done.8.got_x = bf16[2,128,128]{2,1,0:T(8,128)(2,1)S(1)} collective-permute-done((bf16[2,128,128]{2,1,0:T(8,128)(2,1)S(1)}, bf16[2,128,128]{2,1,0:T(8,128)(2,1)S(1)}, u32[]{:S(2)}, u32[]{:S(2)}) %collective-permute-start.8) | collective-permute-done | bytes 65568 | tf_op jit(solution)/shard_map/ppermute | solution.py:309
  77.7 1.7 %collective-permute-done.9.got_y = bf16[2,128,128]{2,1,0:T(8,128)(2,1)S(1)} collective-permute-done((bf16[2,128,128]{2,1,0:T(8,128)(2,1)S(1)}, bf16[2,128,128]{2,1,0:T(8,128)(2,1)S(1)}, u32[]{:S(2)}, u32[]{:S(2)}) %collective-permute-start.9) | collective-permute-done | bytes 65568 | tf_op jit(solution)/shard_map/ppermute | solution.py:310
  79.4 3.4 %all-to-all-done.2.got = bf16[16,88,128]{2,1,0:T(8,128)(2,1)S(1)} async-done(((bf16[16,88,128]{2,1,0:T(8,128)(2,1)}), bf16[16,88,128]{2,1,0:T(8,128)(2,1)S(1)}, u32[]{:S(2)}, u32[]{:S(2)}) %all-to-all-start.2) | async-done | bytes 360480 | tf_op jit(solution)/shard_map/all_to_all | solution.py:311
  82.8 0.0 copy-done
  82.8 0.7 finish.1
  83.4 4.0 %collective-permute-start.10 = (f32[64,128]{1,0:T(8,128)S(1)}, f32[64,128]{1,0:T(8,128)S(1)}, u32[]{:S(2)}, u32[]{:S(2)}) collective-permute-start(f32[64,128]{1,0:T(8,128)S(1)} %get-tuple-element.52.mine), channel_id=1, source_target_pairs={{0,16},{16,0},{1,17},{17,1},{2,18},{18,2},{3,19},{19,3},{4,20},{20... | collective-permute-start | bytes 98312 | tf_op jit(solution)/shard_map/ppermute | solution.py:319
  87.5 0.9 home.1
  88.3 0.0 collective-permute-done.10.other
  88.4 0.6 codes.1
  (2 shorter events, 0.0 us)
Async XLA Ops:
  2.7 4.5 %copy-start.1 = (bf16[64,1408]{1,0:T(8,128)(2,1)S(1)}, bf16[64,1408]{1,0:T(8,128)(2,1)}, u32[]{:S(2)}) copy-start(bf16[64,1408]{1,0:T(8,128)(2,1)} %get-tuple-element.32.pack) | copy-start | bytes 540676
  2.7 14.1 %all-to-all-start = ((bf16[4,128,1024]{2,1,0:T(8,128)(2,1)}), bf16[4,128,1024]{2,1,0:T(8,128)(2,1)S(1)}, u32[]{:S(2)}, u32[]{:S(2)}) async-start(bf16[4,128,1024]{2,1,0:T(8,128)(2,1)} %get-tuple-element.31), calls=%async_computation | async-start | bytes 2097152 | tf_op jit(solution)/shard_map/all_to_all | solution.py:268
  7.2 19.3 %collective-permute-start.2 = (bf16[64,1408]{1,0:T(8,128)(2,1)S(1)}, bf16[64,1408]{1,0:T(8,128)(2,1)S(1)}, u32[]{:S(2)}, u32[]{:S(2)}) collective-permute-start(bf16[64,1408]{1,0:T(8,128)(2,1)S(1)} %copy-done.1), channel_id=1, source_target_pairs={{21,16},{20,17},{23,18},{22,19},{17,20},{16,21},{19,22},{18,23},{2... | collective-permute-start | bytes 540680 | tf_op jit(solution)/shard_map/ppermute | solution.py:267
  14.9 11.6 %collective-permute-start.1 = (bf16[64,1408]{1,0:T(8,128)(2,1)S(1)}, bf16[64,1408]{1,0:T(8,128)(2,1)S(1)}, u32[]{:S(2)}, u32[]{:S(2)}) collective-permute-start(bf16[64,1408]{1,0:T(8,128)(2,1)S(1)} %copy-done.1), channel_id=1, source_target_pairs={{6,0},{3,1},{0,2},{5,3},{2,4},{7,5},{4,6},{1,7},{23,16},{18,17},{1... | collective-permute-start | bytes 540680 | tf_op jit(solution)/shard_map/ppermute | solution.py:267
  16.9 11.9 %collective-permute-start = (bf16[512,1024]{1,0:T(8,128)(2,1)S(1)}, bf16[512,1024]{1,0:T(8,128)(2,1)S(1)}, u32[]{:S(2)}, u32[]{:S(2)}) collective-permute-start(bf16[512,1024]{1,0:T(8,128)(2,1)S(1)} %bitcast.8), channel_id=1, source_target_pairs={{0,16},{16,0},{1,17},{17,1},{2,18},{18,2},{3,19},{19,3},{4,20},{20... | collective-permute-start | bytes 3145736 | tf_op jit(solution)/shard_map/ppermute | solution.py:277
  31.4 23.1 %all-to-all-start.1 = ((bf16[32,32,128]{2,1,0:T(8,128)(2,1)}), bf16[32,32,128]{2,1,0:T(8,128)(2,1)S(1)}, u32[]{:S(2)}, u32[]{:S(2)}) async-start(bf16[32,32,128]{2,1,0:T(8,128)(2,1)} %get-tuple-element.38), calls=%async_computation.1 | async-start | bytes 524288 | tf_op jit(solution)/shard_map/all_to_all | solution.py:304
  39.2 10.8 %collective-permute-start.3 = (bf16[144,128]{1,0:T(8,128)(2,1)S(1)}, bf16[144,128]{1,0:T(8,128)(2,1)S(1)}, u32[]{:S(2)}, u32[]{:S(2)}) collective-permute-start(bf16[144,128]{1,0:T(8,128)(2,1)S(1)} %get-tuple-element.39), channel_id=1, source_target_pairs={{0,6},{1,3},{2,0},{3,5},{4,2},{5,7},{6,4},{7,1},{16,21},{17,20},{1... | collective-permute-start | bytes 110600 | tf_op jit(solution)/shard_map/ppermute | solution.py:298
  45.5 5.9 %collective-permute-start.4 = (bf16[144,128]{1,0:T(8,128)(2,1)S(1)}, bf16[144,128]{1,0:T(8,128)(2,1)S(1)}, u32[]{:S(2)}, u32[]{:S(2)}) collective-permute-start(bf16[144,128]{1,0:T(8,128)(2,1)S(1)} %get-tuple-element.40), channel_id=1, source_target_pairs={{0,0},{1,1},{2,2},{3,3},{4,4},{5,5},{6,6},{7,7},{16,23},{17,18},{1... | collective-permute-start | bytes 110600 | tf_op jit(solution)/shard_map/ppermute | solution.py:298
  47.7 6.8 %collective-permute-start.6 = (bf16[4,128,128]{2,1,0:T(8,128)(2,1)S(1)}, bf16[4,128,128]{2,1,0:T(8,128)(2,1)S(1)}, u32[]{:S(2)}, u32[]{:S(2)}) collective-permute-start(bf16[4,128,128]{2,1,0:T(8,128)(2,1)S(1)} %get-tuple-element.42), channel_id=1, source_target_pairs={{0,16},{16,0},{1,17},{17,1},{2,18},{18,2},{3,19},{19,3},{4,20},{20... | collective-permute-start | bytes 393224 | tf_op jit(solution)/shard_map/ppermute | solution.py:299
  51.4 3.1 %collective-permute-start.5 = (bf16[80,128]{1,0:T(8,128)(2,1)S(1)}, bf16[80,128]{1,0:T(8,128)(2,1)S(1)}, u32[]{:S(2)}, u32[]{:S(2)}) collective-permute-start(bf16[80,128]{1,0:T(8,128)(2,1)S(1)} %get-tuple-element.41), channel_id=1, source_target_pairs={{0,16},{16,0},{1,17},{17,1},{2,18},{18,2},{3,19},{19,3},{4,20},{20... | collective-permute-start | bytes 61448 | tf_op jit(solution)/shard_map/ppermute | solution.py:303
  55.6 27.2 %all-to-all-start.2 = ((bf16[16,88,128]{2,1,0:T(8,128)(2,1)}), bf16[16,88,128]{2,1,0:T(8,128)(2,1)S(1)}, u32[]{:S(2)}, u32[]{:S(2)}) async-start(bf16[16,88,128]{2,1,0:T(8,128)(2,1)} %middle.1), calls=%async_computation.2 | async-start | bytes 720896 | tf_op jit(solution)/shard_map/all_to_all | solution.py:311
  68.2 14.6 %copy-start = (f32[1,256,64]{1,2,0:T(8,128)S(1)}, f32[1,256,64]{1,2,0:T(8,128)}, u32[]{:S(2)}) copy-start(f32[1,256,64]{1,2,0:T(8,128)} %param.5) | copy-start | bytes 196612
  68.2 8.4 %collective-permute-start.7 = (bf16[2,128,128]{2,1,0:T(8,128)(2,1)S(1)}, bf16[2,128,128]{2,1,0:T(8,128)(2,1)S(1)}, u32[]{:S(2)}, u32[]{:S(2)}) collective-permute-start(bf16[2,128,128]{2,1,0:T(8,128)(2,1)S(1)} %get-tuple-element.48), channel_id=1, source_target_pairs={{0,9},{1,8},{8,1},{9,0},{2,11},{3,10},{10,3},{11,2},{4,13},{5,12},... | collective-permute-start | bytes 196616 | tf_op jit(solution)/shard_map/ppermute | solution.py:308
  71.4 6.3 %collective-permute-start.8 = (bf16[2,128,128]{2,1,0:T(8,128)(2,1)S(1)}, bf16[2,128,128]{2,1,0:T(8,128)(2,1)S(1)}, u32[]{:S(2)}, u32[]{:S(2)}) collective-permute-start(bf16[2,128,128]{2,1,0:T(8,128)(2,1)S(1)} %get-tuple-element.49), channel_id=1, source_target_pairs={{0,8},{8,0},{1,9},{9,1},{2,10},{10,2},{3,11},{11,3},{4,12},{12,4},... | collective-permute-start | bytes 196616 | tf_op jit(solution)/shard_map/ppermute | solution.py:309
  74.1 5.3 %collective-permute-start.9 = (bf16[2,128,128]{2,1,0:T(8,128)(2,1)S(1)}, bf16[2,128,128]{2,1,0:T(8,128)(2,1)S(1)}, u32[]{:S(2)}, u32[]{:S(2)}) collective-permute-start(bf16[2,128,128]{2,1,0:T(8,128)(2,1)S(1)} %get-tuple-element.50), channel_id=1, source_target_pairs={{0,1},{1,0},{2,3},{3,2},{4,5},{5,4},{6,7},{7,6},{8,9},{9,8},{10,11... | collective-permute-start | bytes 196616 | tf_op jit(solution)/shard_map/ppermute | solution.py:310
  83.4 4.9 %collective-permute-start.10 = (f32[64,128]{1,0:T(8,128)S(1)}, f32[64,128]{1,0:T(8,128)S(1)}, u32[]{:S(2)}, u32[]{:S(2)}) collective-permute-start(f32[64,128]{1,0:T(8,128)S(1)} %get-tuple-element.52.mine), channel_id=1, source_target_pairs={{0,16},{16,0},{1,17},{17,1},{2,18},{18,2},{3,19},{19,3},{4,20},{20... | collective-permute-start | bytes 98312 | tf_op jit(solution)/shard_map/ppermute | solution.py:319

commit v18 on v17

--- a/solution.py
+++ b/solution.py
@@ -302,9 +302,9 @@
     )
     half = lax.ppermute(give, "core", swap)
     got = lax.all_to_all(send, NEAR, 0, 0, tiled=True)
-    got, half, got_core = lax.optimization_barrier((got, half, got_core))
+    gives = call(second_kernel, "second", [pair, pair, pair], (early, got_core))
+    got, half, *gives = lax.optimization_barrier((got, half, *gives))
     (send,) = call(middle_kernel, "middle", [((16, 88, 128), BF)], (got, keep, half))
-    gives = call(second_kernel, "second", [pair, pair, pair], (early, got_core))
     got_xy = lax.ppermute(gives[2], ("xl", "yl"), [(0, 3), (1, 2), (2, 1), (3, 0)])
     got_x = lax.ppermute(gives[0], "xl", swap)
     got_y = lax.ppermute(gives[1], "yl", swap)

time: 89.7 us -> 89.8 us (level)
  no operation moved by 1% of the time
where the time goes in v18:
time: 89.8 us; the launch traced here: 89.1 us
  starting transfers between devices  68.9 us (77%)
  Pallas kernels  10 us (11%)
  waiting for transfers between devices  9.39 us (10%)
    all_to_all x1, starting transfers between devices, per_device(): got = lax.all_to_all(send, FAR, 0, 0, tiled=True)  12.7 us
    ppermute x2, starting transfers between devices, per_device(): packs.append(lax.ppermute(pack, ('core', 'yh', 'yl'), pairs))  9.63 us
    ppermute x1, starting transfers between devices, per_device(): other = lax.ppermute(mine, 'core', swap)  9.59 us
    ppermute x2, starting transfers between devices, per_device(): moved.append(lax.ppermute(totals[i], ('core', 'yh', 'yl'), pairs))  8.49 us
    pallas_call x9, Pallas kernels, call(): pl.pallas_call(kernel, out_shape=tuple((jax.ShapeDtypeStruct(*o) for o in...  7.93 us
    all_to_all x1, starting transfers between devices, per_device(): got = lax.all_to_all(send, NEAR, 0, 0, tiled=True)  7.74 us
    all_to_all x1, starting transfers between devices, per_device(): lax.all_to_all(copies, ('xl', 'yl'), 0, 0, tiled=True).reshape(512, 1024)  4.45 us
    ppermute x1, starting transfers between devices, per_device(): fresh_other = lax.ppermute(fresh, 'core', swap)  4.04 us
  transfers between devices with their start and end apart: 14, of which 7 were waited for; matrix products, arithmetic and copies ran while one was open for 0% of the time, Pallas kernels for 3%

profile of v18, /device:TPU:1, one launch (start us, length us, event | category | flops | bytes accessed | tf_op | source)
XLA Modules:
  0.0 89.1 jit_solution(13109372083682851842)
XLA Ops:
  0.6 2.1 %open.1 = (bf16[64,1408]{1,0:T(8,128)(2,1)}, bf16[4,128,1024]{2,1,0:T(8,128)(2,1)}) custom-call(bf16[128,1024]{1,0:T(8,128)(2,1)} %samples.1, bf16[64,1024]{1,0:T(8,128)(2,1)} %bitcast.12, f32[64,256]{1,0:T(8,128)} %bitcast.10), custom_call_target="tpu_custom_call" | custom-call | tf_op jit(solution)/shard_map/open/pallas_call | solution.py:248
  2.7 0.0 copy-start.1
  2.7 4.5 %all-to-all-start = ((bf16[4,128,1024]{2,1,0:T(8,128)(2,1)}), bf16[4,128,1024]{2,1,0:T(8,128)(2,1)S(1)}, u32[]{:S(2)}, u32[]{:S(2)}) async-start(bf16[4,128,1024]{2,1,0:T(8,128)(2,1)} %get-tuple-element.33), calls=%async_computation | async-start | bytes 2097152 | tf_op jit(solution)/shard_map/all_to_all | solution.py:268
  7.2 0.0 copy-done.1
  7.2 7.7 %collective-permute-start.2 = (bf16[64,1408]{1,0:T(8,128)(2,1)S(1)}, bf16[64,1408]{1,0:T(8,128)(2,1)S(1)}, u32[]{:S(2)}, u32[]{:S(2)}) collective-permute-start(bf16[64,1408]{1,0:T(8,128)(2,1)S(1)} %copy-done.1), channel_id=1, source_target_pairs={{21,16},{20,17},{23,18},{22,19},{17,20},{16,21},{19,22},{18,23},{2... | collective-permute-start | bytes 540680 | tf_op jit(solution)/shard_map/ppermute | solution.py:267
  14.9 1.9 %collective-permute-start.1 = (bf16[64,1408]{1,0:T(8,128)(2,1)S(1)}, bf16[64,1408]{1,0:T(8,128)(2,1)S(1)}, u32[]{:S(2)}, u32[]{:S(2)}) collective-permute-start(bf16[64,1408]{1,0:T(8,128)(2,1)S(1)} %copy-done.1), channel_id=1, source_target_pairs={{6,0},{3,1},{0,2},{5,3},{2,4},{7,5},{4,6},{1,7},{23,16},{18,17},{1... | collective-permute-start | bytes 540680 | tf_op jit(solution)/shard_map/ppermute | solution.py:267
  16.9 0.0 all-to-all-done
  16.9 9.6 %collective-permute-start = (bf16[512,1024]{1,0:T(8,128)(2,1)S(1)}, bf16[512,1024]{1,0:T(8,128)(2,1)S(1)}, u32[]{:S(2)}, u32[]{:S(2)}) collective-permute-start(bf16[512,1024]{1,0:T(8,128)(2,1)S(1)} %bitcast.8), channel_id=1, source_target_pairs={{0,16},{16,0},{1,17},{17,1},{2,18},{18,2},{3,19},{19,3},{4,20},{20... | collective-permute-start | bytes 3145736 | tf_op jit(solution)/shard_map/ppermute | solution.py:277
  26.5 0.0 collective-permute-done.2.second
  26.5 0.0 collective-permute-done.1.first
  26.5 0.1 prepare.1
  26.6 1.8 %early.1 = (f32[512,256]{1,0:T(8,128)S(1)}, f32[128,1024]{1,0:T(8,128)S(1)}, bf16[4,128,128]{2,1,0:T(8,128)(2,1)S(1)}) custom-call(bf16[512,1024]{1,0:T(8,128)(2,1)S(1)} %bitcast.9, bf16[128,1024]{1,0:T(8,128)(2,1)S(1)} %get-tuple-element.35.turn, bf16[128,512]{1,0:T(8,128)(2,1)S(1)} %get-tuple-element.36.codes_t, bf16[512,256]{1,0:T(8,128)(2,1)S(1)} %get-tuple-element.37.left), custom_call_target="tpu_custom_call" | custom-call | bytes 8000000 | tf_op jit(solution)/shard_map/early/pallas_call | solution.py:236
  28.4 0.3 collective-permute-done.samples
  28.7 2.7 %late.1 = (bf16[32,32,128]{2,1,0:T(8,128)(2,1)}, bf16[4,128,128]{2,1,0:T(8,128)(2,1)S(1)}, bf16[144,128]{1,0:T(8,128)(2,1)S(1)}, bf16[144,128]{1,0:T(8,128)(2,1)S(1)}) custom-call(bf16[512,1024]{1,0:T(8,128)(2,1)S(1)} %collective-permute-done.samples, bf16[128,1024]{1,0:T(8,128)(2,1)S(1)} %get-tuple-element.35.turn, ...), custom_call_target="tpu_custom_call" | custom-call | bytes 8000000 | tf_op jit(solution)/shard_map/late/pallas_call | solution.py:236
  31.4 7.7 %all-to-all-start.1 = ((bf16[32,32,128]{2,1,0:T(8,128)(2,1)}), bf16[32,32,128]{2,1,0:T(8,128)(2,1)S(1)}, u32[]{:S(2)}, u32[]{:S(2)}) async-start(bf16[32,32,128]{2,1,0:T(8,128)(2,1)} %get-tuple-element.40), calls=%async_computation.1 | async-start | bytes 524288 | tf_op jit(solution)/shard_map/all_to_all | solution.py:304
  39.2 6.3 %collective-permute-start.3 = (bf16[144,128]{1,0:T(8,128)(2,1)S(1)}, bf16[144,128]{1,0:T(8,128)(2,1)S(1)}, u32[]{:S(2)}, u32[]{:S(2)}) collective-permute-start(bf16[144,128]{1,0:T(8,128)(2,1)S(1)} %get-tuple-element.41), channel_id=1, source_target_pairs={{0,6},{1,3},{2,0},{3,5},{4,2},{5,7},{6,4},{7,1},{16,21},{17,20},{1... | collective-permute-start | bytes 110600 | tf_op jit(solution)/shard_map/ppermute | solution.py:298
  45.5 2.2 %collective-permute-start.4 = (bf16[144,128]{1,0:T(8,128)(2,1)S(1)}, bf16[144,128]{1,0:T(8,128)(2,1)S(1)}, u32[]{:S(2)}, u32[]{:S(2)}) collective-permute-start(bf16[144,128]{1,0:T(8,128)(2,1)S(1)} %get-tuple-element.42), channel_id=1, source_target_pairs={{0,0},{1,1},{2,2},{3,3},{4,4},{5,5},{6,6},{7,7},{16,23},{17,18},{1... | collective-permute-start | bytes 110600 | tf_op jit(solution)/shard_map/ppermute | solution.py:298
  47.7 1.9 %collective-permute-start.6 = (bf16[4,128,128]{2,1,0:T(8,128)(2,1)S(1)}, bf16[4,128,128]{2,1,0:T(8,128)(2,1)S(1)}, u32[]{:S(2)}, u32[]{:S(2)}) collective-permute-start(bf16[4,128,128]{2,1,0:T(8,128)(2,1)S(1)} %get-tuple-element.45), channel_id=1, source_target_pairs={{0,16},{16,0},{1,17},{17,1},{2,18},{18,2},{3,19},{19,3},{4,20},{20... | collective-permute-start | bytes 393224 | tf_op jit(solution)/shard_map/ppermute | solution.py:299
  49.6 0.4 collective-permute-done.3.first
  50.0 1.4 %collective-permute-done.4.second = bf16[144,128]{1,0:T(8,128)(2,1)S(1)} collective-permute-done((bf16[144,128]{1,0:T(8,128)(2,1)S(1)}, bf16[144,128]{1,0:T(8,128)(2,1)S(1)}, u32[]{:S(2)}, u32[]{:S(2)}) %collective-permute-start.4) | collective-permute-done | bytes 36896 | tf_op jit(solution)/shard_map/ppermute | solution.py:298
  51.4 1.9 %collective-permute-start.5 = (bf16[80,128]{1,0:T(8,128)(2,1)S(1)}, bf16[80,128]{1,0:T(8,128)(2,1)S(1)}, u32[]{:S(2)}, u32[]{:S(2)}) collective-permute-start(bf16[80,128]{1,0:T(8,128)(2,1)S(1)} %get-tuple-element.43), channel_id=1, source_target_pairs={{0,16},{16,0},{1,17},{17,1},{2,18},{18,2},{3,19},{19,3},{4,20},{20... | collective-permute-start | bytes 61448 | tf_op jit(solution)/shard_map/ppermute | solution.py:303
  53.3 0.0 collective-permute-done.6.got_core
  53.4 1.1 %collective-permute-done.5.half = bf16[80,128]{1,0:T(8,128)(2,1)S(1)} collective-permute-done((bf16[80,128]{1,0:T(8,128)(2,1)S(1)}, bf16[80,128]{1,0:T(8,128)(2,1)S(1)}, u32[]{:S(2)}, u32[]{:S(2)}) %collective-permute-start.5) | collective-permute-done | bytes 20512 | tf_op jit(solution)/shard_map/ppermute | solution.py:303
  54.5 0.0 all-to-all-done.1.got
  54.5 1.0 %middle.1 = bf16[16,88,128]{2,1,0:T(8,128)(2,1)} custom-call(bf16[32,32,128]{2,1,0:T(8,128)(2,1)S(1)} %all-to-all-done.1.got, f32[80,128]{1,0:T(8,128)S(1)} %get-tuple-element.50.keep, bf16[80,128]{1,0:T(8,128)(2,1)S(1)} %collective-permute-done.5.half), custom_call_target="tpu_custom_call" | custom-call | tf_op jit(solution)/shard_map/middle/pallas_call | solution.py:236
  55.6 0.0 copy-start
  55.6 12.7 %all-to-all-start.2 = ((bf16[16,88,128]{2,1,0:T(8,128)(2,1)}), bf16[16,88,128]{2,1,0:T(8,128)(2,1)S(1)}, u32[]{:S(2)}, u32[]{:S(2)}) async-start(bf16[16,88,128]{2,1,0:T(8,128)(2,1)} %middle.1), calls=%async_computation.2 | async-start | bytes 720896 | tf_op jit(solution)/shard_map/all_to_all | solution.py:311
  68.3 3.2 %collective-permute-start.7 = (bf16[2,128,128]{2,1,0:T(8,128)(2,1)S(1)}, bf16[2,128,128]{2,1,0:T(8,128)(2,1)S(1)}, u32[]{:S(2)}, u32[]{:S(2)}) collective-permute-start(bf16[2,128,128]{2,1,0:T(8,128)(2,1)S(1)} %get-tuple-element.52), channel_id=1, source_target_pairs={{0,9},{1,8},{8,1},{9,0},{2,11},{3,10},{10,3},{11,2},{4,13},{5,12},... | collective-permute-start | bytes 196616 | tf_op jit(solution)/shard_map/ppermute | solution.py:308
  71.5 2.7 %collective-permute-start.8 = (bf16[2,128,128]{2,1,0:T(8,128)(2,1)S(1)}, bf16[2,128,128]{2,1,0:T(8,128)(2,1)S(1)}, u32[]{:S(2)}, u32[]{:S(2)}) collective-permute-start(bf16[2,128,128]{2,1,0:T(8,128)(2,1)S(1)} %get-tuple-element.53), channel_id=1, source_target_pairs={{0,8},{8,0},{1,9},{9,1},{2,10},{10,2},{3,11},{11,3},{4,12},{12,4},... | collective-permute-start | bytes 196616 | tf_op jit(solution)/shard_map/ppermute | solution.py:309
  74.2 2.5 %collective-permute-start.9 = (bf16[2,128,128]{2,1,0:T(8,128)(2,1)S(1)}, bf16[2,128,128]{2,1,0:T(8,128)(2,1)S(1)}, u32[]{:S(2)}, u32[]{:S(2)}) collective-permute-start(bf16[2,128,128]{2,1,0:T(8,128)(2,1)S(1)} %get-tuple-element.54), channel_id=1, source_target_pairs={{0,1},{1,0},{2,3},{3,2},{4,5},{5,4},{6,7},{7,6},{8,9},{9,8},{10,11... | collective-permute-start | bytes 196616 | tf_op jit(solution)/shard_map/ppermute | solution.py:310
  76.7 0.0 collective-permute-done.7.got_xy
  76.7 1.2 %collective-permute-done.8.got_x = bf16[2,128,128]{2,1,0:T(8,128)(2,1)S(1)} collective-permute-done((bf16[2,128,128]{2,1,0:T(8,128)(2,1)S(1)}, bf16[2,128,128]{2,1,0:T(8,128)(2,1)S(1)}, u32[]{:S(2)}, u32[]{:S(2)}) %collective-permute-start.8) | collective-permute-done | bytes 65568 | tf_op jit(solution)/shard_map/ppermute | solution.py:309
  77.9 1.6 %collective-permute-done.9.got_y = bf16[2,128,128]{2,1,0:T(8,128)(2,1)S(1)} collective-permute-done((bf16[2,128,128]{2,1,0:T(8,128)(2,1)S(1)}, bf16[2,128,128]{2,1,0:T(8,128)(2,1)S(1)}, u32[]{:S(2)}, u32[]{:S(2)}) %collective-permute-start.9) | collective-permute-done | bytes 65568 | tf_op jit(solution)/shard_map/ppermute | solution.py:310
  79.5 3.4 %all-to-all-done.2.got = bf16[16,88,128]{2,1,0:T(8,128)(2,1)S(1)} async-done(((bf16[16,88,128]{2,1,0:T(8,128)(2,1)}), bf16[16,88,128]{2,1,0:T(8,128)(2,1)S(1)}, u32[]{:S(2)}, u32[]{:S(2)}) %all-to-all-start.2) | async-done | bytes 360480 | tf_op jit(solution)/shard_map/all_to_all | solution.py:311
  82.9 0.0 copy-done
  82.9 0.7 finish.1
  83.6 4.0 %collective-permute-start.10 = (f32[64,128]{1,0:T(8,128)S(1)}, f32[64,128]{1,0:T(8,128)S(1)}, u32[]{:S(2)}, u32[]{:S(2)}) collective-permute-start(f32[64,128]{1,0:T(8,128)S(1)} %get-tuple-element.56.mine), channel_id=1, source_target_pairs={{0,16},{16,0},{1,17},{17,1},{2,18},{18,2},{3,19},{19,3},{4,20},{20... | collective-permute-start | bytes 98312 | tf_op jit(solution)/shard_map/ppermute | solution.py:319
  87.6 0.9 home.1
  88.5 0.0 collective-permute-done.10.other
  88.5 0.6 codes.1
  (2 shorter events, 0.0 us)
Async XLA Ops:
  2.7 4.5 %copy-start.1 = (bf16[64,1408]{1,0:T(8,128)(2,1)S(1)}, bf16[64,1408]{1,0:T(8,128)(2,1)}, u32[]{:S(2)}) copy-start(bf16[64,1408]{1,0:T(8,128)(2,1)} %get-tuple-element.34.pack) | copy-start | bytes 540676
  2.7 14.1 %all-to-all-start = ((bf16[4,128,1024]{2,1,0:T(8,128)(2,1)}), bf16[4,128,1024]{2,1,0:T(8,128)(2,1)S(1)}, u32[]{:S(2)}, u32[]{:S(2)}) async-start(bf16[4,128,1024]{2,1,0:T(8,128)(2,1)} %get-tuple-element.33), calls=%async_computation | async-start | bytes 2097152 | tf_op jit(solution)/shard_map/all_to_all | solution.py:268
  7.2 19.3 %collective-permute-start.2 = (bf16[64,1408]{1,0:T(8,128)(2,1)S(1)}, bf16[64,1408]{1,0:T(8,128)(2,1)S(1)}, u32[]{:S(2)}, u32[]{:S(2)}) collective-permute-start(bf16[64,1408]{1,0:T(8,128)(2,1)S(1)} %copy-done.1), channel_id=1, source_target_pairs={{21,16},{20,17},{23,18},{22,19},{17,20},{16,21},{19,22},{18,23},{2... | collective-permute-start | bytes 540680 | tf_op jit(solution)/shard_map/ppermute | solution.py:267
  14.9 11.6 %collective-permute-start.1 = (bf16[64,1408]{1,0:T(8,128)(2,1)S(1)}, bf16[64,1408]{1,0:T(8,128)(2,1)S(1)}, u32[]{:S(2)}, u32[]{:S(2)}) collective-permute-start(bf16[64,1408]{1,0:T(8,128)(2,1)S(1)} %copy-done.1), channel_id=1, source_target_pairs={{6,0},{3,1},{0,2},{5,3},{2,4},{7,5},{4,6},{1,7},{23,16},{18,17},{1... | collective-permute-start | bytes 540680 | tf_op jit(solution)/shard_map/ppermute | solution.py:267
  16.9 11.9 %collective-permute-start = (bf16[512,1024]{1,0:T(8,128)(2,1)S(1)}, bf16[512,1024]{1,0:T(8,128)(2,1)S(1)}, u32[]{:S(2)}, u32[]{:S(2)}) collective-permute-start(bf16[512,1024]{1,0:T(8,128)(2,1)S(1)} %bitcast.8), channel_id=1, source_target_pairs={{0,16},{16,0},{1,17},{17,1},{2,18},{18,2},{3,19},{19,3},{4,20},{20... | collective-permute-start | bytes 3145736 | tf_op jit(solution)/shard_map/ppermute | solution.py:277
  31.4 23.1 %all-to-all-start.1 = ((bf16[32,32,128]{2,1,0:T(8,128)(2,1)}), bf16[32,32,128]{2,1,0:T(8,128)(2,1)S(1)}, u32[]{:S(2)}, u32[]{:S(2)}) async-start(bf16[32,32,128]{2,1,0:T(8,128)(2,1)} %get-tuple-element.40), calls=%async_computation.1 | async-start | bytes 524288 | tf_op jit(solution)/shard_map/all_to_all | solution.py:304
  39.2 10.8 %collective-permute-start.3 = (bf16[144,128]{1,0:T(8,128)(2,1)S(1)}, bf16[144,128]{1,0:T(8,128)(2,1)S(1)}, u32[]{:S(2)}, u32[]{:S(2)}) collective-permute-start(bf16[144,128]{1,0:T(8,128)(2,1)S(1)} %get-tuple-element.41), channel_id=1, source_target_pairs={{0,6},{1,3},{2,0},{3,5},{4,2},{5,7},{6,4},{7,1},{16,21},{17,20},{1... | collective-permute-start | bytes 110600 | tf_op jit(solution)/shard_map/ppermute | solution.py:298
  45.5 5.9 %collective-permute-start.4 = (bf16[144,128]{1,0:T(8,128)(2,1)S(1)}, bf16[144,128]{1,0:T(8,128)(2,1)S(1)}, u32[]{:S(2)}, u32[]{:S(2)}) collective-permute-start(bf16[144,128]{1,0:T(8,128)(2,1)S(1)} %get-tuple-element.42), channel_id=1, source_target_pairs={{0,0},{1,1},{2,2},{3,3},{4,4},{5,5},{6,6},{7,7},{16,23},{17,18},{1... | collective-permute-start | bytes 110600 | tf_op jit(solution)/shard_map/ppermute | solution.py:298
  47.7 5.7 %collective-permute-start.6 = (bf16[4,128,128]{2,1,0:T(8,128)(2,1)S(1)}, bf16[4,128,128]{2,1,0:T(8,128)(2,1)S(1)}, u32[]{:S(2)}, u32[]{:S(2)}) collective-permute-start(bf16[4,128,128]{2,1,0:T(8,128)(2,1)S(1)} %get-tuple-element.45), channel_id=1, source_target_pairs={{0,16},{16,0},{1,17},{17,1},{2,18},{18,2},{3,19},{19,3},{4,20},{20... | collective-permute-start | bytes 393224 | tf_op jit(solution)/shard_map/ppermute | solution.py:299
  51.4 3.1 %collective-permute-start.5 = (bf16[80,128]{1,0:T(8,128)(2,1)S(1)}, bf16[80,128]{1,0:T(8,128)(2,1)S(1)}, u32[]{:S(2)}, u32[]{:S(2)}) collective-permute-start(bf16[80,128]{1,0:T(8,128)(2,1)S(1)} %get-tuple-element.43), channel_id=1, source_target_pairs={{0,16},{16,0},{1,17},{17,1},{2,18},{18,2},{3,19},{19,3},{4,20},{20... | collective-permute-start | bytes 61448 | tf_op jit(solution)/shard_map/ppermute | solution.py:303
  55.6 27.3 %copy-start = (f32[1,256,64]{1,2,0:T(8,128)S(1)}, f32[1,256,64]{1,2,0:T(8,128)}, u32[]{:S(2)}) copy-start(f32[1,256,64]{1,2,0:T(8,128)} %param.5) | copy-start | bytes 196612
  55.6 27.3 %all-to-all-start.2 = ((bf16[16,88,128]{2,1,0:T(8,128)(2,1)}), bf16[16,88,128]{2,1,0:T(8,128)(2,1)S(1)}, u32[]{:S(2)}, u32[]{:S(2)}) async-start(bf16[16,88,128]{2,1,0:T(8,128)(2,1)} %middle.1), calls=%async_computation.2 | async-start | bytes 720896 | tf_op jit(solution)/shard_map/all_to_all | solution.py:311
  68.3 8.4 %collective-permute-start.7 = (bf16[2,128,128]{2,1,0:T(8,128)(2,1)S(1)}, bf16[2,128,128]{2,1,0:T(8,128)(2,1)S(1)}, u32[]{:S(2)}, u32[]{:S(2)}) collective-permute-start(bf16[2,128,128]{2,1,0:T(8,128)(2,1)S(1)} %get-tuple-element.52), channel_id=1, source_target_pairs={{0,9},{1,8},{8,1},{9,0},{2,11},{3,10},{10,3},{11,2},{4,13},{5,12},... | collective-permute-start | bytes 196616 | tf_op jit(solution)/shard_map/ppermute | solution.py:308
  71.5 6.4 %collective-permute-start.8 = (bf16[2,128,128]{2,1,0:T(8,128)(2,1)S(1)}, bf16[2,128,128]{2,1,0:T(8,128)(2,1)S(1)}, u32[]{:S(2)}, u32[]{:S(2)}) collective-permute-start(bf16[2,128,128]{2,1,0:T(8,128)(2,1)S(1)} %get-tuple-element.53), channel_id=1, source_target_pairs={{0,8},{8,0},{1,9},{9,1},{2,10},{10,2},{3,11},{11,3},{4,12},{12,4},... | collective-permute-start | bytes 196616 | tf_op jit(solution)/shard_map/ppermute | solution.py:309
  74.2 5.3 %collective-permute-start.9 = (bf16[2,128,128]{2,1,0:T(8,128)(2,1)S(1)}, bf16[2,128,128]{2,1,0:T(8,128)(2,1)S(1)}, u32[]{:S(2)}, u32[]{:S(2)}) collective-permute-start(bf16[2,128,128]{2,1,0:T(8,128)(2,1)S(1)} %get-tuple-element.54), channel_id=1, source_target_pairs={{0,1},{1,0},{2,3},{3,2},{4,5},{5,4},{6,7},{7,6},{8,9},{9,8},{10,11... | collective-permute-start | bytes 196616 | tf_op jit(solution)/shard_map/ppermute | solution.py:310
  83.6 4.9 %collective-permute-start.10 = (f32[64,128]{1,0:T(8,128)S(1)}, f32[64,128]{1,0:T(8,128)S(1)}, u32[]{:S(2)}, u32[]{:S(2)}) collective-permute-start(f32[64,128]{1,0:T(8,128)S(1)} %get-tuple-element.56.mine), channel_id=1, source_target_pairs={{0,16},{16,0},{1,17},{17,1},{2,18},{18,2},{3,19},{19,3},{4,20},{20... | collective-permute-start | bytes 98312 | tf_op jit(solution)/shard_map/ppermute | solution.py:319
